TPU v7x, 512 devices: a whole 4x8x8 slice. The times are simulated.
512 devices in a mesh: ctx: 64 (over y, z), tp: 8 (over x, core).
Axes of the slice: x: 4, y: 8, z: 8, core: 2. Of those that a mesh axis runs over, the one named last changes fastest.
Arguments:
- queries: bfloat16 [32768, 4096], P('ctx', 'tp'), may hold values from -400 to 400
- keys: bfloat16 [32768, 1024], P('ctx', 'tp'), may hold values from -6 to 6
- values: bfloat16 [32768, 1024], P('ctx', 'tp'), may hold values from -10 to 10
- gates: float32 [32], P('tp'), may hold values from -1 to 4
- out_weight: bfloat16 [4096, 4096], P('tp'), may hold values from -0.09375 to 0.09375
Outputs:
- mixed: bfloat16 [32768, 4096], P(('ctx', 'tp'))
All inputs are finite; a program needn't handle non-finite values.
Results may differ from a plain program's by a relative error of at most 0.017.
Values may be sent and summed in bfloat16 or wider, within the bound.
No kernel may reach another device: no remote copies, remote signals or barrier semaphores. Data moves between devices by JAX's collectives and lax.ppermute only.
A program may use at most 128 MiB of HBM per device.

v0:
```python
import math

import jax
import jax.numpy as jnp
from jax import lax
from jax.sharding import PartitionSpec as P

H = 32
KVH = 8
HD = 128
SEGLEN = 2048


def shifted(block, axis, distance):
    devices = range(lax.axis_size(axis))
    route = [(i - distance, i) for i in devices if i - distance in devices]
    return lax.ppermute(block, axis, route)


def entering(value, axis, combine, identity):
    peers, place = (lax.axis_size(axis), lax.axis_index(axis))
    everything = jax.tree.map(lambda part: lax.all_gather(part, axis), value)
    start = jax.tree.map(
        lambda part, zero: jnp.broadcast_to(jnp.asarray(zero, part.dtype), part.shape),
        value,
        identity,
    )

    def hop(k, before):
        reached = k < place
        new = combine(before, jax.tree.map(lambda part: part[k], everything))
        return jax.tree.map(lambda a, b: jnp.where(reached, a, b), new, before)

    return lax.fori_loop(0, peers, hop, start)


def feature_map(values_in):
    return jax.nn.elu(values_in.astype(jnp.float32)) + 1.0


def join_blocks(earlier, later_part):
    closes_here = later_part[4][0] > 0.5
    done_delta = jnp.where(closes_here, earlier[0] + earlier[2] + later_part[0], earlier[0])
    done_norm = jnp.where(closes_here, earlier[1] + earlier[3] + later_part[1], earlier[1])
    open_delta = jnp.where(closes_here, later_part[2], earlier[2] + later_part[2])
    open_norm = jnp.where(closes_here, later_part[3], earlier[3] + later_part[3])
    closed_flag = jnp.maximum(earlier[4], later_part[4])
    return (done_delta, done_norm, open_delta, open_norm, closed_flag)


def on_device(queries, keys, values, gates, out_weight):
    row_count = queries.shape[0]
    span_count = SEGLEN // row_count
    kv_local = keys.shape[1] // HD
    group_size = H // KVH
    device_index = lax.axis_index("ctx")
    position = device_index % span_count
    key_parts = []
    value_parts = []
    for distance in range(span_count - 1, 0, -1):
        earlier_keys, earlier_values = shifted((keys, values), "ctx", distance)
        key_parts.append(earlier_keys)
        value_parts.append(earlier_values)
    key_all = jnp.concatenate(key_parts + [keys], axis=0)
    value_all = jnp.concatenate(value_parts + [values], axis=0)
    key_span = span_count * row_count
    key_pos = (position - (span_count - 1)) * row_count + jnp.arange(key_span)
    query_pos = position * row_count + jnp.arange(row_count)
    visible = (key_pos[None, :] >= 0) & (key_pos[None, :] <= query_pos[:, None])
    query_heads = queries.reshape(row_count, kv_local, group_size, HD)
    key_heads = key_all.reshape(key_span, kv_local, HD)
    value_heads = value_all.reshape(key_span, kv_local, HD)
    scores = jnp.einsum(
        "tkgd,skd->kgts", query_heads, key_heads, preferred_element_type=jnp.float32
    ) / math.sqrt(HD)
    scores = jnp.where(visible[None, None], scores, -jnp.inf)
    row_max = jnp.max(scores, axis=-1, keepdims=True)
    exponent = jnp.exp(scores - row_max)
    weights = (exponent / jnp.sum(exponent, axis=-1, keepdims=True)).astype(jnp.bfloat16)
    local_out = jnp.einsum(
        "kgts,ske->tkge", weights, value_heads, preferred_element_type=jnp.float32
    )
    key_feat = feature_map(keys).reshape(row_count, kv_local, HD)
    delta_mem = jnp.einsum(
        "tkd,tke->kde",
        key_feat,
        values.astype(jnp.float32).reshape(row_count, kv_local, HD),
        precision=lax.Precision.HIGHEST,
    )
    norm_term = jnp.sum(key_feat, axis=0)
    closes = (position == span_count - 1).astype(jnp.float32)
    leaf_state = (
        delta_mem * closes,
        norm_term * closes,
        delta_mem * (1.0 - closes),
        norm_term * (1.0 - closes),
        closes.reshape(1),
    )
    identity = (
        jnp.zeros_like(delta_mem),
        jnp.zeros_like(norm_term),
        jnp.zeros_like(delta_mem),
        jnp.zeros_like(norm_term),
        jnp.zeros((1,), jnp.float32),
    )
    prefix_state = entering(leaf_state, "ctx", join_blocks, identity)
    memory = prefix_state[0]
    norm_sum = prefix_state[1]
    query_feat = feature_map(query_heads)
    numerator = jnp.einsum("tkgd,kde->tkge", query_feat, memory, precision=lax.Precision.HIGHEST)
    denominator = jnp.einsum("tkgd,kd->tkg", query_feat, norm_sum, precision=lax.Precision.HIGHEST)
    retrieved = numerator / jnp.maximum(denominator, 1.0)[..., None]
    gate_share = jax.nn.sigmoid(gates).reshape(kv_local, group_size)[None, :, :, None]
    attended = (gate_share * retrieved + (1.0 - gate_share) * local_out).astype(jnp.bfloat16)
    attended = attended.reshape(row_count, kv_local * group_size * HD)
    return lax.psum_scatter(
        jnp.dot(attended, out_weight, preferred_element_type=jnp.float32).astype(jnp.bfloat16),
        "tp",
        scatter_dimension=0,
        tiled=True,
    )


def solution(mesh):
    placed = (P("ctx", "tp"), P("ctx", "tp"), P("ctx", "tp"), P("tp"), P("tp", None))
    return jax.shard_map(
        on_device, mesh=mesh, in_specs=placed, out_specs=P(("ctx", "tp"), None), check_vma=False
    )
```

profile of v0, /device:TPU:1, one launch (start us, length us, event | category | flops | bytes accessed | tf_op | source)
XLA Modules:
  0.0 529.7 jit_solution(2006273136216791242)
XLA Ops:
  6.5 2.1 broadcast_multiply_fusion
  9.4 1.7 copy.20
  11.1 5.5 %collective-permute-start.2 = (bf16[512,128]{0,1:T(8,128)(2,1)}, bf16[512,128]{0,1:T(8,128)(2,1)}, u32[]{:S(2)}, u32[]{:S(2)}) collective-permute-start(bf16[512,128]{0,1:T(8,128)(2,1)} %copy.20), channel_id=1, source_target_pairs={{0,8},{8,16},{16,24},{24,32},{32,40},{40,48},{48,56},{56,64},{64,7... | collective-permute-start | bytes 393224 | tf_op jit(solution)/shard_map/ppermute | solution.py:17
  16.6 5.8 %collective-permute-start.1 = (bf16[512,128]{0,1:T(8,128)(2,1)}, bf16[512,128]{0,1:T(8,128)(2,1)}, u32[]{:S(2)}, u32[]{:S(2)}) collective-permute-start(bf16[512,128]{0,1:T(8,128)(2,1)} %copy.20), channel_id=1, source_target_pairs={{0,16},{8,24},{16,32},{24,40},{32,48},{40,56},{48,64},{56,72},{64,... | collective-permute-start | bytes 393224 | tf_op jit(solution)/shard_map/ppermute | solution.py:17
  22.4 5.5 %collective-permute-start.4 = (bf16[512,128]{1,0:T(8,128)(2,1)}, bf16[512,128]{1,0:T(8,128)(2,1)S(1)}, u32[]{:S(2)}, u32[]{:S(2)}) collective-permute-start(bf16[512,128]{1,0:T(8,128)(2,1)} %param.8), channel_id=1, source_target_pairs={{0,16},{8,24},{16,32},{24,40},{32,48},{40,56},{48,64},{56,72},{64,... | collective-permute-start | bytes 393224 | tf_op jit(solution)/shard_map/ppermute | solution.py:17
  27.9 4.4 collective-permute-start.3
  32.3 2.8 collective-permute-start.5
  39.1 118.4 %all-reduce = f32[64]{0:T(128)S(1)} all-reduce(f32[64]{0:T(128)S(1)} %dynamic-update-slice), channel_id=1, replica_groups=mesh['ctx'=64,'tp'=8] {'ctx'}, use_global_device_ids=true, to_apply=%add | all-reduce | flops 64 | bytes 512
  158.5 32.2 %all-gather.5 = f32[64,1,128]{2,1,0:T(1,128)S(1)} all-gather(f32[1,1,128]{2,1,0:T(1,128)S(1)} %get-tuple-element.282), channel_id=5, replica_groups=mesh['ctx'=64,'tp'=8] {'ctx'}, dimensions={0}, use_global_device_ids=true | all-gather | bytes 33280 | tf_op jit(solution)/shard_map/all_gather | solution.py:22
  190.7 31.9 %all-gather.4 = f32[64,1,128]{2,1,0:T(1,128)S(1)} all-gather(f32[1,1,128]{2,1,0:T(1,128)S(1)} %get-tuple-element.283), channel_id=3, replica_groups=mesh['ctx'=64,'tp'=8] {'ctx'}, dimensions={0}, use_global_device_ids=true | all-gather | bytes 33280 | tf_op jit(solution)/shard_map/all_gather | solution.py:22
  225.4 2.9 collective-permute-start
  228.3 4.2 fusion.5
  232.5 5.7 %copy-done = f32[2048,512,4]{1,0,2:T(8,128)} copy-done((f32[2048,512,4]{1,0,2:T(8,128)}, f32[2048,512,4]{1,0,2:T(8,128)S(1)}, u32[]{:S(2)}) %copy-start) | copy-done | bytes 16777240
  238.2 4.2 fusion.4
  242.5 182.9 %while.20 = (s32[]{:T(128)}, f32[1,128,128]{2,1,0:T(8,128)S(1)}, f32[1,128]{1,0:T(1,128)S(1)}, f32[1,128,128]{2,1,0:T(8,128)S(1)}, f32[1,128]{1,0:T(1,128)S(1)},...) while((s32[]{:T(128)}, f32[1,128,128]{2,1,0:T(8,128)S(1)}, ...), condition=%wide.region_2.3_spmd.clone, body=%wide.region_1.2_spmd.clone.sunk | while | flops 148613 | bytes 396462 | solution.py:34
  243.7 1.5 fusion.65
  246.6 1.5 fusion.65
  249.5 1.5 fusion.65
  252.3 1.5 fusion.65
  255.2 1.5 fusion.65
  258.0 1.5 fusion.65
  260.9 1.5 fusion.65
  263.8 1.5 fusion.65
  266.6 1.5 fusion.65
  269.5 1.5 fusion.65
  272.3 1.5 fusion.65
  275.2 1.5 fusion.65
  278.0 1.5 fusion.65
  280.9 1.5 fusion.65
  283.8 1.5 fusion.65
  286.6 1.5 fusion.65
  289.5 1.5 fusion.65
  292.3 1.5 fusion.65
  295.2 1.5 fusion.65
  298.1 1.5 fusion.65
  300.9 1.5 fusion.65
  303.8 1.5 fusion.65
  306.6 1.5 fusion.65
  309.5 1.5 fusion.65
  312.4 1.5 fusion.65
  315.2 1.5 fusion.65
  318.1 1.5 fusion.65
  320.9 1.5 fusion.65
  346.7 1.5 fusion.65
  401.0 1.5 fusion.65
  427.3 8.8 %fusion.20 = bf16[512,1,4,128]{0,3,2,1:T(8,128)(2,1)S(1)} fusion(f32[4,512]{1,0:T(4,128)} %fusion.4, f32[4,512]{1,0:T(4,128)S(1)} %get-tuple-element.284, f32[2048,512,4]{1,0,2:T(8,128)} %copy-done, pred[512,2048]{0,1:T(8,128)(4,1)S(1)} %compare_and_fusion, f32[1,128,512,4]{2,1,3,0:T(8,128)S(1)} %convolution_bitcast_fusion, bf16[512,128]{0,1:T(8,128)(2,1)} %copy.20, ...), kind=kOutput, calls=%fused_computation.32 | convolution fusion | flops 1098121216 | bytes 19947552 | tf_op jit(solution)/shard_map/kgts,ske->tkge/dot_general | solution.py:80
  436.1 4.4 convolution_convert_fusion
  440.5 82.7 %reduce-scatter.2.cloned.1.call-done = bf16[64,4096]{1,0:T(8,128)(2,1)} async-done(((bf16[512,4096]{1,0:T(8,128)(2,1)}), bf16[64,4096]{1,0:T(8,128)(2,1)}) %reduce-scatter.2.cloned.1.call-update) | async-done | bytes 524304 | tf_op jit(solution)/shard_map/reduce_scatter | solution.py:116
  (199 shorter events, 145.1 us)
Async XLA Ops:
  6.5 235.9 %all-gather.11.cloned.1.call-start = ((), (), s32[]{:S(2)}) async-start(), calls=%async_computation.3 | async-start | bytes 4259840 | tf_op jit(solution)/shard_map/all_gather | solution.py:22
  8.6 233.8 %all-gather.9.cloned.1.call-start = ((), (), s32[]{:S(2)}) async-start(), calls=%async_computation.2 | async-start | bytes 4259840 | tf_op jit(solution)/shard_map/all_gather | solution.py:22
  9.4 513.8 %reduce-scatter.2.cloned.1.call-start = ((), (), s32[]{:S(2)}) async-start(), calls=%async_computation.1 | async-start | bytes 4718592 | tf_op jit(solution)/shard_map/reduce_scatter | solution.py:116
  11.1 416.2 %collective-permute-start.2 = (bf16[512,128]{0,1:T(8,128)(2,1)}, bf16[512,128]{0,1:T(8,128)(2,1)}, u32[]{:S(2)}, u32[]{:S(2)}) collective-permute-start(bf16[512,128]{0,1:T(8,128)(2,1)} %copy.20), channel_id=1, source_target_pairs={{0,8},{8,16},{16,24},{24,32},{32,40},{40,48},{48,56},{56,64},{64,7... | collective-permute-start | bytes 393224 | tf_op jit(solution)/shard_map/ppermute | solution.py:17
  16.6 410.7 %collective-permute-start.1 = (bf16[512,128]{0,1:T(8,128)(2,1)}, bf16[512,128]{0,1:T(8,128)(2,1)}, u32[]{:S(2)}, u32[]{:S(2)}) collective-permute-start(bf16[512,128]{0,1:T(8,128)(2,1)} %copy.20), channel_id=1, source_target_pairs={{0,16},{8,24},{16,32},{24,40},{32,48},{40,56},{48,64},{56,72},{64,... | collective-permute-start | bytes 393224 | tf_op jit(solution)/shard_map/ppermute | solution.py:17
  22.4 203.0 %collective-permute-start.4 = (bf16[512,128]{1,0:T(8,128)(2,1)}, bf16[512,128]{1,0:T(8,128)(2,1)S(1)}, u32[]{:S(2)}, u32[]{:S(2)}) collective-permute-start(bf16[512,128]{1,0:T(8,128)(2,1)} %param.8), channel_id=1, source_target_pairs={{0,16},{8,24},{16,32},{24,40},{32,48},{40,56},{48,64},{56,72},{64,... | collective-permute-start | bytes 393224 | tf_op jit(solution)/shard_map/ppermute | solution.py:17
  27.9 200.5 %collective-permute-start.3 = (bf16[512,128]{1,0:T(8,128)(2,1)}, bf16[512,128]{1,0:T(8,128)(2,1)}, u32[]{:S(2)}, u32[]{:S(2)}) collective-permute-start(bf16[512,128]{1,0:T(8,128)(2,1)} %param.8), channel_id=1, source_target_pairs={{0,24},{8,32},{16,40},{24,48},{32,56},{40,64},{48,72},{56,80},{64,... | collective-permute-start | bytes 393224 | tf_op jit(solution)/shard_map/ppermute | solution.py:17
  32.3 196.1 %collective-permute-start.5 = (bf16[512,128]{1,0:T(8,128)(2,1)}, bf16[512,128]{1,0:T(8,128)(2,1)}, u32[]{:S(2)}, u32[]{:S(2)}) collective-permute-start(bf16[512,128]{1,0:T(8,128)(2,1)} %param.8), channel_id=1, source_target_pairs={{0,8},{8,16},{16,24},{24,32},{32,40},{40,48},{48,56},{56,64},{64,7... | collective-permute-start | bytes 393224 | tf_op jit(solution)/shard_map/ppermute | solution.py:17
  225.4 201.8 %collective-permute-start = (bf16[512,128]{0,1:T(8,128)(2,1)}, bf16[512,128]{0,1:T(8,128)(2,1)}, u32[]{:S(2)}, u32[]{:S(2)}) collective-permute-start(bf16[512,128]{0,1:T(8,128)(2,1)} %copy.20), channel_id=1, source_target_pairs={{0,24},{8,32},{16,40},{24,48},{32,56},{40,64},{48,72},{56,80},{64,... | collective-permute-start | bytes 393224 | tf_op jit(solution)/shard_map/ppermute | solution.py:17
  232.5 5.7 %copy-start = (f32[2048,512,4]{1,0,2:T(8,128)}, f32[2048,512,4]{1,0,2:T(8,128)S(1)}, u32[]{:S(2)}) copy-start(f32[2048,512,4]{1,0,2:T(8,128)S(1)} %get-tuple-element.285) | copy-start | bytes 50331652
  427.3 8.8 %copy-start.1 = (bf16[512,4096]{1,0:T(8,128)(2,1)S(1)}, bf16[512,4096]{1,0:T(8,128)(2,1)}, u32[]{:S(2)}) copy-start(bf16[512,4096]{1,0:T(8,128)(2,1)} %param.11) | copy-start | bytes 12582916
Sparse Core Ops, SparseCore 0:
  10.4 100.4 all-gather.10
  113.9 83.3 all-gather.8
  440.6 82.5 reduce-scatter.1
where the time goes:
time: 536 us; the launch traced here: 530 us
  other arithmetic  191 us (36%)
  blocking collectives  182 us (34%)
  waiting for transfers between devices  83.4 us (16%)
  starting transfers between devices  27 us (5%)
  matrix products  20.5 us (4%)
  between operations  13.2 us (2%)
  local copies, waits for them, and re-layouts  9.94 us (2%)
    select_n x128, other arithmetic, hop(): return jax.tree.map(lambda a, b: jnp.where(reached, a, b), new, before)  140 us
    unnamed x1, blocking collectives  118 us
    reduce_scatter x1, waiting for transfers between devices, on_device(): lax.psum_scatter(jnp.dot(attended, out_weight, preferred_element_type=jnp...  82.7 us
    all_gather x2, blocking collectives, entering(): everything = jax.tree.map(lambda part: lax.all_gather(part, axis), value)  64.1 us
    gt x64, other arithmetic, join_blocks(): closes_here = later_part[4][0] > 0.5  41 us
    ppermute x6, starting transfers between devices, shifted(): return lax.ppermute(block, axis, route)  26.9 us
  transfers between devices with their start and end apart: 9, of which 1 were waited for; matrix products, arithmetic and copies ran while one was open for 38% of the time, Pallas kernels for 0%

commit v1 on v0

v1 whole, which is shorter than its diff:
```python
import functools
import math

import jax
import jax.numpy as jnp
from jax import lax
from jax.experimental import pallas as pl
from jax.experimental.pallas import tpu as pltpu
from jax.sharding import PartitionSpec as P

H = 32
KVH = 8
HD = 128
GROUP = H // KVH
ROWS = 512
SPAN = 4
BLOCK = 64
N_CTX = 64
N_TP = 8
CHUNK = 256
LOG2E = 1.4426950408889634
SCALE = LOG2E / math.sqrt(HD)
MASKED = -1e30
F32 = jnp.float32
BF16 = jnp.bfloat16
VM = pl.BlockSpec(memory_space=pltpu.VMEM)
SM = pl.BlockSpec(memory_space=pltpu.SMEM)
NT = (((1,), (1,)), ((), ()))
TN = (((0,), (0,)), ((), ()))


def feature_map(x):
    return jnp.where(x > 0.0, x + 1.0, jnp.exp(jnp.minimum(x, 0.0)))


def split_two(x):
    high = x.astype(BF16)
    return high, (x - high.astype(F32)).astype(BF16)


def call(kernel, out_shape, cost, **kw):
    flops, read, exps = cost
    return pl.pallas_call(
        kernel,
        out_shape=out_shape,
        compiler_params=pltpu.CompilerParams(vmem_limit_bytes=24 * 1024 * 1024),
        cost_estimate=pl.CostEstimate(flops=flops, bytes_accessed=read, transcendentals=exps),
        **kw,
    )


def delta_kernel(k_ref, v_ref, kv_ref, d_ref):
    k = k_ref[...]
    v = v_ref[...]
    kv_ref[:, :HD] = k
    kv_ref[:, HD:] = v
    feat = feature_map(k.astype(F32))
    high, low = split_two(feat)
    d_ref[:HD, :] = lax.dot_general(v, high, TN, preferred_element_type=F32) + lax.dot_general(
        v, low, TN, preferred_element_type=F32
    )
    d_ref[HD:, :] = jnp.broadcast_to(jnp.sum(feat, axis=0, keepdims=True), (8, HD))


def delta_call(keys, values):
    return call(
        delta_kernel,
        (jax.ShapeDtypeStruct((ROWS, 2 * HD), BF16), jax.ShapeDtypeStruct((HD + 8, HD), F32)),
        (2 * 2 * ROWS * HD * HD, 600000, ROWS * HD),
        in_specs=[VM, VM],
        out_specs=(VM, VM),
    )(keys, values)


def values_and_ones(v):
    return jnp.concatenate([v, jnp.ones_like(v)], axis=1)


def own_kernel(q_ref, k_ref, v_ref, acc_ref, top_ref):
    k = k_ref[...]
    wide = values_and_ones(v_ref[...])
    for r in range(ROWS // CHUNK):
        rows = slice(r * CHUNK, (r + 1) * CHUNK)
        seen = (r + 1) * CHUNK
        query_pos = r * CHUNK + lax.broadcasted_iota(jnp.int32, (CHUNK, seen), 0)
        key_pos = lax.broadcasted_iota(jnp.int32, (CHUNK, seen), 1)
        visible = key_pos <= query_pos
        for h in range(GROUP):
            q = q_ref[rows, h * HD : (h + 1) * HD]
            s = lax.dot_general(q, k[:seen], NT, preferred_element_type=F32)
            s = jnp.where(visible, s, MASKED)
            top = jnp.max(s, axis=1, keepdims=True)
            p = jnp.exp2((s - top) * SCALE).astype(BF16)
            acc_ref[h, rows, :] = jnp.dot(p, wide[:seen], preferred_element_type=F32)
            top_ref[h, rows, :] = jnp.broadcast_to(top, (CHUNK, HD))


def own_call(queries, keys, values):
    return call(
        own_kernel,
        (
            jax.ShapeDtypeStruct((GROUP, ROWS, 2 * HD), F32),
            jax.ShapeDtypeStruct((GROUP, ROWS, HD), F32),
        ),
        (GROUP * ROWS * ROWS * HD * 4, 4000000, GROUP * ROWS * ROWS),
        in_specs=[VM, VM, VM],
        out_specs=(VM, VM),
    )(queries, keys, values)


def last_kernel(
    place_ref, gate_ref, q_ref, kv1_ref, kv2_ref, kv3_ref, acc_in, top_in, mem_ref, keep_ref, send_ref, acc_ref, top_ref, out_ref
):
    position = place_ref[0]
    x = place_ref[1]
    core = place_ref[2]
    acc_ref[...] = acc_in[...]
    top_ref[...] = top_in[...]
    for d, kv_ref in ((1, kv1_ref), (2, kv2_ref), (3, kv3_ref)):

        @pl.when(position >= d)
        def _():
            k = kv_ref[:, :HD]
            wide = values_and_ones(kv_ref[:, HD:])
            for r in range(ROWS // CHUNK):
                rows = slice(r * CHUNK, (r + 1) * CHUNK)
                for h in range(GROUP):
                    q = q_ref[rows, h * HD : (h + 1) * HD]
                    s = lax.dot_general(q, k, NT, preferred_element_type=F32)
                    before = top_ref[h, rows, :]
                    top = jnp.maximum(before, jnp.max(s, axis=1, keepdims=True))
                    shrink = jnp.exp2((before - top) * SCALE)
                    p = jnp.exp2((s - top[:, :1]) * SCALE).astype(BF16)
                    pv = jnp.dot(p, wide, preferred_element_type=F32)
                    acc_ref[h, rows, :] = acc_ref[h, rows, :] * jnp.concatenate([shrink, shrink], axis=1) + pv
                    top_ref[h, rows, :] = top

    mem = jnp.concatenate(
        [mem_ref[:HD, :], jnp.broadcast_to(mem_ref[HD : HD + 1, :], (HD, HD))], axis=0
    )
    mem_high, mem_low = split_two(mem)
    mem_twice = jnp.concatenate([mem_high, mem_high], axis=1)
    for h in range(GROUP):
        gate = jax.nn.sigmoid(jnp.full((1, HD), gate_ref[h], F32))
        feat = feature_map(q_ref[:, h * HD : (h + 1) * HD].astype(F32))
        high, low = split_two(feat)
        both = jnp.concatenate([high, low], axis=1)
        read = lax.dot_general(both, mem_twice, NT, preferred_element_type=F32)
        read = read + lax.dot_general(high, mem_low, NT, preferred_element_type=F32)
        retrieved = read[:, :HD] / jnp.maximum(read[:, HD:], 1.0)
        local = acc_ref[h, :, :HD] / acc_ref[h, :, HD:]
        out_ref[:, h * HD : (h + 1) * HD] = (gate * retrieved + (1.0 - gate) * local).astype(BF16)
    for b in range(N_TP // 2):
        mine = pl.multiple_of((2 * b + core) * BLOCK, BLOCK)
        other = pl.multiple_of((2 * b + 1 - core) * BLOCK, BLOCK)
        keep_ref[b * BLOCK : (b + 1) * BLOCK, :] = out_ref[pl.ds(mine, BLOCK), :]
        send_ref[b * BLOCK : (b + 1) * BLOCK, :] = out_ref[pl.ds(other, BLOCK), :]


def last_call(place, gates, queries, kv1, kv2, kv3, acc, top, mem):
    half = jax.ShapeDtypeStruct((ROWS // 2, GROUP * HD), BF16)
    return call(
        last_kernel,
        (half, half),
        (3 * GROUP * ROWS * ROWS * HD * 4, 6000000, 3 * GROUP * ROWS * ROWS),
        in_specs=[SM, SM] + [VM] * 7,
        out_specs=(VM, VM),
        scratch_shapes=[
            pltpu.VMEM((GROUP, ROWS, 2 * HD), F32),
            pltpu.VMEM((GROUP, ROWS, HD), F32),
            pltpu.VMEM((ROWS, GROUP * HD), BF16),
        ],
    )(place, gates, queries, kv1, kv2, kv3, acc, top, mem)


def project_kernel(keep_ref, got_ref, w_own_ref, w_other_ref, out_ref):
    out = jnp.dot(keep_ref[...], w_own_ref[...], preferred_element_type=F32)
    out = out + jnp.dot(got_ref[...], w_other_ref[...], preferred_element_type=F32)
    out_ref[...] = out.astype(BF16)


def project_call(keep, got, w_own, w_other):
    rows, depth = keep.shape
    width = w_own.shape[1]
    tile = 512
    whole = pl.BlockSpec((rows, depth), lambda j: (0, 0))
    strip = pl.BlockSpec((depth, tile), lambda j: (0, j))
    return call(
        project_kernel,
        jax.ShapeDtypeStruct((rows, width), BF16),
        (4 * rows * depth * width, 12000000, 0),
        grid=(width // tile,),
        in_specs=[whole, whole, strip, strip],
        out_specs=pl.BlockSpec((rows, tile), lambda j: (0, j)),
    )(keep, got, w_own, w_other)


def along_z(step):
    return [(i, i + step) for i in range(N_CTX) if i // SPAN == (i + step) // SPAN]


def along_y(step):
    return [(i, i + 8 * step) for i in range(N_CTX - 8 * step)]


def swap(bit, size):
    return [(i, i ^ bit) for i in range(size)]


def on_device(queries, keys, values, gates, out_weight):
    ctx = lax.axis_index("ctx")
    tp = lax.axis_index("tp")
    place = jnp.stack([ctx % SPAN, tp // 2, tp % 2]).astype(jnp.int32)
    kv, delta = delta_call(keys, values)
    kv1, kv2, kv3 = [lax.ppermute(kv, "ctx", along_z(d)) for d in (1, 2, 3)]
    w_other = lax.ppermute(out_weight, "tp", swap(1, N_TP))
    before = lax.ppermute(delta, "ctx", along_y(1))
    before = before + lax.ppermute(delta + before, "ctx", along_y(2))
    before = before + lax.ppermute(delta + before, "ctx", along_y(4))
    lower = (ctx % 8) < SPAN
    mem = before + lax.ppermute(before + jnp.where(lower, delta, 0.0), "ctx", swap(4, N_CTX))
    mem = mem + lax.ppermute(mem, "ctx", swap(1, N_CTX))
    mem = mem + lax.ppermute(mem, "ctx", swap(2, N_CTX))
    acc, top = own_call(queries, keys, values)
    keep, send = last_call(place, gates, queries, kv1, kv2, kv3, acc, top, mem)
    got = lax.ppermute(send, "tp", swap(1, N_TP))
    partial = project_call(keep, got, out_weight, w_other)
    parts = lax.all_to_all(
        partial.reshape(N_TP // 2, BLOCK, -1), "tp", 0, 0, tiled=True,
        axis_index_groups=[[0, 2, 4, 6], [1, 3, 5, 7]],
    )
    return jnp.sum(parts.astype(F32), axis=0).astype(BF16)


def solution(mesh):
    placed = (P("ctx", "tp"), P("ctx", "tp"), P("ctx", "tp"), P("tp"), P("tp", None))
    return jax.shard_map(
        on_device, mesh=mesh, in_specs=placed, out_specs=P(("ctx", "tp"), None), check_vma=False
    )
```

time: 536 us -> 119 us (0.22)
  the two profiles are of different devices: /device:TPU:1 before, /device:TPU:224 now
where the time goes in v1:
time: 119 us
  waiting for transfers between devices  35.7 us (30%)
  blocking collectives  30.7 us (26%)
  starting transfers between devices  28.8 us (24%)
  Pallas kernels  17 us (14%)
  local copies, waits for them, and re-layouts  4.67 us (4%)
  other arithmetic  1.41 us (1%)
    all_to_all x1, blocking collectives, on_device(): lax.all_to_all(partial.reshape(N_TP // 2, BLOCK, -1), 'tp', 0, 0, tiled=T...  30.7 us
    ppermute x1, waiting for transfers between devices, on_device(): mem = mem + lax.ppermute(mem, 'ctx', swap(1, N_CTX))  13.6 us
    ppermute x1, waiting for transfers between devices, on_device(): before = before + lax.ppermute(delta + before, 'ctx', along_y(4))  8.79 us
    pallas_call x1, Pallas kernels, last_call(): call(last_kernel, (half, half), (3 * GROUP * ROWS * ROWS * HD * 4, 600000...  8.57 us
    ppermute x1, starting transfers between devices, on_device(): lax.ppermute(before + jnp.where(lower, delta, 0.0), 'ctx', swap(4, N_CTX))  8.22 us
    pallas_call x1, Pallas kernels, project_call(): call(project_kernel, jax.ShapeDtypeStruct((rows, width), BF16), (4 * rows...  6.73 us
    ppermute x1, waiting for transfers between devices, on_device(): before = before + lax.ppermute(delta + before, 'ctx', along_y(2))  6.38 us
    ppermute x1, waiting for transfers between devices, on_device(): before = lax.ppermute(delta, 'ctx', along_y(1))  5.09 us
  transfers between devices with their start and end apart: 11, of which 6 were waited for; matrix products, arithmetic and copies ran while one was open for 0% of the time, Pallas kernels for 9%

profile of v1, /device:TPU:224, one launch (start us, length us, event | category | flops | bytes accessed | tf_op | source)
XLA Modules:
  0.0 118.5 jit_solution(12007198903676860566)
XLA Ops:
  0.0 1.9 %collective-permute-start.10 = (bf16[512,4096]{1,0:T(8,128)(2,1)}, bf16[512,4096]{1,0:T(8,128)(2,1)}, u32[]{:S(2)}, u32[]{:S(2)}) collective-permute-start(bf16[512,4096]{1,0:T(8,128)(2,1)} %w_own_ref.1), channel_id=1, source_target_pairs={{0,1},{1,0},{2,3},{3,2},{4,5},{5,4},{6,7},{7,6},{8,9},{9,8},{10,11... | collective-permute-start | bytes 12582920 | tf_op jit(solution)/shard_map/ppermute | solution.py:216
  1.9 0.0 copy-start.1
  1.9 0.9 copy-done.1
  2.8 0.0 copy-start.3
  2.8 0.9 copy-done.3
  3.7 0.0 copy-start.6
  3.7 0.0 copy-start.7
  3.7 0.3 shard_map.55
  4.1 2.6 %collective-permute-start.3 = (f32[136,128]{1,0:T(8,128)S(1)}, f32[136,128]{1,0:T(8,128)S(1)}, u32[]{:S(2)}, u32[]{:S(2)}) collective-permute-start(f32[136,128]{1,0:T(8,128)S(1)} %get-tuple-element.14), channel_id=1, source_target_pairs={{0,64},{8,72},{16,80},{24,88},{32,96},{40,104},{48,112},{56,120},{... | collective-permute-start | bytes 208904 | tf_op jit(solution)/shard_map/ppermute | solution.py:217
  6.7 5.1 %collective-permute-done.3 = f32[136,128]{1,0:T(8,128)S(1)} collective-permute-done((f32[136,128]{1,0:T(8,128)S(1)}, f32[136,128]{1,0:T(8,128)S(1)}, u32[]{:S(2)}, u32[]{:S(2)}) %collective-permute-start.3) | collective-permute-done | bytes 69664 | tf_op jit(solution)/shard_map/ppermute | solution.py:217
  11.8 1.9 %collective-permute-start.4 = (f32[136,128]{1,0:T(8,128)S(1)}, f32[136,128]{1,0:T(8,128)S(1)}, u32[]{:S(2)}, u32[]{:S(2)}) collective-permute-start(f32[136,128]{1,0:T(8,128)S(1)} %add.37), channel_id=1, source_target_pairs={{0,128},{8,136},{16,144},{24,152},{32,160},{40,168},{48,176},{56,1... | collective-permute-start | bytes 208904 | tf_op jit(solution)/shard_map/ppermute | solution.py:218
  13.7 6.4 %collective-permute-done.4 = f32[136,128]{1,0:T(8,128)S(1)} collective-permute-done((f32[136,128]{1,0:T(8,128)S(1)}, f32[136,128]{1,0:T(8,128)S(1)}, u32[]{:S(2)}, u32[]{:S(2)}) %collective-permute-start.4) | collective-permute-done | bytes 69664 | tf_op jit(solution)/shard_map/ppermute | solution.py:218
  20.1 1.3 %collective-permute-start.5 = (f32[136,128]{1,0:T(8,128)S(1)}, f32[136,128]{1,0:T(8,128)S(1)}, u32[]{:S(2)}, u32[]{:S(2)}) collective-permute-start(f32[136,128]{1,0:T(8,128)S(1)} %get-tuple-element.19), channel_id=1, source_target_pairs={{0,256},{8,264},{16,272},{24,280},{32,288},{40,296},{48,304},{56,3... | collective-permute-start | bytes 208904 | tf_op jit(solution)/shard_map/ppermute | solution.py:219
  21.4 8.8 %collective-permute-done.5 = f32[136,128]{1,0:T(8,128)S(1)} collective-permute-done((f32[136,128]{1,0:T(8,128)S(1)}, f32[136,128]{1,0:T(8,128)S(1)}, u32[]{:S(2)}, u32[]{:S(2)}) %collective-permute-start.5) | collective-permute-done | bytes 69664 | tf_op jit(solution)/shard_map/ppermute | solution.py:219
  30.2 8.2 %collective-permute-start.6 = (f32[136,128]{1,0:T(8,128)S(1)}, f32[136,128]{1,0:T(8,128)S(1)}, u32[]{:S(2)}, u32[]{:S(2)}) collective-permute-start(f32[136,128]{1,0:T(8,128)S(1)} %get-tuple-element.17), channel_id=1, source_target_pairs={{0,32},{8,40},{16,48},{24,56},{32,0},{40,8},{48,16},{56,24},{64,96... | collective-permute-start | bytes 208904 | tf_op jit(solution)/shard_map/ppermute | solution.py:221
  38.5 1.3 %collective-permute-start.2 = (bf16[512,256]{1,0:T(8,128)(2,1)S(1)}, bf16[512,256]{1,0:T(8,128)(2,1)S(1)}, u32[]{:S(2)}, u32[]{:S(2)}) collective-permute-start(bf16[512,256]{1,0:T(8,128)(2,1)S(1)} %get-tuple-element.11), channel_id=1, source_target_pairs={{0,24},{32,56},{64,88},{96,120},{128,152},{160,184},{192,216},{224... | collective-permute-start | bytes 786440 | tf_op jit(solution)/shard_map/ppermute | solution.py:215
  39.8 1.3 %collective-permute-start.1 = (bf16[512,256]{1,0:T(8,128)(2,1)S(1)}, bf16[512,256]{1,0:T(8,128)(2,1)S(1)}, u32[]{:S(2)}, u32[]{:S(2)}) collective-permute-start(bf16[512,256]{1,0:T(8,128)(2,1)S(1)} %get-tuple-element.11), channel_id=1, source_target_pairs={{0,16},{8,24},{32,48},{40,56},{64,80},{72,88},{96,112},{104,120},{... | collective-permute-start | bytes 786440 | tf_op jit(solution)/shard_map/ppermute | solution.py:215
  41.0 1.3 %collective-permute-start = (bf16[512,256]{1,0:T(8,128)(2,1)S(1)}, bf16[512,256]{1,0:T(8,128)(2,1)S(1)}, u32[]{:S(2)}, u32[]{:S(2)}) collective-permute-start(bf16[512,256]{1,0:T(8,128)(2,1)S(1)} %get-tuple-element.11), channel_id=1, source_target_pairs={{0,8},{8,16},{16,24},{32,40},{40,48},{48,56},{64,72},{72,80},{80,8... | collective-permute-start | bytes 786440 | tf_op jit(solution)/shard_map/ppermute | solution.py:215
  42.4 0.0 collective-permute-done.6
  42.4 4.6 %collective-permute-start.7 = (f32[136,128]{1,0:T(8,128)S(1)}, f32[136,128]{1,0:T(8,128)S(1)}, u32[]{:S(2)}, u32[]{:S(2)}) collective-permute-start(f32[136,128]{1,0:T(8,128)S(1)} %add.43), channel_id=1, source_target_pairs={{0,8},{8,0},{16,24},{24,16},{32,40},{40,32},{48,56},{56,48},{64,72... | collective-permute-start | bytes 208904 | tf_op jit(solution)/shard_map/ppermute | solution.py:222
  47.0 13.6 %collective-permute-done.7 = f32[136,128]{1,0:T(8,128)S(1)} collective-permute-done((f32[136,128]{1,0:T(8,128)S(1)}, f32[136,128]{1,0:T(8,128)S(1)}, u32[]{:S(2)}, u32[]{:S(2)}) %collective-permute-start.7) | collective-permute-done | bytes 69664 | tf_op jit(solution)/shard_map/ppermute | solution.py:222
  60.6 2.5 %collective-permute-start.8 = (f32[136,128]{1,0:T(8,128)S(1)}, f32[136,128]{1,0:T(8,128)S(1)}, u32[]{:S(2)}, u32[]{:S(2)}) collective-permute-start(f32[136,128]{1,0:T(8,128)S(1)} %add.44), channel_id=1, source_target_pairs={{0,16},{8,24},{16,0},{24,8},{32,48},{40,56},{48,32},{56,40},{64,80... | collective-permute-start | bytes 208904 | tf_op jit(solution)/shard_map/ppermute | solution.py:223
  63.1 0.1 pad_add_fusion.place_ref
  63.2 0.0 copy-start.2
  63.2 0.9 copy-done.2
  64.1 0.0 copy-start.4
  64.1 0.9 copy-done.4
  65.0 0.0 copy-start.5
  65.0 1.0 copy-done.5
  66.0 1.4 %shard_map.56 = (f32[4,512,256]{2,1,0:T(8,128)S(1)}, f32[4,512,128]{2,1,0:T(8,128)S(1)}) custom-call(bf16[512,512]{1,0:T(8,128)(2,1)S(1)} %copy-done.5, bf16[512,128]{1,0:T(8,128)(2,1)S(1)} %copy-done.2, bf16[512,128]{1,0:T(8,128)(2,1)S(1)} %copy-done.4), custom_call_target="tpu_custom_call" | custom-call | flops 536870912 | bytes 4000000 | tf_op jit(solution)/shard_map/pallas_call | solution.py:99
  67.4 0.3 collective-permute-done.8
  67.7 0.0 collective-permute-done.2.kv3_ref
  67.7 0.0 collective-permute-done.1.kv2_ref
  67.7 0.0 collective-permute-done.kv1_ref
  67.8 0.0 copy-done.6
  67.8 0.0 copy-done.7
  67.8 0.0 copy-start
  67.8 8.6 %shard_map.57 = (bf16[256,512]{1,0:T(8,128)(2,1)S(1)}, bf16[256,512]{1,0:T(8,128)(2,1)S(1)}) custom-call(s32[3]{0:T(128)S(1)} %pad_add_fusion.place_ref, f32[4]{0:T(128)S(1)} %copy-done.7, bf16[512,512]{1,0:T(8,128)(2,1)S(1)} %copy-done.6, bf16[512,256]{1,0:T(8,128)(2,1)S(1)} %collective-permute-done.kv1_ref, ...), custom_call_target="tpu_custom_call" | custom-call | flops 1610612736 | bytes 6000000 | tf_op jit(solution)/shard_map/pallas_call | solution.py:162
  76.4 1.9 %collective-permute-start.9 = (bf16[256,512]{1,0:T(8,128)(2,1)S(1)}, bf16[256,512]{1,0:T(8,128)(2,1)S(1)}, u32[]{:S(2)}, u32[]{:S(2)}) collective-permute-start(bf16[256,512]{1,0:T(8,128)(2,1)S(1)} %get-tuple-element.16), channel_id=1, source_target_pairs={{0,1},{1,0},{2,3},{3,2},{4,5},{5,4},{6,7},{7,6},{8,9},{9,8},{10,11... | collective-permute-start | bytes 786440 | tf_op jit(solution)/shard_map/ppermute | solution.py:226
  78.3 1.5 %collective-permute-done.9.got_ref = bf16[256,512]{1,0:T(8,128)(2,1)S(1)} collective-permute-done((bf16[256,512]{1,0:T(8,128)(2,1)S(1)}, bf16[256,512]{1,0:T(8,128)(2,1)S(1)}, u32[]{:S(2)}, u32[]{:S(2)}) %collective-permute-start.9) | collective-permute-done | bytes 262176 | tf_op jit(solution)/shard_map/ppermute | solution.py:226
  79.8 0.0 collective-permute-done.10.w_other_ref
  79.8 0.0 copy-done
  79.8 6.7 %shard_map.58 = bf16[256,4096]{1,0:T(8,128)(2,1)S(1)} custom-call(bf16[256,512]{1,0:T(8,128)(2,1)S(1)} %get-tuple-element.15.keep_ref, bf16[256,512]{1,0:T(8,128)(2,1)S(1)} %collective-permute-done.9.got_ref, bf16[512,4096]{1,0:T(8,128)(2,1)S(1)} %copy-done, bf16[512,4096]{1,0:T(8,128)(2,1)} %collective-permute-done.10.w_other_ref), custom_call_target="tpu_custom_call" | custom-call | flops 2147483648 | bytes 12000000 | tf_op jit(solution)/shard_map/pallas_call | solution.py:188
  86.5 30.7 %all_to_all.5 = bf16[4,64,4096]{2,1,0:T(8,128)(2,1)S(1)} all-to-all(bf16[4,64,4096]{2,1,0:T(8,128)(2,1)S(1)} %bitcast.4), channel_id=1, replica_groups={{0,2,4,6},{1,3,5,7},{8,10,12,14},{9,11,13,15},{16,18,20,22},{17,19,21,2..., dimensions={0} | all-to-all | bytes 4194304 | tf_op jit(solution)/shard_map/all_to_all | solution.py:228
  117.3 1.3 %reduce_sum.12 = bf16[64,4096]{1,0:T(8,128)(2,1)} reduce(bf16[4,64,4096]{2,1,0:T(8,128)(2,1)S(1)} %all_to_all.5, bf16[]{:T(256)} %constant.56.clone.1), dimensions={0}, to_apply=%region_0.1 | reduce | flops 786432 | bytes 2621442 | tf_op jit(solution)/shard_map/reduce_sum | solution.py:232
  (6 shorter events, 0.1 us)
Async XLA Ops:
  0.0 79.8 %collective-permute-start.10 = (bf16[512,4096]{1,0:T(8,128)(2,1)}, bf16[512,4096]{1,0:T(8,128)(2,1)}, u32[]{:S(2)}, u32[]{:S(2)}) collective-permute-start(bf16[512,4096]{1,0:T(8,128)(2,1)} %w_own_ref.1), channel_id=1, source_target_pairs={{0,1},{1,0},{2,3},{3,2},{4,5},{5,4},{6,7},{7,6},{8,9},{9,8},{10,11... | collective-permute-start | bytes 12582920 | tf_op jit(solution)/shard_map/ppermute | solution.py:216
  1.9 0.9 copy-start.1
  2.8 0.9 copy-start.3
  3.7 64.0 %copy-start.6 = (bf16[512,512]{1,0:T(8,128)(2,1)S(1)}, bf16[512,512]{1,0:T(8,128)(2,1)}, u32[]{:S(2)}) copy-start(bf16[512,512]{1,0:T(8,128)(2,1)} %q_ref.3) | copy-start | bytes 1572868
  3.7 64.0 %copy-start.7 = (f32[4]{0:T(128)S(1)}, f32[4]{0:T(128)}, u32[]{:S(2)}) copy-start(f32[4]{0:T(128)} %gate_ref.1) | copy-start | bytes 52
  4.1 7.7 %collective-permute-start.3 = (f32[136,128]{1,0:T(8,128)S(1)}, f32[136,128]{1,0:T(8,128)S(1)}, u32[]{:S(2)}, u32[]{:S(2)}) collective-permute-start(f32[136,128]{1,0:T(8,128)S(1)} %get-tuple-element.14), channel_id=1, source_target_pairs={{0,64},{8,72},{16,80},{24,88},{32,96},{40,104},{48,112},{56,120},{... | collective-permute-start | bytes 208904 | tf_op jit(solution)/shard_map/ppermute | solution.py:217
  11.8 8.3 %collective-permute-start.4 = (f32[136,128]{1,0:T(8,128)S(1)}, f32[136,128]{1,0:T(8,128)S(1)}, u32[]{:S(2)}, u32[]{:S(2)}) collective-permute-start(f32[136,128]{1,0:T(8,128)S(1)} %add.37), channel_id=1, source_target_pairs={{0,128},{8,136},{16,144},{24,152},{32,160},{40,168},{48,176},{56,1... | collective-permute-start | bytes 208904 | tf_op jit(solution)/shard_map/ppermute | solution.py:218
  20.1 10.1 %collective-permute-start.5 = (f32[136,128]{1,0:T(8,128)S(1)}, f32[136,128]{1,0:T(8,128)S(1)}, u32[]{:S(2)}, u32[]{:S(2)}) collective-permute-start(f32[136,128]{1,0:T(8,128)S(1)} %get-tuple-element.19), channel_id=1, source_target_pairs={{0,256},{8,264},{16,272},{24,280},{32,288},{40,296},{48,304},{56,3... | collective-permute-start | bytes 208904 | tf_op jit(solution)/shard_map/ppermute | solution.py:219
  30.2 12.1 %collective-permute-start.6 = (f32[136,128]{1,0:T(8,128)S(1)}, f32[136,128]{1,0:T(8,128)S(1)}, u32[]{:S(2)}, u32[]{:S(2)}) collective-permute-start(f32[136,128]{1,0:T(8,128)S(1)} %get-tuple-element.17), channel_id=1, source_target_pairs={{0,32},{8,40},{16,48},{24,56},{32,0},{40,8},{48,16},{56,24},{64,96... | collective-permute-start | bytes 208904 | tf_op jit(solution)/shard_map/ppermute | solution.py:221
  38.5 29.3 %collective-permute-start.2 = (bf16[512,256]{1,0:T(8,128)(2,1)S(1)}, bf16[512,256]{1,0:T(8,128)(2,1)S(1)}, u32[]{:S(2)}, u32[]{:S(2)}) collective-permute-start(bf16[512,256]{1,0:T(8,128)(2,1)S(1)} %get-tuple-element.11), channel_id=1, source_target_pairs={{0,24},{32,56},{64,88},{96,120},{128,152},{160,184},{192,216},{224... | collective-permute-start | bytes 786440 | tf_op jit(solution)/shard_map/ppermute | solution.py:215
  39.8 28.0 %collective-permute-start.1 = (bf16[512,256]{1,0:T(8,128)(2,1)S(1)}, bf16[512,256]{1,0:T(8,128)(2,1)S(1)}, u32[]{:S(2)}, u32[]{:S(2)}) collective-permute-start(bf16[512,256]{1,0:T(8,128)(2,1)S(1)} %get-tuple-element.11), channel_id=1, source_target_pairs={{0,16},{8,24},{32,48},{40,56},{64,80},{72,88},{96,112},{104,120},{... | collective-permute-start | bytes 786440 | tf_op jit(solution)/shard_map/ppermute | solution.py:215
  41.0 26.7 %collective-permute-start = (bf16[512,256]{1,0:T(8,128)(2,1)S(1)}, bf16[512,256]{1,0:T(8,128)(2,1)S(1)}, u32[]{:S(2)}, u32[]{:S(2)}) collective-permute-start(bf16[512,256]{1,0:T(8,128)(2,1)S(1)} %get-tuple-element.11), channel_id=1, source_target_pairs={{0,8},{8,16},{16,24},{32,40},{40,48},{48,56},{64,72},{72,80},{80,8... | collective-permute-start | bytes 786440 | tf_op jit(solution)/shard_map/ppermute | solution.py:215
  42.4 18.2 %collective-permute-start.7 = (f32[136,128]{1,0:T(8,128)S(1)}, f32[136,128]{1,0:T(8,128)S(1)}, u32[]{:S(2)}, u32[]{:S(2)}) collective-permute-start(f32[136,128]{1,0:T(8,128)S(1)} %add.43), channel_id=1, source_target_pairs={{0,8},{8,0},{16,24},{24,16},{32,40},{40,32},{48,56},{56,48},{64,72... | collective-permute-start | bytes 208904 | tf_op jit(solution)/shard_map/ppermute | solution.py:222
  60.6 7.1 %collective-permute-start.8 = (f32[136,128]{1,0:T(8,128)S(1)}, f32[136,128]{1,0:T(8,128)S(1)}, u32[]{:S(2)}, u32[]{:S(2)}) collective-permute-start(f32[136,128]{1,0:T(8,128)S(1)} %add.44), channel_id=1, source_target_pairs={{0,16},{8,24},{16,0},{24,8},{32,48},{40,56},{48,32},{56,40},{64,80... | collective-permute-start | bytes 208904 | tf_op jit(solution)/shard_map/ppermute | solution.py:223
  63.2 0.9 copy-start.2
  64.1 0.9 copy-start.4
  65.0 1.0 copy-start.5
  67.8 12.0 %copy-start = (bf16[512,4096]{1,0:T(8,128)(2,1)S(1)}, bf16[512,4096]{1,0:T(8,128)(2,1)}, u32[]{:S(2)}) copy-start(bf16[512,4096]{1,0:T(8,128)(2,1)} %w_own_ref.1) | copy-start | bytes 12582916
  76.4 3.4 %collective-permute-start.9 = (bf16[256,512]{1,0:T(8,128)(2,1)S(1)}, bf16[256,512]{1,0:T(8,128)(2,1)S(1)}, u32[]{:S(2)}, u32[]{:S(2)}) collective-permute-start(bf16[256,512]{1,0:T(8,128)(2,1)S(1)} %get-tuple-element.16), channel_id=1, source_target_pairs={{0,1},{1,0},{2,3},{3,2},{4,5},{5,4},{6,7},{7,6},{8,9},{9,8},{10,11... | collective-permute-start | bytes 786440 | tf_op jit(solution)/shard_map/ppermute | solution.py:226

commit v2 on v1

v2 whole, which is shorter than its diff:
```python
import functools
import math

import jax
import jax.numpy as jnp
from jax import lax
from jax.experimental import pallas as pl
from jax.experimental.pallas import tpu as pltpu
from jax.sharding import PartitionSpec as P

H = 32
KVH = 8
HD = 128
GROUP = H // KVH
ROWS = 512
SPAN = 4
BLOCK = 64
N_CTX = 64
N_TP = 8
CHUNK = 256
LOG2E = 1.4426950408889634
SCALE = LOG2E / math.sqrt(HD)
MASKED = -1e30
F32 = jnp.float32
BF16 = jnp.bfloat16
VM = pl.BlockSpec(memory_space=pltpu.VMEM)
SM = pl.BlockSpec(memory_space=pltpu.SMEM)
NT = (((1,), (1,)), ((), ()))
TN = (((0,), (0,)), ((), ()))


def feature_map(x):
    return jnp.where(x > 0.0, x + 1.0, jnp.exp(jnp.minimum(x, 0.0)))


def split_two(x):
    high = x.astype(BF16)
    return high, (x - high.astype(F32)).astype(BF16)


def call(kernel, out_shape, cost, **kw):
    flops, read, exps = cost
    return pl.pallas_call(
        kernel,
        out_shape=out_shape,
        compiler_params=pltpu.CompilerParams(vmem_limit_bytes=24 * 1024 * 1024),
        cost_estimate=pl.CostEstimate(flops=flops, bytes_accessed=read, transcendentals=exps),
        **kw,
    )


def delta_kernel(k_ref, v_ref, kv_ref, d_ref):
    k = k_ref[...]
    v = v_ref[...]
    kv_ref[:, :HD] = k
    kv_ref[:, HD:] = v
    feat = feature_map(k.astype(F32))
    high, low = split_two(feat)
    d_ref[:HD, :] = lax.dot_general(v, high, TN, preferred_element_type=F32) + lax.dot_general(
        v, low, TN, preferred_element_type=F32
    )
    d_ref[HD:, :] = jnp.broadcast_to(jnp.sum(feat, axis=0, keepdims=True), (16, HD))


def delta_call(keys, values):
    return call(
        delta_kernel,
        (jax.ShapeDtypeStruct((ROWS, 2 * HD), BF16), jax.ShapeDtypeStruct((HD + 16, HD), F32)),
        (2 * 2 * ROWS * HD * HD, 600000, ROWS * HD),
        in_specs=[VM, VM],
        out_specs=(VM, VM),
    )(keys, values)


def values_and_ones(v):
    return jnp.concatenate([v, jnp.ones_like(v)], axis=1)


def own_kernel(q_ref, k_ref, v_ref, acc_ref, top_ref):
    k = k_ref[...]
    wide = values_and_ones(v_ref[...])
    for r in range(ROWS // CHUNK):
        rows = slice(r * CHUNK, (r + 1) * CHUNK)
        seen = (r + 1) * CHUNK
        query_pos = r * CHUNK + lax.broadcasted_iota(jnp.int32, (CHUNK, seen), 0)
        key_pos = lax.broadcasted_iota(jnp.int32, (CHUNK, seen), 1)
        visible = key_pos <= query_pos
        for h in range(GROUP):
            q = q_ref[rows, h * HD : (h + 1) * HD]
            s = lax.dot_general(q, k[:seen], NT, preferred_element_type=F32)
            s = jnp.where(visible, s, MASKED)
            top = jnp.max(s, axis=1, keepdims=True)
            p = jnp.exp2((s - top) * SCALE).astype(BF16)
            acc_ref[h, rows, :] = jnp.dot(p, wide[:seen], preferred_element_type=F32)
            top_ref[h, rows, :] = jnp.broadcast_to(top, (CHUNK, HD))


def own_call(queries, keys, values):
    return call(
        own_kernel,
        (
            jax.ShapeDtypeStruct((GROUP, ROWS, 2 * HD), F32),
            jax.ShapeDtypeStruct((GROUP, ROWS, HD), F32),
        ),
        (GROUP * ROWS * ROWS * HD * 4, 4000000, GROUP * ROWS * ROWS),
        in_specs=[VM, VM, VM],
        out_specs=(VM, VM),
    )(queries, keys, values)


def step_kernel(distance, place_ref, q_ref, kv_ref, acc_in, top_in, acc_ref, top_ref):
    @pl.when(place_ref[0] >= distance)
    def _():
        k = kv_ref[:, :HD]
        wide = values_and_ones(kv_ref[:, HD:])
        for r in range(ROWS // CHUNK):
            rows = slice(r * CHUNK, (r + 1) * CHUNK)
            for h in range(GROUP):
                q = q_ref[rows, h * HD : (h + 1) * HD]
                s = lax.dot_general(q, k, NT, preferred_element_type=F32)
                before = top_in[h, rows, :]
                top = jnp.maximum(before, jnp.max(s, axis=1, keepdims=True))
                shrink = jnp.exp2((before - top) * SCALE)
                p = jnp.exp2((s - top[:, :1]) * SCALE).astype(BF16)
                pv = jnp.dot(p, wide, preferred_element_type=F32)
                acc_ref[h, rows, :] = acc_in[h, rows, :] * jnp.concatenate([shrink, shrink], axis=1) + pv
                top_ref[h, rows, :] = top


def step_call(distance, place, queries, kv, acc, top):
    return call(
        functools.partial(step_kernel, distance),
        (
            jax.ShapeDtypeStruct((GROUP, ROWS, 2 * HD), F32),
            jax.ShapeDtypeStruct((GROUP, ROWS, HD), F32),
        ),
        (GROUP * ROWS * ROWS * HD * 4, 4000000, GROUP * ROWS * ROWS),
        in_specs=[SM] + [VM] * 4,
        out_specs=(VM, VM),
        input_output_aliases={3: 0, 4: 1},
    )(place, queries, kv, acc, top)


def merge_kernel(place_ref, gate_ref, q_ref, acc_ref, mem_a, mem_b, keep_ref, send_ref, out_ref):
    x = place_ref[1]
    core = place_ref[2]
    mem = mem_a[...] + mem_b[...].astype(F32)
    mem = jnp.concatenate([mem[:HD, :], jnp.broadcast_to(mem[HD : HD + 1, :], (HD, HD))], axis=0)
    mem_high, mem_low = split_two(mem)
    mem_twice = jnp.concatenate([mem_high, mem_high], axis=1)
    for h in range(GROUP):
        gate = jax.nn.sigmoid(jnp.full((1, HD), gate_ref[h], F32))
        feat = feature_map(q_ref[:, h * HD : (h + 1) * HD].astype(F32))
        high, low = split_two(feat)
        both = jnp.concatenate([high, low], axis=1)
        read = lax.dot_general(both, mem_twice, NT, preferred_element_type=F32)
        read = read + lax.dot_general(high, mem_low, NT, preferred_element_type=F32)
        retrieved = read[:, :HD] / jnp.maximum(read[:, HD:], 1.0)
        local = acc_ref[h, :, :HD] / acc_ref[h, :, HD:]
        out_ref[:, h * HD : (h + 1) * HD] = (gate * retrieved + (1.0 - gate) * local).astype(BF16)
    for b in range(N_TP // 2):
        chip = (x + b) % (N_TP // 2)
        mine = pl.multiple_of((2 * chip + core) * BLOCK, BLOCK)
        other = pl.multiple_of((2 * chip + 1 - core) * BLOCK, BLOCK)
        keep_ref[b * BLOCK : (b + 1) * BLOCK, :] = out_ref[pl.ds(mine, BLOCK), :]
        send_ref[b * BLOCK : (b + 1) * BLOCK, :] = out_ref[pl.ds(other, BLOCK), :]


def merge_call(place, gates, queries, acc, mem_a, mem_b):
    half = jax.ShapeDtypeStruct((ROWS // 2, GROUP * HD), BF16)
    return call(
        merge_kernel,
        (half, half),
        (6 * ROWS * GROUP * HD * HD * 2, 4000000, ROWS * GROUP * HD),
        in_specs=[SM, SM] + [VM] * 4,
        out_specs=(VM, VM),
        scratch_shapes=[pltpu.VMEM((ROWS, GROUP * HD), BF16)],
    )(place, gates, queries, acc, mem_a, mem_b)


def project_kernel(keep_ref, got_ref, w_own_ref, w_other_ref, own_ref, right_ref, left_ref, far_a_ref, far_b_ref):
    width = w_own_ref.shape[1]
    tile = 512
    for j in range(width // tile):
        cols = slice(j * tile, (j + 1) * tile)
        out = jnp.dot(keep_ref[...], w_own_ref[:, cols], preferred_element_type=F32)
        out = out + jnp.dot(got_ref[...], w_other_ref[:, cols], preferred_element_type=F32)
        out = out.astype(BF16)
        own_ref[:, cols] = out[:BLOCK]
        right_ref[:, cols] = out[BLOCK : 2 * BLOCK]
        left_ref[:, cols] = out[3 * BLOCK :]
        far_ref = far_a_ref if j < width // tile // 2 else far_b_ref
        at = j % (width // tile // 2) * tile
        far_ref[:, at : at + tile] = out[2 * BLOCK : 3 * BLOCK]


def project_call(keep, got, w_own, w_other):
    rows, depth = keep.shape
    width = w_own.shape[1]
    whole = jax.ShapeDtypeStruct((BLOCK, width), BF16)
    half = jax.ShapeDtypeStruct((BLOCK, width // 2), BF16)
    return call(
        project_kernel,
        (whole, whole, whole, half, half),
        (4 * rows * depth * width, 12000000, 0),
        in_specs=[VM] * 4,
        out_specs=(VM,) * 5,
    )(keep, got, w_own, w_other)


def along_z(step):
    return [(i, i + step) for i in range(N_CTX) if i // SPAN == (i + step) // SPAN]


def along_y(step):
    return [(i, i + 8 * step) for i in range(N_CTX - 8 * step)]


def swap(bit, size):
    return [(i, i ^ bit) for i in range(size)]


def after(x, *others):
    return lax.optimization_barrier((x, others))[0]


def turned(step):
    return [(i, (i + 2 * step) % N_TP) for i in range(N_TP)]


def on_device(queries, keys, values, gates, out_weight):
    ctx = lax.axis_index("ctx")
    tp = lax.axis_index("tp")
    place = jnp.stack([ctx % SPAN, tp // 2, tp % 2]).astype(jnp.int32)
    send = lambda x, route: lax.ppermute(x.astype(BF16), "ctx", route)
    kv, delta = delta_call(keys, values)
    kv1, kv2, kv3 = [send(kv, along_z(d)) for d in (1, 2, 3)]
    got = send(delta, along_y(1))
    acc, top = own_call(queries, keys, values)
    before = after(got, acc).astype(F32)
    got = send(delta + before, along_y(2))
    acc, top = step_call(1, place, queries, kv1, acc, top)
    before = before + after(got, acc).astype(F32)
    got = send(delta + before, along_y(4))
    acc, top = step_call(2, place, queries, kv2, acc, top)
    before = before + after(got, acc).astype(F32)
    lower = (ctx % 8) < SPAN
    got = send(before + jnp.where(lower, delta, 0.0), swap(4, N_CTX))
    acc, top = step_call(3, place, queries, kv3, acc, top)
    mem = before + after(got, acc).astype(F32)
    got = send(mem, swap(1, N_CTX))
    w_other = lax.ppermute(out_weight, "tp", swap(1, N_TP))
    mem = mem + after(got, w_other).astype(F32)
    got = send(mem, swap(2, N_CTX))
    keep, give = merge_call(place, gates, queries, acc, mem, got)
    got = lax.ppermute(give, "tp", swap(1, N_TP))
    own, right, left, far_a, far_b = project_call(keep, got, out_weight, w_other)
    from_left = lax.ppermute(far_a, "tp", turned(1))
    from_right = lax.ppermute(far_b, "tp", turned(-1))
    half = far_a.shape[1]
    right = jnp.concatenate([right[:, :half] + from_left, right[:, half:]], axis=1)
    left = jnp.concatenate([left[:, :half], left[:, half:] + from_right], axis=1)
    from_left = lax.ppermute(right, "tp", turned(1))
    from_right = lax.ppermute(left, "tp", turned(-1))
    return (own.astype(F32) + from_left.astype(F32) + from_right.astype(F32)).astype(BF16)


def solution(mesh):
    placed = (P("ctx", "tp"), P("ctx", "tp"), P("ctx", "tp"), P("tp"), P("tp", None))
    return jax.shard_map(
        on_device, mesh=mesh, in_specs=placed, out_specs=P(("ctx", "tp"), None), check_vma=False
    )
```

time: 119 us -> 107 us (0.90)
  the two profiles are of different devices: /device:TPU:224 before, /device:TPU:6 now
where the time goes in v2:
time: 107 us
  starting transfers between devices  63.2 us (59%)
  waiting for transfers between devices  27.9 us (26%)
  Pallas kernels  9.34 us (9%)
  local copies, waits for them, and re-layouts  4.67 us (4%)
  other arithmetic  1.35 us (1%)
    ppermute x9, starting transfers between devices, on_device(): send = lambda x, route: lax.ppermute(x.astype(BF16), 'ctx', route)  47.5 us
    ppermute x1, waiting for transfers between devices, on_device(): from_left = lax.ppermute(right, 'tp', turned(1))  9.06 us
    ppermute x9, waiting for transfers between devices, on_device(): send = lambda x, route: lax.ppermute(x.astype(BF16), 'ctx', route)  8.51 us
    unnamed x14, local copies, waits for them, and re-layouts  4.67 us
    ppermute x1, waiting for transfers between devices, on_device(): from_right = lax.ppermute(left, 'tp', turned(-1))  4.63 us
    pallas_call x1, Pallas kernels, project_call(): call(project_kernel, (whole, whole, whole, half, half), (4 * rows * depth...  4.52 us
    ppermute x1, waiting for transfers between devices, on_device(): from_left = lax.ppermute(far_a, 'tp', turned(1))  4.38 us
    ppermute x1, starting transfers between devices, on_device(): from_left = lax.ppermute(right, 'tp', turned(1))  3.59 us
  transfers between devices with their start and end apart: 15, of which 9 were waited for; matrix products, arithmetic and copies ran while one was open for 0% of the time, Pallas kernels for 3%

profile of v2, /device:TPU:6, one launch (start us, length us, event | category | flops | bytes accessed | tf_op | source)
XLA Modules:
  0.0 106.8 jit_solution(10994255923481711266)
XLA Ops:
  0.0 1.9 %collective-permute-start.8 = (bf16[512,4096]{1,0:T(8,128)(2,1)}, bf16[512,4096]{1,0:T(8,128)(2,1)}, u32[]{:S(2)}, u32[]{:S(2)}) collective-permute-start(bf16[512,4096]{1,0:T(8,128)(2,1)} %w_own_ref.1), channel_id=1, source_target_pairs={{0,1},{1,0},{2,3},{3,2},{4,5},{5,4},{6,7},{7,6},{8,9},{9,8},{10,11... | collective-permute-start | bytes 12582920 | tf_op jit(solution)/shard_map/ppermute | solution.py:252
  1.9 0.0 copy-start.2
  1.9 0.9 copy-done.2
  2.8 0.9 copy-done.4
  3.7 0.3 shard_map.55
  4.1 4.3 %collective-permute-start.2 = (bf16[512,256]{1,0:T(8,128)(2,1)S(1)}, bf16[512,256]{1,0:T(8,128)(2,1)S(1)}, u32[]{:S(2)}, u32[]{:S(2)}) collective-permute-start(bf16[512,256]{1,0:T(8,128)(2,1)S(1)} %get-tuple-element.26), channel_id=1, source_target_pairs={{0,8},{8,16},{16,24},{32,40},{40,48},{48,56},{64,72},{72,80},{80,8... | collective-permute-start | bytes 786440 | tf_op jit(solution)/shard_map/ppermute | solution.py:235
  8.4 6.1 %collective-permute-start.1 = (bf16[512,256]{1,0:T(8,128)(2,1)S(1)}, bf16[512,256]{1,0:T(8,128)(2,1)S(1)}, u32[]{:S(2)}, u32[]{:S(2)}) collective-permute-start(bf16[512,256]{1,0:T(8,128)(2,1)S(1)} %get-tuple-element.26), channel_id=1, source_target_pairs={{0,16},{8,24},{32,48},{40,56},{64,80},{72,88},{96,112},{104,120},{... | collective-permute-start | bytes 786440 | tf_op jit(solution)/shard_map/ppermute | solution.py:235
  14.5 1.3 %collective-permute-start = (bf16[512,256]{1,0:T(8,128)(2,1)S(1)}, bf16[512,256]{1,0:T(8,128)(2,1)S(1)}, u32[]{:S(2)}, u32[]{:S(2)}) collective-permute-start(bf16[512,256]{1,0:T(8,128)(2,1)S(1)} %get-tuple-element.26), channel_id=1, source_target_pairs={{0,24},{32,56},{64,88},{96,120},{128,152},{160,184},{192,216},{224... | collective-permute-start | bytes 786440 | tf_op jit(solution)/shard_map/ppermute | solution.py:235
  15.8 3.5 %collective-permute-start.3 = (bf16[144,128]{1,0:T(8,128)(2,1)S(1)}, bf16[144,128]{1,0:T(8,128)(2,1)S(1)}, u32[]{:S(2)}, u32[]{:S(2)}) collective-permute-start(bf16[144,128]{1,0:T(8,128)(2,1)S(1)} %convert_element_type.45), channel_id=1, source_target_pairs={{0,64},{8,72},{16,80},{24,88},{32,96},{40,104},{48,112},{56,120},{... | collective-permute-start | bytes 110600 | tf_op jit(solution)/shard_map/ppermute | solution.py:235
  19.3 0.1 pad_add_fusion.place_ref
  19.4 1.0 copy-done
  20.4 0.9 copy-done.3
  21.3 0.9 copy-done.5
  22.2 1.4 %shard_map.56 = (f32[4,512,256]{2,1,0:T(8,128)S(1)}, f32[4,512,128]{2,1,0:T(8,128)S(1)}) custom-call(bf16[512,512]{1,0:T(8,128)(2,1)S(1)} %copy-done, bf16[512,128]{1,0:T(8,128)(2,1)S(1)} %copy-done.3, bf16[512,128]{1,0:T(8,128)(2,1)S(1)} %copy-done.5), custom_call_target="tpu_custom_call" | custom-call | flops 536870912 | bytes 4000000 | tf_op jit(solution)/shard_map/pallas_call | solution.py:99
  23.6 0.0 collective-permute-done.3
  23.7 4.5 %collective-permute-start.4 = (bf16[144,128]{1,0:T(8,128)(2,1)S(1)}, bf16[144,128]{1,0:T(8,128)(2,1)S(1)}, u32[]{:S(2)}, u32[]{:S(2)}) collective-permute-start(bf16[144,128]{1,0:T(8,128)(2,1)S(1)} %fusion), channel_id=1, source_target_pairs={{0,128},{8,136},{16,144},{24,152},{32,160},{40,168},{48,176},{56,1... | collective-permute-start | bytes 110600 | tf_op jit(solution)/shard_map/ppermute | solution.py:235
  28.2 0.0 collective-permute-done.2.kv_ref
  28.2 0.6 shard_map.57
  28.7 1.0 collective-permute-done.4
  29.8 8.9 %collective-permute-start.5 = (bf16[144,128]{1,0:T(8,128)(2,1)S(1)}, bf16[144,128]{1,0:T(8,128)(2,1)S(1)}, u32[]{:S(2)}, u32[]{:S(2)}) collective-permute-start(bf16[144,128]{1,0:T(8,128)(2,1)S(1)} %add_convert_fusion.2), channel_id=1, source_target_pairs={{0,256},{8,264},{16,272},{24,280},{32,288},{40,296},{48,304},{56,3... | collective-permute-start | bytes 110600 | tf_op jit(solution)/shard_map/ppermute | solution.py:235
  38.7 0.0 collective-permute-done.1.kv_ref
  38.8 0.6 shard_map.58
  39.3 1.0 collective-permute-done.5
  40.4 8.2 %collective-permute-start.6 = (bf16[144,128]{1,0:T(8,128)(2,1)S(1)}, bf16[144,128]{1,0:T(8,128)(2,1)S(1)}, u32[]{:S(2)}, u32[]{:S(2)}) collective-permute-start(bf16[144,128]{1,0:T(8,128)(2,1)S(1)} %add_convert_fusion.1), channel_id=1, source_target_pairs={{0,32},{8,40},{16,48},{24,56},{32,0},{40,8},{48,16},{56,24},{64,96... | collective-permute-start | bytes 110600 | tf_op jit(solution)/shard_map/ppermute | solution.py:235
  48.6 0.0 collective-permute-done.kv_ref
  48.6 0.0 copy-start.6
  48.6 0.0 copy-start.1
  48.7 0.6 shard_map.59
  49.2 1.4 %collective-permute-done.6 = bf16[144,128]{1,0:T(8,128)(2,1)S(1)} collective-permute-done((bf16[144,128]{1,0:T(8,128)(2,1)S(1)}, bf16[144,128]{1,0:T(8,128)(2,1)S(1)}, u32[]{:S(2)}, u32[]{:S(2)}) %collective-permute-start.6) | collective-permute-done | bytes 36896 | tf_op jit(solution)/shard_map/ppermute | solution.py:235
  50.6 2.8 %collective-permute-start.7 = (bf16[144,128]{1,0:T(8,128)(2,1)S(1)}, bf16[144,128]{1,0:T(8,128)(2,1)S(1)}, u32[]{:S(2)}, u32[]{:S(2)}) collective-permute-start(bf16[144,128]{1,0:T(8,128)(2,1)S(1)} %fusion.1), channel_id=1, source_target_pairs={{0,8},{8,0},{16,24},{24,16},{32,40},{40,32},{48,56},{56,48},{64,72... | collective-permute-start | bytes 110600 | tf_op jit(solution)/shard_map/ppermute | solution.py:235
  53.4 3.1 %collective-permute-done.7 = bf16[144,128]{1,0:T(8,128)(2,1)S(1)} collective-permute-done((bf16[144,128]{1,0:T(8,128)(2,1)S(1)}, bf16[144,128]{1,0:T(8,128)(2,1)S(1)}, u32[]{:S(2)}, u32[]{:S(2)}) %collective-permute-start.7) | collective-permute-done | bytes 36896 | tf_op jit(solution)/shard_map/ppermute | solution.py:235
  56.5 0.0 collective-permute-done.8.w_other_ref
  56.5 7.9 %collective-permute-start.9 = (bf16[144,128]{1,0:T(8,128)(2,1)S(1)}, bf16[144,128]{1,0:T(8,128)(2,1)S(1)}, u32[]{:S(2)}, u32[]{:S(2)}) collective-permute-start(bf16[144,128]{1,0:T(8,128)(2,1)S(1)} %get-tuple-element.47), channel_id=1, source_target_pairs={{0,16},{8,24},{16,0},{24,8},{32,48},{40,56},{48,32},{56,40},{64,80... | collective-permute-start | bytes 110600 | tf_op jit(solution)/shard_map/ppermute | solution.py:235
  64.4 1.9 %collective-permute-done.9.mem_b = bf16[144,128]{1,0:T(8,128)(2,1)S(1)} collective-permute-done((bf16[144,128]{1,0:T(8,128)(2,1)S(1)}, bf16[144,128]{1,0:T(8,128)(2,1)S(1)}, u32[]{:S(2)}, u32[]{:S(2)}) %collective-permute-start.9) | collective-permute-done | bytes 36896 | tf_op jit(solution)/shard_map/ppermute | solution.py:235
  66.4 0.0 copy-done.6
  66.4 1.5 %shard_map.60 = (bf16[256,512]{1,0:T(8,128)(2,1)S(1)}, bf16[256,512]{1,0:T(8,128)(2,1)S(1)}) custom-call(s32[3]{0:T(128)S(1)} %pad_add_fusion.place_ref, f32[4]{0:T(128)S(1)} %copy-done.6, bf16[512,512]{1,0:T(8,128)(2,1)S(1)} %copy-done, f32[4,512,256]{2,1,0:T(8,128)S(1)} %get-tuple-element.33.acc_ref, f32[144,128]{1,0:T(8,128)S(1)} %get-tuple-element.48.mem_a, ...), custom_call_target="tpu_custom_call" | custom-call | flops 402653184 | bytes 4000000 | tf_op jit(solution)/shard_map/pallas_call | solution.py:171
  67.8 2.1 %collective-permute-start.10 = (bf16[256,512]{1,0:T(8,128)(2,1)S(1)}, bf16[256,512]{1,0:T(8,128)(2,1)S(1)}, u32[]{:S(2)}, u32[]{:S(2)}) collective-permute-start(bf16[256,512]{1,0:T(8,128)(2,1)S(1)} %get-tuple-element.41), channel_id=1, source_target_pairs={{0,1},{1,0},{2,3},{3,2},{4,5},{5,4},{6,7},{7,6},{8,9},{9,8},{10,11... | collective-permute-start | bytes 786440 | tf_op jit(solution)/shard_map/ppermute | solution.py:256
  69.9 1.3 %collective-permute-done.10.got_ref = bf16[256,512]{1,0:T(8,128)(2,1)S(1)} collective-permute-done((bf16[256,512]{1,0:T(8,128)(2,1)S(1)}, bf16[256,512]{1,0:T(8,128)(2,1)S(1)}, u32[]{:S(2)}, u32[]{:S(2)}) %collective-permute-start.10) | collective-permute-done | bytes 262176 | tf_op jit(solution)/shard_map/ppermute | solution.py:256
  71.3 4.5 %shard_map.61 = (bf16[64,4096]{1,0:T(8,128)(2,1)S(1)}, bf16[64,4096]{1,0:T(8,128)(2,1)S(1)}, bf16[64,4096]{1,0:T(8,128)(2,1)S(1)}, bf16[64,2048]{1,0:T(8,128)(2,1)S(1)}, bf16[64,2048]{1,0:T(8,128)(2,1)S(1)}) custom-call(bf16[256,512]{1,0:T(8,128)(2,1)S(1)} %get-tuple-element.40.keep_ref, bf16[256,512]{1,0:T(8,128)(2,1)S(1)} %collective-permute-done.10.got_ref, ...), custom_call_target="tpu_custom_call" | custom-call | flops 2147483648 | bytes 12000000 | tf_op jit(solution)/shard_map/pallas_call | solution.py:202
  75.8 2.4 %collective-permute-start.11 = (bf16[64,2048]{1,0:T(8,128)(2,1)S(1)}, bf16[64,2048]{1,0:T(8,128)(2,1)S(1)}, u32[]{:S(2)}, u32[]{:S(2)}) collective-permute-start(bf16[64,2048]{1,0:T(8,128)(2,1)S(1)} %get-tuple-element.44), channel_id=1, source_target_pairs={{0,2},{1,3},{2,4},{3,5},{4,6},{5,7},{6,0},{7,1},{8,10},{9,11},{10,... | collective-permute-start | bytes 786440 | tf_op jit(solution)/shard_map/ppermute | solution.py:258
  78.2 3.5 %collective-permute-start.13 = (bf16[64,2048]{1,0:T(8,128)(2,1)S(1)}, bf16[64,2048]{1,0:T(8,128)(2,1)S(1)}, u32[]{:S(2)}, u32[]{:S(2)}) collective-permute-start(bf16[64,2048]{1,0:T(8,128)(2,1)S(1)} %get-tuple-element.46), channel_id=1, source_target_pairs={{0,6},{1,7},{2,0},{3,1},{4,2},{5,3},{6,4},{7,5},{8,14},{9,15},{10,... | collective-permute-start | bytes 786440 | tf_op jit(solution)/shard_map/ppermute | solution.py:259
  81.6 4.4 %collective-permute-done.11 = bf16[64,2048]{1,0:T(8,128)(2,1)S(1)} collective-permute-done((bf16[64,2048]{1,0:T(8,128)(2,1)S(1)}, bf16[64,2048]{1,0:T(8,128)(2,1)S(1)}, u32[]{:S(2)}, u32[]{:S(2)}) %collective-permute-start.11) | collective-permute-done | bytes 262176 | tf_op jit(solution)/shard_map/ppermute | solution.py:258
  86.1 3.6 %collective-permute-start.12 = (bf16[64,4096]{1,0:T(8,128)(2,1)S(1)}, bf16[64,4096]{1,0:T(8,128)(2,1)S(1)}, u32[]{:S(2)}, u32[]{:S(2)}) collective-permute-start(bf16[64,4096]{1,0:T(8,128)(2,1)S(1)} %pad_maximum_fusion), channel_id=1, source_target_pairs={{0,2},{1,3},{2,4},{3,5},{4,6},{5,7},{6,0},{7,1},{8,10},{9,11},{10,... | collective-permute-start | bytes 1572872 | tf_op jit(solution)/shard_map/ppermute | solution.py:263
  89.7 0.0 collective-permute-done.13
  89.8 2.3 %collective-permute-start.14 = (bf16[64,4096]{1,0:T(8,128)(2,1)S(1)}, bf16[64,4096]{1,0:T(8,128)(2,1)S(1)}, u32[]{:S(2)}, u32[]{:S(2)}) collective-permute-start(bf16[64,4096]{1,0:T(8,128)(2,1)S(1)} %pad_maximum_fusion.1), channel_id=1, source_target_pairs={{0,6},{1,7},{2,0},{3,1},{4,2},{5,3},{6,4},{7,5},{8,14},{9,15},{10,... | collective-permute-start | bytes 1572872 | tf_op jit(solution)/shard_map/ppermute | solution.py:264
  92.1 9.1 %collective-permute-done.12 = bf16[64,4096]{1,0:T(8,128)(2,1)S(1)} collective-permute-done((bf16[64,4096]{1,0:T(8,128)(2,1)S(1)}, bf16[64,4096]{1,0:T(8,128)(2,1)S(1)}, u32[]{:S(2)}, u32[]{:S(2)}) %collective-permute-start.12) | collective-permute-done | bytes 524320 | tf_op jit(solution)/shard_map/ppermute | solution.py:263
  101.1 4.6 %collective-permute-done.14 = bf16[64,4096]{1,0:T(8,128)(2,1)S(1)} collective-permute-done((bf16[64,4096]{1,0:T(8,128)(2,1)S(1)}, bf16[64,4096]{1,0:T(8,128)(2,1)S(1)}, u32[]{:S(2)}, u32[]{:S(2)}) %collective-permute-start.14) | collective-permute-done | bytes 524320 | tf_op jit(solution)/shard_map/ppermute | solution.py:264
  105.8 1.0 add_convert_fusion
  (15 shorter events, 0.3 us)
Async XLA Ops:
  0.0 56.5 %collective-permute-start.8 = (bf16[512,4096]{1,0:T(8,128)(2,1)}, bf16[512,4096]{1,0:T(8,128)(2,1)}, u32[]{:S(2)}, u32[]{:S(2)}) collective-permute-start(bf16[512,4096]{1,0:T(8,128)(2,1)} %w_own_ref.1), channel_id=1, source_target_pairs={{0,1},{1,0},{2,3},{3,2},{4,5},{5,4},{6,7},{7,6},{8,9},{9,8},{10,11... | collective-permute-start | bytes 12582920 | tf_op jit(solution)/shard_map/ppermute | solution.py:252
  1.9 0.9 copy-start.2
  2.8 0.9 copy-start.4
  4.1 24.1 %collective-permute-start.2 = (bf16[512,256]{1,0:T(8,128)(2,1)S(1)}, bf16[512,256]{1,0:T(8,128)(2,1)S(1)}, u32[]{:S(2)}, u32[]{:S(2)}) collective-permute-start(bf16[512,256]{1,0:T(8,128)(2,1)S(1)} %get-tuple-element.26), channel_id=1, source_target_pairs={{0,8},{8,16},{16,24},{32,40},{40,48},{48,56},{64,72},{72,80},{80,8... | collective-permute-start | bytes 786440 | tf_op jit(solution)/shard_map/ppermute | solution.py:235
  8.4 30.4 %collective-permute-start.1 = (bf16[512,256]{1,0:T(8,128)(2,1)S(1)}, bf16[512,256]{1,0:T(8,128)(2,1)S(1)}, u32[]{:S(2)}, u32[]{:S(2)}) collective-permute-start(bf16[512,256]{1,0:T(8,128)(2,1)S(1)} %get-tuple-element.26), channel_id=1, source_target_pairs={{0,16},{8,24},{32,48},{40,56},{64,80},{72,88},{96,112},{104,120},{... | collective-permute-start | bytes 786440 | tf_op jit(solution)/shard_map/ppermute | solution.py:235
  14.5 34.2 %collective-permute-start = (bf16[512,256]{1,0:T(8,128)(2,1)S(1)}, bf16[512,256]{1,0:T(8,128)(2,1)S(1)}, u32[]{:S(2)}, u32[]{:S(2)}) collective-permute-start(bf16[512,256]{1,0:T(8,128)(2,1)S(1)} %get-tuple-element.26), channel_id=1, source_target_pairs={{0,24},{32,56},{64,88},{96,120},{128,152},{160,184},{192,216},{224... | collective-permute-start | bytes 786440 | tf_op jit(solution)/shard_map/ppermute | solution.py:235
  15.8 7.9 %collective-permute-start.3 = (bf16[144,128]{1,0:T(8,128)(2,1)S(1)}, bf16[144,128]{1,0:T(8,128)(2,1)S(1)}, u32[]{:S(2)}, u32[]{:S(2)}) collective-permute-start(bf16[144,128]{1,0:T(8,128)(2,1)S(1)} %convert_element_type.45), channel_id=1, source_target_pairs={{0,64},{8,72},{16,80},{24,88},{32,96},{40,104},{48,112},{56,120},{... | collective-permute-start | bytes 110600 | tf_op jit(solution)/shard_map/ppermute | solution.py:235
  19.4 1.0 copy-start
  20.4 0.9 copy-start.3
  21.3 0.9 copy-start.5
  23.7 6.1 %collective-permute-start.4 = (bf16[144,128]{1,0:T(8,128)(2,1)S(1)}, bf16[144,128]{1,0:T(8,128)(2,1)S(1)}, u32[]{:S(2)}, u32[]{:S(2)}) collective-permute-start(bf16[144,128]{1,0:T(8,128)(2,1)S(1)} %fusion), channel_id=1, source_target_pairs={{0,128},{8,136},{16,144},{24,152},{32,160},{40,168},{48,176},{56,1... | collective-permute-start | bytes 110600 | tf_op jit(solution)/shard_map/ppermute | solution.py:235
  29.8 10.6 %collective-permute-start.5 = (bf16[144,128]{1,0:T(8,128)(2,1)S(1)}, bf16[144,128]{1,0:T(8,128)(2,1)S(1)}, u32[]{:S(2)}, u32[]{:S(2)}) collective-permute-start(bf16[144,128]{1,0:T(8,128)(2,1)S(1)} %add_convert_fusion.2), channel_id=1, source_target_pairs={{0,256},{8,264},{16,272},{24,280},{32,288},{40,296},{48,304},{56,3... | collective-permute-start | bytes 110600 | tf_op jit(solution)/shard_map/ppermute | solution.py:235
  40.4 10.2 %collective-permute-start.6 = (bf16[144,128]{1,0:T(8,128)(2,1)S(1)}, bf16[144,128]{1,0:T(8,128)(2,1)S(1)}, u32[]{:S(2)}, u32[]{:S(2)}) collective-permute-start(bf16[144,128]{1,0:T(8,128)(2,1)S(1)} %add_convert_fusion.1), channel_id=1, source_target_pairs={{0,32},{8,40},{16,48},{24,56},{32,0},{40,8},{48,16},{56,24},{64,96... | collective-permute-start | bytes 110600 | tf_op jit(solution)/shard_map/ppermute | solution.py:235
  48.6 17.7 %copy-start.6 = (f32[4]{0:T(128)S(1)}, f32[4]{0:T(128)}, u32[]{:S(2)}) copy-start(f32[4]{0:T(128)} %gate_ref.1) | copy-start | bytes 52
  48.6 22.6 %copy-start.1 = (bf16[512,4096]{1,0:T(8,128)(2,1)S(1)}, bf16[512,4096]{1,0:T(8,128)(2,1)}, u32[]{:S(2)}) copy-start(bf16[512,4096]{1,0:T(8,128)(2,1)} %w_own_ref.1) | copy-start | bytes 12582916
  50.6 5.9 %collective-permute-start.7 = (bf16[144,128]{1,0:T(8,128)(2,1)S(1)}, bf16[144,128]{1,0:T(8,128)(2,1)S(1)}, u32[]{:S(2)}, u32[]{:S(2)}) collective-permute-start(bf16[144,128]{1,0:T(8,128)(2,1)S(1)} %fusion.1), channel_id=1, source_target_pairs={{0,8},{8,0},{16,24},{24,16},{32,40},{40,32},{48,56},{56,48},{64,72... | collective-permute-start | bytes 110600 | tf_op jit(solution)/shard_map/ppermute | solution.py:235
  56.5 9.8 %collective-permute-start.9 = (bf16[144,128]{1,0:T(8,128)(2,1)S(1)}, bf16[144,128]{1,0:T(8,128)(2,1)S(1)}, u32[]{:S(2)}, u32[]{:S(2)}) collective-permute-start(bf16[144,128]{1,0:T(8,128)(2,1)S(1)} %get-tuple-element.47), channel_id=1, source_target_pairs={{0,16},{8,24},{16,0},{24,8},{32,48},{40,56},{48,32},{56,40},{64,80... | collective-permute-start | bytes 110600 | tf_op jit(solution)/shard_map/ppermute | solution.py:235
  67.8 3.4 %collective-permute-start.10 = (bf16[256,512]{1,0:T(8,128)(2,1)S(1)}, bf16[256,512]{1,0:T(8,128)(2,1)S(1)}, u32[]{:S(2)}, u32[]{:S(2)}) collective-permute-start(bf16[256,512]{1,0:T(8,128)(2,1)S(1)} %get-tuple-element.41), channel_id=1, source_target_pairs={{0,1},{1,0},{2,3},{3,2},{4,5},{5,4},{6,7},{7,6},{8,9},{9,8},{10,11... | collective-permute-start | bytes 786440 | tf_op jit(solution)/shard_map/ppermute | solution.py:256
  75.8 10.2 %collective-permute-start.11 = (bf16[64,2048]{1,0:T(8,128)(2,1)S(1)}, bf16[64,2048]{1,0:T(8,128)(2,1)S(1)}, u32[]{:S(2)}, u32[]{:S(2)}) collective-permute-start(bf16[64,2048]{1,0:T(8,128)(2,1)S(1)} %get-tuple-element.44), channel_id=1, source_target_pairs={{0,2},{1,3},{2,4},{3,5},{4,6},{5,7},{6,0},{7,1},{8,10},{9,11},{10,... | collective-permute-start | bytes 786440 | tf_op jit(solution)/shard_map/ppermute | solution.py:258
  78.2 11.5 %collective-permute-start.13 = (bf16[64,2048]{1,0:T(8,128)(2,1)S(1)}, bf16[64,2048]{1,0:T(8,128)(2,1)S(1)}, u32[]{:S(2)}, u32[]{:S(2)}) collective-permute-start(bf16[64,2048]{1,0:T(8,128)(2,1)S(1)} %get-tuple-element.46), channel_id=1, source_target_pairs={{0,6},{1,7},{2,0},{3,1},{4,2},{5,3},{6,4},{7,5},{8,14},{9,15},{10,... | collective-permute-start | bytes 786440 | tf_op jit(solution)/shard_map/ppermute | solution.py:259
  86.1 15.0 %collective-permute-start.12 = (bf16[64,4096]{1,0:T(8,128)(2,1)S(1)}, bf16[64,4096]{1,0:T(8,128)(2,1)S(1)}, u32[]{:S(2)}, u32[]{:S(2)}) collective-permute-start(bf16[64,4096]{1,0:T(8,128)(2,1)S(1)} %pad_maximum_fusion), channel_id=1, source_target_pairs={{0,2},{1,3},{2,4},{3,5},{4,6},{5,7},{6,0},{7,1},{8,10},{9,11},{10,... | collective-permute-start | bytes 1572872 | tf_op jit(solution)/shard_map/ppermute | solution.py:263
  89.8 16.0 %collective-permute-start.14 = (bf16[64,4096]{1,0:T(8,128)(2,1)S(1)}, bf16[64,4096]{1,0:T(8,128)(2,1)S(1)}, u32[]{:S(2)}, u32[]{:S(2)}) collective-permute-start(bf16[64,4096]{1,0:T(8,128)(2,1)S(1)} %pad_maximum_fusion.1), channel_id=1, source_target_pairs={{0,6},{1,7},{2,0},{3,1},{4,2},{5,3},{6,4},{7,5},{8,14},{9,15},{10,... | collective-permute-start | bytes 1572872 | tf_op jit(solution)/shard_map/ppermute | solution.py:264

commit v3 on v2

--- a/solution.py
+++ b/solution.py
@@ -49,36 +49,37 @@
     )
 
 
-def delta_kernel(k_ref, v_ref, kv_ref, d_ref):
-    k = k_ref[...]
-    v = v_ref[...]
-    kv_ref[:, :HD] = k
-    kv_ref[:, HD:] = v
-    feat = feature_map(k.astype(F32))
+def delta_kernel(kv_ref, d_ref, d16_ref):
+    v = kv_ref[:, HD:]
+    feat = feature_map(kv_ref[:, :HD].astype(F32))
     high, low = split_two(feat)
-    d_ref[:HD, :] = lax.dot_general(v, high, TN, preferred_element_type=F32) + lax.dot_general(
+    delta = lax.dot_general(v, high, TN, preferred_element_type=F32) + lax.dot_general(
         v, low, TN, preferred_element_type=F32
     )
-    d_ref[HD:, :] = jnp.broadcast_to(jnp.sum(feat, axis=0, keepdims=True), (16, HD))
-
-
-def delta_call(keys, values):
+    norm = jnp.broadcast_to(jnp.sum(feat, axis=0, keepdims=True), (16, HD))
+    d_ref[:HD, :] = delta
+    d_ref[HD:, :] = norm
+    d16_ref[:HD, :] = delta.astype(BF16)
+    d16_ref[HD:, :] = norm.astype(BF16)
+
+
+def delta_call(kv):
     return call(
         delta_kernel,
-        (jax.ShapeDtypeStruct((ROWS, 2 * HD), BF16), jax.ShapeDtypeStruct((HD + 16, HD), F32)),
-        (2 * 2 * ROWS * HD * HD, 600000, ROWS * HD),
-        in_specs=[VM, VM],
-        out_specs=(VM, VM),
-    )(keys, values)
+        (jax.ShapeDtypeStruct((HD + 16, HD), F32), jax.ShapeDtypeStruct((HD + 16, HD), BF16)),
+        (2 * 2 * ROWS * HD * HD, 400000, ROWS * HD),
+        in_specs=[VM],
+        out_specs=(VM, VM),
+    )(kv)
 
 
 def values_and_ones(v):
     return jnp.concatenate([v, jnp.ones_like(v)], axis=1)
 
 
-def own_kernel(q_ref, k_ref, v_ref, acc_ref, top_ref):
-    k = k_ref[...]
-    wide = values_and_ones(v_ref[...])
+def own_kernel(q_ref, kv_ref, acc_ref, top_ref):
+    k = kv_ref[:, :HD]
+    wide = values_and_ones(kv_ref[:, HD:])
     for r in range(ROWS // CHUNK):
         rows = slice(r * CHUNK, (r + 1) * CHUNK)
         seen = (r + 1) * CHUNK
@@ -95,7 +96,7 @@
             top_ref[h, rows, :] = jnp.broadcast_to(top, (CHUNK, HD))
 
 
-def own_call(queries, keys, values):
+def own_call(queries, kv):
     return call(
         own_kernel,
         (
@@ -103,9 +104,9 @@
             jax.ShapeDtypeStruct((GROUP, ROWS, HD), F32),
         ),
         (GROUP * ROWS * ROWS * HD * 4, 4000000, GROUP * ROWS * ROWS),
-        in_specs=[VM, VM, VM],
-        out_specs=(VM, VM),
-    )(queries, keys, values)
+        in_specs=[VM, VM],
+        out_specs=(VM, VM),
+    )(queries, kv)
 
 
 def step_kernel(distance, place_ref, q_ref, kv_ref, acc_in, top_in, acc_ref, top_ref):
@@ -121,10 +122,15 @@
                 before = top_in[h, rows, :]
                 top = jnp.maximum(before, jnp.max(s, axis=1, keepdims=True))
                 shrink = jnp.exp2((before - top) * SCALE)
-                p = jnp.exp2((s - top[:, :1]) * SCALE).astype(BF16)
+                p = jnp.exp2((s - jnp.concatenate([top] * SPAN, axis=1)) * SCALE).astype(BF16)
                 pv = jnp.dot(p, wide, preferred_element_type=F32)
                 acc_ref[h, rows, :] = acc_in[h, rows, :] * jnp.concatenate([shrink, shrink], axis=1) + pv
                 top_ref[h, rows, :] = top
+
+    @pl.when(place_ref[0] < distance)
+    def _():
+        acc_ref[...] = acc_in[...]
+        top_ref[...] = top_in[...]
 
 
 def step_call(distance, place, queries, kv, acc, top):
@@ -137,14 +143,13 @@
         (GROUP * ROWS * ROWS * HD * 4, 4000000, GROUP * ROWS * ROWS),
         in_specs=[SM] + [VM] * 4,
         out_specs=(VM, VM),
-        input_output_aliases={3: 0, 4: 1},
     )(place, queries, kv, acc, top)
 
 
-def merge_kernel(place_ref, gate_ref, q_ref, acc_ref, mem_a, mem_b, keep_ref, send_ref, out_ref):
+def merge_kernel(place_ref, gate_ref, q_ref, acc_ref, mem0, mem1, mem2, mem3, keep_ref, send_ref, out_ref):
     x = place_ref[1]
     core = place_ref[2]
-    mem = mem_a[...] + mem_b[...].astype(F32)
+    mem = mem0[...] + mem1[...].astype(F32) + (mem2[...].astype(F32) + mem3[...].astype(F32))
     mem = jnp.concatenate([mem[:HD, :], jnp.broadcast_to(mem[HD : HD + 1, :], (HD, HD))], axis=0)
     mem_high, mem_low = split_two(mem)
     mem_twice = jnp.concatenate([mem_high, mem_high], axis=1)
@@ -166,46 +171,59 @@
         send_ref[b * BLOCK : (b + 1) * BLOCK, :] = out_ref[pl.ds(other, BLOCK), :]
 
 
-def merge_call(place, gates, queries, acc, mem_a, mem_b):
+def merge_call(place, gates, queries, acc, mems):
     half = jax.ShapeDtypeStruct((ROWS // 2, GROUP * HD), BF16)
     return call(
         merge_kernel,
         (half, half),
         (6 * ROWS * GROUP * HD * HD * 2, 4000000, ROWS * GROUP * HD),
-        in_specs=[SM, SM] + [VM] * 4,
+        in_specs=[SM, SM] + [VM] * 6,
         out_specs=(VM, VM),
         scratch_shapes=[pltpu.VMEM((ROWS, GROUP * HD), BF16)],
-    )(place, gates, queries, acc, mem_a, mem_b)
-
-
-def project_kernel(keep_ref, got_ref, w_own_ref, w_other_ref, own_ref, right_ref, left_ref, far_a_ref, far_b_ref):
-    width = w_own_ref.shape[1]
+    )(place, gates, queries, acc, *mems)
+
+
+def project_kernel(first, keep_ref, got_ref, w_own_ref, w_other_ref, own_ref, right_ref, far_ref, left_ref):
+    width = own_ref.shape[1]
     tile = 512
     for j in range(width // tile):
         cols = slice(j * tile, (j + 1) * tile)
-        out = jnp.dot(keep_ref[...], w_own_ref[:, cols], preferred_element_type=F32)
-        out = out + jnp.dot(got_ref[...], w_other_ref[:, cols], preferred_element_type=F32)
+        from_w = slice(first + j * tile, first + (j + 1) * tile)
+        out = jnp.dot(keep_ref[...], w_own_ref[:, from_w], preferred_element_type=F32)
+        out = out + jnp.dot(got_ref[...], w_other_ref[:, from_w], preferred_element_type=F32)
         out = out.astype(BF16)
-        own_ref[:, cols] = out[:BLOCK]
-        right_ref[:, cols] = out[BLOCK : 2 * BLOCK]
-        left_ref[:, cols] = out[3 * BLOCK :]
-        far_ref = far_a_ref if j < width // tile // 2 else far_b_ref
-        at = j % (width // tile // 2) * tile
-        far_ref[:, at : at + tile] = out[2 * BLOCK : 3 * BLOCK]
-
-
-def project_call(keep, got, w_own, w_other):
+        for b, ref in enumerate((own_ref, right_ref, far_ref, left_ref)):
+            ref[:, cols] = out[b * BLOCK : (b + 1) * BLOCK]
+
+
+def project_call(first, keep, got, w_own, w_other):
     rows, depth = keep.shape
-    width = w_own.shape[1]
-    whole = jax.ShapeDtypeStruct((BLOCK, width), BF16)
-    half = jax.ShapeDtypeStruct((BLOCK, width // 2), BF16)
-    return call(
-        project_kernel,
-        (whole, whole, whole, half, half),
-        (4 * rows * depth * width, 12000000, 0),
+    half = w_own.shape[1] // 2
+    return call(
+        functools.partial(project_kernel, first),
+        (jax.ShapeDtypeStruct((BLOCK, half), BF16),) * 4,
+        (4 * rows * depth * half, 6000000, 0),
         in_specs=[VM] * 4,
-        out_specs=(VM,) * 5,
+        out_specs=(VM,) * 4,
     )(keep, got, w_own, w_other)
+
+
+def total_kernel(own_a, left_a, right_a, own_b, left_b, right_b, out_ref):
+    half = own_a.shape[1]
+    for first, parts in ((0, (own_a, left_a, right_a)), (half, (own_b, left_b, right_b))):
+        total = parts[0][...].astype(F32) + parts[1][...].astype(F32) + parts[2][...].astype(F32)
+        out_ref[:, first : first + half] = total.astype(BF16)
+
+
+def total_call(*parts):
+    rows, half = parts[0].shape
+    return call(
+        total_kernel,
+        jax.ShapeDtypeStruct((rows, 2 * half), BF16),
+        (6 * rows * half, 2000000, 0),
+        in_specs=[VM] * 6,
+        out_specs=VM,
+    )(*parts)
 
 
 def along_z(step):
@@ -233,36 +251,39 @@
     tp = lax.axis_index("tp")
     place = jnp.stack([ctx % SPAN, tp // 2, tp % 2]).astype(jnp.int32)
     send = lambda x, route: lax.ppermute(x.astype(BF16), "ctx", route)
-    kv, delta = delta_call(keys, values)
-    kv1, kv2, kv3 = [send(kv, along_z(d)) for d in (1, 2, 3)]
-    got = send(delta, along_y(1))
-    acc, top = own_call(queries, keys, values)
-    before = after(got, acc).astype(F32)
+    kv = jnp.concatenate([keys, values], axis=1)
+    delta, delta16 = delta_call(kv)
+    kv1 = send(kv, along_z(1))
+    got = send(delta16, along_y(1))
+    before = got.astype(F32)
+    kv2 = send(after(kv, got), along_z(2))
     got = send(delta + before, along_y(2))
-    acc, top = step_call(1, place, queries, kv1, acc, top)
+    acc, top = own_call(queries, kv)
+    kv3 = send(after(kv, got), along_z(3))
+    w_other = lax.ppermute(out_weight, "tp", swap(1, N_TP))
     before = before + after(got, acc).astype(F32)
     got = send(delta + before, along_y(4))
-    acc, top = step_call(2, place, queries, kv2, acc, top)
+    acc, top = step_call(1, place, queries, kv1, acc, top)
     before = before + after(got, acc).astype(F32)
     lower = (ctx % 8) < SPAN
     got = send(before + jnp.where(lower, delta, 0.0), swap(4, N_CTX))
+    acc, top = step_call(2, place, queries, kv2, acc, top)
+    mem = before + after(got, acc).astype(F32)
+    mem16 = mem.astype(BF16)
+    mems = [send(mem16, swap(k, N_CTX)) for k in (1, 2, 3)]
     acc, top = step_call(3, place, queries, kv3, acc, top)
-    mem = before + after(got, acc).astype(F32)
-    got = send(mem, swap(1, N_CTX))
-    w_other = lax.ppermute(out_weight, "tp", swap(1, N_TP))
-    mem = mem + after(got, w_other).astype(F32)
-    got = send(mem, swap(2, N_CTX))
-    keep, give = merge_call(place, gates, queries, acc, mem, got)
+    mems = [after(m, acc) for m in mems]
+    keep, give = merge_call(place, gates, queries, acc, [mem] + mems)
     got = lax.ppermute(give, "tp", swap(1, N_TP))
-    own, right, left, far_a, far_b = project_call(keep, got, out_weight, w_other)
-    from_left = lax.ppermute(far_a, "tp", turned(1))
-    from_right = lax.ppermute(far_b, "tp", turned(-1))
-    half = far_a.shape[1]
-    right = jnp.concatenate([right[:, :half] + from_left, right[:, half:]], axis=1)
-    left = jnp.concatenate([left[:, :half], left[:, half:] + from_right], axis=1)
-    from_left = lax.ppermute(right, "tp", turned(1))
-    from_right = lax.ppermute(left, "tp", turned(-1))
-    return (own.astype(F32) + from_left.astype(F32) + from_right.astype(F32)).astype(BF16)
+    own_a, right_a, far_a, left_a = project_call(0, keep, got, out_weight, w_other)
+    far_a = lax.ppermute(far_a, "tp", turned(1))
+    left_a = lax.ppermute(left_a, "tp", turned(-1))
+    own_b, right_b, far_b, left_b = project_call(own_a.shape[1], keep, got, out_weight, w_other)
+    far_b = lax.ppermute(far_b, "tp", turned(-1))
+    right_b = lax.ppermute(right_b, "tp", turned(1))
+    right_a = lax.ppermute(right_a + far_a, "tp", turned(1))
+    left_b = lax.ppermute(left_b + far_b, "tp", turned(-1))
+    return total_call(own_a, left_a, right_a, own_b, left_b, right_b)
 
 
 def solution(mesh):

time: 107 us -> 103 us (0.963)
  the two profiles are of different devices: /device:TPU:6 before, /device:TPU:1 now
where the time goes in v3:
time: 103 us; the launch traced here: 101 us
  starting transfers between devices  72.6 us (70%)
  Pallas kernels  14.4 us (14%)
  waiting for transfers between devices  11 us (11%)
  local copies, waits for them, and re-layouts  2.91 us (3%)
    ppermute x10, starting transfers between devices, on_device(): send = lambda x, route: lax.ppermute(x.astype(BF16), 'ctx', route)  41.9 us
    ppermute x1, starting transfers between devices, on_device(): w_other = lax.ppermute(out_weight, 'tp', swap(1, N_TP))  8.78 us
    pallas_call x2, Pallas kernels, project_call(): call(functools.partial(project_kernel, first), (jax.ShapeDtypeStruct((BLO...  6.93 us
    ppermute x1, starting transfers between devices, on_device(): left_a = lax.ppermute(left_a, 'tp', turned(-1))  4.4 us
    ppermute x1, starting transfers between devices, on_device(): far_b = lax.ppermute(far_b, 'tp', turned(-1))  4.39 us
    ppermute x1, starting transfers between devices, on_device(): got = lax.ppermute(give, 'tp', swap(1, N_TP))  3.85 us
    ppermute x1, starting transfers between devices, on_device(): left_b = lax.ppermute(left_b + far_b, 'tp', turned(-1))  3.36 us
    pallas_call x3, Pallas kernels, step_call(): call(functools.partial(step_kernel, distance), (jax.ShapeDtypeStruct((GRO...  3.28 us
  transfers between devices with their start and end apart: 18, of which 7 were waited for; matrix products, arithmetic and copies ran while one was open for 2% of the time, Pallas kernels for 10%

profile of v3, /device:TPU:1, one launch (start us, length us, event | category | flops | bytes accessed | tf_op | source)
XLA Modules:
  0.0 101.5 jit_solution(13167088157940323053)
XLA Ops:
  0.0 8.8 %collective-permute-start.11 = (bf16[512,4096]{1,0:T(8,128)(2,1)}, bf16[512,4096]{1,0:T(8,128)(2,1)}, u32[]{:S(2)}, u32[]{:S(2)}) collective-permute-start(bf16[512,4096]{1,0:T(8,128)(2,1)} %w_own_ref.3), channel_id=1, source_target_pairs={{0,1},{1,0},{2,3},{3,2},{4,5},{5,4},{6,7},{7,6},{8,9},{9,8},{10,11... | collective-permute-start | bytes 12582920 | tf_op jit(solution)/shard_map/ppermute | solution.py:263
  8.8 0.9 constant_dynamic-update-slice_fusion.1
  9.7 0.9 constant_dynamic-update-slice_fusion.kv_ref
  10.7 1.3 %collective-permute-start.4 = (bf16[512,256]{1,0:T(8,128)(2,1)S(1)}, bf16[512,256]{1,0:T(8,128)(2,1)S(1)}, u32[]{:S(2)}, u32[]{:S(2)}) collective-permute-start(bf16[512,256]{1,0:T(8,128)(2,1)S(1)} %constant_dynamic-update-slice_fusion.kv_ref), channel_id=1, source_target_pairs={{0,8},{8,16},{16,24},{32,40},{40,48},{48,56},{64,72},{72,80},{80,8... | collective-permute-start | bytes 786440 | tf_op jit(solution)/shard_map/ppermute | solution.py:253
  12.0 0.3 shard_map.55
  12.3 1.3 %collective-permute-start = (bf16[144,128]{1,0:T(8,128)(2,1)S(1)}, bf16[144,128]{1,0:T(8,128)(2,1)S(1)}, u32[]{:S(2)}, u32[]{:S(2)}) collective-permute-start(bf16[144,128]{1,0:T(8,128)(2,1)S(1)} %get-tuple-element.33), channel_id=1, source_target_pairs={{0,64},{8,72},{16,80},{24,88},{32,96},{40,104},{48,112},{56,120},{... | collective-permute-start | bytes 110600 | tf_op jit(solution)/shard_map/ppermute | solution.py:253
  13.6 0.1 pad_add_fusion.place_ref
  13.7 0.9 collective-permute-done
  14.6 3.9 %collective-permute-start.1 = (bf16[144,128]{1,0:T(8,128)(2,1)S(1)}, bf16[144,128]{1,0:T(8,128)(2,1)S(1)}, u32[]{:S(2)}, u32[]{:S(2)}) collective-permute-start(bf16[144,128]{1,0:T(8,128)(2,1)S(1)} %fusion), channel_id=1, source_target_pairs={{0,128},{8,136},{16,144},{24,152},{32,160},{40,168},{48,176},{56,1... | collective-permute-start | bytes 110600 | tf_op jit(solution)/shard_map/ppermute | solution.py:253
  18.5 0.0 copy-start.1
  18.6 1.0 %copy-done.1 = bf16[512,512]{1,0:T(8,128)(2,1)S(1)} copy-done((bf16[512,512]{1,0:T(8,128)(2,1)S(1)}, bf16[512,512]{1,0:T(8,128)(2,1)}, u32[]{:S(2)}) %copy-start.1) | copy-done | bytes 524312
  19.6 1.4 %shard_map.56 = (f32[4,512,256]{2,1,0:T(8,128)S(1)}, f32[4,512,128]{2,1,0:T(8,128)S(1)}) custom-call(bf16[512,512]{1,0:T(8,128)(2,1)S(1)} %copy-done.1, bf16[512,256]{1,0:T(8,128)(2,1)S(1)} %constant_dynamic-update-slice_fusion.kv_ref), custom_call_target="tpu_custom_call" | custom-call | flops 536870912 | bytes 4000000 | tf_op jit(solution)/shard_map/pallas_call | solution.py:100
  21.0 6.1 %collective-permute-start.3 = (bf16[512,256]{1,0:T(8,128)(2,1)S(1)}, bf16[512,256]{1,0:T(8,128)(2,1)S(1)}, u32[]{:S(2)}, u32[]{:S(2)}) collective-permute-start(bf16[512,256]{1,0:T(8,128)(2,1)S(1)} %constant_dynamic-update-slice_fusion.kv_ref), channel_id=1, source_target_pairs={{0,16},{8,24},{32,48},{40,56},{64,80},{72,88},{96,112},{104,120},{... | collective-permute-start | bytes 786440 | tf_op jit(solution)/shard_map/ppermute | solution.py:253
  27.1 0.0 collective-permute-done.1
  27.2 6.1 %collective-permute-start.5 = (bf16[144,128]{1,0:T(8,128)(2,1)S(1)}, bf16[144,128]{1,0:T(8,128)(2,1)S(1)}, u32[]{:S(2)}, u32[]{:S(2)}) collective-permute-start(bf16[144,128]{1,0:T(8,128)(2,1)S(1)} %add_convert_fusion.1), channel_id=1, source_target_pairs={{0,256},{8,264},{16,272},{24,280},{32,288},{40,296},{48,304},{56,3... | collective-permute-start | bytes 110600 | tf_op jit(solution)/shard_map/ppermute | solution.py:253
  33.2 1.5 %collective-permute-start.2 = (bf16[512,256]{1,0:T(8,128)(2,1)S(1)}, bf16[512,256]{1,0:T(8,128)(2,1)S(1)}, u32[]{:S(2)}, u32[]{:S(2)}) collective-permute-start(bf16[512,256]{1,0:T(8,128)(2,1)S(1)} %constant_dynamic-update-slice_fusion.kv_ref), channel_id=1, source_target_pairs={{0,24},{32,56},{64,88},{96,120},{128,152},{160,184},{192,216},{224... | collective-permute-start | bytes 786440 | tf_op jit(solution)/shard_map/ppermute | solution.py:253
  34.8 0.8 shard_map.57
  35.5 0.0 collective-permute-done.5
  35.6 7.9 %collective-permute-start.6 = (bf16[144,128]{1,0:T(8,128)(2,1)S(1)}, bf16[144,128]{1,0:T(8,128)(2,1)S(1)}, u32[]{:S(2)}, u32[]{:S(2)}) collective-permute-start(bf16[144,128]{1,0:T(8,128)(2,1)S(1)} %add_convert_fusion), channel_id=1, source_target_pairs={{0,32},{8,40},{16,48},{24,56},{32,0},{40,8},{48,16},{56,24},{64,96... | collective-permute-start | bytes 110600 | tf_op jit(solution)/shard_map/ppermute | solution.py:253
  43.5 0.8 shard_map.58
  44.3 1.0 collective-permute-done.6
  45.3 3.5 %collective-permute-start.9 = (bf16[144,128]{1,0:T(8,128)(2,1)S(1)}, bf16[144,128]{1,0:T(8,128)(2,1)S(1)}, u32[]{:S(2)}, u32[]{:S(2)}) collective-permute-start(bf16[144,128]{1,0:T(8,128)(2,1)S(1)} %get-tuple-element.59), channel_id=1, source_target_pairs={{0,24},{8,16},{16,8},{24,0},{32,56},{40,48},{48,40},{56,32},{64,88... | collective-permute-start | bytes 110600 | tf_op jit(solution)/shard_map/ppermute | solution.py:253
  48.8 8.1 %collective-permute-start.8 = (bf16[144,128]{1,0:T(8,128)(2,1)S(1)}, bf16[144,128]{1,0:T(8,128)(2,1)S(1)}, u32[]{:S(2)}, u32[]{:S(2)}) collective-permute-start(bf16[144,128]{1,0:T(8,128)(2,1)S(1)} %get-tuple-element.59), channel_id=1, source_target_pairs={{0,16},{8,24},{16,0},{24,8},{32,48},{40,56},{48,32},{56,40},{64,80... | collective-permute-start | bytes 110600 | tf_op jit(solution)/shard_map/ppermute | solution.py:253
  56.9 2.2 %collective-permute-start.7 = (bf16[144,128]{1,0:T(8,128)(2,1)S(1)}, bf16[144,128]{1,0:T(8,128)(2,1)S(1)}, u32[]{:S(2)}, u32[]{:S(2)}) collective-permute-start(bf16[144,128]{1,0:T(8,128)(2,1)S(1)} %get-tuple-element.59), channel_id=1, source_target_pairs={{0,8},{8,0},{16,24},{24,16},{32,40},{40,32},{48,56},{56,48},{64,72... | collective-permute-start | bytes 110600 | tf_op jit(solution)/shard_map/ppermute | solution.py:253
  59.1 0.0 copy-start
  59.1 1.8 %shard_map.59 = (f32[4,512,256]{2,1,0:T(8,128)S(1)}, f32[4,512,128]{2,1,0:T(8,128)}) custom-call(s32[3]{0:T(128)S(1)} %pad_add_fusion.place_ref, bf16[512,512]{1,0:T(8,128)(2,1)S(1)} %copy-done.1, bf16[512,256]{1,0:T(8,128)(2,1)S(1)} %collective-permute-done.2.kv_ref, f32[4,512,256]{2,1,0:T(8,128)S(1)} %get-tuple-element.40.acc_in, ...), custom_call_target="tpu_custom_call" | custom-call | flops 536870912 | bytes 4000000 | tf_op jit(solution)/shard_map/pallas_call | solution.py:137
  60.9 0.0 collective-permute-done.8.mem2
  60.9 0.7 collective-permute-done.7.mem1
  61.6 1.5 %shard_map.60 = (bf16[256,512]{1,0:T(8,128)(2,1)S(1)}, bf16[256,512]{1,0:T(8,128)(2,1)S(1)}) custom-call(s32[3]{0:T(128)S(1)} %pad_add_fusion.place_ref, f32[4]{0:T(128)S(1)} %copy-done.2, bf16[512,512]{1,0:T(8,128)(2,1)S(1)} %copy-done.1, f32[4,512,256]{2,1,0:T(8,128)S(1)} %get-tuple-element.42.acc_ref, f32[144,128]{1,0:T(8,128)S(1)} %get-tuple-element.60.mem0, ...), custom_call_target="tpu_custom_call" | custom-call | flops 402653184 | bytes 4000000 | tf_op jit(solution)/shard_map/pallas_call | solution.py:176
  63.0 3.9 %collective-permute-start.10 = (bf16[256,512]{1,0:T(8,128)(2,1)S(1)}, bf16[256,512]{1,0:T(8,128)(2,1)S(1)}, u32[]{:S(2)}, u32[]{:S(2)}) collective-permute-start(bf16[256,512]{1,0:T(8,128)(2,1)S(1)} %get-tuple-element.50), channel_id=1, source_target_pairs={{0,1},{1,0},{2,3},{3,2},{4,5},{5,4},{6,7},{7,6},{8,9},{9,8},{10,11... | collective-permute-start | bytes 786440 | tf_op jit(solution)/shard_map/ppermute | solution.py:277
  66.9 1.1 %collective-permute-done.10.got_ref = bf16[256,512]{1,0:T(8,128)(2,1)S(1)} collective-permute-done((bf16[256,512]{1,0:T(8,128)(2,1)S(1)}, bf16[256,512]{1,0:T(8,128)(2,1)S(1)}, u32[]{:S(2)}, u32[]{:S(2)}) %collective-permute-start.10) | collective-permute-done | bytes 262176 | tf_op jit(solution)/shard_map/ppermute | solution.py:277
  68.0 0.0 collective-permute-done.11.w_other_ref
  68.0 3.5 %shard_map.62 = (bf16[64,2048]{1,0:T(8,128)(2,1)S(1)}, bf16[64,2048]{1,0:T(8,128)(2,1)S(1)}, bf16[64,2048]{1,0:T(8,128)(2,1)S(1)}, bf16[64,2048]{1,0:T(8,128)(2,1)S(1)}) custom-call(bf16[256,512]{1,0:T(8,128)(2,1)S(1)} %get-tuple-element.49.keep_ref, bf16[256,512]{1,0:T(8,128)(2,1)S(1)} %collective-permute-done.10.got_ref, bf16[512,4096]{1,0:T(8,128)(2,1)S(1)} %copy-done, ...), custom_call_target="tpu_custom_call" | custom-call | flops 1073741824 | bytes 6000000 | tf_op jit(solution)/shard_map/pallas_call | solution.py:202
  71.5 4.4 %collective-permute-start.15 = (bf16[64,2048]{1,0:T(8,128)(2,1)S(1)}, bf16[64,2048]{1,0:T(8,128)(2,1)S(1)}, u32[]{:S(2)}, u32[]{:S(2)}) collective-permute-start(bf16[64,2048]{1,0:T(8,128)(2,1)S(1)} %get-tuple-element.57), channel_id=1, source_target_pairs={{0,6},{1,7},{2,0},{3,1},{4,2},{5,3},{6,4},{7,5},{8,14},{9,15},{10,... | collective-permute-start | bytes 786440 | tf_op jit(solution)/shard_map/ppermute | solution.py:282
  75.9 3.5 %shard_map.61 = (bf16[64,2048]{1,0:T(8,128)(2,1)S(1)}, bf16[64,2048]{1,0:T(8,128)(2,1)S(1)}, bf16[64,2048]{1,0:T(8,128)(2,1)S(1)}, bf16[64,2048]{1,0:T(8,128)(2,1)S(1)}) custom-call(bf16[256,512]{1,0:T(8,128)(2,1)S(1)} %get-tuple-element.49.keep_ref, bf16[256,512]{1,0:T(8,128)(2,1)S(1)} %collective-permute-done.10.got_ref, bf16[512,4096]{1,0:T(8,128)(2,1)S(1)} %copy-done, ...), custom_call_target="tpu_custom_call" | custom-call | flops 1073741824 | bytes 6000000 | tf_op jit(solution)/shard_map/pallas_call | solution.py:202
  79.4 1.9 %collective-permute-start.13 = (bf16[64,2048]{1,0:T(8,128)(2,1)S(1)}, bf16[64,2048]{1,0:T(8,128)(2,1)S(1)}, u32[]{:S(2)}, u32[]{:S(2)}) collective-permute-start(bf16[64,2048]{1,0:T(8,128)(2,1)S(1)} %get-tuple-element.54), channel_id=1, source_target_pairs={{0,2},{1,3},{2,4},{3,5},{4,6},{5,7},{6,0},{7,1},{8,10},{9,11},{10,... | collective-permute-start | bytes 786440 | tf_op jit(solution)/shard_map/ppermute | solution.py:279
  81.3 2.1 %collective-permute-start.17 = (bf16[64,2048]{1,0:T(8,128)(2,1)S(1)}, bf16[64,2048]{1,0:T(8,128)(2,1)S(1)}, u32[]{:S(2)}, u32[]{:S(2)}) collective-permute-start(bf16[64,2048]{1,0:T(8,128)(2,1)S(1)} %get-tuple-element.58), channel_id=1, source_target_pairs={{0,2},{1,3},{2,4},{3,5},{4,6},{5,7},{6,0},{7,1},{8,10},{9,11},{10,... | collective-permute-start | bytes 786440 | tf_op jit(solution)/shard_map/ppermute | solution.py:283
  83.4 4.4 %collective-permute-start.12 = (bf16[64,2048]{1,0:T(8,128)(2,1)S(1)}, bf16[64,2048]{1,0:T(8,128)(2,1)S(1)}, u32[]{:S(2)}, u32[]{:S(2)}) collective-permute-start(bf16[64,2048]{1,0:T(8,128)(2,1)S(1)} %get-tuple-element.52), channel_id=1, source_target_pairs={{0,6},{1,7},{2,0},{3,1},{4,2},{5,3},{6,4},{7,5},{8,14},{9,15},{10,... | collective-permute-start | bytes 786440 | tf_op jit(solution)/shard_map/ppermute | solution.py:280
  87.8 0.0 collective-permute-done.15
  87.8 0.1 add.45
  87.9 3.4 %collective-permute-start.16 = (bf16[64,2048]{1,0:T(8,128)(2,1)S(1)}, bf16[64,2048]{1,0:T(8,128)(2,1)S(1)}, u32[]{:S(2)}, u32[]{:S(2)}) collective-permute-start(bf16[64,2048]{1,0:T(8,128)(2,1)S(1)} %add.45), channel_id=1, source_target_pairs={{0,6},{1,7},{2,0},{3,1},{4,2},{5,3},{6,4},{7,5},{8,14},{9,15},{10,... | collective-permute-start | bytes 786440 | tf_op jit(solution)/shard_map/ppermute | solution.py:285
  91.3 0.0 collective-permute-done.13
  91.3 0.1 add.44
  91.4 1.9 %collective-permute-start.14 = (bf16[64,2048]{1,0:T(8,128)(2,1)S(1)}, bf16[64,2048]{1,0:T(8,128)(2,1)S(1)}, u32[]{:S(2)}, u32[]{:S(2)}) collective-permute-start(bf16[64,2048]{1,0:T(8,128)(2,1)S(1)} %add.44), channel_id=1, source_target_pairs={{0,2},{1,3},{2,4},{3,5},{4,6},{5,7},{6,0},{7,1},{8,10},{9,11},{10,... | collective-permute-start | bytes 786440 | tf_op jit(solution)/shard_map/ppermute | solution.py:284
  93.3 2.0 %collective-permute-done.17.right_b = bf16[64,2048]{1,0:T(8,128)(2,1)S(1)} collective-permute-done((bf16[64,2048]{1,0:T(8,128)(2,1)S(1)}, bf16[64,2048]{1,0:T(8,128)(2,1)S(1)}, u32[]{:S(2)}, u32[]{:S(2)}) %collective-permute-start.17) | collective-permute-done | bytes 262176 | tf_op jit(solution)/shard_map/ppermute | solution.py:283
  95.3 2.9 %collective-permute-done.16.left_b = bf16[64,2048]{1,0:T(8,128)(2,1)S(1)} collective-permute-done((bf16[64,2048]{1,0:T(8,128)(2,1)S(1)}, bf16[64,2048]{1,0:T(8,128)(2,1)S(1)}, u32[]{:S(2)}, u32[]{:S(2)}) %collective-permute-start.16) | collective-permute-done | bytes 262176 | tf_op jit(solution)/shard_map/ppermute | solution.py:285
  98.2 2.3 %collective-permute-done.14.right_a = bf16[64,2048]{1,0:T(8,128)(2,1)S(1)} collective-permute-done((bf16[64,2048]{1,0:T(8,128)(2,1)S(1)}, bf16[64,2048]{1,0:T(8,128)(2,1)S(1)}, u32[]{:S(2)}, u32[]{:S(2)}) %collective-permute-start.14) | collective-permute-done | bytes 262176 | tf_op jit(solution)/shard_map/ppermute | solution.py:284
  100.5 1.0 shard_map.63
  (12 shorter events, 0.1 us)
Async XLA Ops:
  0.0 68.0 %collective-permute-start.11 = (bf16[512,4096]{1,0:T(8,128)(2,1)}, bf16[512,4096]{1,0:T(8,128)(2,1)}, u32[]{:S(2)}, u32[]{:S(2)}) collective-permute-start(bf16[512,4096]{1,0:T(8,128)(2,1)} %w_own_ref.3), channel_id=1, source_target_pairs={{0,1},{1,0},{2,3},{3,2},{4,5},{5,4},{6,7},{7,6},{8,9},{9,8},{10,11... | collective-permute-start | bytes 12582920 | tf_op jit(solution)/shard_map/ppermute | solution.py:263
  10.7 24.1 %collective-permute-start.4 = (bf16[512,256]{1,0:T(8,128)(2,1)S(1)}, bf16[512,256]{1,0:T(8,128)(2,1)S(1)}, u32[]{:S(2)}, u32[]{:S(2)}) collective-permute-start(bf16[512,256]{1,0:T(8,128)(2,1)S(1)} %constant_dynamic-update-slice_fusion.kv_ref), channel_id=1, source_target_pairs={{0,8},{8,16},{16,24},{32,40},{40,48},{48,56},{64,72},{72,80},{80,8... | collective-permute-start | bytes 786440 | tf_op jit(solution)/shard_map/ppermute | solution.py:253
  12.3 2.3 %collective-permute-start = (bf16[144,128]{1,0:T(8,128)(2,1)S(1)}, bf16[144,128]{1,0:T(8,128)(2,1)S(1)}, u32[]{:S(2)}, u32[]{:S(2)}) collective-permute-start(bf16[144,128]{1,0:T(8,128)(2,1)S(1)} %get-tuple-element.33), channel_id=1, source_target_pairs={{0,64},{8,72},{16,80},{24,88},{32,96},{40,104},{48,112},{56,120},{... | collective-permute-start | bytes 110600 | tf_op jit(solution)/shard_map/ppermute | solution.py:253
  14.6 12.5 %collective-permute-start.1 = (bf16[144,128]{1,0:T(8,128)(2,1)S(1)}, bf16[144,128]{1,0:T(8,128)(2,1)S(1)}, u32[]{:S(2)}, u32[]{:S(2)}) collective-permute-start(bf16[144,128]{1,0:T(8,128)(2,1)S(1)} %fusion), channel_id=1, source_target_pairs={{0,128},{8,136},{16,144},{24,152},{32,160},{40,168},{48,176},{56,1... | collective-permute-start | bytes 110600 | tf_op jit(solution)/shard_map/ppermute | solution.py:253
  18.5 1.0 %copy-start.1 = (bf16[512,512]{1,0:T(8,128)(2,1)S(1)}, bf16[512,512]{1,0:T(8,128)(2,1)}, u32[]{:S(2)}) copy-start(bf16[512,512]{1,0:T(8,128)(2,1)} %q_ref.9) | copy-start | bytes 1572868
  21.0 22.5 %collective-permute-start.3 = (bf16[512,256]{1,0:T(8,128)(2,1)S(1)}, bf16[512,256]{1,0:T(8,128)(2,1)S(1)}, u32[]{:S(2)}, u32[]{:S(2)}) collective-permute-start(bf16[512,256]{1,0:T(8,128)(2,1)S(1)} %constant_dynamic-update-slice_fusion.kv_ref), channel_id=1, source_target_pairs={{0,16},{8,24},{32,48},{40,56},{64,80},{72,88},{96,112},{104,120},{... | collective-permute-start | bytes 786440 | tf_op jit(solution)/shard_map/ppermute | solution.py:253
  27.2 8.4 %collective-permute-start.5 = (bf16[144,128]{1,0:T(8,128)(2,1)S(1)}, bf16[144,128]{1,0:T(8,128)(2,1)S(1)}, u32[]{:S(2)}, u32[]{:S(2)}) collective-permute-start(bf16[144,128]{1,0:T(8,128)(2,1)S(1)} %add_convert_fusion.1), channel_id=1, source_target_pairs={{0,256},{8,264},{16,272},{24,280},{32,288},{40,296},{48,304},{56,3... | collective-permute-start | bytes 110600 | tf_op jit(solution)/shard_map/ppermute | solution.py:253
  33.2 25.8 %collective-permute-start.2 = (bf16[512,256]{1,0:T(8,128)(2,1)S(1)}, bf16[512,256]{1,0:T(8,128)(2,1)S(1)}, u32[]{:S(2)}, u32[]{:S(2)}) collective-permute-start(bf16[512,256]{1,0:T(8,128)(2,1)S(1)} %constant_dynamic-update-slice_fusion.kv_ref), channel_id=1, source_target_pairs={{0,24},{32,56},{64,88},{96,120},{128,152},{160,184},{192,216},{224... | collective-permute-start | bytes 786440 | tf_op jit(solution)/shard_map/ppermute | solution.py:253
  35.6 9.7 %collective-permute-start.6 = (bf16[144,128]{1,0:T(8,128)(2,1)S(1)}, bf16[144,128]{1,0:T(8,128)(2,1)S(1)}, u32[]{:S(2)}, u32[]{:S(2)}) collective-permute-start(bf16[144,128]{1,0:T(8,128)(2,1)S(1)} %add_convert_fusion), channel_id=1, source_target_pairs={{0,32},{8,40},{16,48},{24,56},{32,0},{40,8},{48,16},{56,24},{64,96... | collective-permute-start | bytes 110600 | tf_op jit(solution)/shard_map/ppermute | solution.py:253
  45.3 16.3 %copy-start.2 = (f32[4]{0:T(128)S(1)}, f32[4]{0:T(128)}, u32[]{:S(2)}) copy-start(f32[4]{0:T(128)} %gate_ref.1) | copy-start | bytes 52
  45.3 15.6 %collective-permute-start.9 = (bf16[144,128]{1,0:T(8,128)(2,1)S(1)}, bf16[144,128]{1,0:T(8,128)(2,1)S(1)}, u32[]{:S(2)}, u32[]{:S(2)}) collective-permute-start(bf16[144,128]{1,0:T(8,128)(2,1)S(1)} %get-tuple-element.59), channel_id=1, source_target_pairs={{0,24},{8,16},{16,8},{24,0},{32,56},{40,48},{48,40},{56,32},{64,88... | collective-permute-start | bytes 110600 | tf_op jit(solution)/shard_map/ppermute | solution.py:253
  48.8 12.1 %collective-permute-start.8 = (bf16[144,128]{1,0:T(8,128)(2,1)S(1)}, bf16[144,128]{1,0:T(8,128)(2,1)S(1)}, u32[]{:S(2)}, u32[]{:S(2)}) collective-permute-start(bf16[144,128]{1,0:T(8,128)(2,1)S(1)} %get-tuple-element.59), channel_id=1, source_target_pairs={{0,16},{8,24},{16,0},{24,8},{32,48},{40,56},{48,32},{56,40},{64,80... | collective-permute-start | bytes 110600 | tf_op jit(solution)/shard_map/ppermute | solution.py:253
  56.9 4.7 %collective-permute-start.7 = (bf16[144,128]{1,0:T(8,128)(2,1)S(1)}, bf16[144,128]{1,0:T(8,128)(2,1)S(1)}, u32[]{:S(2)}, u32[]{:S(2)}) collective-permute-start(bf16[144,128]{1,0:T(8,128)(2,1)S(1)} %get-tuple-element.59), channel_id=1, source_target_pairs={{0,8},{8,0},{16,24},{24,16},{32,40},{40,32},{48,56},{56,48},{64,72... | collective-permute-start | bytes 110600 | tf_op jit(solution)/shard_map/ppermute | solution.py:253
  59.1 9.0 %copy-start = (bf16[512,4096]{1,0:T(8,128)(2,1)S(1)}, bf16[512,4096]{1,0:T(8,128)(2,1)}, u32[]{:S(2)}) copy-start(bf16[512,4096]{1,0:T(8,128)(2,1)} %w_own_ref.3) | copy-start | bytes 12582916
  63.0 5.0 %collective-permute-start.10 = (bf16[256,512]{1,0:T(8,128)(2,1)S(1)}, bf16[256,512]{1,0:T(8,128)(2,1)S(1)}, u32[]{:S(2)}, u32[]{:S(2)}) collective-permute-start(bf16[256,512]{1,0:T(8,128)(2,1)S(1)} %get-tuple-element.50), channel_id=1, source_target_pairs={{0,1},{1,0},{2,3},{3,2},{4,5},{5,4},{6,7},{7,6},{8,9},{9,8},{10,11... | collective-permute-start | bytes 786440 | tf_op jit(solution)/shard_map/ppermute | solution.py:277
  71.5 16.3 %collective-permute-start.15 = (bf16[64,2048]{1,0:T(8,128)(2,1)S(1)}, bf16[64,2048]{1,0:T(8,128)(2,1)S(1)}, u32[]{:S(2)}, u32[]{:S(2)}) collective-permute-start(bf16[64,2048]{1,0:T(8,128)(2,1)S(1)} %get-tuple-element.57), channel_id=1, source_target_pairs={{0,6},{1,7},{2,0},{3,1},{4,2},{5,3},{6,4},{7,5},{8,14},{9,15},{10,... | collective-permute-start | bytes 786440 | tf_op jit(solution)/shard_map/ppermute | solution.py:282
  79.4 11.9 %collective-permute-start.13 = (bf16[64,2048]{1,0:T(8,128)(2,1)S(1)}, bf16[64,2048]{1,0:T(8,128)(2,1)S(1)}, u32[]{:S(2)}, u32[]{:S(2)}) collective-permute-start(bf16[64,2048]{1,0:T(8,128)(2,1)S(1)} %get-tuple-element.54), channel_id=1, source_target_pairs={{0,2},{1,3},{2,4},{3,5},{4,6},{5,7},{6,0},{7,1},{8,10},{9,11},{10,... | collective-permute-start | bytes 786440 | tf_op jit(solution)/shard_map/ppermute | solution.py:279
  81.3 14.0 %collective-permute-start.17 = (bf16[64,2048]{1,0:T(8,128)(2,1)S(1)}, bf16[64,2048]{1,0:T(8,128)(2,1)S(1)}, u32[]{:S(2)}, u32[]{:S(2)}) collective-permute-start(bf16[64,2048]{1,0:T(8,128)(2,1)S(1)} %get-tuple-element.58), channel_id=1, source_target_pairs={{0,2},{1,3},{2,4},{3,5},{4,6},{5,7},{6,0},{7,1},{8,10},{9,11},{10,... | collective-permute-start | bytes 786440 | tf_op jit(solution)/shard_map/ppermute | solution.py:283
  83.4 11.9 %collective-permute-start.12 = (bf16[64,2048]{1,0:T(8,128)(2,1)S(1)}, bf16[64,2048]{1,0:T(8,128)(2,1)S(1)}, u32[]{:S(2)}, u32[]{:S(2)}) collective-permute-start(bf16[64,2048]{1,0:T(8,128)(2,1)S(1)} %get-tuple-element.52), channel_id=1, source_target_pairs={{0,6},{1,7},{2,0},{3,1},{4,2},{5,3},{6,4},{7,5},{8,14},{9,15},{10,... | collective-permute-start | bytes 786440 | tf_op jit(solution)/shard_map/ppermute | solution.py:280
  87.9 10.3 %collective-permute-start.16 = (bf16[64,2048]{1,0:T(8,128)(2,1)S(1)}, bf16[64,2048]{1,0:T(8,128)(2,1)S(1)}, u32[]{:S(2)}, u32[]{:S(2)}) collective-permute-start(bf16[64,2048]{1,0:T(8,128)(2,1)S(1)} %add.45), channel_id=1, source_target_pairs={{0,6},{1,7},{2,0},{3,1},{4,2},{5,3},{6,4},{7,5},{8,14},{9,15},{10,... | collective-permute-start | bytes 786440 | tf_op jit(solution)/shard_map/ppermute | solution.py:285
  91.4 9.1 %collective-permute-start.14 = (bf16[64,2048]{1,0:T(8,128)(2,1)S(1)}, bf16[64,2048]{1,0:T(8,128)(2,1)S(1)}, u32[]{:S(2)}, u32[]{:S(2)}) collective-permute-start(bf16[64,2048]{1,0:T(8,128)(2,1)S(1)} %add.44), channel_id=1, source_target_pairs={{0,2},{1,3},{2,4},{3,5},{4,6},{5,7},{6,0},{7,1},{8,10},{9,11},{10,... | collective-permute-start | bytes 786440 | tf_op jit(solution)/shard_map/ppermute | solution.py:284

commit v4 on v3

--- a/solution.py
+++ b/solution.py
@@ -109,7 +109,15 @@
     )(queries, kv)
 
 
-def step_kernel(distance, place_ref, q_ref, kv_ref, acc_in, top_in, acc_ref, top_ref):
+def step_kernel(distance, place_ref, q_ref, kv_ref, acc_in, top_in, *rest):
+    if distance == SPAN - 1:
+        w_hbm, acc_ref, w_ref, sem = rest
+        top_ref = None
+        copy = pltpu.make_async_copy(w_hbm, w_ref, sem)
+        copy.start()
+    else:
+        acc_ref, top_ref = rest
+
     @pl.when(place_ref[0] >= distance)
     def _():
         k = kv_ref[:, :HD]
@@ -125,31 +133,39 @@
                 p = jnp.exp2((s - jnp.concatenate([top] * SPAN, axis=1)) * SCALE).astype(BF16)
                 pv = jnp.dot(p, wide, preferred_element_type=F32)
                 acc_ref[h, rows, :] = acc_in[h, rows, :] * jnp.concatenate([shrink, shrink], axis=1) + pv
-                top_ref[h, rows, :] = top
+                if top_ref is not None:
+                    top_ref[h, rows, :] = top
 
     @pl.when(place_ref[0] < distance)
     def _():
         acc_ref[...] = acc_in[...]
-        top_ref[...] = top_in[...]
-
-
-def step_call(distance, place, queries, kv, acc, top):
+        if top_ref is not None:
+            top_ref[...] = top_in[...]
+
+    if distance == SPAN - 1:
+        copy.wait()
+
+
+def step_call(distance, place, queries, kv, acc, top, *weights):
+    last = distance == SPAN - 1
+    state = (
+        jax.ShapeDtypeStruct((GROUP, ROWS, 2 * HD), F32),
+        jax.ShapeDtypeStruct((GROUP, ROWS, HD), F32),
+    )
     return call(
         functools.partial(step_kernel, distance),
-        (
-            jax.ShapeDtypeStruct((GROUP, ROWS, 2 * HD), F32),
-            jax.ShapeDtypeStruct((GROUP, ROWS, HD), F32),
-        ),
+        (state[0], jax.ShapeDtypeStruct(weights[0].shape, BF16)) if last else state,
         (GROUP * ROWS * ROWS * HD * 4, 4000000, GROUP * ROWS * ROWS),
-        in_specs=[SM] + [VM] * 4,
+        in_specs=[SM] + [VM] * 4 + [pl.BlockSpec(memory_space=pl.ANY)] * len(weights),
         out_specs=(VM, VM),
-    )(place, queries, kv, acc, top)
-
-
-def merge_kernel(place_ref, gate_ref, q_ref, acc_ref, mem0, mem1, mem2, mem3, keep_ref, send_ref, out_ref):
+        scratch_shapes=[pltpu.SemaphoreType.DMA] * len(weights),
+    )(place, queries, kv, acc, top, *weights)
+
+
+def merge_kernel(place_ref, gate_ref, q_ref, acc_ref, mem0, mem1, keep_ref, send_ref, out_ref):
     x = place_ref[1]
     core = place_ref[2]
-    mem = mem0[...] + mem1[...].astype(F32) + (mem2[...].astype(F32) + mem3[...].astype(F32))
+    mem = mem0[...] + mem1[...].astype(F32)
     mem = jnp.concatenate([mem[:HD, :], jnp.broadcast_to(mem[HD : HD + 1, :], (HD, HD))], axis=0)
     mem_high, mem_low = split_two(mem)
     mem_twice = jnp.concatenate([mem_high, mem_high], axis=1)
@@ -171,16 +187,16 @@
         send_ref[b * BLOCK : (b + 1) * BLOCK, :] = out_ref[pl.ds(other, BLOCK), :]
 
 
-def merge_call(place, gates, queries, acc, mems):
+def merge_call(place, gates, queries, acc, mem0, mem1):
     half = jax.ShapeDtypeStruct((ROWS // 2, GROUP * HD), BF16)
     return call(
         merge_kernel,
         (half, half),
         (6 * ROWS * GROUP * HD * HD * 2, 4000000, ROWS * GROUP * HD),
-        in_specs=[SM, SM] + [VM] * 6,
+        in_specs=[SM, SM] + [VM] * 4,
         out_specs=(VM, VM),
         scratch_shapes=[pltpu.VMEM((ROWS, GROUP * HD), BF16)],
-    )(place, gates, queries, acc, *mems)
+    )(place, gates, queries, acc, mem0, mem1)
 
 
 def project_kernel(first, keep_ref, got_ref, w_own_ref, w_other_ref, own_ref, right_ref, far_ref, left_ref):
@@ -251,29 +267,26 @@
     tp = lax.axis_index("tp")
     place = jnp.stack([ctx % SPAN, tp // 2, tp % 2]).astype(jnp.int32)
     send = lambda x, route: lax.ppermute(x.astype(BF16), "ctx", route)
-    kv = jnp.concatenate([keys, values], axis=1)
+    kv = jnp.pad(keys, ((0, 0), (0, HD))) + jnp.pad(values, ((0, 0), (HD, 0)))
     delta, delta16 = delta_call(kv)
-    kv1 = send(kv, along_z(1))
-    got = send(delta16, along_y(1))
-    before = got.astype(F32)
-    kv2 = send(after(kv, got), along_z(2))
-    got = send(delta + before, along_y(2))
+    w_other = lax.ppermute(out_weight, "tp", swap(1, N_TP))
+    segment = [send(delta16, swap(k, N_CTX)) for k in (1, 2, 3)]
+    kv1, kv2, kv3 = [send(kv, along_z(d)) for d in (1, 2, 3)]
+    segment = delta + sum(part.astype(F32) for part in segment)
+    other = send(segment, swap(4, N_CTX))
     acc, top = own_call(queries, kv)
-    kv3 = send(after(kv, got), along_z(3))
-    w_other = lax.ppermute(out_weight, "tp", swap(1, N_TP))
-    before = before + after(got, acc).astype(F32)
-    got = send(delta + before, along_y(4))
+    other = after(other, acc).astype(F32)
+    line = segment + other
+    start = jnp.where(ctx % 8 >= SPAN, other, 0.0)
+    before = send(line, along_y(1))
     acc, top = step_call(1, place, queries, kv1, acc, top)
-    before = before + after(got, acc).astype(F32)
-    lower = (ctx % 8) < SPAN
-    got = send(before + jnp.where(lower, delta, 0.0), swap(4, N_CTX))
+    before = after(before, acc).astype(F32)
+    more = send(line + before, along_y(2))
     acc, top = step_call(2, place, queries, kv2, acc, top)
-    mem = before + after(got, acc).astype(F32)
-    mem16 = mem.astype(BF16)
-    mems = [send(mem16, swap(k, N_CTX)) for k in (1, 2, 3)]
-    acc, top = step_call(3, place, queries, kv3, acc, top)
-    mems = [after(m, acc) for m in mems]
-    keep, give = merge_call(place, gates, queries, acc, [mem] + mems)
+    before = before + after(more, acc).astype(F32)
+    far = send(line + before, along_y(4))
+    acc, w_other = step_call(3, place, queries, kv3, acc, top, w_other)
+    keep, give = merge_call(place, gates, queries, acc, start + before, far)
     got = lax.ppermute(give, "tp", swap(1, N_TP))
     own_a, right_a, far_a, left_a = project_call(0, keep, got, out_weight, w_other)
     far_a = lax.ppermute(far_a, "tp", turned(1))

time: 103 us -> 106 us (1.029)
  waiting for transfers between devices: 11 us -> 17.2 us
  Pallas kernels: 14.4 us -> 11.2 us
  local copies, waits for them, and re-layouts: 2.91 us -> 1.05 us
  starting transfers between devices: 72.6 us -> 74.1 us
    ppermute x10, waiting for transfers between devices: 2.62 us -> 8.86 us  [on_device(): send = lambda x, route: lax.ppermute(x.astype(BF16), 'ctx', route)]
    pallas_call x2, Pallas kernels: 6.93 us -> 2.53 us  [project_call(): call(functools.partial(project_kernel, first), (jax.ShapeDtypeStruct((BLO...]
    ppermute x1, starting transfers between devices: 3.85 us -> 6.22 us  [on_device(): got = lax.ppermute(give, 'tp', swap(1, N_TP))]
    pallas_call x3, Pallas kernels: 3.28 us -> 4.53 us  [step_call(): call(functools.partial(step_kernel, distance), (state[0], jax.ShapeDtypeS...]
  transfers between devices with their start and end apart: 18 -> 18, of which waited for: 7 -> 7; matrix products, arithmetic and copies ran while one was open for 2% -> 1% of each run, Pallas kernels for 10% -> 7%
where the time goes in v4:
time: 106 us; the launch traced here: 105 us
  starting transfers between devices  74.1 us (70%)
  waiting for transfers between devices  17.2 us (16%)
  Pallas kernels  11.2 us (11%)
  other arithmetic  1.3 us (1%)
    ppermute x10, starting transfers between devices, on_device(): send = lambda x, route: lax.ppermute(x.astype(BF16), 'ctx', route)  41 us
    ppermute x10, waiting for transfers between devices, on_device(): send = lambda x, route: lax.ppermute(x.astype(BF16), 'ctx', route)  8.86 us
    ppermute x1, starting transfers between devices, on_device(): w_other = lax.ppermute(out_weight, 'tp', swap(1, N_TP))  8.78 us
    ppermute x1, starting transfers between devices, on_device(): got = lax.ppermute(give, 'tp', swap(1, N_TP))  6.22 us
    pallas_call x3, Pallas kernels, step_call(): call(functools.partial(step_kernel, distance), (state[0], jax.ShapeDtypeS...  4.53 us
    ppermute x1, starting transfers between devices, on_device(): left_a = lax.ppermute(left_a, 'tp', turned(-1))  4.4 us
    ppermute x1, starting transfers between devices, on_device(): far_b = lax.ppermute(far_b, 'tp', turned(-1))  4.39 us
    ppermute x1, starting transfers between devices, on_device(): left_b = lax.ppermute(left_b + far_b, 'tp', turned(-1))  3.36 us
  transfers between devices with their start and end apart: 18, of which 7 were waited for; matrix products, arithmetic and copies ran while one was open for 1% of the time, Pallas kernels for 7%

profile of v4, /device:TPU:1, one launch (start us, length us, event | category | flops | bytes accessed | tf_op | source)
XLA Modules:
  0.0 105.2 jit_solution(3708675861129318737)
XLA Ops:
  0.0 8.8 %collective-permute-start.3 = (bf16[512,4096]{1,0:T(8,128)(2,1)}, bf16[512,4096]{1,0:T(8,128)(2,1)}, u32[]{:S(2)}, u32[]{:S(2)}) collective-permute-start(bf16[512,4096]{1,0:T(8,128)(2,1)} %w_own_ref.3), channel_id=1, source_target_pairs={{0,1},{1,0},{2,3},{3,2},{4,5},{5,4},{6,7},{7,6},{8,9},{9,8},{10,11... | collective-permute-start | bytes 12582920 | tf_op jit(solution)/shard_map/ppermute | solution.py:272
  8.8 1.0 pad_add_fusion.kv_ref
  9.8 0.3 shard_map.59
  10.1 2.2 %collective-permute-start.6 = (bf16[144,128]{1,0:T(8,128)(2,1)S(1)}, bf16[144,128]{1,0:T(8,128)(2,1)S(1)}, u32[]{:S(2)}, u32[]{:S(2)}) collective-permute-start(bf16[144,128]{1,0:T(8,128)(2,1)S(1)} %get-tuple-element.36), channel_id=1, source_target_pairs={{0,24},{8,16},{16,8},{24,0},{32,56},{40,48},{48,40},{56,32},{64,88... | collective-permute-start | bytes 110600 | tf_op jit(solution)/shard_map/ppermute | solution.py:269
  12.3 1.9 %collective-permute-start.5 = (bf16[144,128]{1,0:T(8,128)(2,1)S(1)}, bf16[144,128]{1,0:T(8,128)(2,1)S(1)}, u32[]{:S(2)}, u32[]{:S(2)}) collective-permute-start(bf16[144,128]{1,0:T(8,128)(2,1)S(1)} %get-tuple-element.36), channel_id=1, source_target_pairs={{0,16},{8,24},{16,0},{24,8},{32,48},{40,56},{48,32},{56,40},{64,80... | collective-permute-start | bytes 110600 | tf_op jit(solution)/shard_map/ppermute | solution.py:269
  14.3 5.1 %collective-permute-start.4 = (bf16[144,128]{1,0:T(8,128)(2,1)S(1)}, bf16[144,128]{1,0:T(8,128)(2,1)S(1)}, u32[]{:S(2)}, u32[]{:S(2)}) collective-permute-start(bf16[144,128]{1,0:T(8,128)(2,1)S(1)} %get-tuple-element.36), channel_id=1, source_target_pairs={{0,8},{8,0},{16,24},{24,16},{32,40},{40,32},{48,56},{56,48},{64,72... | collective-permute-start | bytes 110600 | tf_op jit(solution)/shard_map/ppermute | solution.py:269
  19.4 1.9 %collective-permute-start.2 = (bf16[512,256]{1,0:T(8,128)(2,1)S(1)}, bf16[512,256]{1,0:T(8,128)(2,1)S(1)}, u32[]{:S(2)}, u32[]{:S(2)}) collective-permute-start(bf16[512,256]{1,0:T(8,128)(2,1)S(1)} %pad_add_fusion.kv_ref), channel_id=1, source_target_pairs={{0,8},{8,16},{16,24},{32,40},{40,48},{48,56},{64,72},{72,80},{80,8... | collective-permute-start | bytes 786440 | tf_op jit(solution)/shard_map/ppermute | solution.py:269
  21.4 0.1 pad_add_fusion.1.place_ref
  21.4 0.0 collective-permute-done.6
  21.4 2.5 %collective-permute-start.1 = (bf16[512,256]{1,0:T(8,128)(2,1)S(1)}, bf16[512,256]{1,0:T(8,128)(2,1)S(1)}, u32[]{:S(2)}, u32[]{:S(2)}) collective-permute-start(bf16[512,256]{1,0:T(8,128)(2,1)S(1)} %pad_add_fusion.kv_ref), channel_id=1, source_target_pairs={{0,16},{8,24},{32,48},{40,56},{64,80},{72,88},{96,112},{104,120},{... | collective-permute-start | bytes 786440 | tf_op jit(solution)/shard_map/ppermute | solution.py:269
  24.0 1.3 %collective-permute-start = (bf16[512,256]{1,0:T(8,128)(2,1)S(1)}, bf16[512,256]{1,0:T(8,128)(2,1)S(1)}, u32[]{:S(2)}, u32[]{:S(2)}) collective-permute-start(bf16[512,256]{1,0:T(8,128)(2,1)S(1)} %pad_add_fusion.kv_ref), channel_id=1, source_target_pairs={{0,24},{32,56},{64,88},{96,120},{128,152},{160,184},{192,216},{224... | collective-permute-start | bytes 786440 | tf_op jit(solution)/shard_map/ppermute | solution.py:269
  25.3 0.0 collective-permute-done.4
  25.3 7.9 %collective-permute-start.7 = (bf16[144,128]{1,0:T(8,128)(2,1)S(1)}, bf16[144,128]{1,0:T(8,128)(2,1)S(1)}, u32[]{:S(2)}, u32[]{:S(2)}) collective-permute-start(bf16[144,128]{1,0:T(8,128)(2,1)S(1)} %get-tuple-element.51), channel_id=1, source_target_pairs={{0,32},{8,40},{16,48},{24,56},{32,0},{40,8},{48,16},{56,24},{64,96... | collective-permute-start | bytes 110600 | tf_op jit(solution)/shard_map/ppermute | solution.py:269
  33.3 0.0 copy-start.1
  33.3 1.0 copy-done.1
  34.3 1.4 %shard_map.55 = (f32[4,512,256]{2,1,0:T(8,128)S(1)}, f32[4,512,128]{2,1,0:T(8,128)S(1)}) custom-call(bf16[512,512]{1,0:T(8,128)(2,1)S(1)} %copy-done.1, bf16[512,256]{1,0:T(8,128)(2,1)S(1)} %pad_add_fusion.kv_ref), custom_call_target="tpu_custom_call" | custom-call | flops 536870912 | bytes 4000000 | tf_op jit(solution)/shard_map/pallas_call | solution.py:100
  35.7 8.3 %collective-permute-done.7 = bf16[144,128]{1,0:T(8,128)(2,1)S(1)} collective-permute-done((bf16[144,128]{1,0:T(8,128)(2,1)S(1)}, bf16[144,128]{1,0:T(8,128)(2,1)S(1)}, u32[]{:S(2)}, u32[]{:S(2)}) %collective-permute-start.7) | collective-permute-done | bytes 36896 | tf_op jit(solution)/shard_map/ppermute | solution.py:269
  44.0 3.2 %collective-permute-start.8 = (bf16[144,128]{1,0:T(8,128)(2,1)S(1)}, bf16[144,128]{1,0:T(8,128)(2,1)S(1)}, u32[]{:S(2)}, u32[]{:S(2)}) collective-permute-start(bf16[144,128]{1,0:T(8,128)(2,1)S(1)} %fusion.2), channel_id=1, source_target_pairs={{0,64},{8,72},{16,80},{24,88},{32,96},{40,104},{48,112},{56,120},{... | collective-permute-start | bytes 110600 | tf_op jit(solution)/shard_map/ppermute | solution.py:269
  47.2 0.0 collective-permute-done.2.kv_ref
  47.3 0.8 shard_map.56
  48.0 0.3 collective-permute-done.8
  48.3 4.7 %collective-permute-start.9 = (bf16[144,128]{1,0:T(8,128)(2,1)S(1)}, bf16[144,128]{1,0:T(8,128)(2,1)S(1)}, u32[]{:S(2)}, u32[]{:S(2)}) collective-permute-start(bf16[144,128]{1,0:T(8,128)(2,1)S(1)} %fusion.1), channel_id=1, source_target_pairs={{0,128},{8,136},{16,144},{24,152},{32,160},{40,168},{48,176},{56,1... | collective-permute-start | bytes 110600 | tf_op jit(solution)/shard_map/ppermute | solution.py:269
  53.0 0.0 collective-permute-done.1.kv_ref
  53.0 0.8 shard_map.57
  53.8 0.3 collective-permute-done.9
  54.1 10.2 %collective-permute-start.10 = (bf16[144,128]{1,0:T(8,128)(2,1)S(1)}, bf16[144,128]{1,0:T(8,128)(2,1)S(1)}, u32[]{:S(2)}, u32[]{:S(2)}) collective-permute-start(bf16[144,128]{1,0:T(8,128)(2,1)S(1)} %get-tuple-element.53), channel_id=1, source_target_pairs={{0,256},{8,264},{16,272},{24,280},{32,288},{40,296},{48,304},{56,3... | collective-permute-start | bytes 110600 | tf_op jit(solution)/shard_map/ppermute | solution.py:269
  64.3 0.0 collective-permute-done.3.rest_0_
  64.3 0.0 copy-start.2
  64.3 0.0 copy-start
  64.3 3.0 %shard_map.58 = (f32[4,512,256]{2,1,0:T(8,128)S(1)}, bf16[512,4096]{1,0:T(8,128)(2,1)S(1)}) custom-call(s32[3]{0:T(128)S(1)} %pad_add_fusion.1.place_ref, bf16[512,512]{1,0:T(8,128)(2,1)S(1)} %copy-done.1, bf16[512,256]{1,0:T(8,128)(2,1)S(1)} %collective-permute-done.kv_ref, f32[4,512,256]{2,1,0:T(8,128)S(1)} %get-tuple-element.32.acc_in, ...), custom_call_target="tpu_custom_call" | custom-call | flops 536870912 | bytes 4000000 | tf_op jit(solution)/shard_map/pallas_call | solution.py:155
  67.4 1.5 %shard_map.60 = (bf16[256,512]{1,0:T(8,128)(2,1)S(1)}, bf16[256,512]{1,0:T(8,128)(2,1)S(1)}) custom-call(s32[3]{0:T(128)S(1)} %pad_add_fusion.1.place_ref, f32[4]{0:T(128)S(1)} %copy-done.2, bf16[512,512]{1,0:T(8,128)(2,1)S(1)} %copy-done.1, f32[4,512,256]{2,1,0:T(8,128)S(1)} %get-tuple-element.34.acc_ref, f32[144,128]{1,0:T(8,128)S(1)} %get-tuple-element.54.mem0, ...), custom_call_target="tpu_custom_call" | custom-call | flops 402653184 | bytes 4000000 | tf_op jit(solution)/shard_map/pallas_call | solution.py:192
  68.8 6.2 %collective-permute-start.11 = (bf16[256,512]{1,0:T(8,128)(2,1)S(1)}, bf16[256,512]{1,0:T(8,128)(2,1)S(1)}, u32[]{:S(2)}, u32[]{:S(2)}) collective-permute-start(bf16[256,512]{1,0:T(8,128)(2,1)S(1)} %get-tuple-element.41), channel_id=1, source_target_pairs={{0,1},{1,0},{2,3},{3,2},{4,5},{5,4},{6,7},{7,6},{8,9},{9,8},{10,11... | collective-permute-start | bytes 786440 | tf_op jit(solution)/shard_map/ppermute | solution.py:290
  75.1 1.1 %collective-permute-done.11.got_ref = bf16[256,512]{1,0:T(8,128)(2,1)S(1)} collective-permute-done((bf16[256,512]{1,0:T(8,128)(2,1)S(1)}, bf16[256,512]{1,0:T(8,128)(2,1)S(1)}, u32[]{:S(2)}, u32[]{:S(2)}) %collective-permute-start.11) | collective-permute-done | bytes 262176 | tf_op jit(solution)/shard_map/ppermute | solution.py:290
  76.2 1.3 %shard_map.62 = (bf16[64,2048]{1,0:T(8,128)(2,1)S(1)}, bf16[64,2048]{1,0:T(8,128)(2,1)S(1)}, bf16[64,2048]{1,0:T(8,128)(2,1)S(1)}, bf16[64,2048]{1,0:T(8,128)(2,1)S(1)}) custom-call(bf16[256,512]{1,0:T(8,128)(2,1)S(1)} %get-tuple-element.40.keep_ref, bf16[256,512]{1,0:T(8,128)(2,1)S(1)} %collective-permute-done.11.got_ref, bf16[512,4096]{1,0:T(8,128)(2,1)S(1)} %copy-done, ...), custom_call_target="tpu_custom_call" | custom-call | flops 1073741824 | bytes 6000000 | tf_op jit(solution)/shard_map/pallas_call | solution.py:218
  77.5 4.4 %collective-permute-start.15 = (bf16[64,2048]{1,0:T(8,128)(2,1)S(1)}, bf16[64,2048]{1,0:T(8,128)(2,1)S(1)}, u32[]{:S(2)}, u32[]{:S(2)}) collective-permute-start(bf16[64,2048]{1,0:T(8,128)(2,1)S(1)} %get-tuple-element.49), channel_id=1, source_target_pairs={{0,6},{1,7},{2,0},{3,1},{4,2},{5,3},{6,4},{7,5},{8,14},{9,15},{10,... | collective-permute-start | bytes 786440 | tf_op jit(solution)/shard_map/ppermute | solution.py:295
  81.9 1.3 %shard_map.61 = (bf16[64,2048]{1,0:T(8,128)(2,1)S(1)}, bf16[64,2048]{1,0:T(8,128)(2,1)S(1)}, bf16[64,2048]{1,0:T(8,128)(2,1)S(1)}, bf16[64,2048]{1,0:T(8,128)(2,1)S(1)}) custom-call(bf16[256,512]{1,0:T(8,128)(2,1)S(1)} %get-tuple-element.40.keep_ref, bf16[256,512]{1,0:T(8,128)(2,1)S(1)} %collective-permute-done.11.got_ref, bf16[512,4096]{1,0:T(8,128)(2,1)S(1)} %copy-done, ...), custom_call_target="tpu_custom_call" | custom-call | flops 1073741824 | bytes 6000000 | tf_op jit(solution)/shard_map/pallas_call | solution.py:218
  83.1 1.9 %collective-permute-start.13 = (bf16[64,2048]{1,0:T(8,128)(2,1)S(1)}, bf16[64,2048]{1,0:T(8,128)(2,1)S(1)}, u32[]{:S(2)}, u32[]{:S(2)}) collective-permute-start(bf16[64,2048]{1,0:T(8,128)(2,1)S(1)} %get-tuple-element.46), channel_id=1, source_target_pairs={{0,2},{1,3},{2,4},{3,5},{4,6},{5,7},{6,0},{7,1},{8,10},{9,11},{10,... | collective-permute-start | bytes 786440 | tf_op jit(solution)/shard_map/ppermute | solution.py:292
  85.1 2.1 %collective-permute-start.17 = (bf16[64,2048]{1,0:T(8,128)(2,1)S(1)}, bf16[64,2048]{1,0:T(8,128)(2,1)S(1)}, u32[]{:S(2)}, u32[]{:S(2)}) collective-permute-start(bf16[64,2048]{1,0:T(8,128)(2,1)S(1)} %get-tuple-element.50), channel_id=1, source_target_pairs={{0,2},{1,3},{2,4},{3,5},{4,6},{5,7},{6,0},{7,1},{8,10},{9,11},{10,... | collective-permute-start | bytes 786440 | tf_op jit(solution)/shard_map/ppermute | solution.py:296
  87.2 4.4 %collective-permute-start.12 = (bf16[64,2048]{1,0:T(8,128)(2,1)S(1)}, bf16[64,2048]{1,0:T(8,128)(2,1)S(1)}, u32[]{:S(2)}, u32[]{:S(2)}) collective-permute-start(bf16[64,2048]{1,0:T(8,128)(2,1)S(1)} %get-tuple-element.44), channel_id=1, source_target_pairs={{0,6},{1,7},{2,0},{3,1},{4,2},{5,3},{6,4},{7,5},{8,14},{9,15},{10,... | collective-permute-start | bytes 786440 | tf_op jit(solution)/shard_map/ppermute | solution.py:293
  91.6 0.0 collective-permute-done.15
  91.6 0.1 add.61
  91.7 3.4 %collective-permute-start.16 = (bf16[64,2048]{1,0:T(8,128)(2,1)S(1)}, bf16[64,2048]{1,0:T(8,128)(2,1)S(1)}, u32[]{:S(2)}, u32[]{:S(2)}) collective-permute-start(bf16[64,2048]{1,0:T(8,128)(2,1)S(1)} %add.61), channel_id=1, source_target_pairs={{0,6},{1,7},{2,0},{3,1},{4,2},{5,3},{6,4},{7,5},{8,14},{9,15},{10,... | collective-permute-start | bytes 786440 | tf_op jit(solution)/shard_map/ppermute | solution.py:298
  95.0 0.1 add.60
  95.1 1.9 %collective-permute-start.14 = (bf16[64,2048]{1,0:T(8,128)(2,1)S(1)}, bf16[64,2048]{1,0:T(8,128)(2,1)S(1)}, u32[]{:S(2)}, u32[]{:S(2)}) collective-permute-start(bf16[64,2048]{1,0:T(8,128)(2,1)S(1)} %add.60), channel_id=1, source_target_pairs={{0,2},{1,3},{2,4},{3,5},{4,6},{5,7},{6,0},{7,1},{8,10},{9,11},{10,... | collective-permute-start | bytes 786440 | tf_op jit(solution)/shard_map/ppermute | solution.py:297
  97.0 2.0 %collective-permute-done.17.right_b = bf16[64,2048]{1,0:T(8,128)(2,1)S(1)} collective-permute-done((bf16[64,2048]{1,0:T(8,128)(2,1)S(1)}, bf16[64,2048]{1,0:T(8,128)(2,1)S(1)}, u32[]{:S(2)}, u32[]{:S(2)}) %collective-permute-start.17) | collective-permute-done | bytes 262176 | tf_op jit(solution)/shard_map/ppermute | solution.py:296
  99.1 2.9 %collective-permute-done.16.left_b = bf16[64,2048]{1,0:T(8,128)(2,1)S(1)} collective-permute-done((bf16[64,2048]{1,0:T(8,128)(2,1)S(1)}, bf16[64,2048]{1,0:T(8,128)(2,1)S(1)}, u32[]{:S(2)}, u32[]{:S(2)}) %collective-permute-start.16) | collective-permute-done | bytes 262176 | tf_op jit(solution)/shard_map/ppermute | solution.py:298
  101.9 2.3 %collective-permute-done.14.right_a = bf16[64,2048]{1,0:T(8,128)(2,1)S(1)} collective-permute-done((bf16[64,2048]{1,0:T(8,128)(2,1)S(1)}, bf16[64,2048]{1,0:T(8,128)(2,1)S(1)}, u32[]{:S(2)}, u32[]{:S(2)}) %collective-permute-start.14) | collective-permute-done | bytes 262176 | tf_op jit(solution)/shard_map/ppermute | solution.py:297
  104.2 1.0 shard_map.63
  (11 shorter events, 0.1 us)
Async XLA Ops:
  0.0 64.3 %collective-permute-start.3 = (bf16[512,4096]{1,0:T(8,128)(2,1)}, bf16[512,4096]{1,0:T(8,128)(2,1)}, u32[]{:S(2)}, u32[]{:S(2)}) collective-permute-start(bf16[512,4096]{1,0:T(8,128)(2,1)} %w_own_ref.3), channel_id=1, source_target_pairs={{0,1},{1,0},{2,3},{3,2},{4,5},{5,4},{6,7},{7,6},{8,9},{9,8},{10,11... | collective-permute-start | bytes 12582920 | tf_op jit(solution)/shard_map/ppermute | solution.py:272
  10.1 11.3 %collective-permute-start.6 = (bf16[144,128]{1,0:T(8,128)(2,1)S(1)}, bf16[144,128]{1,0:T(8,128)(2,1)S(1)}, u32[]{:S(2)}, u32[]{:S(2)}) collective-permute-start(bf16[144,128]{1,0:T(8,128)(2,1)S(1)} %get-tuple-element.36), channel_id=1, source_target_pairs={{0,24},{8,16},{16,8},{24,0},{32,56},{40,48},{48,40},{56,32},{64,88... | collective-permute-start | bytes 110600 | tf_op jit(solution)/shard_map/ppermute | solution.py:269
  12.3 11.6 %collective-permute-start.5 = (bf16[144,128]{1,0:T(8,128)(2,1)S(1)}, bf16[144,128]{1,0:T(8,128)(2,1)S(1)}, u32[]{:S(2)}, u32[]{:S(2)}) collective-permute-start(bf16[144,128]{1,0:T(8,128)(2,1)S(1)} %get-tuple-element.36), channel_id=1, source_target_pairs={{0,16},{8,24},{16,0},{24,8},{32,48},{40,56},{48,32},{56,40},{64,80... | collective-permute-start | bytes 110600 | tf_op jit(solution)/shard_map/ppermute | solution.py:269
  14.3 11.0 %collective-permute-start.4 = (bf16[144,128]{1,0:T(8,128)(2,1)S(1)}, bf16[144,128]{1,0:T(8,128)(2,1)S(1)}, u32[]{:S(2)}, u32[]{:S(2)}) collective-permute-start(bf16[144,128]{1,0:T(8,128)(2,1)S(1)} %get-tuple-element.36), channel_id=1, source_target_pairs={{0,8},{8,0},{16,24},{24,16},{32,40},{40,32},{48,56},{56,48},{64,72... | collective-permute-start | bytes 110600 | tf_op jit(solution)/shard_map/ppermute | solution.py:269
  19.4 27.9 %collective-permute-start.2 = (bf16[512,256]{1,0:T(8,128)(2,1)S(1)}, bf16[512,256]{1,0:T(8,128)(2,1)S(1)}, u32[]{:S(2)}, u32[]{:S(2)}) collective-permute-start(bf16[512,256]{1,0:T(8,128)(2,1)S(1)} %pad_add_fusion.kv_ref), channel_id=1, source_target_pairs={{0,8},{8,16},{16,24},{32,40},{40,48},{48,56},{64,72},{72,80},{80,8... | collective-permute-start | bytes 786440 | tf_op jit(solution)/shard_map/ppermute | solution.py:269
  21.4 31.6 %collective-permute-start.1 = (bf16[512,256]{1,0:T(8,128)(2,1)S(1)}, bf16[512,256]{1,0:T(8,128)(2,1)S(1)}, u32[]{:S(2)}, u32[]{:S(2)}) collective-permute-start(bf16[512,256]{1,0:T(8,128)(2,1)S(1)} %pad_add_fusion.kv_ref), channel_id=1, source_target_pairs={{0,16},{8,24},{32,48},{40,56},{64,80},{72,88},{96,112},{104,120},{... | collective-permute-start | bytes 786440 | tf_op jit(solution)/shard_map/ppermute | solution.py:269
  24.0 40.3 %collective-permute-start = (bf16[512,256]{1,0:T(8,128)(2,1)S(1)}, bf16[512,256]{1,0:T(8,128)(2,1)S(1)}, u32[]{:S(2)}, u32[]{:S(2)}) collective-permute-start(bf16[512,256]{1,0:T(8,128)(2,1)S(1)} %pad_add_fusion.kv_ref), channel_id=1, source_target_pairs={{0,24},{32,56},{64,88},{96,120},{128,152},{160,184},{192,216},{224... | collective-permute-start | bytes 786440 | tf_op jit(solution)/shard_map/ppermute | solution.py:269
  25.3 18.7 %collective-permute-start.7 = (bf16[144,128]{1,0:T(8,128)(2,1)S(1)}, bf16[144,128]{1,0:T(8,128)(2,1)S(1)}, u32[]{:S(2)}, u32[]{:S(2)}) collective-permute-start(bf16[144,128]{1,0:T(8,128)(2,1)S(1)} %get-tuple-element.51), channel_id=1, source_target_pairs={{0,32},{8,40},{16,48},{24,56},{32,0},{40,8},{48,16},{56,24},{64,96... | collective-permute-start | bytes 110600 | tf_op jit(solution)/shard_map/ppermute | solution.py:269
  33.3 1.0 copy-start.1
  44.0 4.2 %collective-permute-start.8 = (bf16[144,128]{1,0:T(8,128)(2,1)S(1)}, bf16[144,128]{1,0:T(8,128)(2,1)S(1)}, u32[]{:S(2)}, u32[]{:S(2)}) collective-permute-start(bf16[144,128]{1,0:T(8,128)(2,1)S(1)} %fusion.2), channel_id=1, source_target_pairs={{0,64},{8,72},{16,80},{24,88},{32,96},{40,104},{48,112},{56,120},{... | collective-permute-start | bytes 110600 | tf_op jit(solution)/shard_map/ppermute | solution.py:269
  48.3 5.7 %collective-permute-start.9 = (bf16[144,128]{1,0:T(8,128)(2,1)S(1)}, bf16[144,128]{1,0:T(8,128)(2,1)S(1)}, u32[]{:S(2)}, u32[]{:S(2)}) collective-permute-start(bf16[144,128]{1,0:T(8,128)(2,1)S(1)} %fusion.1), channel_id=1, source_target_pairs={{0,128},{8,136},{16,144},{24,152},{32,160},{40,168},{48,176},{56,1... | collective-permute-start | bytes 110600 | tf_op jit(solution)/shard_map/ppermute | solution.py:269
  54.1 13.3 %collective-permute-start.10 = (bf16[144,128]{1,0:T(8,128)(2,1)S(1)}, bf16[144,128]{1,0:T(8,128)(2,1)S(1)}, u32[]{:S(2)}, u32[]{:S(2)}) collective-permute-start(bf16[144,128]{1,0:T(8,128)(2,1)S(1)} %get-tuple-element.53), channel_id=1, source_target_pairs={{0,256},{8,264},{16,272},{24,280},{32,288},{40,296},{48,304},{56,3... | collective-permute-start | bytes 110600 | tf_op jit(solution)/shard_map/ppermute | solution.py:269
  64.3 3.1 %copy-start.2 = (f32[4]{0:T(128)S(1)}, f32[4]{0:T(128)}, u32[]{:S(2)}) copy-start(f32[4]{0:T(128)} %gate_ref.1) | copy-start | bytes 52
  64.3 11.9 %copy-start = (bf16[512,4096]{1,0:T(8,128)(2,1)S(1)}, bf16[512,4096]{1,0:T(8,128)(2,1)}, u32[]{:S(2)}) copy-start(bf16[512,4096]{1,0:T(8,128)(2,1)} %w_own_ref.3) | copy-start | bytes 12582916
  68.8 7.4 %collective-permute-start.11 = (bf16[256,512]{1,0:T(8,128)(2,1)S(1)}, bf16[256,512]{1,0:T(8,128)(2,1)S(1)}, u32[]{:S(2)}, u32[]{:S(2)}) collective-permute-start(bf16[256,512]{1,0:T(8,128)(2,1)S(1)} %get-tuple-element.41), channel_id=1, source_target_pairs={{0,1},{1,0},{2,3},{3,2},{4,5},{5,4},{6,7},{7,6},{8,9},{9,8},{10,11... | collective-permute-start | bytes 786440 | tf_op jit(solution)/shard_map/ppermute | solution.py:290
  77.5 14.1 %collective-permute-start.15 = (bf16[64,2048]{1,0:T(8,128)(2,1)S(1)}, bf16[64,2048]{1,0:T(8,128)(2,1)S(1)}, u32[]{:S(2)}, u32[]{:S(2)}) collective-permute-start(bf16[64,2048]{1,0:T(8,128)(2,1)S(1)} %get-tuple-element.49), channel_id=1, source_target_pairs={{0,6},{1,7},{2,0},{3,1},{4,2},{5,3},{6,4},{7,5},{8,14},{9,15},{10,... | collective-permute-start | bytes 786440 | tf_op jit(solution)/shard_map/ppermute | solution.py:295
  83.1 11.9 %collective-permute-start.13 = (bf16[64,2048]{1,0:T(8,128)(2,1)S(1)}, bf16[64,2048]{1,0:T(8,128)(2,1)S(1)}, u32[]{:S(2)}, u32[]{:S(2)}) collective-permute-start(bf16[64,2048]{1,0:T(8,128)(2,1)S(1)} %get-tuple-element.46), channel_id=1, source_target_pairs={{0,2},{1,3},{2,4},{3,5},{4,6},{5,7},{6,0},{7,1},{8,10},{9,11},{10,... | collective-permute-start | bytes 786440 | tf_op jit(solution)/shard_map/ppermute | solution.py:292
  85.1 14.0 %collective-permute-start.17 = (bf16[64,2048]{1,0:T(8,128)(2,1)S(1)}, bf16[64,2048]{1,0:T(8,128)(2,1)S(1)}, u32[]{:S(2)}, u32[]{:S(2)}) collective-permute-start(bf16[64,2048]{1,0:T(8,128)(2,1)S(1)} %get-tuple-element.50), channel_id=1, source_target_pairs={{0,2},{1,3},{2,4},{3,5},{4,6},{5,7},{6,0},{7,1},{8,10},{9,11},{10,... | collective-permute-start | bytes 786440 | tf_op jit(solution)/shard_map/ppermute | solution.py:296
  87.2 11.9 %collective-permute-start.12 = (bf16[64,2048]{1,0:T(8,128)(2,1)S(1)}, bf16[64,2048]{1,0:T(8,128)(2,1)S(1)}, u32[]{:S(2)}, u32[]{:S(2)}) collective-permute-start(bf16[64,2048]{1,0:T(8,128)(2,1)S(1)} %get-tuple-element.44), channel_id=1, source_target_pairs={{0,6},{1,7},{2,0},{3,1},{4,2},{5,3},{6,4},{7,5},{8,14},{9,15},{10,... | collective-permute-start | bytes 786440 | tf_op jit(solution)/shard_map/ppermute | solution.py:293
  91.7 10.3 %collective-permute-start.16 = (bf16[64,2048]{1,0:T(8,128)(2,1)S(1)}, bf16[64,2048]{1,0:T(8,128)(2,1)S(1)}, u32[]{:S(2)}, u32[]{:S(2)}) collective-permute-start(bf16[64,2048]{1,0:T(8,128)(2,1)S(1)} %add.61), channel_id=1, source_target_pairs={{0,6},{1,7},{2,0},{3,1},{4,2},{5,3},{6,4},{7,5},{8,14},{9,15},{10,... | collective-permute-start | bytes 786440 | tf_op jit(solution)/shard_map/ppermute | solution.py:298
  95.1 9.1 %collective-permute-start.14 = (bf16[64,2048]{1,0:T(8,128)(2,1)S(1)}, bf16[64,2048]{1,0:T(8,128)(2,1)S(1)}, u32[]{:S(2)}, u32[]{:S(2)}) collective-permute-start(bf16[64,2048]{1,0:T(8,128)(2,1)S(1)} %add.60), channel_id=1, source_target_pairs={{0,2},{1,3},{2,4},{3,5},{4,6},{5,7},{6,0},{7,1},{8,10},{9,11},{10,... | collective-permute-start | bytes 786440 | tf_op jit(solution)/shard_map/ppermute | solution.py:297

commit v5 on v4

--- a/solution.py
+++ b/solution.py
@@ -43,7 +43,7 @@
     return pl.pallas_call(
         kernel,
         out_shape=out_shape,
-        compiler_params=pltpu.CompilerParams(vmem_limit_bytes=24 * 1024 * 1024),
+        compiler_params=pltpu.CompilerParams(vmem_limit_bytes=16 * 1024 * 1024),
         cost_estimate=pl.CostEstimate(flops=flops, bytes_accessed=read, transcendentals=exps),
         **kw,
     )
@@ -109,15 +109,7 @@
     )(queries, kv)
 
 
-def step_kernel(distance, place_ref, q_ref, kv_ref, acc_in, top_in, *rest):
-    if distance == SPAN - 1:
-        w_hbm, acc_ref, w_ref, sem = rest
-        top_ref = None
-        copy = pltpu.make_async_copy(w_hbm, w_ref, sem)
-        copy.start()
-    else:
-        acc_ref, top_ref = rest
-
+def step_kernel(distance, place_ref, q_ref, kv_ref, acc_in, top_in, acc_ref, top_ref=None):
     @pl.when(place_ref[0] >= distance)
     def _():
         k = kv_ref[:, :HD]
@@ -142,24 +134,37 @@
         if top_ref is not None:
             top_ref[...] = top_in[...]
 
-    if distance == SPAN - 1:
-        copy.wait()
-
-
-def step_call(distance, place, queries, kv, acc, top, *weights):
-    last = distance == SPAN - 1
+
+def step_call(distance, place, queries, kv, acc, top):
     state = (
         jax.ShapeDtypeStruct((GROUP, ROWS, 2 * HD), F32),
         jax.ShapeDtypeStruct((GROUP, ROWS, HD), F32),
     )
+    kept = state[: 1 if distance == SPAN - 1 else 2]
     return call(
         functools.partial(step_kernel, distance),
-        (state[0], jax.ShapeDtypeStruct(weights[0].shape, BF16)) if last else state,
+        kept,
         (GROUP * ROWS * ROWS * HD * 4, 4000000, GROUP * ROWS * ROWS),
-        in_specs=[SM] + [VM] * 4 + [pl.BlockSpec(memory_space=pl.ANY)] * len(weights),
-        out_specs=(VM, VM),
-        scratch_shapes=[pltpu.SemaphoreType.DMA] * len(weights),
-    )(place, queries, kv, acc, top, *weights)
+        in_specs=[SM] + [VM] * 4,
+        out_specs=(VM,) * len(kept),
+    )(place, queries, kv, acc, top)
+
+
+def stage_kernel(w_hbm, w_ref, sem):
+    copy = pltpu.make_async_copy(w_hbm, w_ref, sem)
+    copy.start()
+    copy.wait()
+
+
+def stage_call(w):
+    return call(
+        stage_kernel,
+        jax.ShapeDtypeStruct(w.shape, w.dtype),
+        (0, 8000000, 0),
+        in_specs=[pl.BlockSpec(memory_space=pl.ANY)],
+        out_specs=VM,
+        scratch_shapes=[pltpu.SemaphoreType.DMA],
+    )(w)
 
 
 def merge_kernel(place_ref, gate_ref, q_ref, acc_ref, mem0, mem1, keep_ref, send_ref, out_ref):
@@ -270,22 +275,25 @@
     kv = jnp.pad(keys, ((0, 0), (0, HD))) + jnp.pad(values, ((0, 0), (HD, 0)))
     delta, delta16 = delta_call(kv)
     w_other = lax.ppermute(out_weight, "tp", swap(1, N_TP))
-    segment = [send(delta16, swap(k, N_CTX)) for k in (1, 2, 3)]
     kv1, kv2, kv3 = [send(kv, along_z(d)) for d in (1, 2, 3)]
-    segment = delta + sum(part.astype(F32) for part in segment)
+    more = send(delta16, swap(1, N_CTX))
+    acc, top = own_call(queries, kv)
+    segment = delta + after(more, acc).astype(F32)
+    more = send(segment, swap(2, N_CTX))
+    acc, top = step_call(1, place, queries, kv1, acc, top)
+    segment = segment + after(more, acc).astype(F32)
     other = send(segment, swap(4, N_CTX))
-    acc, top = own_call(queries, kv)
+    acc, top = step_call(2, place, queries, kv2, acc, top)
     other = after(other, acc).astype(F32)
     line = segment + other
     start = jnp.where(ctx % 8 >= SPAN, other, 0.0)
     before = send(line, along_y(1))
-    acc, top = step_call(1, place, queries, kv1, acc, top)
+    (acc,) = step_call(3, place, queries, kv3, acc, top)
     before = after(before, acc).astype(F32)
-    more = send(line + before, along_y(2))
-    acc, top = step_call(2, place, queries, kv2, acc, top)
-    before = before + after(more, acc).astype(F32)
+    before = before + send(line + before, along_y(2)).astype(F32)
     far = send(line + before, along_y(4))
-    acc, w_other = step_call(3, place, queries, kv3, acc, top, w_other)
+    w_other = stage_call(w_other)
+    far = after(far, w_other)
     keep, give = merge_call(place, gates, queries, acc, start + before, far)
     got = lax.ppermute(give, "tp", swap(1, N_TP))
     own_a, right_a, far_a, left_a = project_call(0, keep, got, out_weight, w_other)

time: 106 us -> 107 us (level); the launches traced: 105 us -> 105 us
  starting transfers between devices: 74.1 us -> 68.4 us
  waiting for transfers between devices: 17.2 us -> 22.3 us
    ppermute x10 -> x9, starting transfers between devices: 41 us -> 34.3 us  [on_device(): send = lambda x, route: lax.ppermute(x.astype(BF16), 'ctx', route)]
    ppermute x10 -> x9, waiting for transfers between devices: 8.86 us -> 13.9 us  [on_device(): send = lambda x, route: lax.ppermute(x.astype(BF16), 'ctx', route)]
    ppermute x1, starting transfers between devices: 6.22 us -> 7.3 us  [on_device(): got = lax.ppermute(give, 'tp', swap(1, N_TP))]
    pallas_call x3 -> x4, Pallas kernels: 4.53 us -> 4.55 us  [the longest x1 2.35 us: stage_call(): call(stage_kernel, jax.ShapeDtypeStruct(w.shape, w.dtype), (0, 8000000, 0...]
  transfers between devices with their start and end apart: 18 -> 17, of which waited for: 7 -> 9; matrix products, arithmetic and copies ran while one was open for 1% -> 1% of each run, Pallas kernels for 7% -> 7%
where the time goes in v5:
time: 107 us; the launch traced here: 105 us
  starting transfers between devices  68.4 us (64%)
  waiting for transfers between devices  22.3 us (21%)
  Pallas kernels  11.2 us (10%)
  other arithmetic  1.32 us (1%)
    ppermute x9, starting transfers between devices, on_device(): send = lambda x, route: lax.ppermute(x.astype(BF16), 'ctx', route)  34.3 us
    ppermute x9, waiting for transfers between devices, on_device(): send = lambda x, route: lax.ppermute(x.astype(BF16), 'ctx', route)  13.9 us
    ppermute x1, starting transfers between devices, on_device(): w_other = lax.ppermute(out_weight, 'tp', swap(1, N_TP))  8.78 us
    ppermute x1, starting transfers between devices, on_device(): got = lax.ppermute(give, 'tp', swap(1, N_TP))  7.3 us
    ppermute x1, starting transfers between devices, on_device(): left_a = lax.ppermute(left_a, 'tp', turned(-1))  4.4 us
    ppermute x1, starting transfers between devices, on_device(): far_b = lax.ppermute(far_b, 'tp', turned(-1))  4.38 us
    ppermute x1, starting transfers between devices, on_device(): left_b = lax.ppermute(left_b + far_b, 'tp', turned(-1))  3.36 us
    ppermute x1, waiting for transfers between devices, on_device(): left_b = lax.ppermute(left_b + far_b, 'tp', turned(-1))  2.89 us
  transfers between devices with their start and end apart: 17, of which 9 were waited for; matrix products, arithmetic and copies ran while one was open for 1% of the time, Pallas kernels for 7%

profile of v5, /device:TPU:1, one launch (start us, length us, event | category | flops | bytes accessed | tf_op | source)
XLA Modules:
  0.0 104.6 jit_solution(7986208220329800183)
XLA Ops:
  0.0 8.8 %collective-permute-start.9 = (bf16[512,4096]{1,0:T(8,128)(2,1)}, bf16[512,4096]{1,0:T(8,128)(2,1)}, u32[]{:S(2)}, u32[]{:S(2)}) collective-permute-start(bf16[512,4096]{1,0:T(8,128)(2,1)} %w_own_ref.3), channel_id=1, source_target_pairs={{0,1},{1,0},{2,3},{3,2},{4,5},{5,4},{6,7},{7,6},{8,9},{9,8},{10,11... | collective-permute-start | bytes 12582920 | tf_op jit(solution)/shard_map/ppermute | solution.py:277
  8.8 1.0 pad_add_fusion.kv_ref
  9.8 1.3 %collective-permute-start.2 = (bf16[512,256]{1,0:T(8,128)(2,1)S(1)}, bf16[512,256]{1,0:T(8,128)(2,1)S(1)}, u32[]{:S(2)}, u32[]{:S(2)}) collective-permute-start(bf16[512,256]{1,0:T(8,128)(2,1)S(1)} %pad_add_fusion.kv_ref), channel_id=1, source_target_pairs={{0,8},{8,16},{16,24},{32,40},{40,48},{48,56},{64,72},{72,80},{80,8... | collective-permute-start | bytes 786440 | tf_op jit(solution)/shard_map/ppermute | solution.py:274
  11.1 3.1 %collective-permute-start.1 = (bf16[512,256]{1,0:T(8,128)(2,1)S(1)}, bf16[512,256]{1,0:T(8,128)(2,1)S(1)}, u32[]{:S(2)}, u32[]{:S(2)}) collective-permute-start(bf16[512,256]{1,0:T(8,128)(2,1)S(1)} %pad_add_fusion.kv_ref), channel_id=1, source_target_pairs={{0,16},{8,24},{32,48},{40,56},{64,80},{72,88},{96,112},{104,120},{... | collective-permute-start | bytes 786440 | tf_op jit(solution)/shard_map/ppermute | solution.py:274
  14.3 1.3 %collective-permute-start = (bf16[512,256]{1,0:T(8,128)(2,1)S(1)}, bf16[512,256]{1,0:T(8,128)(2,1)S(1)}, u32[]{:S(2)}, u32[]{:S(2)}) collective-permute-start(bf16[512,256]{1,0:T(8,128)(2,1)S(1)} %pad_add_fusion.kv_ref), channel_id=1, source_target_pairs={{0,24},{32,56},{64,88},{96,120},{128,152},{160,184},{192,216},{224... | collective-permute-start | bytes 786440 | tf_op jit(solution)/shard_map/ppermute | solution.py:274
  15.6 0.3 shard_map.59
  15.9 1.9 %collective-permute-start.3 = (bf16[144,128]{1,0:T(8,128)(2,1)S(1)}, bf16[144,128]{1,0:T(8,128)(2,1)S(1)}, u32[]{:S(2)}, u32[]{:S(2)}) collective-permute-start(bf16[144,128]{1,0:T(8,128)(2,1)S(1)} %get-tuple-element.35), channel_id=1, source_target_pairs={{0,8},{8,0},{16,24},{24,16},{32,40},{40,32},{48,56},{56,48},{64,72... | collective-permute-start | bytes 110600 | tf_op jit(solution)/shard_map/ppermute | solution.py:274
  17.8 0.1 pad_add_fusion.1.place_ref
  17.9 1.0 copy-done.1
  18.9 1.4 %shard_map.55 = (f32[4,512,256]{2,1,0:T(8,128)S(1)}, f32[4,512,128]{2,1,0:T(8,128)S(1)}) custom-call(bf16[512,512]{1,0:T(8,128)(2,1)S(1)} %copy-done.1, bf16[512,256]{1,0:T(8,128)(2,1)S(1)} %pad_add_fusion.kv_ref), custom_call_target="tpu_custom_call" | custom-call | flops 536870912 | bytes 4000000 | tf_op jit(solution)/shard_map/pallas_call | solution.py:100
  20.4 8.7 %collective-permute-done.3 = bf16[144,128]{1,0:T(8,128)(2,1)S(1)} collective-permute-done((bf16[144,128]{1,0:T(8,128)(2,1)S(1)}, bf16[144,128]{1,0:T(8,128)(2,1)S(1)}, u32[]{:S(2)}, u32[]{:S(2)}) %collective-permute-start.3) | collective-permute-done | bytes 36896 | tf_op jit(solution)/shard_map/ppermute | solution.py:274
  29.1 1.9 %collective-permute-start.4 = (bf16[144,128]{1,0:T(8,128)(2,1)S(1)}, bf16[144,128]{1,0:T(8,128)(2,1)S(1)}, u32[]{:S(2)}, u32[]{:S(2)}) collective-permute-start(bf16[144,128]{1,0:T(8,128)(2,1)S(1)} %fusion.2), channel_id=1, source_target_pairs={{0,16},{8,24},{16,0},{24,8},{32,48},{40,56},{48,32},{56,40},{64,80... | collective-permute-start | bytes 110600 | tf_op jit(solution)/shard_map/ppermute | solution.py:274
  31.0 0.0 collective-permute-done.2.kv_ref
  31.0 0.8 shard_map.56
  31.8 2.9 %collective-permute-done.4 = bf16[144,128]{1,0:T(8,128)(2,1)S(1)} collective-permute-done((bf16[144,128]{1,0:T(8,128)(2,1)S(1)}, bf16[144,128]{1,0:T(8,128)(2,1)S(1)}, u32[]{:S(2)}, u32[]{:S(2)}) %collective-permute-start.4) | collective-permute-done | bytes 36896 | tf_op jit(solution)/shard_map/ppermute | solution.py:274
  34.7 6.9 %collective-permute-start.5 = (bf16[144,128]{1,0:T(8,128)(2,1)S(1)}, bf16[144,128]{1,0:T(8,128)(2,1)S(1)}, u32[]{:S(2)}, u32[]{:S(2)}) collective-permute-start(bf16[144,128]{1,0:T(8,128)(2,1)S(1)} %fusion.3), channel_id=1, source_target_pairs={{0,32},{8,40},{16,48},{24,56},{32,0},{40,8},{48,16},{56,24},{64,96... | collective-permute-start | bytes 110600 | tf_op jit(solution)/shard_map/ppermute | solution.py:274
  41.6 0.8 shard_map.57
  42.4 1.0 collective-permute-done.5
  43.4 2.8 %collective-permute-start.6 = (bf16[144,128]{1,0:T(8,128)(2,1)S(1)}, bf16[144,128]{1,0:T(8,128)(2,1)S(1)}, u32[]{:S(2)}, u32[]{:S(2)}) collective-permute-start(bf16[144,128]{1,0:T(8,128)(2,1)S(1)} %get-tuple-element.51), channel_id=1, source_target_pairs={{0,64},{8,72},{16,80},{24,88},{32,96},{40,104},{48,112},{56,120},{... | collective-permute-start | bytes 110600 | tf_op jit(solution)/shard_map/ppermute | solution.py:274
  46.2 0.0 collective-permute-done.kv_ref
  46.2 0.7 shard_map.58.acc_ref
  46.9 0.3 collective-permute-done.6
  47.2 4.7 %collective-permute-start.7 = (bf16[144,128]{1,0:T(8,128)(2,1)S(1)}, bf16[144,128]{1,0:T(8,128)(2,1)S(1)}, u32[]{:S(2)}, u32[]{:S(2)}) collective-permute-start(bf16[144,128]{1,0:T(8,128)(2,1)S(1)} %fusion.1), channel_id=1, source_target_pairs={{0,128},{8,136},{16,144},{24,152},{32,160},{40,168},{48,176},{56,1... | collective-permute-start | bytes 110600 | tf_op jit(solution)/shard_map/ppermute | solution.py:274
  51.9 1.0 collective-permute-done.7
  53.0 0.0 copy-start.2
  53.0 0.0 copy-start.3
  53.0 10.3 %collective-permute-start.8 = (bf16[144,128]{1,0:T(8,128)(2,1)S(1)}, bf16[144,128]{1,0:T(8,128)(2,1)S(1)}, u32[]{:S(2)}, u32[]{:S(2)}) collective-permute-start(bf16[144,128]{1,0:T(8,128)(2,1)S(1)} %get-tuple-element.53), channel_id=1, source_target_pairs={{0,256},{8,264},{16,272},{24,280},{32,288},{40,296},{48,304},{56,3... | collective-permute-start | bytes 110600 | tf_op jit(solution)/shard_map/ppermute | solution.py:274
  63.4 0.0 copy-start
  63.4 2.3 %shard_map.60.w_other_ref = bf16[512,4096]{1,0:T(8,128)(2,1)S(1)} custom-call(bf16[512,4096]{1,0:T(8,128)(2,1)} %collective-permute-done.9.w_hbm), custom_call_target="tpu_custom_call" | custom-call | bytes 8000000 | tf_op jit(solution)/shard_map/pallas_call | solution.py:160
  65.7 0.0 collective-permute-done.8.mem1
  65.8 1.4 %shard_map.61 = (bf16[256,512]{1,0:T(8,128)(2,1)S(1)}, bf16[256,512]{1,0:T(8,128)(2,1)S(1)}) custom-call(s32[3]{0:T(128)S(1)} %pad_add_fusion.1.place_ref, f32[4]{0:T(128)S(1)} %copy-done.3, bf16[512,512]{1,0:T(8,128)(2,1)S(1)} %copy-done.2, f32[4,512,256]{2,1,0:T(8,128)S(1)} %shard_map.58.acc_ref, f32[144,128]{1,0:T(8,128)S(1)} %get-tuple-element.54.mem0, ...), custom_call_target="tpu_custom_call" | custom-call | flops 402653184 | bytes 4000000 | tf_op jit(solution)/shard_map/pallas_call | solution.py:197
  67.2 7.3 %collective-permute-start.10 = (bf16[256,512]{1,0:T(8,128)(2,1)S(1)}, bf16[256,512]{1,0:T(8,128)(2,1)S(1)}, u32[]{:S(2)}, u32[]{:S(2)}) collective-permute-start(bf16[256,512]{1,0:T(8,128)(2,1)S(1)} %get-tuple-element.42), channel_id=1, source_target_pairs={{0,1},{1,0},{2,3},{3,2},{4,5},{5,4},{6,7},{7,6},{8,9},{9,8},{10,11... | collective-permute-start | bytes 786440 | tf_op jit(solution)/shard_map/ppermute | solution.py:298
  74.5 1.1 %collective-permute-done.10.got_ref = bf16[256,512]{1,0:T(8,128)(2,1)S(1)} collective-permute-done((bf16[256,512]{1,0:T(8,128)(2,1)S(1)}, bf16[256,512]{1,0:T(8,128)(2,1)S(1)}, u32[]{:S(2)}, u32[]{:S(2)}) %collective-permute-start.10) | collective-permute-done | bytes 262176 | tf_op jit(solution)/shard_map/ppermute | solution.py:298
  75.7 1.2 %shard_map.63 = (bf16[64,2048]{1,0:T(8,128)(2,1)S(1)}, bf16[64,2048]{1,0:T(8,128)(2,1)S(1)}, bf16[64,2048]{1,0:T(8,128)(2,1)S(1)}, bf16[64,2048]{1,0:T(8,128)(2,1)S(1)}) custom-call(bf16[256,512]{1,0:T(8,128)(2,1)S(1)} %get-tuple-element.41.keep_ref, bf16[256,512]{1,0:T(8,128)(2,1)S(1)} %collective-permute-done.10.got_ref, bf16[512,4096]{1,0:T(8,128)(2,1)S(1)} %copy-done, ...), custom_call_target="tpu_custom_call" | custom-call | flops 1073741824 | bytes 6000000 | tf_op jit(solution)/shard_map/pallas_call | solution.py:223
  76.9 4.4 %collective-permute-start.14 = (bf16[64,2048]{1,0:T(8,128)(2,1)S(1)}, bf16[64,2048]{1,0:T(8,128)(2,1)S(1)}, u32[]{:S(2)}, u32[]{:S(2)}) collective-permute-start(bf16[64,2048]{1,0:T(8,128)(2,1)S(1)} %get-tuple-element.49), channel_id=1, source_target_pairs={{0,6},{1,7},{2,0},{3,1},{4,2},{5,3},{6,4},{7,5},{8,14},{9,15},{10,... | collective-permute-start | bytes 786440 | tf_op jit(solution)/shard_map/ppermute | solution.py:303
  81.3 1.2 %shard_map.62 = (bf16[64,2048]{1,0:T(8,128)(2,1)S(1)}, bf16[64,2048]{1,0:T(8,128)(2,1)S(1)}, bf16[64,2048]{1,0:T(8,128)(2,1)S(1)}, bf16[64,2048]{1,0:T(8,128)(2,1)S(1)}) custom-call(bf16[256,512]{1,0:T(8,128)(2,1)S(1)} %get-tuple-element.41.keep_ref, bf16[256,512]{1,0:T(8,128)(2,1)S(1)} %collective-permute-done.10.got_ref, bf16[512,4096]{1,0:T(8,128)(2,1)S(1)} %copy-done, ...), custom_call_target="tpu_custom_call" | custom-call | flops 1073741824 | bytes 6000000 | tf_op jit(solution)/shard_map/pallas_call | solution.py:223
  82.6 1.9 %collective-permute-start.12 = (bf16[64,2048]{1,0:T(8,128)(2,1)S(1)}, bf16[64,2048]{1,0:T(8,128)(2,1)S(1)}, u32[]{:S(2)}, u32[]{:S(2)}) collective-permute-start(bf16[64,2048]{1,0:T(8,128)(2,1)S(1)} %get-tuple-element.46), channel_id=1, source_target_pairs={{0,2},{1,3},{2,4},{3,5},{4,6},{5,7},{6,0},{7,1},{8,10},{9,11},{10,... | collective-permute-start | bytes 786440 | tf_op jit(solution)/shard_map/ppermute | solution.py:300
  84.5 2.1 %collective-permute-start.16 = (bf16[64,2048]{1,0:T(8,128)(2,1)S(1)}, bf16[64,2048]{1,0:T(8,128)(2,1)S(1)}, u32[]{:S(2)}, u32[]{:S(2)}) collective-permute-start(bf16[64,2048]{1,0:T(8,128)(2,1)S(1)} %get-tuple-element.50), channel_id=1, source_target_pairs={{0,2},{1,3},{2,4},{3,5},{4,6},{5,7},{6,0},{7,1},{8,10},{9,11},{10,... | collective-permute-start | bytes 786440 | tf_op jit(solution)/shard_map/ppermute | solution.py:304
  86.6 4.4 %collective-permute-start.11 = (bf16[64,2048]{1,0:T(8,128)(2,1)S(1)}, bf16[64,2048]{1,0:T(8,128)(2,1)S(1)}, u32[]{:S(2)}, u32[]{:S(2)}) collective-permute-start(bf16[64,2048]{1,0:T(8,128)(2,1)S(1)} %get-tuple-element.44), channel_id=1, source_target_pairs={{0,6},{1,7},{2,0},{3,1},{4,2},{5,3},{6,4},{7,5},{8,14},{9,15},{10,... | collective-permute-start | bytes 786440 | tf_op jit(solution)/shard_map/ppermute | solution.py:301
  91.0 0.0 collective-permute-done.14
  91.0 0.1 add.57
  91.1 3.4 %collective-permute-start.15 = (bf16[64,2048]{1,0:T(8,128)(2,1)S(1)}, bf16[64,2048]{1,0:T(8,128)(2,1)S(1)}, u32[]{:S(2)}, u32[]{:S(2)}) collective-permute-start(bf16[64,2048]{1,0:T(8,128)(2,1)S(1)} %add.57), channel_id=1, source_target_pairs={{0,6},{1,7},{2,0},{3,1},{4,2},{5,3},{6,4},{7,5},{8,14},{9,15},{10,... | collective-permute-start | bytes 786440 | tf_op jit(solution)/shard_map/ppermute | solution.py:306
  94.5 0.1 add.56
  94.5 1.9 %collective-permute-start.13 = (bf16[64,2048]{1,0:T(8,128)(2,1)S(1)}, bf16[64,2048]{1,0:T(8,128)(2,1)S(1)}, u32[]{:S(2)}, u32[]{:S(2)}) collective-permute-start(bf16[64,2048]{1,0:T(8,128)(2,1)S(1)} %add.56), channel_id=1, source_target_pairs={{0,2},{1,3},{2,4},{3,5},{4,6},{5,7},{6,0},{7,1},{8,10},{9,11},{10,... | collective-permute-start | bytes 786440 | tf_op jit(solution)/shard_map/ppermute | solution.py:305
  96.5 2.0 %collective-permute-done.16.right_b = bf16[64,2048]{1,0:T(8,128)(2,1)S(1)} collective-permute-done((bf16[64,2048]{1,0:T(8,128)(2,1)S(1)}, bf16[64,2048]{1,0:T(8,128)(2,1)S(1)}, u32[]{:S(2)}, u32[]{:S(2)}) %collective-permute-start.16) | collective-permute-done | bytes 262176 | tf_op jit(solution)/shard_map/ppermute | solution.py:304
  98.5 2.9 %collective-permute-done.15.left_b = bf16[64,2048]{1,0:T(8,128)(2,1)S(1)} collective-permute-done((bf16[64,2048]{1,0:T(8,128)(2,1)S(1)}, bf16[64,2048]{1,0:T(8,128)(2,1)S(1)}, u32[]{:S(2)}, u32[]{:S(2)}) %collective-permute-start.15) | collective-permute-done | bytes 262176 | tf_op jit(solution)/shard_map/ppermute | solution.py:306
  101.4 2.3 %collective-permute-done.13.right_a = bf16[64,2048]{1,0:T(8,128)(2,1)S(1)} collective-permute-done((bf16[64,2048]{1,0:T(8,128)(2,1)S(1)}, bf16[64,2048]{1,0:T(8,128)(2,1)S(1)}, u32[]{:S(2)}, u32[]{:S(2)}) %collective-permute-start.13) | collective-permute-done | bytes 262176 | tf_op jit(solution)/shard_map/ppermute | solution.py:305
  103.7 1.0 shard_map.64
  (13 shorter events, 0.1 us)
Async XLA Ops:
  0.0 63.3 %collective-permute-start.9 = (bf16[512,4096]{1,0:T(8,128)(2,1)}, bf16[512,4096]{1,0:T(8,128)(2,1)}, u32[]{:S(2)}, u32[]{:S(2)}) collective-permute-start(bf16[512,4096]{1,0:T(8,128)(2,1)} %w_own_ref.3), channel_id=1, source_target_pairs={{0,1},{1,0},{2,3},{3,2},{4,5},{5,4},{6,7},{7,6},{8,9},{9,8},{10,11... | collective-permute-start | bytes 12582920 | tf_op jit(solution)/shard_map/ppermute | solution.py:277
  9.8 21.2 %collective-permute-start.2 = (bf16[512,256]{1,0:T(8,128)(2,1)S(1)}, bf16[512,256]{1,0:T(8,128)(2,1)S(1)}, u32[]{:S(2)}, u32[]{:S(2)}) collective-permute-start(bf16[512,256]{1,0:T(8,128)(2,1)S(1)} %pad_add_fusion.kv_ref), channel_id=1, source_target_pairs={{0,8},{8,16},{16,24},{32,40},{40,48},{48,56},{64,72},{72,80},{80,8... | collective-permute-start | bytes 786440 | tf_op jit(solution)/shard_map/ppermute | solution.py:274
  11.1 30.5 %collective-permute-start.1 = (bf16[512,256]{1,0:T(8,128)(2,1)S(1)}, bf16[512,256]{1,0:T(8,128)(2,1)S(1)}, u32[]{:S(2)}, u32[]{:S(2)}) collective-permute-start(bf16[512,256]{1,0:T(8,128)(2,1)S(1)} %pad_add_fusion.kv_ref), channel_id=1, source_target_pairs={{0,16},{8,24},{32,48},{40,56},{64,80},{72,88},{96,112},{104,120},{... | collective-permute-start | bytes 786440 | tf_op jit(solution)/shard_map/ppermute | solution.py:274
  14.3 31.9 %collective-permute-start = (bf16[512,256]{1,0:T(8,128)(2,1)S(1)}, bf16[512,256]{1,0:T(8,128)(2,1)S(1)}, u32[]{:S(2)}, u32[]{:S(2)}) collective-permute-start(bf16[512,256]{1,0:T(8,128)(2,1)S(1)} %pad_add_fusion.kv_ref), channel_id=1, source_target_pairs={{0,24},{32,56},{64,88},{96,120},{128,152},{160,184},{192,216},{224... | collective-permute-start | bytes 786440 | tf_op jit(solution)/shard_map/ppermute | solution.py:274
  15.9 13.2 %collective-permute-start.3 = (bf16[144,128]{1,0:T(8,128)(2,1)S(1)}, bf16[144,128]{1,0:T(8,128)(2,1)S(1)}, u32[]{:S(2)}, u32[]{:S(2)}) collective-permute-start(bf16[144,128]{1,0:T(8,128)(2,1)S(1)} %get-tuple-element.35), channel_id=1, source_target_pairs={{0,8},{8,0},{16,24},{24,16},{32,40},{40,32},{48,56},{56,48},{64,72... | collective-permute-start | bytes 110600 | tf_op jit(solution)/shard_map/ppermute | solution.py:274
  17.9 1.0 copy-start.1
  29.1 5.6 %collective-permute-start.4 = (bf16[144,128]{1,0:T(8,128)(2,1)S(1)}, bf16[144,128]{1,0:T(8,128)(2,1)S(1)}, u32[]{:S(2)}, u32[]{:S(2)}) collective-permute-start(bf16[144,128]{1,0:T(8,128)(2,1)S(1)} %fusion.2), channel_id=1, source_target_pairs={{0,16},{8,24},{16,0},{24,8},{32,48},{40,56},{48,32},{56,40},{64,80... | collective-permute-start | bytes 110600 | tf_op jit(solution)/shard_map/ppermute | solution.py:274
  34.7 8.6 %collective-permute-start.5 = (bf16[144,128]{1,0:T(8,128)(2,1)S(1)}, bf16[144,128]{1,0:T(8,128)(2,1)S(1)}, u32[]{:S(2)}, u32[]{:S(2)}) collective-permute-start(bf16[144,128]{1,0:T(8,128)(2,1)S(1)} %fusion.3), channel_id=1, source_target_pairs={{0,32},{8,40},{16,48},{24,56},{32,0},{40,8},{48,16},{56,24},{64,96... | collective-permute-start | bytes 110600 | tf_op jit(solution)/shard_map/ppermute | solution.py:274
  43.4 3.9 %collective-permute-start.6 = (bf16[144,128]{1,0:T(8,128)(2,1)S(1)}, bf16[144,128]{1,0:T(8,128)(2,1)S(1)}, u32[]{:S(2)}, u32[]{:S(2)}) collective-permute-start(bf16[144,128]{1,0:T(8,128)(2,1)S(1)} %get-tuple-element.51), channel_id=1, source_target_pairs={{0,64},{8,72},{16,80},{24,88},{32,96},{40,104},{48,112},{56,120},{... | collective-permute-start | bytes 110600 | tf_op jit(solution)/shard_map/ppermute | solution.py:274
  47.2 5.7 %collective-permute-start.7 = (bf16[144,128]{1,0:T(8,128)(2,1)S(1)}, bf16[144,128]{1,0:T(8,128)(2,1)S(1)}, u32[]{:S(2)}, u32[]{:S(2)}) collective-permute-start(bf16[144,128]{1,0:T(8,128)(2,1)S(1)} %fusion.1), channel_id=1, source_target_pairs={{0,128},{8,136},{16,144},{24,152},{32,160},{40,168},{48,176},{56,1... | collective-permute-start | bytes 110600 | tf_op jit(solution)/shard_map/ppermute | solution.py:274
  53.0 12.8 %copy-start.2 = (bf16[512,512]{1,0:T(8,128)(2,1)S(1)}, bf16[512,512]{1,0:T(8,128)(2,1)}, u32[]{:S(2)}) copy-start(bf16[512,512]{1,0:T(8,128)(2,1)} %q_ref.9) | copy-start | bytes 1572868
  53.0 12.8 %copy-start.3 = (f32[4]{0:T(128)S(1)}, f32[4]{0:T(128)}, u32[]{:S(2)}) copy-start(f32[4]{0:T(128)} %gate_ref.1) | copy-start | bytes 52
  53.0 12.7 %collective-permute-start.8 = (bf16[144,128]{1,0:T(8,128)(2,1)S(1)}, bf16[144,128]{1,0:T(8,128)(2,1)S(1)}, u32[]{:S(2)}, u32[]{:S(2)}) collective-permute-start(bf16[144,128]{1,0:T(8,128)(2,1)S(1)} %get-tuple-element.53), channel_id=1, source_target_pairs={{0,256},{8,264},{16,272},{24,280},{32,288},{40,296},{48,304},{56,3... | collective-permute-start | bytes 110600 | tf_op jit(solution)/shard_map/ppermute | solution.py:274
  63.4 12.3 %copy-start = (bf16[512,4096]{1,0:T(8,128)(2,1)S(1)}, bf16[512,4096]{1,0:T(8,128)(2,1)}, u32[]{:S(2)}) copy-start(bf16[512,4096]{1,0:T(8,128)(2,1)} %w_own_ref.3) | copy-start | bytes 12582916
  67.2 8.5 %collective-permute-start.10 = (bf16[256,512]{1,0:T(8,128)(2,1)S(1)}, bf16[256,512]{1,0:T(8,128)(2,1)S(1)}, u32[]{:S(2)}, u32[]{:S(2)}) collective-permute-start(bf16[256,512]{1,0:T(8,128)(2,1)S(1)} %get-tuple-element.42), channel_id=1, source_target_pairs={{0,1},{1,0},{2,3},{3,2},{4,5},{5,4},{6,7},{7,6},{8,9},{9,8},{10,11... | collective-permute-start | bytes 786440 | tf_op jit(solution)/shard_map/ppermute | solution.py:298
  76.9 14.1 %collective-permute-start.14 = (bf16[64,2048]{1,0:T(8,128)(2,1)S(1)}, bf16[64,2048]{1,0:T(8,128)(2,1)S(1)}, u32[]{:S(2)}, u32[]{:S(2)}) collective-permute-start(bf16[64,2048]{1,0:T(8,128)(2,1)S(1)} %get-tuple-element.49), channel_id=1, source_target_pairs={{0,6},{1,7},{2,0},{3,1},{4,2},{5,3},{6,4},{7,5},{8,14},{9,15},{10,... | collective-permute-start | bytes 786440 | tf_op jit(solution)/shard_map/ppermute | solution.py:303
  82.6 11.9 %collective-permute-start.12 = (bf16[64,2048]{1,0:T(8,128)(2,1)S(1)}, bf16[64,2048]{1,0:T(8,128)(2,1)S(1)}, u32[]{:S(2)}, u32[]{:S(2)}) collective-permute-start(bf16[64,2048]{1,0:T(8,128)(2,1)S(1)} %get-tuple-element.46), channel_id=1, source_target_pairs={{0,2},{1,3},{2,4},{3,5},{4,6},{5,7},{6,0},{7,1},{8,10},{9,11},{10,... | collective-permute-start | bytes 786440 | tf_op jit(solution)/shard_map/ppermute | solution.py:300
  84.5 14.0 %collective-permute-start.16 = (bf16[64,2048]{1,0:T(8,128)(2,1)S(1)}, bf16[64,2048]{1,0:T(8,128)(2,1)S(1)}, u32[]{:S(2)}, u32[]{:S(2)}) collective-permute-start(bf16[64,2048]{1,0:T(8,128)(2,1)S(1)} %get-tuple-element.50), channel_id=1, source_target_pairs={{0,2},{1,3},{2,4},{3,5},{4,6},{5,7},{6,0},{7,1},{8,10},{9,11},{10,... | collective-permute-start | bytes 786440 | tf_op jit(solution)/shard_map/ppermute | solution.py:304
  86.6 11.9 %collective-permute-start.11 = (bf16[64,2048]{1,0:T(8,128)(2,1)S(1)}, bf16[64,2048]{1,0:T(8,128)(2,1)S(1)}, u32[]{:S(2)}, u32[]{:S(2)}) collective-permute-start(bf16[64,2048]{1,0:T(8,128)(2,1)S(1)} %get-tuple-element.44), channel_id=1, source_target_pairs={{0,6},{1,7},{2,0},{3,1},{4,2},{5,3},{6,4},{7,5},{8,14},{9,15},{10,... | collective-permute-start | bytes 786440 | tf_op jit(solution)/shard_map/ppermute | solution.py:301
  91.1 10.3 %collective-permute-start.15 = (bf16[64,2048]{1,0:T(8,128)(2,1)S(1)}, bf16[64,2048]{1,0:T(8,128)(2,1)S(1)}, u32[]{:S(2)}, u32[]{:S(2)}) collective-permute-start(bf16[64,2048]{1,0:T(8,128)(2,1)S(1)} %add.57), channel_id=1, source_target_pairs={{0,6},{1,7},{2,0},{3,1},{4,2},{5,3},{6,4},{7,5},{8,14},{9,15},{10,... | collective-permute-start | bytes 786440 | tf_op jit(solution)/shard_map/ppermute | solution.py:306
  94.5 9.1 %collective-permute-start.13 = (bf16[64,2048]{1,0:T(8,128)(2,1)S(1)}, bf16[64,2048]{1,0:T(8,128)(2,1)S(1)}, u32[]{:S(2)}, u32[]{:S(2)}) collective-permute-start(bf16[64,2048]{1,0:T(8,128)(2,1)S(1)} %add.56), channel_id=1, source_target_pairs={{0,2},{1,3},{2,4},{3,5},{4,6},{5,7},{6,0},{7,1},{8,10},{9,11},{10,... | collective-permute-start | bytes 786440 | tf_op jit(solution)/shard_map/ppermute | solution.py:305

commit v6 on v5

--- a/solution.py
+++ b/solution.py
@@ -150,27 +150,14 @@
     )(place, queries, kv, acc, top)
 
 
-def stage_kernel(w_hbm, w_ref, sem):
+def merge_kernel(
+    place_ref, gate_ref, q_ref, acc_ref, mem0, mem1, mem2, mem3, w_hbm, keep_ref, send_ref, w_ref, out_ref, sem
+):
     copy = pltpu.make_async_copy(w_hbm, w_ref, sem)
     copy.start()
-    copy.wait()
-
-
-def stage_call(w):
-    return call(
-        stage_kernel,
-        jax.ShapeDtypeStruct(w.shape, w.dtype),
-        (0, 8000000, 0),
-        in_specs=[pl.BlockSpec(memory_space=pl.ANY)],
-        out_specs=VM,
-        scratch_shapes=[pltpu.SemaphoreType.DMA],
-    )(w)
-
-
-def merge_kernel(place_ref, gate_ref, q_ref, acc_ref, mem0, mem1, keep_ref, send_ref, out_ref):
     x = place_ref[1]
     core = place_ref[2]
-    mem = mem0[...] + mem1[...].astype(F32)
+    mem = mem0[...] + mem1[...].astype(F32) + (mem2[...].astype(F32) + mem3[...].astype(F32))
     mem = jnp.concatenate([mem[:HD, :], jnp.broadcast_to(mem[HD : HD + 1, :], (HD, HD))], axis=0)
     mem_high, mem_low = split_two(mem)
     mem_twice = jnp.concatenate([mem_high, mem_high], axis=1)
@@ -190,18 +177,19 @@
         other = pl.multiple_of((2 * chip + 1 - core) * BLOCK, BLOCK)
         keep_ref[b * BLOCK : (b + 1) * BLOCK, :] = out_ref[pl.ds(mine, BLOCK), :]
         send_ref[b * BLOCK : (b + 1) * BLOCK, :] = out_ref[pl.ds(other, BLOCK), :]
-
-
-def merge_call(place, gates, queries, acc, mem0, mem1):
+    copy.wait()
+
+
+def merge_call(place, gates, queries, acc, mems, w):
     half = jax.ShapeDtypeStruct((ROWS // 2, GROUP * HD), BF16)
     return call(
         merge_kernel,
-        (half, half),
-        (6 * ROWS * GROUP * HD * HD * 2, 4000000, ROWS * GROUP * HD),
-        in_specs=[SM, SM] + [VM] * 4,
-        out_specs=(VM, VM),
-        scratch_shapes=[pltpu.VMEM((ROWS, GROUP * HD), BF16)],
-    )(place, gates, queries, acc, mem0, mem1)
+        (half, half, jax.ShapeDtypeStruct(w.shape, w.dtype)),
+        (6 * ROWS * GROUP * HD * HD * 2, 8000000, ROWS * GROUP * HD),
+        in_specs=[SM, SM] + [VM] * 6 + [pl.BlockSpec(memory_space=pl.ANY)],
+        out_specs=(VM,) * 3,
+        scratch_shapes=[pltpu.VMEM((ROWS, GROUP * HD), BF16), pltpu.SemaphoreType.DMA],
+    )(place, gates, queries, acc, *mems, w)
 
 
 def project_kernel(first, keep_ref, got_ref, w_own_ref, w_other_ref, own_ref, right_ref, far_ref, left_ref):
@@ -276,25 +264,21 @@
     delta, delta16 = delta_call(kv)
     w_other = lax.ppermute(out_weight, "tp", swap(1, N_TP))
     kv1, kv2, kv3 = [send(kv, along_z(d)) for d in (1, 2, 3)]
-    more = send(delta16, swap(1, N_CTX))
+    got = send(delta16, along_y(1))
     acc, top = own_call(queries, kv)
-    segment = delta + after(more, acc).astype(F32)
-    more = send(segment, swap(2, N_CTX))
+    before = after(got, acc).astype(F32)
+    got = send(delta + before, along_y(2))
     acc, top = step_call(1, place, queries, kv1, acc, top)
-    segment = segment + after(more, acc).astype(F32)
-    other = send(segment, swap(4, N_CTX))
+    before = before + after(got, acc).astype(F32)
+    got = send(delta + before, along_y(4))
     acc, top = step_call(2, place, queries, kv2, acc, top)
-    other = after(other, acc).astype(F32)
-    line = segment + other
-    start = jnp.where(ctx % 8 >= SPAN, other, 0.0)
-    before = send(line, along_y(1))
+    before = before + after(got, acc).astype(F32)
+    lower = ctx % 8 < SPAN
+    got = send(before + jnp.where(lower, delta, 0.0), swap(4, N_CTX))
     (acc,) = step_call(3, place, queries, kv3, acc, top)
-    before = after(before, acc).astype(F32)
-    before = before + send(line + before, along_y(2)).astype(F32)
-    far = send(line + before, along_y(4))
-    w_other = stage_call(w_other)
-    far = after(far, w_other)
-    keep, give = merge_call(place, gates, queries, acc, start + before, far)
+    mem = before + after(got, acc).astype(F32)
+    mems = [mem] + [send(mem, swap(k, N_CTX)) for k in (1, 2, 3)]
+    keep, give, w_other = merge_call(place, gates, queries, acc, mems, w_other)
     got = lax.ppermute(give, "tp", swap(1, N_TP))
     own_a, right_a, far_a, left_a = project_call(0, keep, got, out_weight, w_other)
     far_a = lax.ppermute(far_a, "tp", turned(1))

time: 107 us -> 101 us (0.944)
  waiting for transfers between devices: 22.3 us -> 12 us
  starting transfers between devices: 68.4 us -> 74.2 us
    ppermute x9 -> x10, waiting for transfers between devices: 13.9 us -> 3.65 us  [on_device(): send = lambda x, route: lax.ppermute(x.astype(BF16), 'ctx', route)]
    ppermute x9 -> x10, starting transfers between devices: 34.3 us -> 40.1 us  [on_device(): send = lambda x, route: lax.ppermute(x.astype(BF16), 'ctx', route)]
    pallas_call x2 -> x1, Pallas kernels: 3.79 us -> 3.04 us  [merge_call(): call(merge_kernel, (half, half, jax.ShapeDtypeStruct(w.shape, w.dtype)),...]
  transfers between devices with their start and end apart: 17 -> 18, of which waited for: 9 -> 9; matrix products, arithmetic and copies ran while one was open for 1% -> 1% of each run, Pallas kernels for 7% -> 5%
where the time goes in v6:
time: 101 us; the launch traced here: 99.3 us
  starting transfers between devices  74.2 us (73%)
  waiting for transfers between devices  12 us (12%)
  Pallas kernels  10.4 us (10%)
  other arithmetic  1.3 us (1%)
  local copies, waits for them, and re-layouts  1.05 us (1%)
    ppermute x10, starting transfers between devices, on_device(): send = lambda x, route: lax.ppermute(x.astype(BF16), 'ctx', route)  40.1 us
    ppermute x1, starting transfers between devices, on_device(): w_other = lax.ppermute(out_weight, 'tp', swap(1, N_TP))  8.78 us
    ppermute x1, starting transfers between devices, on_device(): got = lax.ppermute(give, 'tp', swap(1, N_TP))  7.25 us
    ppermute x1, starting transfers between devices, on_device(): left_a = lax.ppermute(left_a, 'tp', turned(-1))  4.4 us
    ppermute x1, starting transfers between devices, on_device(): far_b = lax.ppermute(far_b, 'tp', turned(-1))  4.39 us
    ppermute x10, waiting for transfers between devices, on_device(): send = lambda x, route: lax.ppermute(x.astype(BF16), 'ctx', route)  3.65 us
    ppermute x1, starting transfers between devices, on_device(): left_b = lax.ppermute(left_b + far_b, 'tp', turned(-1))  3.36 us
    pallas_call x1, Pallas kernels, merge_call(): call(merge_kernel, (half, half, jax.ShapeDtypeStruct(w.shape, w.dtype)),...  3.04 us
  transfers between devices with their start and end apart: 18, of which 9 were waited for; matrix products, arithmetic and copies ran while one was open for 1% of the time, Pallas kernels for 5%

profile of v6, /device:TPU:1, one launch (start us, length us, event | category | flops | bytes accessed | tf_op | source)
XLA Modules:
  0.0 99.3 jit_solution(5663839787237829595)
XLA Ops:
  0.0 8.8 %collective-permute-start.10 = (bf16[512,4096]{1,0:T(8,128)(2,1)}, bf16[512,4096]{1,0:T(8,128)(2,1)}, u32[]{:S(2)}, u32[]{:S(2)}) collective-permute-start(bf16[512,4096]{1,0:T(8,128)(2,1)} %w_own_ref.3), channel_id=1, source_target_pairs={{0,1},{1,0},{2,3},{3,2},{4,5},{5,4},{6,7},{7,6},{8,9},{9,8},{10,11... | collective-permute-start | bytes 12582920 | tf_op jit(solution)/shard_map/ppermute | solution.py:265
  8.8 1.0 %pad_add_fusion.kv_ref = bf16[512,256]{1,0:T(8,128)(2,1)S(1)} fusion(bf16[512,128]{1,0:T(8,128)(2,1)} %param.7, bf16[512,128]{1,0:T(8,128)(2,1)} %param.6), kind=kLoop, calls=%fused_computation | loop fusion | flops 524288 | bytes 524288 | tf_op jit(solution)/shard_map/add | solution.py:263
  9.8 1.3 %collective-permute-start.2 = (bf16[512,256]{1,0:T(8,128)(2,1)S(1)}, bf16[512,256]{1,0:T(8,128)(2,1)S(1)}, u32[]{:S(2)}, u32[]{:S(2)}) collective-permute-start(bf16[512,256]{1,0:T(8,128)(2,1)S(1)} %pad_add_fusion.kv_ref), channel_id=1, source_target_pairs={{0,8},{8,16},{16,24},{32,40},{40,48},{48,56},{64,72},{72,80},{80,8... | collective-permute-start | bytes 786440 | tf_op jit(solution)/shard_map/ppermute | solution.py:262
  11.1 3.1 %collective-permute-start.1 = (bf16[512,256]{1,0:T(8,128)(2,1)S(1)}, bf16[512,256]{1,0:T(8,128)(2,1)S(1)}, u32[]{:S(2)}, u32[]{:S(2)}) collective-permute-start(bf16[512,256]{1,0:T(8,128)(2,1)S(1)} %pad_add_fusion.kv_ref), channel_id=1, source_target_pairs={{0,16},{8,24},{32,48},{40,56},{64,80},{72,88},{96,112},{104,120},{... | collective-permute-start | bytes 786440 | tf_op jit(solution)/shard_map/ppermute | solution.py:262
  14.3 1.3 %collective-permute-start = (bf16[512,256]{1,0:T(8,128)(2,1)S(1)}, bf16[512,256]{1,0:T(8,128)(2,1)S(1)}, u32[]{:S(2)}, u32[]{:S(2)}) collective-permute-start(bf16[512,256]{1,0:T(8,128)(2,1)S(1)} %pad_add_fusion.kv_ref), channel_id=1, source_target_pairs={{0,24},{32,56},{64,88},{96,120},{128,152},{160,184},{192,216},{224... | collective-permute-start | bytes 786440 | tf_op jit(solution)/shard_map/ppermute | solution.py:262
  15.6 0.3 shard_map.59
  15.9 3.2 %collective-permute-start.3 = (bf16[144,128]{1,0:T(8,128)(2,1)S(1)}, bf16[144,128]{1,0:T(8,128)(2,1)S(1)}, u32[]{:S(2)}, u32[]{:S(2)}) collective-permute-start(bf16[144,128]{1,0:T(8,128)(2,1)S(1)} %get-tuple-element.34), channel_id=1, source_target_pairs={{0,64},{8,72},{16,80},{24,88},{32,96},{40,104},{48,112},{56,120},{... | collective-permute-start | bytes 110600 | tf_op jit(solution)/shard_map/ppermute | solution.py:262
  19.1 0.1 pad_add_fusion.1.place_ref
  19.2 1.0 %copy-done.1 = bf16[512,512]{1,0:T(8,128)(2,1)S(1)} copy-done((bf16[512,512]{1,0:T(8,128)(2,1)S(1)}, bf16[512,512]{1,0:T(8,128)(2,1)}, u32[]{:S(2)}) %copy-start.1) | copy-done | bytes 524312
  20.2 1.4 %shard_map.55 = (f32[4,512,256]{2,1,0:T(8,128)S(1)}, f32[4,512,128]{2,1,0:T(8,128)S(1)}) custom-call(bf16[512,512]{1,0:T(8,128)(2,1)S(1)} %copy-done.1, bf16[512,256]{1,0:T(8,128)(2,1)S(1)} %pad_add_fusion.kv_ref), custom_call_target="tpu_custom_call" | custom-call | flops 536870912 | bytes 4000000 | tf_op jit(solution)/shard_map/pallas_call | solution.py:100
  21.6 0.0 collective-permute-done.3
  21.7 4.2 %collective-permute-start.4 = (bf16[144,128]{1,0:T(8,128)(2,1)S(1)}, bf16[144,128]{1,0:T(8,128)(2,1)S(1)}, u32[]{:S(2)}, u32[]{:S(2)}) collective-permute-start(bf16[144,128]{1,0:T(8,128)(2,1)S(1)} %fusion), channel_id=1, source_target_pairs={{0,128},{8,136},{16,144},{24,152},{32,160},{40,168},{48,176},{56,1... | collective-permute-start | bytes 110600 | tf_op jit(solution)/shard_map/ppermute | solution.py:262
  25.9 0.0 collective-permute-done.2.kv_ref
  25.9 0.8 shard_map.56
  26.7 0.3 collective-permute-done.4
  27.0 9.5 %collective-permute-start.5 = (bf16[144,128]{1,0:T(8,128)(2,1)S(1)}, bf16[144,128]{1,0:T(8,128)(2,1)S(1)}, u32[]{:S(2)}, u32[]{:S(2)}) collective-permute-start(bf16[144,128]{1,0:T(8,128)(2,1)S(1)} %add_convert_fusion.1), channel_id=1, source_target_pairs={{0,256},{8,264},{16,272},{24,280},{32,288},{40,296},{48,304},{56,3... | collective-permute-start | bytes 110600 | tf_op jit(solution)/shard_map/ppermute | solution.py:262
  36.5 0.0 collective-permute-done.1.kv_ref
  36.5 0.8 shard_map.57
  37.2 0.3 collective-permute-done.5
  37.5 7.9 %collective-permute-start.6 = (bf16[144,128]{1,0:T(8,128)(2,1)S(1)}, bf16[144,128]{1,0:T(8,128)(2,1)S(1)}, u32[]{:S(2)}, u32[]{:S(2)}) collective-permute-start(bf16[144,128]{1,0:T(8,128)(2,1)S(1)} %add_convert_fusion), channel_id=1, source_target_pairs={{0,32},{8,40},{16,48},{24,56},{32,0},{40,8},{48,16},{56,24},{64,96... | collective-permute-start | bytes 110600 | tf_op jit(solution)/shard_map/ppermute | solution.py:262
  45.5 0.0 collective-permute-done.kv_ref
  45.5 0.0 copy-start.2
  45.5 0.7 shard_map.58.acc_ref
  46.2 0.6 collective-permute-done.6
  46.8 4.7 %collective-permute-start.9 = (bf16[144,128]{1,0:T(8,128)(2,1)S(1)}, bf16[144,128]{1,0:T(8,128)(2,1)S(1)}, u32[]{:S(2)}, u32[]{:S(2)}) collective-permute-start(bf16[144,128]{1,0:T(8,128)(2,1)S(1)} %get-tuple-element.51), channel_id=1, source_target_pairs={{0,24},{8,16},{16,8},{24,0},{32,56},{40,48},{48,40},{56,32},{64,88... | collective-permute-start | bytes 110600 | tf_op jit(solution)/shard_map/ppermute | solution.py:262
  51.5 2.6 %collective-permute-start.8 = (bf16[144,128]{1,0:T(8,128)(2,1)S(1)}, bf16[144,128]{1,0:T(8,128)(2,1)S(1)}, u32[]{:S(2)}, u32[]{:S(2)}) collective-permute-start(bf16[144,128]{1,0:T(8,128)(2,1)S(1)} %get-tuple-element.51), channel_id=1, source_target_pairs={{0,16},{8,24},{16,0},{24,8},{32,48},{40,56},{48,32},{56,40},{64,80... | collective-permute-start | bytes 110600 | tf_op jit(solution)/shard_map/ppermute | solution.py:262
  54.2 2.2 %collective-permute-start.7 = (bf16[144,128]{1,0:T(8,128)(2,1)S(1)}, bf16[144,128]{1,0:T(8,128)(2,1)S(1)}, u32[]{:S(2)}, u32[]{:S(2)}) collective-permute-start(bf16[144,128]{1,0:T(8,128)(2,1)S(1)} %get-tuple-element.51), channel_id=1, source_target_pairs={{0,8},{8,0},{16,24},{24,16},{32,40},{40,32},{48,56},{56,48},{64,72... | collective-permute-start | bytes 110600 | tf_op jit(solution)/shard_map/ppermute | solution.py:262
  56.4 0.0 collective-permute-done.9.mem3
  56.4 0.8 collective-permute-done.8.mem2
  57.1 1.7 %collective-permute-done.7.mem1 = bf16[144,128]{1,0:T(8,128)(2,1)S(1)} collective-permute-done((bf16[144,128]{1,0:T(8,128)(2,1)S(1)}, bf16[144,128]{1,0:T(8,128)(2,1)S(1)}, u32[]{:S(2)}, u32[]{:S(2)}) %collective-permute-start.7) | collective-permute-done | bytes 36896 | tf_op jit(solution)/shard_map/ppermute | solution.py:262
  58.9 3.0 %shard_map.60 = (bf16[256,512]{1,0:T(8,128)(2,1)S(1)}, bf16[256,512]{1,0:T(8,128)(2,1)S(1)}, bf16[512,4096]{1,0:T(8,128)(2,1)S(1)}) custom-call(s32[3]{0:T(128)S(1)} %pad_add_fusion.1.place_ref, f32[4]{0:T(128)S(1)} %copy-done.2, bf16[512,512]{1,0:T(8,128)(2,1)S(1)} %copy-done.1, f32[4,512,256]{2,1,0:T(8,128)S(1)} %shard_map.58.acc_ref, ...), custom_call_target="tpu_custom_call" | custom-call | flops 402653184 | bytes 8000000 | tf_op jit(solution)/shard_map/pallas_call | solution.py:185
  61.9 7.2 %collective-permute-start.11 = (bf16[256,512]{1,0:T(8,128)(2,1)S(1)}, bf16[256,512]{1,0:T(8,128)(2,1)S(1)}, u32[]{:S(2)}, u32[]{:S(2)}) collective-permute-start(bf16[256,512]{1,0:T(8,128)(2,1)S(1)} %get-tuple-element.41), channel_id=1, source_target_pairs={{0,1},{1,0},{2,3},{3,2},{4,5},{5,4},{6,7},{7,6},{8,9},{9,8},{10,11... | collective-permute-start | bytes 786440 | tf_op jit(solution)/shard_map/ppermute | solution.py:282
  69.2 1.1 %collective-permute-done.11.got_ref = bf16[256,512]{1,0:T(8,128)(2,1)S(1)} collective-permute-done((bf16[256,512]{1,0:T(8,128)(2,1)S(1)}, bf16[256,512]{1,0:T(8,128)(2,1)S(1)}, u32[]{:S(2)}, u32[]{:S(2)}) %collective-permute-start.11) | collective-permute-done | bytes 262176 | tf_op jit(solution)/shard_map/ppermute | solution.py:282
  70.3 1.2 %shard_map.62 = (bf16[64,2048]{1,0:T(8,128)(2,1)S(1)}, bf16[64,2048]{1,0:T(8,128)(2,1)S(1)}, bf16[64,2048]{1,0:T(8,128)(2,1)S(1)}, bf16[64,2048]{1,0:T(8,128)(2,1)S(1)}) custom-call(bf16[256,512]{1,0:T(8,128)(2,1)S(1)} %get-tuple-element.40.keep_ref, bf16[256,512]{1,0:T(8,128)(2,1)S(1)} %collective-permute-done.11.got_ref, bf16[512,4096]{1,0:T(8,128)(2,1)S(1)} %copy-done, ...), custom_call_target="tpu_custom_call" | custom-call | flops 1073741824 | bytes 6000000 | tf_op jit(solution)/shard_map/pallas_call | solution.py:211
  71.6 4.4 %collective-permute-start.15 = (bf16[64,2048]{1,0:T(8,128)(2,1)S(1)}, bf16[64,2048]{1,0:T(8,128)(2,1)S(1)}, u32[]{:S(2)}, u32[]{:S(2)}) collective-permute-start(bf16[64,2048]{1,0:T(8,128)(2,1)S(1)} %get-tuple-element.49), channel_id=1, source_target_pairs={{0,6},{1,7},{2,0},{3,1},{4,2},{5,3},{6,4},{7,5},{8,14},{9,15},{10,... | collective-permute-start | bytes 786440 | tf_op jit(solution)/shard_map/ppermute | solution.py:287
  76.0 1.2 %shard_map.61 = (bf16[64,2048]{1,0:T(8,128)(2,1)S(1)}, bf16[64,2048]{1,0:T(8,128)(2,1)S(1)}, bf16[64,2048]{1,0:T(8,128)(2,1)S(1)}, bf16[64,2048]{1,0:T(8,128)(2,1)S(1)}) custom-call(bf16[256,512]{1,0:T(8,128)(2,1)S(1)} %get-tuple-element.40.keep_ref, bf16[256,512]{1,0:T(8,128)(2,1)S(1)} %collective-permute-done.11.got_ref, bf16[512,4096]{1,0:T(8,128)(2,1)S(1)} %copy-done, ...), custom_call_target="tpu_custom_call" | custom-call | flops 1073741824 | bytes 6000000 | tf_op jit(solution)/shard_map/pallas_call | solution.py:211
  77.2 1.9 %collective-permute-start.13 = (bf16[64,2048]{1,0:T(8,128)(2,1)S(1)}, bf16[64,2048]{1,0:T(8,128)(2,1)S(1)}, u32[]{:S(2)}, u32[]{:S(2)}) collective-permute-start(bf16[64,2048]{1,0:T(8,128)(2,1)S(1)} %get-tuple-element.46), channel_id=1, source_target_pairs={{0,2},{1,3},{2,4},{3,5},{4,6},{5,7},{6,0},{7,1},{8,10},{9,11},{10,... | collective-permute-start | bytes 786440 | tf_op jit(solution)/shard_map/ppermute | solution.py:284
  79.2 2.1 %collective-permute-start.17 = (bf16[64,2048]{1,0:T(8,128)(2,1)S(1)}, bf16[64,2048]{1,0:T(8,128)(2,1)S(1)}, u32[]{:S(2)}, u32[]{:S(2)}) collective-permute-start(bf16[64,2048]{1,0:T(8,128)(2,1)S(1)} %get-tuple-element.50), channel_id=1, source_target_pairs={{0,2},{1,3},{2,4},{3,5},{4,6},{5,7},{6,0},{7,1},{8,10},{9,11},{10,... | collective-permute-start | bytes 786440 | tf_op jit(solution)/shard_map/ppermute | solution.py:288
  81.3 4.4 %collective-permute-start.12 = (bf16[64,2048]{1,0:T(8,128)(2,1)S(1)}, bf16[64,2048]{1,0:T(8,128)(2,1)S(1)}, u32[]{:S(2)}, u32[]{:S(2)}) collective-permute-start(bf16[64,2048]{1,0:T(8,128)(2,1)S(1)} %get-tuple-element.44), channel_id=1, source_target_pairs={{0,6},{1,7},{2,0},{3,1},{4,2},{5,3},{6,4},{7,5},{8,14},{9,15},{10,... | collective-permute-start | bytes 786440 | tf_op jit(solution)/shard_map/ppermute | solution.py:285
  85.7 0.0 collective-permute-done.15
  85.7 0.1 add.53
  85.7 3.4 %collective-permute-start.16 = (bf16[64,2048]{1,0:T(8,128)(2,1)S(1)}, bf16[64,2048]{1,0:T(8,128)(2,1)S(1)}, u32[]{:S(2)}, u32[]{:S(2)}) collective-permute-start(bf16[64,2048]{1,0:T(8,128)(2,1)S(1)} %add.53), channel_id=1, source_target_pairs={{0,6},{1,7},{2,0},{3,1},{4,2},{5,3},{6,4},{7,5},{8,14},{9,15},{10,... | collective-permute-start | bytes 786440 | tf_op jit(solution)/shard_map/ppermute | solution.py:290
  89.1 0.1 add.52
  89.2 1.9 %collective-permute-start.14 = (bf16[64,2048]{1,0:T(8,128)(2,1)S(1)}, bf16[64,2048]{1,0:T(8,128)(2,1)S(1)}, u32[]{:S(2)}, u32[]{:S(2)}) collective-permute-start(bf16[64,2048]{1,0:T(8,128)(2,1)S(1)} %add.52), channel_id=1, source_target_pairs={{0,2},{1,3},{2,4},{3,5},{4,6},{5,7},{6,0},{7,1},{8,10},{9,11},{10,... | collective-permute-start | bytes 786440 | tf_op jit(solution)/shard_map/ppermute | solution.py:289
  91.1 2.0 %collective-permute-done.17.right_b = bf16[64,2048]{1,0:T(8,128)(2,1)S(1)} collective-permute-done((bf16[64,2048]{1,0:T(8,128)(2,1)S(1)}, bf16[64,2048]{1,0:T(8,128)(2,1)S(1)}, u32[]{:S(2)}, u32[]{:S(2)}) %collective-permute-start.17) | collective-permute-done | bytes 262176 | tf_op jit(solution)/shard_map/ppermute | solution.py:288
  93.2 2.9 %collective-permute-done.16.left_b = bf16[64,2048]{1,0:T(8,128)(2,1)S(1)} collective-permute-done((bf16[64,2048]{1,0:T(8,128)(2,1)S(1)}, bf16[64,2048]{1,0:T(8,128)(2,1)S(1)}, u32[]{:S(2)}, u32[]{:S(2)}) %collective-permute-start.16) | collective-permute-done | bytes 262176 | tf_op jit(solution)/shard_map/ppermute | solution.py:290
  96.0 2.3 %collective-permute-done.14.right_a = bf16[64,2048]{1,0:T(8,128)(2,1)S(1)} collective-permute-done((bf16[64,2048]{1,0:T(8,128)(2,1)S(1)}, bf16[64,2048]{1,0:T(8,128)(2,1)S(1)}, u32[]{:S(2)}, u32[]{:S(2)}) %collective-permute-start.14) | collective-permute-done | bytes 262176 | tf_op jit(solution)/shard_map/ppermute | solution.py:289
  98.3 1.0 shard_map.63
  (11 shorter events, 0.1 us)
Async XLA Ops:
  0.0 58.9 %collective-permute-start.10 = (bf16[512,4096]{1,0:T(8,128)(2,1)}, bf16[512,4096]{1,0:T(8,128)(2,1)}, u32[]{:S(2)}, u32[]{:S(2)}) collective-permute-start(bf16[512,4096]{1,0:T(8,128)(2,1)} %w_own_ref.3), channel_id=1, source_target_pairs={{0,1},{1,0},{2,3},{3,2},{4,5},{5,4},{6,7},{7,6},{8,9},{9,8},{10,11... | collective-permute-start | bytes 12582920 | tf_op jit(solution)/shard_map/ppermute | solution.py:265
  9.8 16.1 %collective-permute-start.2 = (bf16[512,256]{1,0:T(8,128)(2,1)S(1)}, bf16[512,256]{1,0:T(8,128)(2,1)S(1)}, u32[]{:S(2)}, u32[]{:S(2)}) collective-permute-start(bf16[512,256]{1,0:T(8,128)(2,1)S(1)} %pad_add_fusion.kv_ref), channel_id=1, source_target_pairs={{0,8},{8,16},{16,24},{32,40},{40,48},{48,56},{64,72},{72,80},{80,8... | collective-permute-start | bytes 786440 | tf_op jit(solution)/shard_map/ppermute | solution.py:262
  11.1 25.4 %collective-permute-start.1 = (bf16[512,256]{1,0:T(8,128)(2,1)S(1)}, bf16[512,256]{1,0:T(8,128)(2,1)S(1)}, u32[]{:S(2)}, u32[]{:S(2)}) collective-permute-start(bf16[512,256]{1,0:T(8,128)(2,1)S(1)} %pad_add_fusion.kv_ref), channel_id=1, source_target_pairs={{0,16},{8,24},{32,48},{40,56},{64,80},{72,88},{96,112},{104,120},{... | collective-permute-start | bytes 786440 | tf_op jit(solution)/shard_map/ppermute | solution.py:262
  14.3 31.2 %collective-permute-start = (bf16[512,256]{1,0:T(8,128)(2,1)S(1)}, bf16[512,256]{1,0:T(8,128)(2,1)S(1)}, u32[]{:S(2)}, u32[]{:S(2)}) collective-permute-start(bf16[512,256]{1,0:T(8,128)(2,1)S(1)} %pad_add_fusion.kv_ref), channel_id=1, source_target_pairs={{0,24},{32,56},{64,88},{96,120},{128,152},{160,184},{192,216},{224... | collective-permute-start | bytes 786440 | tf_op jit(solution)/shard_map/ppermute | solution.py:262
  15.9 5.8 %collective-permute-start.3 = (bf16[144,128]{1,0:T(8,128)(2,1)S(1)}, bf16[144,128]{1,0:T(8,128)(2,1)S(1)}, u32[]{:S(2)}, u32[]{:S(2)}) collective-permute-start(bf16[144,128]{1,0:T(8,128)(2,1)S(1)} %get-tuple-element.34), channel_id=1, source_target_pairs={{0,64},{8,72},{16,80},{24,88},{32,96},{40,104},{48,112},{56,120},{... | collective-permute-start | bytes 110600 | tf_op jit(solution)/shard_map/ppermute | solution.py:262
  19.2 1.0 %copy-start.1 = (bf16[512,512]{1,0:T(8,128)(2,1)S(1)}, bf16[512,512]{1,0:T(8,128)(2,1)}, u32[]{:S(2)}) copy-start(bf16[512,512]{1,0:T(8,128)(2,1)} %q_ref.9) | copy-start | bytes 1572868
  21.7 5.3 %collective-permute-start.4 = (bf16[144,128]{1,0:T(8,128)(2,1)S(1)}, bf16[144,128]{1,0:T(8,128)(2,1)S(1)}, u32[]{:S(2)}, u32[]{:S(2)}) collective-permute-start(bf16[144,128]{1,0:T(8,128)(2,1)S(1)} %fusion), channel_id=1, source_target_pairs={{0,128},{8,136},{16,144},{24,152},{32,160},{40,168},{48,176},{56,1... | collective-permute-start | bytes 110600 | tf_op jit(solution)/shard_map/ppermute | solution.py:262
  27.0 10.5 %collective-permute-start.5 = (bf16[144,128]{1,0:T(8,128)(2,1)S(1)}, bf16[144,128]{1,0:T(8,128)(2,1)S(1)}, u32[]{:S(2)}, u32[]{:S(2)}) collective-permute-start(bf16[144,128]{1,0:T(8,128)(2,1)S(1)} %add_convert_fusion.1), channel_id=1, source_target_pairs={{0,256},{8,264},{16,272},{24,280},{32,288},{40,296},{48,304},{56,3... | collective-permute-start | bytes 110600 | tf_op jit(solution)/shard_map/ppermute | solution.py:262
  37.5 9.3 %collective-permute-start.6 = (bf16[144,128]{1,0:T(8,128)(2,1)S(1)}, bf16[144,128]{1,0:T(8,128)(2,1)S(1)}, u32[]{:S(2)}, u32[]{:S(2)}) collective-permute-start(bf16[144,128]{1,0:T(8,128)(2,1)S(1)} %add_convert_fusion), channel_id=1, source_target_pairs={{0,32},{8,40},{16,48},{24,56},{32,0},{40,8},{48,16},{56,24},{64,96... | collective-permute-start | bytes 110600 | tf_op jit(solution)/shard_map/ppermute | solution.py:262
  45.5 13.4 %copy-start.2 = (f32[4]{0:T(128)S(1)}, f32[4]{0:T(128)}, u32[]{:S(2)}) copy-start(f32[4]{0:T(128)} %gate_ref.1) | copy-start | bytes 52
  46.8 9.5 %collective-permute-start.9 = (bf16[144,128]{1,0:T(8,128)(2,1)S(1)}, bf16[144,128]{1,0:T(8,128)(2,1)S(1)}, u32[]{:S(2)}, u32[]{:S(2)}) collective-permute-start(bf16[144,128]{1,0:T(8,128)(2,1)S(1)} %get-tuple-element.51), channel_id=1, source_target_pairs={{0,24},{8,16},{16,8},{24,0},{32,56},{40,48},{48,40},{56,32},{64,88... | collective-permute-start | bytes 110600 | tf_op jit(solution)/shard_map/ppermute | solution.py:262
  51.5 5.6 %collective-permute-start.8 = (bf16[144,128]{1,0:T(8,128)(2,1)S(1)}, bf16[144,128]{1,0:T(8,128)(2,1)S(1)}, u32[]{:S(2)}, u32[]{:S(2)}) collective-permute-start(bf16[144,128]{1,0:T(8,128)(2,1)S(1)} %get-tuple-element.51), channel_id=1, source_target_pairs={{0,16},{8,24},{16,0},{24,8},{32,48},{40,56},{48,32},{56,40},{64,80... | collective-permute-start | bytes 110600 | tf_op jit(solution)/shard_map/ppermute | solution.py:262
  54.2 4.7 %collective-permute-start.7 = (bf16[144,128]{1,0:T(8,128)(2,1)S(1)}, bf16[144,128]{1,0:T(8,128)(2,1)S(1)}, u32[]{:S(2)}, u32[]{:S(2)}) collective-permute-start(bf16[144,128]{1,0:T(8,128)(2,1)S(1)} %get-tuple-element.51), channel_id=1, source_target_pairs={{0,8},{8,0},{16,24},{24,16},{32,40},{40,32},{48,56},{56,48},{64,72... | collective-permute-start | bytes 110600 | tf_op jit(solution)/shard_map/ppermute | solution.py:262
  58.9 11.4 %copy-start = (bf16[512,4096]{1,0:T(8,128)(2,1)S(1)}, bf16[512,4096]{1,0:T(8,128)(2,1)}, u32[]{:S(2)}) copy-start(bf16[512,4096]{1,0:T(8,128)(2,1)} %w_own_ref.3) | copy-start | bytes 12582916
  61.9 8.4 %collective-permute-start.11 = (bf16[256,512]{1,0:T(8,128)(2,1)S(1)}, bf16[256,512]{1,0:T(8,128)(2,1)S(1)}, u32[]{:S(2)}, u32[]{:S(2)}) collective-permute-start(bf16[256,512]{1,0:T(8,128)(2,1)S(1)} %get-tuple-element.41), channel_id=1, source_target_pairs={{0,1},{1,0},{2,3},{3,2},{4,5},{5,4},{6,7},{7,6},{8,9},{9,8},{10,11... | collective-permute-start | bytes 786440 | tf_op jit(solution)/shard_map/ppermute | solution.py:282
  71.6 14.1 %collective-permute-start.15 = (bf16[64,2048]{1,0:T(8,128)(2,1)S(1)}, bf16[64,2048]{1,0:T(8,128)(2,1)S(1)}, u32[]{:S(2)}, u32[]{:S(2)}) collective-permute-start(bf16[64,2048]{1,0:T(8,128)(2,1)S(1)} %get-tuple-element.49), channel_id=1, source_target_pairs={{0,6},{1,7},{2,0},{3,1},{4,2},{5,3},{6,4},{7,5},{8,14},{9,15},{10,... | collective-permute-start | bytes 786440 | tf_op jit(solution)/shard_map/ppermute | solution.py:287
  77.2 11.9 %collective-permute-start.13 = (bf16[64,2048]{1,0:T(8,128)(2,1)S(1)}, bf16[64,2048]{1,0:T(8,128)(2,1)S(1)}, u32[]{:S(2)}, u32[]{:S(2)}) collective-permute-start(bf16[64,2048]{1,0:T(8,128)(2,1)S(1)} %get-tuple-element.46), channel_id=1, source_target_pairs={{0,2},{1,3},{2,4},{3,5},{4,6},{5,7},{6,0},{7,1},{8,10},{9,11},{10,... | collective-permute-start | bytes 786440 | tf_op jit(solution)/shard_map/ppermute | solution.py:284
  79.2 14.0 %collective-permute-start.17 = (bf16[64,2048]{1,0:T(8,128)(2,1)S(1)}, bf16[64,2048]{1,0:T(8,128)(2,1)S(1)}, u32[]{:S(2)}, u32[]{:S(2)}) collective-permute-start(bf16[64,2048]{1,0:T(8,128)(2,1)S(1)} %get-tuple-element.50), channel_id=1, source_target_pairs={{0,2},{1,3},{2,4},{3,5},{4,6},{5,7},{6,0},{7,1},{8,10},{9,11},{10,... | collective-permute-start | bytes 786440 | tf_op jit(solution)/shard_map/ppermute | solution.py:288
  81.3 11.9 %collective-permute-start.12 = (bf16[64,2048]{1,0:T(8,128)(2,1)S(1)}, bf16[64,2048]{1,0:T(8,128)(2,1)S(1)}, u32[]{:S(2)}, u32[]{:S(2)}) collective-permute-start(bf16[64,2048]{1,0:T(8,128)(2,1)S(1)} %get-tuple-element.44), channel_id=1, source_target_pairs={{0,6},{1,7},{2,0},{3,1},{4,2},{5,3},{6,4},{7,5},{8,14},{9,15},{10,... | collective-permute-start | bytes 786440 | tf_op jit(solution)/shard_map/ppermute | solution.py:285
  85.7 10.3 %collective-permute-start.16 = (bf16[64,2048]{1,0:T(8,128)(2,1)S(1)}, bf16[64,2048]{1,0:T(8,128)(2,1)S(1)}, u32[]{:S(2)}, u32[]{:S(2)}) collective-permute-start(bf16[64,2048]{1,0:T(8,128)(2,1)S(1)} %add.53), channel_id=1, source_target_pairs={{0,6},{1,7},{2,0},{3,1},{4,2},{5,3},{6,4},{7,5},{8,14},{9,15},{10,... | collective-permute-start | bytes 786440 | tf_op jit(solution)/shard_map/ppermute | solution.py:290
  89.2 9.1 %collective-permute-start.14 = (bf16[64,2048]{1,0:T(8,128)(2,1)S(1)}, bf16[64,2048]{1,0:T(8,128)(2,1)S(1)}, u32[]{:S(2)}, u32[]{:S(2)}) collective-permute-start(bf16[64,2048]{1,0:T(8,128)(2,1)S(1)} %add.52), channel_id=1, source_target_pairs={{0,2},{1,3},{2,4},{3,5},{4,6},{5,7},{6,0},{7,1},{8,10},{9,11},{10,... | collective-permute-start | bytes 786440 | tf_op jit(solution)/shard_map/ppermute | solution.py:289

commit v7 on v5

--- a/solution.py
+++ b/solution.py
@@ -275,25 +275,22 @@
     kv = jnp.pad(keys, ((0, 0), (0, HD))) + jnp.pad(values, ((0, 0), (HD, 0)))
     delta, delta16 = delta_call(kv)
     w_other = lax.ppermute(out_weight, "tp", swap(1, N_TP))
+    segment = [send(delta16, swap(k, N_CTX)) for k in (1, 2, 3)]
     kv1, kv2, kv3 = [send(kv, along_z(d)) for d in (1, 2, 3)]
-    more = send(delta16, swap(1, N_CTX))
-    acc, top = own_call(queries, kv)
-    segment = delta + after(more, acc).astype(F32)
-    more = send(segment, swap(2, N_CTX))
-    acc, top = step_call(1, place, queries, kv1, acc, top)
-    segment = segment + after(more, acc).astype(F32)
-    other = send(segment, swap(4, N_CTX))
-    acc, top = step_call(2, place, queries, kv2, acc, top)
-    other = after(other, acc).astype(F32)
+    segment = delta + sum(part.astype(F32) for part in segment)
+    other = send(segment, swap(4, N_CTX)).astype(F32)
     line = segment + other
     start = jnp.where(ctx % 8 >= SPAN, other, 0.0)
     before = send(line, along_y(1))
+    acc, top = own_call(queries, kv)
+    before = after(before, acc).astype(F32)
+    more = send(line + before, along_y(2))
+    acc, top = step_call(1, place, queries, kv1, acc, top)
+    before = before + after(more, acc).astype(F32)
+    far = send(line + before, along_y(4))
+    w_other = stage_call(after(w_other, acc))
+    acc, top = step_call(2, place, queries, after(kv2, w_other), acc, top)
     (acc,) = step_call(3, place, queries, kv3, acc, top)
-    before = after(before, acc).astype(F32)
-    before = before + send(line + before, along_y(2)).astype(F32)
-    far = send(line + before, along_y(4))
-    w_other = stage_call(w_other)
-    far = after(far, w_other)
     keep, give = merge_call(place, gates, queries, acc, start + before, far)
     got = lax.ppermute(give, "tp", swap(1, N_TP))
     own_a, right_a, far_a, left_a = project_call(0, keep, got, out_weight, w_other)

time: 107 us -> 106 us (level); the launches traced: 105 us -> 105 us
  starting transfers between devices: 68.4 us -> 72.8 us
  waiting for transfers between devices: 22.3 us -> 18.8 us
    ppermute x9 -> x10, starting transfers between devices: 34.3 us -> 39.8 us  [on_device(): send = lambda x, route: lax.ppermute(x.astype(BF16), 'ctx', route)]
    ppermute x9 -> x10, waiting for transfers between devices: 13.9 us -> 10.4 us  [on_device(): send = lambda x, route: lax.ppermute(x.astype(BF16), 'ctx', route)]
    ppermute x1, starting transfers between devices: 7.3 us -> 6.14 us  [on_device(): got = lax.ppermute(give, 'tp', swap(1, N_TP))]
  transfers between devices with their start and end apart: 17 -> 18, of which waited for: 9 -> 6; matrix products, arithmetic and copies ran while one was open for 1% -> 1% of each run, Pallas kernels for 7% -> 7%
where the time goes in v7:
time: 106 us; the launch traced here: 105 us
  starting transfers between devices  72.8 us (69%)
  waiting for transfers between devices  18.8 us (18%)
  Pallas kernels  11 us (10%)
  other arithmetic  1.31 us (1%)
  local copies, waits for them, and re-layouts  1.06 us (1%)
    ppermute x10, starting transfers between devices, on_device(): send = lambda x, route: lax.ppermute(x.astype(BF16), 'ctx', route)  39.8 us
    ppermute x10, waiting for transfers between devices, on_device(): send = lambda x, route: lax.ppermute(x.astype(BF16), 'ctx', route)  10.4 us
    ppermute x1, starting transfers between devices, on_device(): w_other = lax.ppermute(out_weight, 'tp', swap(1, N_TP))  8.78 us
    ppermute x1, starting transfers between devices, on_device(): got = lax.ppermute(give, 'tp', swap(1, N_TP))  6.14 us
    ppermute x1, starting transfers between devices, on_device(): left_a = lax.ppermute(left_a, 'tp', turned(-1))  4.4 us
    ppermute x1, starting transfers between devices, on_device(): far_b = lax.ppermute(far_b, 'tp', turned(-1))  4.38 us
    ppermute x1, starting transfers between devices, on_device(): left_b = lax.ppermute(left_b + far_b, 'tp', turned(-1))  3.36 us
    ppermute x1, waiting for transfers between devices, on_device(): left_b = lax.ppermute(left_b + far_b, 'tp', turned(-1))  2.88 us
  transfers between devices with their start and end apart: 18, of which 6 were waited for; matrix products, arithmetic and copies ran while one was open for 1% of the time, Pallas kernels for 7%

profile of v7, /device:TPU:1, one launch (start us, length us, event | category | flops | bytes accessed | tf_op | source)
XLA Modules:
  0.0 105.4 jit_solution(10220395231727312229)
XLA Ops:
  0.0 8.8 %collective-permute-start.2 = (bf16[512,4096]{1,0:T(8,128)(2,1)}, bf16[512,4096]{1,0:T(8,128)(2,1)}, u32[]{:S(2)}, u32[]{:S(2)}) collective-permute-start(bf16[512,4096]{1,0:T(8,128)(2,1)} %w_own_ref.3), channel_id=1, source_target_pairs={{0,1},{1,0},{2,3},{3,2},{4,5},{5,4},{6,7},{7,6},{8,9},{9,8},{10,11... | collective-permute-start | bytes 12582920 | tf_op jit(solution)/shard_map/ppermute | solution.py:277
  8.8 1.0 pad_add_fusion.kv_ref
  9.8 0.3 shard_map.60
  10.1 1.9 %collective-permute-start.4 = (bf16[144,128]{1,0:T(8,128)(2,1)S(1)}, bf16[144,128]{1,0:T(8,128)(2,1)S(1)}, u32[]{:S(2)}, u32[]{:S(2)}) collective-permute-start(bf16[144,128]{1,0:T(8,128)(2,1)S(1)} %get-tuple-element.36), channel_id=1, source_target_pairs={{0,8},{8,0},{16,24},{24,16},{32,40},{40,32},{48,56},{56,48},{64,72... | collective-permute-start | bytes 110600 | tf_op jit(solution)/shard_map/ppermute | solution.py:274
  12.0 2.5 %collective-permute-start.5 = (bf16[144,128]{1,0:T(8,128)(2,1)S(1)}, bf16[144,128]{1,0:T(8,128)(2,1)S(1)}, u32[]{:S(2)}, u32[]{:S(2)}) collective-permute-start(bf16[144,128]{1,0:T(8,128)(2,1)S(1)} %get-tuple-element.36), channel_id=1, source_target_pairs={{0,16},{8,24},{16,0},{24,8},{32,48},{40,56},{48,32},{56,40},{64,80... | collective-permute-start | bytes 110600 | tf_op jit(solution)/shard_map/ppermute | solution.py:274
  14.5 4.8 %collective-permute-start.6 = (bf16[144,128]{1,0:T(8,128)(2,1)S(1)}, bf16[144,128]{1,0:T(8,128)(2,1)S(1)}, u32[]{:S(2)}, u32[]{:S(2)}) collective-permute-start(bf16[144,128]{1,0:T(8,128)(2,1)S(1)} %get-tuple-element.36), channel_id=1, source_target_pairs={{0,24},{8,16},{16,8},{24,0},{32,56},{40,48},{48,40},{56,32},{64,88... | collective-permute-start | bytes 110600 | tf_op jit(solution)/shard_map/ppermute | solution.py:274
  19.4 1.3 %collective-permute-start.3 = (bf16[512,256]{1,0:T(8,128)(2,1)S(1)}, bf16[512,256]{1,0:T(8,128)(2,1)S(1)}, u32[]{:S(2)}, u32[]{:S(2)}) collective-permute-start(bf16[512,256]{1,0:T(8,128)(2,1)S(1)} %pad_add_fusion.kv_ref), channel_id=1, source_target_pairs={{0,8},{8,16},{16,24},{32,40},{40,48},{48,56},{64,72},{72,80},{80,8... | collective-permute-start | bytes 786440 | tf_op jit(solution)/shard_map/ppermute | solution.py:274
  20.7 0.0 collective-permute-done.4
  20.7 3.1 %collective-permute-start.1 = (bf16[512,256]{1,0:T(8,128)(2,1)S(1)}, bf16[512,256]{1,0:T(8,128)(2,1)S(1)}, u32[]{:S(2)}, u32[]{:S(2)}) collective-permute-start(bf16[512,256]{1,0:T(8,128)(2,1)S(1)} %pad_add_fusion.kv_ref), channel_id=1, source_target_pairs={{0,16},{8,24},{32,48},{40,56},{64,80},{72,88},{96,112},{104,120},{... | collective-permute-start | bytes 786440 | tf_op jit(solution)/shard_map/ppermute | solution.py:274
  23.9 0.0 collective-permute-done.5
  23.9 1.3 %collective-permute-start = (bf16[512,256]{1,0:T(8,128)(2,1)S(1)}, bf16[512,256]{1,0:T(8,128)(2,1)S(1)}, u32[]{:S(2)}, u32[]{:S(2)}) collective-permute-start(bf16[512,256]{1,0:T(8,128)(2,1)S(1)} %pad_add_fusion.kv_ref), channel_id=1, source_target_pairs={{0,24},{32,56},{64,88},{96,120},{128,152},{160,184},{192,216},{224... | collective-permute-start | bytes 786440 | tf_op jit(solution)/shard_map/ppermute | solution.py:274
  25.2 0.0 collective-permute-done.6
  25.3 7.9 %collective-permute-start.7 = (bf16[144,128]{1,0:T(8,128)(2,1)S(1)}, bf16[144,128]{1,0:T(8,128)(2,1)S(1)}, u32[]{:S(2)}, u32[]{:S(2)}) collective-permute-start(bf16[144,128]{1,0:T(8,128)(2,1)S(1)} %get-tuple-element.49), channel_id=1, source_target_pairs={{0,32},{8,40},{16,48},{24,56},{32,0},{40,8},{48,16},{56,24},{64,96... | collective-permute-start | bytes 110600 | tf_op jit(solution)/shard_map/ppermute | solution.py:274
  33.2 0.1 pad_add_fusion.1.place_ref
  33.3 10.1 %collective-permute-done.7 = bf16[144,128]{1,0:T(8,128)(2,1)S(1)} collective-permute-done((bf16[144,128]{1,0:T(8,128)(2,1)S(1)}, bf16[144,128]{1,0:T(8,128)(2,1)S(1)}, u32[]{:S(2)}, u32[]{:S(2)}) %collective-permute-start.7) | collective-permute-done | bytes 36896 | tf_op jit(solution)/shard_map/ppermute | solution.py:274
  43.4 3.2 %collective-permute-start.8 = (bf16[144,128]{1,0:T(8,128)(2,1)S(1)}, bf16[144,128]{1,0:T(8,128)(2,1)S(1)}, u32[]{:S(2)}, u32[]{:S(2)}) collective-permute-start(bf16[144,128]{1,0:T(8,128)(2,1)S(1)} %fusion.2), channel_id=1, source_target_pairs={{0,64},{8,72},{16,80},{24,88},{32,96},{40,104},{48,112},{56,120},{... | collective-permute-start | bytes 110600 | tf_op jit(solution)/shard_map/ppermute | solution.py:274
  46.6 0.0 copy-start.1
  46.6 1.0 copy-done.1
  47.7 1.4 %shard_map.55 = (f32[4,512,256]{2,1,0:T(8,128)S(1)}, f32[4,512,128]{2,1,0:T(8,128)S(1)}) custom-call(bf16[512,512]{1,0:T(8,128)(2,1)S(1)} %copy-done.1, bf16[512,256]{1,0:T(8,128)(2,1)S(1)} %pad_add_fusion.kv_ref), custom_call_target="tpu_custom_call" | custom-call | flops 536870912 | bytes 4000000 | tf_op jit(solution)/shard_map/pallas_call | solution.py:100
  49.1 0.0 collective-permute-done.8
  49.1 4.2 %collective-permute-start.9 = (bf16[144,128]{1,0:T(8,128)(2,1)S(1)}, bf16[144,128]{1,0:T(8,128)(2,1)S(1)}, u32[]{:S(2)}, u32[]{:S(2)}) collective-permute-start(bf16[144,128]{1,0:T(8,128)(2,1)S(1)} %fusion.1), channel_id=1, source_target_pairs={{0,128},{8,136},{16,144},{24,152},{32,160},{40,168},{48,176},{56,1... | collective-permute-start | bytes 110600 | tf_op jit(solution)/shard_map/ppermute | solution.py:274
  53.4 0.8 shard_map.56
  54.1 0.3 collective-permute-done.9
  54.4 0.0 copy-start.2
  54.4 9.4 %collective-permute-start.10 = (bf16[144,128]{1,0:T(8,128)(2,1)S(1)}, bf16[144,128]{1,0:T(8,128)(2,1)S(1)}, u32[]{:S(2)}, u32[]{:S(2)}) collective-permute-start(bf16[144,128]{1,0:T(8,128)(2,1)S(1)} %get-tuple-element.51), channel_id=1, source_target_pairs={{0,256},{8,264},{16,272},{24,280},{32,288},{40,296},{48,304},{56,3... | collective-permute-start | bytes 110600 | tf_op jit(solution)/shard_map/ppermute | solution.py:274
  63.9 0.0 collective-permute-done.2.w_hbm
  63.9 2.2 %shard_map.57.w_other_ref = bf16[512,4096]{1,0:T(8,128)(2,1)S(1)} custom-call(bf16[512,4096]{1,0:T(8,128)(2,1)} %collective-permute-done.2.w_hbm), custom_call_target="tpu_custom_call" | custom-call | bytes 8000000 | tf_op jit(solution)/shard_map/pallas_call | solution.py:160
  66.1 0.8 shard_map.58
  66.9 0.0 copy-start.3
  66.9 0.0 copy-start
  66.9 0.7 shard_map.59.acc_ref
  67.6 1.5 %shard_map.61 = (bf16[256,512]{1,0:T(8,128)(2,1)S(1)}, bf16[256,512]{1,0:T(8,128)(2,1)S(1)}) custom-call(s32[3]{0:T(128)S(1)} %pad_add_fusion.1.place_ref, f32[4]{0:T(128)S(1)} %copy-done.3, bf16[512,512]{1,0:T(8,128)(2,1)S(1)} %copy-done.2, f32[4,512,256]{2,1,0:T(8,128)S(1)} %shard_map.59.acc_ref, f32[144,128]{1,0:T(8,128)S(1)} %get-tuple-element.52.mem0, ...), custom_call_target="tpu_custom_call" | custom-call | flops 402653184 | bytes 4000000 | tf_op jit(solution)/shard_map/pallas_call | solution.py:197
  69.1 6.1 %collective-permute-start.11 = (bf16[256,512]{1,0:T(8,128)(2,1)S(1)}, bf16[256,512]{1,0:T(8,128)(2,1)S(1)}, u32[]{:S(2)}, u32[]{:S(2)}) collective-permute-start(bf16[256,512]{1,0:T(8,128)(2,1)S(1)} %get-tuple-element.40), channel_id=1, source_target_pairs={{0,1},{1,0},{2,3},{3,2},{4,5},{5,4},{6,7},{7,6},{8,9},{9,8},{10,11... | collective-permute-start | bytes 786440 | tf_op jit(solution)/shard_map/ppermute | solution.py:295
  75.2 1.1 %collective-permute-done.11.got_ref = bf16[256,512]{1,0:T(8,128)(2,1)S(1)} collective-permute-done((bf16[256,512]{1,0:T(8,128)(2,1)S(1)}, bf16[256,512]{1,0:T(8,128)(2,1)S(1)}, u32[]{:S(2)}, u32[]{:S(2)}) %collective-permute-start.11) | collective-permute-done | bytes 262176 | tf_op jit(solution)/shard_map/ppermute | solution.py:295
  76.4 1.2 %shard_map.63 = (bf16[64,2048]{1,0:T(8,128)(2,1)S(1)}, bf16[64,2048]{1,0:T(8,128)(2,1)S(1)}, bf16[64,2048]{1,0:T(8,128)(2,1)S(1)}, bf16[64,2048]{1,0:T(8,128)(2,1)S(1)}) custom-call(bf16[256,512]{1,0:T(8,128)(2,1)S(1)} %get-tuple-element.39.keep_ref, bf16[256,512]{1,0:T(8,128)(2,1)S(1)} %collective-permute-done.11.got_ref, bf16[512,4096]{1,0:T(8,128)(2,1)S(1)} %copy-done, ...), custom_call_target="tpu_custom_call" | custom-call | flops 1073741824 | bytes 6000000 | tf_op jit(solution)/shard_map/pallas_call | solution.py:223
  77.6 4.4 %collective-permute-start.15 = (bf16[64,2048]{1,0:T(8,128)(2,1)S(1)}, bf16[64,2048]{1,0:T(8,128)(2,1)S(1)}, u32[]{:S(2)}, u32[]{:S(2)}) collective-permute-start(bf16[64,2048]{1,0:T(8,128)(2,1)S(1)} %get-tuple-element.47), channel_id=1, source_target_pairs={{0,6},{1,7},{2,0},{3,1},{4,2},{5,3},{6,4},{7,5},{8,14},{9,15},{10,... | collective-permute-start | bytes 786440 | tf_op jit(solution)/shard_map/ppermute | solution.py:300
  82.0 1.2 %shard_map.62 = (bf16[64,2048]{1,0:T(8,128)(2,1)S(1)}, bf16[64,2048]{1,0:T(8,128)(2,1)S(1)}, bf16[64,2048]{1,0:T(8,128)(2,1)S(1)}, bf16[64,2048]{1,0:T(8,128)(2,1)S(1)}) custom-call(bf16[256,512]{1,0:T(8,128)(2,1)S(1)} %get-tuple-element.39.keep_ref, bf16[256,512]{1,0:T(8,128)(2,1)S(1)} %collective-permute-done.11.got_ref, bf16[512,4096]{1,0:T(8,128)(2,1)S(1)} %copy-done, ...), custom_call_target="tpu_custom_call" | custom-call | flops 1073741824 | bytes 6000000 | tf_op jit(solution)/shard_map/pallas_call | solution.py:223
  83.3 1.9 %collective-permute-start.13 = (bf16[64,2048]{1,0:T(8,128)(2,1)S(1)}, bf16[64,2048]{1,0:T(8,128)(2,1)S(1)}, u32[]{:S(2)}, u32[]{:S(2)}) collective-permute-start(bf16[64,2048]{1,0:T(8,128)(2,1)S(1)} %get-tuple-element.44), channel_id=1, source_target_pairs={{0,2},{1,3},{2,4},{3,5},{4,6},{5,7},{6,0},{7,1},{8,10},{9,11},{10,... | collective-permute-start | bytes 786440 | tf_op jit(solution)/shard_map/ppermute | solution.py:297
  85.2 2.1 %collective-permute-start.17 = (bf16[64,2048]{1,0:T(8,128)(2,1)S(1)}, bf16[64,2048]{1,0:T(8,128)(2,1)S(1)}, u32[]{:S(2)}, u32[]{:S(2)}) collective-permute-start(bf16[64,2048]{1,0:T(8,128)(2,1)S(1)} %get-tuple-element.48), channel_id=1, source_target_pairs={{0,2},{1,3},{2,4},{3,5},{4,6},{5,7},{6,0},{7,1},{8,10},{9,11},{10,... | collective-permute-start | bytes 786440 | tf_op jit(solution)/shard_map/ppermute | solution.py:301
  87.3 4.4 %collective-permute-start.12 = (bf16[64,2048]{1,0:T(8,128)(2,1)S(1)}, bf16[64,2048]{1,0:T(8,128)(2,1)S(1)}, u32[]{:S(2)}, u32[]{:S(2)}) collective-permute-start(bf16[64,2048]{1,0:T(8,128)(2,1)S(1)} %get-tuple-element.42), channel_id=1, source_target_pairs={{0,6},{1,7},{2,0},{3,1},{4,2},{5,3},{6,4},{7,5},{8,14},{9,15},{10,... | collective-permute-start | bytes 786440 | tf_op jit(solution)/shard_map/ppermute | solution.py:298
  91.7 0.1 add.61
  91.8 3.4 %collective-permute-start.16 = (bf16[64,2048]{1,0:T(8,128)(2,1)S(1)}, bf16[64,2048]{1,0:T(8,128)(2,1)S(1)}, u32[]{:S(2)}, u32[]{:S(2)}) collective-permute-start(bf16[64,2048]{1,0:T(8,128)(2,1)S(1)} %add.61), channel_id=1, source_target_pairs={{0,6},{1,7},{2,0},{3,1},{4,2},{5,3},{6,4},{7,5},{8,14},{9,15},{10,... | collective-permute-start | bytes 786440 | tf_op jit(solution)/shard_map/ppermute | solution.py:303
  95.2 0.1 add.60
  95.2 1.9 %collective-permute-start.14 = (bf16[64,2048]{1,0:T(8,128)(2,1)S(1)}, bf16[64,2048]{1,0:T(8,128)(2,1)S(1)}, u32[]{:S(2)}, u32[]{:S(2)}) collective-permute-start(bf16[64,2048]{1,0:T(8,128)(2,1)S(1)} %add.60), channel_id=1, source_target_pairs={{0,2},{1,3},{2,4},{3,5},{4,6},{5,7},{6,0},{7,1},{8,10},{9,11},{10,... | collective-permute-start | bytes 786440 | tf_op jit(solution)/shard_map/ppermute | solution.py:302
  97.2 2.0 %collective-permute-done.17.right_b = bf16[64,2048]{1,0:T(8,128)(2,1)S(1)} collective-permute-done((bf16[64,2048]{1,0:T(8,128)(2,1)S(1)}, bf16[64,2048]{1,0:T(8,128)(2,1)S(1)}, u32[]{:S(2)}, u32[]{:S(2)}) %collective-permute-start.17) | collective-permute-done | bytes 262176 | tf_op jit(solution)/shard_map/ppermute | solution.py:301
  99.2 2.9 %collective-permute-done.16.left_b = bf16[64,2048]{1,0:T(8,128)(2,1)S(1)} collective-permute-done((bf16[64,2048]{1,0:T(8,128)(2,1)S(1)}, bf16[64,2048]{1,0:T(8,128)(2,1)S(1)}, u32[]{:S(2)}, u32[]{:S(2)}) %collective-permute-start.16) | collective-permute-done | bytes 262176 | tf_op jit(solution)/shard_map/ppermute | solution.py:303
  102.1 2.3 %collective-permute-done.14.right_a = bf16[64,2048]{1,0:T(8,128)(2,1)S(1)} collective-permute-done((bf16[64,2048]{1,0:T(8,128)(2,1)S(1)}, bf16[64,2048]{1,0:T(8,128)(2,1)S(1)}, u32[]{:S(2)}, u32[]{:S(2)}) %collective-permute-start.14) | collective-permute-done | bytes 262176 | tf_op jit(solution)/shard_map/ppermute | solution.py:302
  104.4 1.0 shard_map.64
  (14 shorter events, 0.1 us)
Async XLA Ops:
  0.0 63.9 %collective-permute-start.2 = (bf16[512,4096]{1,0:T(8,128)(2,1)}, bf16[512,4096]{1,0:T(8,128)(2,1)}, u32[]{:S(2)}, u32[]{:S(2)}) collective-permute-start(bf16[512,4096]{1,0:T(8,128)(2,1)} %w_own_ref.3), channel_id=1, source_target_pairs={{0,1},{1,0},{2,3},{3,2},{4,5},{5,4},{6,7},{7,6},{8,9},{9,8},{10,11... | collective-permute-start | bytes 12582920 | tf_op jit(solution)/shard_map/ppermute | solution.py:277
  10.1 10.6 %collective-permute-start.4 = (bf16[144,128]{1,0:T(8,128)(2,1)S(1)}, bf16[144,128]{1,0:T(8,128)(2,1)S(1)}, u32[]{:S(2)}, u32[]{:S(2)}) collective-permute-start(bf16[144,128]{1,0:T(8,128)(2,1)S(1)} %get-tuple-element.36), channel_id=1, source_target_pairs={{0,8},{8,0},{16,24},{24,16},{32,40},{40,32},{48,56},{56,48},{64,72... | collective-permute-start | bytes 110600 | tf_op jit(solution)/shard_map/ppermute | solution.py:274
  12.0 11.9 %collective-permute-start.5 = (bf16[144,128]{1,0:T(8,128)(2,1)S(1)}, bf16[144,128]{1,0:T(8,128)(2,1)S(1)}, u32[]{:S(2)}, u32[]{:S(2)}) collective-permute-start(bf16[144,128]{1,0:T(8,128)(2,1)S(1)} %get-tuple-element.36), channel_id=1, source_target_pairs={{0,16},{8,24},{16,0},{24,8},{32,48},{40,56},{48,32},{56,40},{64,80... | collective-permute-start | bytes 110600 | tf_op jit(solution)/shard_map/ppermute | solution.py:274
  14.5 10.7 %collective-permute-start.6 = (bf16[144,128]{1,0:T(8,128)(2,1)S(1)}, bf16[144,128]{1,0:T(8,128)(2,1)S(1)}, u32[]{:S(2)}, u32[]{:S(2)}) collective-permute-start(bf16[144,128]{1,0:T(8,128)(2,1)S(1)} %get-tuple-element.36), channel_id=1, source_target_pairs={{0,24},{8,16},{16,8},{24,0},{32,56},{40,48},{48,40},{56,32},{64,88... | collective-permute-start | bytes 110600 | tf_op jit(solution)/shard_map/ppermute | solution.py:274
  19.4 34.0 %collective-permute-start.3 = (bf16[512,256]{1,0:T(8,128)(2,1)S(1)}, bf16[512,256]{1,0:T(8,128)(2,1)S(1)}, u32[]{:S(2)}, u32[]{:S(2)}) collective-permute-start(bf16[512,256]{1,0:T(8,128)(2,1)S(1)} %pad_add_fusion.kv_ref), channel_id=1, source_target_pairs={{0,8},{8,16},{16,24},{32,40},{40,48},{48,56},{64,72},{72,80},{80,8... | collective-permute-start | bytes 786440 | tf_op jit(solution)/shard_map/ppermute | solution.py:274
  20.7 45.3 %collective-permute-start.1 = (bf16[512,256]{1,0:T(8,128)(2,1)S(1)}, bf16[512,256]{1,0:T(8,128)(2,1)S(1)}, u32[]{:S(2)}, u32[]{:S(2)}) collective-permute-start(bf16[512,256]{1,0:T(8,128)(2,1)S(1)} %pad_add_fusion.kv_ref), channel_id=1, source_target_pairs={{0,16},{8,24},{32,48},{40,56},{64,80},{72,88},{96,112},{104,120},{... | collective-permute-start | bytes 786440 | tf_op jit(solution)/shard_map/ppermute | solution.py:274
  23.9 43.0 %collective-permute-start = (bf16[512,256]{1,0:T(8,128)(2,1)S(1)}, bf16[512,256]{1,0:T(8,128)(2,1)S(1)}, u32[]{:S(2)}, u32[]{:S(2)}) collective-permute-start(bf16[512,256]{1,0:T(8,128)(2,1)S(1)} %pad_add_fusion.kv_ref), channel_id=1, source_target_pairs={{0,24},{32,56},{64,88},{96,120},{128,152},{160,184},{192,216},{224... | collective-permute-start | bytes 786440 | tf_op jit(solution)/shard_map/ppermute | solution.py:274
  25.3 18.2 %collective-permute-start.7 = (bf16[144,128]{1,0:T(8,128)(2,1)S(1)}, bf16[144,128]{1,0:T(8,128)(2,1)S(1)}, u32[]{:S(2)}, u32[]{:S(2)}) collective-permute-start(bf16[144,128]{1,0:T(8,128)(2,1)S(1)} %get-tuple-element.49), channel_id=1, source_target_pairs={{0,32},{8,40},{16,48},{24,56},{32,0},{40,8},{48,16},{56,24},{64,96... | collective-permute-start | bytes 110600 | tf_op jit(solution)/shard_map/ppermute | solution.py:274
  43.4 5.7 %collective-permute-start.8 = (bf16[144,128]{1,0:T(8,128)(2,1)S(1)}, bf16[144,128]{1,0:T(8,128)(2,1)S(1)}, u32[]{:S(2)}, u32[]{:S(2)}) collective-permute-start(bf16[144,128]{1,0:T(8,128)(2,1)S(1)} %fusion.2), channel_id=1, source_target_pairs={{0,64},{8,72},{16,80},{24,88},{32,96},{40,104},{48,112},{56,120},{... | collective-permute-start | bytes 110600 | tf_op jit(solution)/shard_map/ppermute | solution.py:274
  46.6 1.0 copy-start.1
  49.1 5.3 %collective-permute-start.9 = (bf16[144,128]{1,0:T(8,128)(2,1)S(1)}, bf16[144,128]{1,0:T(8,128)(2,1)S(1)}, u32[]{:S(2)}, u32[]{:S(2)}) collective-permute-start(bf16[144,128]{1,0:T(8,128)(2,1)S(1)} %fusion.1), channel_id=1, source_target_pairs={{0,128},{8,136},{16,144},{24,152},{32,160},{40,168},{48,176},{56,1... | collective-permute-start | bytes 110600 | tf_op jit(solution)/shard_map/ppermute | solution.py:274
  54.4 11.7 %copy-start.2 = (bf16[512,512]{1,0:T(8,128)(2,1)S(1)}, bf16[512,512]{1,0:T(8,128)(2,1)}, u32[]{:S(2)}) copy-start(bf16[512,512]{1,0:T(8,128)(2,1)} %q_ref.9) | copy-start | bytes 1572868
  54.4 13.2 %collective-permute-start.10 = (bf16[144,128]{1,0:T(8,128)(2,1)S(1)}, bf16[144,128]{1,0:T(8,128)(2,1)S(1)}, u32[]{:S(2)}, u32[]{:S(2)}) collective-permute-start(bf16[144,128]{1,0:T(8,128)(2,1)S(1)} %get-tuple-element.51), channel_id=1, source_target_pairs={{0,256},{8,264},{16,272},{24,280},{32,288},{40,296},{48,304},{56,3... | collective-permute-start | bytes 110600 | tf_op jit(solution)/shard_map/ppermute | solution.py:274
  66.9 0.7 copy-start.3
  66.9 9.5 %copy-start = (bf16[512,4096]{1,0:T(8,128)(2,1)S(1)}, bf16[512,4096]{1,0:T(8,128)(2,1)}, u32[]{:S(2)}) copy-start(bf16[512,4096]{1,0:T(8,128)(2,1)} %w_own_ref.3) | copy-start | bytes 12582916
  69.1 7.3 %collective-permute-start.11 = (bf16[256,512]{1,0:T(8,128)(2,1)S(1)}, bf16[256,512]{1,0:T(8,128)(2,1)S(1)}, u32[]{:S(2)}, u32[]{:S(2)}) collective-permute-start(bf16[256,512]{1,0:T(8,128)(2,1)S(1)} %get-tuple-element.40), channel_id=1, source_target_pairs={{0,1},{1,0},{2,3},{3,2},{4,5},{5,4},{6,7},{7,6},{8,9},{9,8},{10,11... | collective-permute-start | bytes 786440 | tf_op jit(solution)/shard_map/ppermute | solution.py:295
  77.6 14.1 %collective-permute-start.15 = (bf16[64,2048]{1,0:T(8,128)(2,1)S(1)}, bf16[64,2048]{1,0:T(8,128)(2,1)S(1)}, u32[]{:S(2)}, u32[]{:S(2)}) collective-permute-start(bf16[64,2048]{1,0:T(8,128)(2,1)S(1)} %get-tuple-element.47), channel_id=1, source_target_pairs={{0,6},{1,7},{2,0},{3,1},{4,2},{5,3},{6,4},{7,5},{8,14},{9,15},{10,... | collective-permute-start | bytes 786440 | tf_op jit(solution)/shard_map/ppermute | solution.py:300
  83.3 11.9 %collective-permute-start.13 = (bf16[64,2048]{1,0:T(8,128)(2,1)S(1)}, bf16[64,2048]{1,0:T(8,128)(2,1)S(1)}, u32[]{:S(2)}, u32[]{:S(2)}) collective-permute-start(bf16[64,2048]{1,0:T(8,128)(2,1)S(1)} %get-tuple-element.44), channel_id=1, source_target_pairs={{0,2},{1,3},{2,4},{3,5},{4,6},{5,7},{6,0},{7,1},{8,10},{9,11},{10,... | collective-permute-start | bytes 786440 | tf_op jit(solution)/shard_map/ppermute | solution.py:297
  85.2 14.0 %collective-permute-start.17 = (bf16[64,2048]{1,0:T(8,128)(2,1)S(1)}, bf16[64,2048]{1,0:T(8,128)(2,1)S(1)}, u32[]{:S(2)}, u32[]{:S(2)}) collective-permute-start(bf16[64,2048]{1,0:T(8,128)(2,1)S(1)} %get-tuple-element.48), channel_id=1, source_target_pairs={{0,2},{1,3},{2,4},{3,5},{4,6},{5,7},{6,0},{7,1},{8,10},{9,11},{10,... | collective-permute-start | bytes 786440 | tf_op jit(solution)/shard_map/ppermute | solution.py:301
  87.3 11.9 %collective-permute-start.12 = (bf16[64,2048]{1,0:T(8,128)(2,1)S(1)}, bf16[64,2048]{1,0:T(8,128)(2,1)S(1)}, u32[]{:S(2)}, u32[]{:S(2)}) collective-permute-start(bf16[64,2048]{1,0:T(8,128)(2,1)S(1)} %get-tuple-element.42), channel_id=1, source_target_pairs={{0,6},{1,7},{2,0},{3,1},{4,2},{5,3},{6,4},{7,5},{8,14},{9,15},{10,... | collective-permute-start | bytes 786440 | tf_op jit(solution)/shard_map/ppermute | solution.py:298
  91.8 10.3 %collective-permute-start.16 = (bf16[64,2048]{1,0:T(8,128)(2,1)S(1)}, bf16[64,2048]{1,0:T(8,128)(2,1)S(1)}, u32[]{:S(2)}, u32[]{:S(2)}) collective-permute-start(bf16[64,2048]{1,0:T(8,128)(2,1)S(1)} %add.61), channel_id=1, source_target_pairs={{0,6},{1,7},{2,0},{3,1},{4,2},{5,3},{6,4},{7,5},{8,14},{9,15},{10,... | collective-permute-start | bytes 786440 | tf_op jit(solution)/shard_map/ppermute | solution.py:303
  95.2 9.1 %collective-permute-start.14 = (bf16[64,2048]{1,0:T(8,128)(2,1)S(1)}, bf16[64,2048]{1,0:T(8,128)(2,1)S(1)}, u32[]{:S(2)}, u32[]{:S(2)}) collective-permute-start(bf16[64,2048]{1,0:T(8,128)(2,1)S(1)} %add.60), channel_id=1, source_target_pairs={{0,2},{1,3},{2,4},{3,5},{4,6},{5,7},{6,0},{7,1},{8,10},{9,11},{10,... | collective-permute-start | bytes 786440 | tf_op jit(solution)/shard_map/ppermute | solution.py:302

commit v8 on v7

--- a/solution.py
+++ b/solution.py
@@ -77,7 +77,8 @@
     return jnp.concatenate([v, jnp.ones_like(v)], axis=1)
 
 
-def own_kernel(q_ref, kv_ref, acc_ref, top_ref):
+def own_kernel(q_ref, kv_ref, order, acc_ref, top_ref):
+    del order
     k = kv_ref[:, :HD]
     wide = values_and_ones(kv_ref[:, HD:])
     for r in range(ROWS // CHUNK):
@@ -96,7 +97,7 @@
             top_ref[h, rows, :] = jnp.broadcast_to(top, (CHUNK, HD))
 
 
-def own_call(queries, kv):
+def own_call(queries, kv, order):
     return call(
         own_kernel,
         (
@@ -104,12 +105,14 @@
             jax.ShapeDtypeStruct((GROUP, ROWS, HD), F32),
         ),
         (GROUP * ROWS * ROWS * HD * 4, 4000000, GROUP * ROWS * ROWS),
-        in_specs=[VM, VM],
+        in_specs=[VM, VM, pl.BlockSpec(memory_space=pl.ANY)],
         out_specs=(VM, VM),
-    )(queries, kv)
-
-
-def step_kernel(distance, place_ref, q_ref, kv_ref, acc_in, top_in, acc_ref, top_ref=None):
+    )(queries, kv, order)
+
+
+def step_kernel(distance, place_ref, q_ref, kv_ref, acc_in, top_in, order, acc_ref, top_ref=None):
+    del order
+
     @pl.when(place_ref[0] >= distance)
     def _():
         k = kv_ref[:, :HD]
@@ -135,7 +138,7 @@
             top_ref[...] = top_in[...]
 
 
-def step_call(distance, place, queries, kv, acc, top):
+def step_call(distance, place, queries, kv, acc, top, order):
     state = (
         jax.ShapeDtypeStruct((GROUP, ROWS, 2 * HD), F32),
         jax.ShapeDtypeStruct((GROUP, ROWS, HD), F32),
@@ -145,9 +148,9 @@
         functools.partial(step_kernel, distance),
         kept,
         (GROUP * ROWS * ROWS * HD * 4, 4000000, GROUP * ROWS * ROWS),
-        in_specs=[SM] + [VM] * 4,
+        in_specs=[SM] + [VM] * 4 + [pl.BlockSpec(memory_space=pl.ANY)],
         out_specs=(VM,) * len(kept),
-    )(place, queries, kv, acc, top)
+    )(place, queries, kv, acc, top, order)
 
 
 def stage_kernel(w_hbm, w_ref, sem):
@@ -167,10 +170,10 @@
     )(w)
 
 
-def merge_kernel(place_ref, gate_ref, q_ref, acc_ref, mem0, mem1, keep_ref, send_ref, out_ref):
+def merge_kernel(place_ref, gate_ref, q_ref, acc_ref, mem0, mem1, mem2, mem3, keep_ref, send_ref, out_ref):
     x = place_ref[1]
     core = place_ref[2]
-    mem = mem0[...] + mem1[...].astype(F32)
+    mem = mem0[...] + mem1[...].astype(F32) + (mem2[...].astype(F32) + mem3[...].astype(F32))
     mem = jnp.concatenate([mem[:HD, :], jnp.broadcast_to(mem[HD : HD + 1, :], (HD, HD))], axis=0)
     mem_high, mem_low = split_two(mem)
     mem_twice = jnp.concatenate([mem_high, mem_high], axis=1)
@@ -192,16 +195,16 @@
         send_ref[b * BLOCK : (b + 1) * BLOCK, :] = out_ref[pl.ds(other, BLOCK), :]
 
 
-def merge_call(place, gates, queries, acc, mem0, mem1):
+def merge_call(place, gates, queries, acc, mems):
     half = jax.ShapeDtypeStruct((ROWS // 2, GROUP * HD), BF16)
     return call(
         merge_kernel,
         (half, half),
         (6 * ROWS * GROUP * HD * HD * 2, 4000000, ROWS * GROUP * HD),
-        in_specs=[SM, SM] + [VM] * 4,
+        in_specs=[SM, SM] + [VM] * 6,
         out_specs=(VM, VM),
         scratch_shapes=[pltpu.VMEM((ROWS, GROUP * HD), BF16)],
-    )(place, gates, queries, acc, mem0, mem1)
+    )(place, gates, queries, acc, *mems)
 
 
 def project_kernel(first, keep_ref, got_ref, w_own_ref, w_other_ref, own_ref, right_ref, far_ref, left_ref):
@@ -259,6 +262,10 @@
     return [(i, i ^ bit) for i in range(size)]
 
 
+def other_half():
+    return [(i, i // 8 * 8 + (i % 8 + (1 if i % SPAN == SPAN - 1 else 5)) % 8) for i in range(N_CTX)]
+
+
 def after(x, *others):
     return lax.optimization_barrier((x, others))[0]
 
@@ -278,20 +285,23 @@
     segment = [send(delta16, swap(k, N_CTX)) for k in (1, 2, 3)]
     kv1, kv2, kv3 = [send(kv, along_z(d)) for d in (1, 2, 3)]
     segment = delta + sum(part.astype(F32) for part in segment)
-    other = send(segment, swap(4, N_CTX)).astype(F32)
+    other = send(segment, other_half())
+    w_other = stage_call(w_other)
+    other = after(other, w_other).astype(F32)
     line = segment + other
     start = jnp.where(ctx % 8 >= SPAN, other, 0.0)
-    before = send(line, along_y(1))
-    acc, top = own_call(queries, kv)
-    before = after(before, acc).astype(F32)
-    more = send(line + before, along_y(2))
-    acc, top = step_call(1, place, queries, kv1, acc, top)
-    before = before + after(more, acc).astype(F32)
-    far = send(line + before, along_y(4))
-    w_other = stage_call(after(w_other, acc))
-    acc, top = step_call(2, place, queries, after(kv2, w_other), acc, top)
-    (acc,) = step_call(3, place, queries, kv3, acc, top)
-    keep, give = merge_call(place, gates, queries, acc, start + before, far)
+    sent = line.astype(BF16)
+    got = send(sent, swap(8, N_CTX))
+    acc, top = own_call(queries, kv, sent)
+    got = after(got, acc).astype(F32)
+    start = start + jnp.where(ctx // 8 % 2 == 1, got, 0.0)
+    sent = (line + got).astype(BF16)
+    pairs = [send(sent, along_y(2 * k)) for k in (1, 2, 3)]
+    acc, top = step_call(1, place, queries, kv1, acc, top, sent)
+    acc, top = step_call(2, place, queries, kv2, acc, top, sent)
+    (acc,) = step_call(3, place, queries, kv3, acc, top, sent)
+    pairs = [after(part, acc) for part in pairs]
+    keep, give = merge_call(place, gates, queries, acc, [start] + pairs)
     got = lax.ppermute(give, "tp", swap(1, N_TP))
     own_a, right_a, far_a, left_a = project_call(0, keep, got, out_weight, w_other)
     far_a = lax.ppermute(far_a, "tp", turned(1))

time: 106 us -> 91.8 us (0.87)
  the two profiles are of different devices: /device:TPU:1 before, /device:TPU:64 now
where the time goes in v8:
time: 91.8 us; the launch traced here: 91.2 us
  starting transfers between devices  64 us (70%)
  waiting for transfers between devices  12.9 us (14%)
  Pallas kernels  12.6 us (14%)
  other arithmetic  1.28 us (1%)
    ppermute x11, starting transfers between devices, on_device(): send = lambda x, route: lax.ppermute(x.astype(BF16), 'ctx', route)  40.7 us
    ppermute x1, starting transfers between devices, on_device(): far_b = lax.ppermute(far_b, 'tp', turned(-1))  4.67 us
    ppermute x1, starting transfers between devices, on_device(): left_a = lax.ppermute(left_a, 'tp', turned(-1))  4.4 us
    ppermute x1, starting transfers between devices, on_device(): left_b = lax.ppermute(left_b + far_b, 'tp', turned(-1))  3.92 us
    pallas_call x3, Pallas kernels, step_call(): call(functools.partial(step_kernel, distance), kept, (GROUP * ROWS * ROWS...  3.75 us
    ppermute x11, waiting for transfers between devices, on_device(): send = lambda x, route: lax.ppermute(x.astype(BF16), 'ctx', route)  3.25 us
    ppermute x1, waiting for transfers between devices, on_device(): right_a = lax.ppermute(right_a + far_a, 'tp', turned(1))  3.25 us
    ppermute x1, waiting for transfers between devices, on_device(): left_b = lax.ppermute(left_b + far_b, 'tp', turned(-1))  3.11 us
  transfers between devices with their start and end apart: 19, of which 6 were waited for; matrix products, arithmetic and copies ran while one was open for 1% of the time, Pallas kernels for 10%

profile of v8, /device:TPU:64, one launch (start us, length us, event | category | flops | bytes accessed | tf_op | source)
XLA Modules:
  0.0 91.2 jit_solution(3464032055698116760)
XLA Ops:
  0.0 1.9 %collective-permute-start.7 = (bf16[512,4096]{1,0:T(8,128)(2,1)}, bf16[512,4096]{1,0:T(8,128)(2,1)}, u32[]{:S(2)}, u32[]{:S(2)}) collective-permute-start(bf16[512,4096]{1,0:T(8,128)(2,1)} %w_own_ref.3), channel_id=1, source_target_pairs={{0,1},{1,0},{2,3},{3,2},{4,5},{5,4},{6,7},{7,6},{8,9},{9,8},{10,11... | collective-permute-start | bytes 12582920 | tf_op jit(solution)/shard_map/ppermute | solution.py:284
  1.9 1.0 %pad_add_fusion.kv_ref = bf16[512,256]{1,0:T(8,128)(2,1)S(1)} fusion(bf16[512,128]{1,0:T(8,128)(2,1)} %param.7, bf16[512,128]{1,0:T(8,128)(2,1)} %param.6), kind=kLoop, calls=%fused_computation | loop fusion | flops 524288 | bytes 524288 | tf_op jit(solution)/shard_map/add | solution.py:282
  2.9 0.3 shard_map.55
  3.2 6.9 %collective-permute-start.3 = (bf16[144,128]{1,0:T(8,128)(2,1)S(1)}, bf16[144,128]{1,0:T(8,128)(2,1)S(1)}, u32[]{:S(2)}, u32[]{:S(2)}) collective-permute-start(bf16[144,128]{1,0:T(8,128)(2,1)S(1)} %get-tuple-element.29), channel_id=1, source_target_pairs={{0,8},{8,0},{16,24},{24,16},{32,40},{40,32},{48,56},{56,48},{64,72... | collective-permute-start | bytes 110600 | tf_op jit(solution)/shard_map/ppermute | solution.py:281
  10.2 1.9 %collective-permute-start.4 = (bf16[144,128]{1,0:T(8,128)(2,1)S(1)}, bf16[144,128]{1,0:T(8,128)(2,1)S(1)}, u32[]{:S(2)}, u32[]{:S(2)}) collective-permute-start(bf16[144,128]{1,0:T(8,128)(2,1)S(1)} %get-tuple-element.29), channel_id=1, source_target_pairs={{0,16},{8,24},{16,0},{24,8},{32,48},{40,56},{48,32},{56,40},{64,80... | collective-permute-start | bytes 110600 | tf_op jit(solution)/shard_map/ppermute | solution.py:281
  12.1 3.4 %collective-permute-start.5 = (bf16[144,128]{1,0:T(8,128)(2,1)S(1)}, bf16[144,128]{1,0:T(8,128)(2,1)S(1)}, u32[]{:S(2)}, u32[]{:S(2)}) collective-permute-start(bf16[144,128]{1,0:T(8,128)(2,1)S(1)} %get-tuple-element.29), channel_id=1, source_target_pairs={{0,24},{8,16},{16,8},{24,0},{32,56},{40,48},{48,40},{56,32},{64,88... | collective-permute-start | bytes 110600 | tf_op jit(solution)/shard_map/ppermute | solution.py:281
  15.5 2.5 %collective-permute-start.2 = (bf16[512,256]{1,0:T(8,128)(2,1)S(1)}, bf16[512,256]{1,0:T(8,128)(2,1)S(1)}, u32[]{:S(2)}, u32[]{:S(2)}) collective-permute-start(bf16[512,256]{1,0:T(8,128)(2,1)S(1)} %pad_add_fusion.kv_ref), channel_id=1, source_target_pairs={{0,8},{8,16},{16,24},{32,40},{40,48},{48,56},{64,72},{72,80},{80,8... | collective-permute-start | bytes 786440 | tf_op jit(solution)/shard_map/ppermute | solution.py:281
  18.0 0.0 collective-permute-done.3
  18.0 2.8 %collective-permute-start.1 = (bf16[512,256]{1,0:T(8,128)(2,1)S(1)}, bf16[512,256]{1,0:T(8,128)(2,1)S(1)}, u32[]{:S(2)}, u32[]{:S(2)}) collective-permute-start(bf16[512,256]{1,0:T(8,128)(2,1)S(1)} %pad_add_fusion.kv_ref), channel_id=1, source_target_pairs={{0,16},{8,24},{32,48},{40,56},{64,80},{72,88},{96,112},{104,120},{... | collective-permute-start | bytes 786440 | tf_op jit(solution)/shard_map/ppermute | solution.py:281
  20.8 0.0 collective-permute-done.4
  20.8 0.7 collective-permute-start
  21.5 0.0 collective-permute-done.5
  21.5 7.3 %collective-permute-start.6 = (bf16[144,128]{1,0:T(8,128)(2,1)S(1)}, bf16[144,128]{1,0:T(8,128)(2,1)S(1)}, u32[]{:S(2)}, u32[]{:S(2)}) collective-permute-start(bf16[144,128]{1,0:T(8,128)(2,1)S(1)} %get-tuple-element.51), channel_id=1, source_target_pairs={{0,40},{8,48},{16,56},{24,32},{32,8},{40,16},{48,24},{56,0},{64,10... | collective-permute-start | bytes 110600 | tf_op jit(solution)/shard_map/ppermute | solution.py:281
  28.9 0.1 pad_add_fusion.1.place_ref
  28.9 0.0 collective-permute-done.7.w_hbm
  28.9 2.3 %shard_map.56.w_other_ref = bf16[512,4096]{1,0:T(8,128)(2,1)S(1)} custom-call(bf16[512,4096]{1,0:T(8,128)(2,1)} %collective-permute-done.7.w_hbm), custom_call_target="tpu_custom_call" | custom-call | bytes 8000000 | tf_op jit(solution)/shard_map/pallas_call | solution.py:163
  31.2 2.3 %collective-permute-done.6 = bf16[144,128]{1,0:T(8,128)(2,1)S(1)} collective-permute-done((bf16[144,128]{1,0:T(8,128)(2,1)S(1)}, bf16[144,128]{1,0:T(8,128)(2,1)S(1)}, u32[]{:S(2)}, u32[]{:S(2)}) %collective-permute-start.6) | collective-permute-done | bytes 36896 | tf_op jit(solution)/shard_map/ppermute | solution.py:281
  33.5 3.5 %collective-permute-start.8 = (bf16[144,128]{1,0:T(8,128)(2,1)S(1)}, bf16[144,128]{1,0:T(8,128)(2,1)S(1)}, u32[]{:S(2)}, u32[]{:S(2)}) collective-permute-start(bf16[144,128]{1,0:T(8,128)(2,1)S(1)} %fusion.2.order), channel_id=1, source_target_pairs={{0,64},{8,72},{16,80},{24,88},{32,96},{40,104},{48,112},{56,120},{... | collective-permute-start | bytes 110600 | tf_op jit(solution)/shard_map/ppermute | solution.py:281
  37.0 1.4 %shard_map.57 = (f32[4,512,256]{2,1,0:T(8,128)S(1)}, f32[4,512,128]{2,1,0:T(8,128)S(1)}) custom-call(bf16[512,512]{1,0:T(8,128)(2,1)S(1)} %copy-done.1, bf16[512,256]{1,0:T(8,128)(2,1)S(1)} %pad_add_fusion.kv_ref, bf16[144,128]{1,0:T(8,128)(2,1)S(1)} %fusion.2.order), custom_call_target="tpu_custom_call" | custom-call | flops 536870912 | bytes 4000000 | tf_op jit(solution)/shard_map/pallas_call | solution.py:101
  38.4 0.9 %collective-permute-done.8 = bf16[144,128]{1,0:T(8,128)(2,1)S(1)} collective-permute-done((bf16[144,128]{1,0:T(8,128)(2,1)S(1)}, bf16[144,128]{1,0:T(8,128)(2,1)S(1)}, u32[]{:S(2)}, u32[]{:S(2)}) %collective-permute-start.8) | collective-permute-done | bytes 36896 | tf_op jit(solution)/shard_map/ppermute | solution.py:281
  39.4 6.2 %collective-permute-start.11 = (bf16[144,128]{1,0:T(8,128)(2,1)S(1)}, bf16[144,128]{1,0:T(8,128)(2,1)S(1)}, u32[]{:S(2)}, u32[]{:S(2)}) collective-permute-start(bf16[144,128]{1,0:T(8,128)(2,1)S(1)} %get-tuple-element.54.order), channel_id=1, source_target_pairs={{0,384},{8,392},{16,400},{24,408},{32,416},{40,424},{48,432},{56,4... | collective-permute-start | bytes 110600 | tf_op jit(solution)/shard_map/ppermute | solution.py:281
  45.6 2.2 %collective-permute-start.10 = (bf16[144,128]{1,0:T(8,128)(2,1)S(1)}, bf16[144,128]{1,0:T(8,128)(2,1)S(1)}, u32[]{:S(2)}, u32[]{:S(2)}) collective-permute-start(bf16[144,128]{1,0:T(8,128)(2,1)S(1)} %get-tuple-element.54.order), channel_id=1, source_target_pairs={{0,256},{8,264},{16,272},{24,280},{32,288},{40,296},{48,304},{56,3... | collective-permute-start | bytes 110600 | tf_op jit(solution)/shard_map/ppermute | solution.py:281
  47.8 0.0 collective-permute-done.2.kv_ref
  47.8 3.3 %collective-permute-start.9 = (bf16[144,128]{1,0:T(8,128)(2,1)S(1)}, bf16[144,128]{1,0:T(8,128)(2,1)S(1)}, u32[]{:S(2)}, u32[]{:S(2)}) collective-permute-start(bf16[144,128]{1,0:T(8,128)(2,1)S(1)} %get-tuple-element.54.order), channel_id=1, source_target_pairs={{0,128},{8,136},{16,144},{24,152},{32,160},{40,168},{48,176},{56,1... | collective-permute-start | bytes 110600 | tf_op jit(solution)/shard_map/ppermute | solution.py:281
  51.2 2.3 %shard_map.58 = (f32[4,512,256]{2,1,0:T(8,128)S(1)}, f32[4,512,128]{2,1,0:T(8,128)S(1)}) custom-call(s32[3]{0:T(128)S(1)} %pad_add_fusion.1.place_ref, bf16[512,512]{1,0:T(8,128)(2,1)S(1)} %copy-done.1, bf16[512,256]{1,0:T(8,128)(2,1)S(1)} %collective-permute-done.2.kv_ref, f32[4,512,256]{2,1,0:T(8,128)S(1)} %get-tuple-element.31.acc_in, ...), custom_call_target="tpu_custom_call" | custom-call | flops 536870912 | bytes 4000000 | tf_op jit(solution)/shard_map/pallas_call | solution.py:147
  53.5 0.8 shard_map.59
  54.3 0.0 copy-start.2
  54.3 0.0 copy-start
  54.3 0.7 shard_map.60.acc_ref
  55.0 0.0 collective-permute-done.11.mem3
  55.0 0.0 collective-permute-done.10.mem2
  55.0 1.5 %shard_map.61 = (bf16[256,512]{1,0:T(8,128)(2,1)S(1)}, bf16[256,512]{1,0:T(8,128)(2,1)S(1)}) custom-call(s32[3]{0:T(128)S(1)} %pad_add_fusion.1.place_ref, f32[4]{0:T(128)S(1)} %copy-done.2, bf16[512,512]{1,0:T(8,128)(2,1)S(1)} %copy-done.1, f32[4,512,256]{2,1,0:T(8,128)S(1)} %shard_map.60.acc_ref, f32[144,128]{1,0:T(8,128)S(1)} %get-tuple-element.53.mem0, ...), custom_call_target="tpu_custom_call" | custom-call | flops 402653184 | bytes 4000000 | tf_op jit(solution)/shard_map/pallas_call | solution.py:200
  56.5 1.9 %collective-permute-start.12 = (bf16[256,512]{1,0:T(8,128)(2,1)S(1)}, bf16[256,512]{1,0:T(8,128)(2,1)S(1)}, u32[]{:S(2)}, u32[]{:S(2)}) collective-permute-start(bf16[256,512]{1,0:T(8,128)(2,1)S(1)} %get-tuple-element.42), channel_id=1, source_target_pairs={{0,1},{1,0},{2,3},{3,2},{4,5},{5,4},{6,7},{7,6},{8,9},{9,8},{10,11... | collective-permute-start | bytes 786440 | tf_op jit(solution)/shard_map/ppermute | solution.py:305
  58.4 1.5 %collective-permute-done.12.got_ref = bf16[256,512]{1,0:T(8,128)(2,1)S(1)} collective-permute-done((bf16[256,512]{1,0:T(8,128)(2,1)S(1)}, bf16[256,512]{1,0:T(8,128)(2,1)S(1)}, u32[]{:S(2)}, u32[]{:S(2)}) %collective-permute-start.12) | collective-permute-done | bytes 262176 | tf_op jit(solution)/shard_map/ppermute | solution.py:305
  59.9 1.2 %shard_map.63 = (bf16[64,2048]{1,0:T(8,128)(2,1)S(1)}, bf16[64,2048]{1,0:T(8,128)(2,1)S(1)}, bf16[64,2048]{1,0:T(8,128)(2,1)S(1)}, bf16[64,2048]{1,0:T(8,128)(2,1)S(1)}) custom-call(bf16[256,512]{1,0:T(8,128)(2,1)S(1)} %get-tuple-element.41.keep_ref, bf16[256,512]{1,0:T(8,128)(2,1)S(1)} %collective-permute-done.12.got_ref, bf16[512,4096]{1,0:T(8,128)(2,1)S(1)} %copy-done, ...), custom_call_target="tpu_custom_call" | custom-call | flops 1073741824 | bytes 6000000 | tf_op jit(solution)/shard_map/pallas_call | solution.py:226
  61.2 4.7 %collective-permute-start.16 = (bf16[64,2048]{1,0:T(8,128)(2,1)S(1)}, bf16[64,2048]{1,0:T(8,128)(2,1)S(1)}, u32[]{:S(2)}, u32[]{:S(2)}) collective-permute-start(bf16[64,2048]{1,0:T(8,128)(2,1)S(1)} %get-tuple-element.49), channel_id=1, source_target_pairs={{0,6},{1,7},{2,0},{3,1},{4,2},{5,3},{6,4},{7,5},{8,14},{9,15},{10,... | collective-permute-start | bytes 786440 | tf_op jit(solution)/shard_map/ppermute | solution.py:310
  65.9 1.2 %shard_map.62 = (bf16[64,2048]{1,0:T(8,128)(2,1)S(1)}, bf16[64,2048]{1,0:T(8,128)(2,1)S(1)}, bf16[64,2048]{1,0:T(8,128)(2,1)S(1)}, bf16[64,2048]{1,0:T(8,128)(2,1)S(1)}) custom-call(bf16[256,512]{1,0:T(8,128)(2,1)S(1)} %get-tuple-element.41.keep_ref, bf16[256,512]{1,0:T(8,128)(2,1)S(1)} %collective-permute-done.12.got_ref, bf16[512,4096]{1,0:T(8,128)(2,1)S(1)} %copy-done, ...), custom_call_target="tpu_custom_call" | custom-call | flops 1073741824 | bytes 6000000 | tf_op jit(solution)/shard_map/pallas_call | solution.py:226
  67.1 1.9 %collective-permute-start.14 = (bf16[64,2048]{1,0:T(8,128)(2,1)S(1)}, bf16[64,2048]{1,0:T(8,128)(2,1)S(1)}, u32[]{:S(2)}, u32[]{:S(2)}) collective-permute-start(bf16[64,2048]{1,0:T(8,128)(2,1)S(1)} %get-tuple-element.46), channel_id=1, source_target_pairs={{0,2},{1,3},{2,4},{3,5},{4,6},{5,7},{6,0},{7,1},{8,10},{9,11},{10,... | collective-permute-start | bytes 786440 | tf_op jit(solution)/shard_map/ppermute | solution.py:307
  69.0 2.7 %collective-permute-start.18 = (bf16[64,2048]{1,0:T(8,128)(2,1)S(1)}, bf16[64,2048]{1,0:T(8,128)(2,1)S(1)}, u32[]{:S(2)}, u32[]{:S(2)}) collective-permute-start(bf16[64,2048]{1,0:T(8,128)(2,1)S(1)} %get-tuple-element.50), channel_id=1, source_target_pairs={{0,2},{1,3},{2,4},{3,5},{4,6},{5,7},{6,0},{7,1},{8,10},{9,11},{10,... | collective-permute-start | bytes 786440 | tf_op jit(solution)/shard_map/ppermute | solution.py:311
  71.7 4.4 %collective-permute-start.13 = (bf16[64,2048]{1,0:T(8,128)(2,1)S(1)}, bf16[64,2048]{1,0:T(8,128)(2,1)S(1)}, u32[]{:S(2)}, u32[]{:S(2)}) collective-permute-start(bf16[64,2048]{1,0:T(8,128)(2,1)S(1)} %get-tuple-element.44), channel_id=1, source_target_pairs={{0,6},{1,7},{2,0},{3,1},{4,2},{5,3},{6,4},{7,5},{8,14},{9,15},{10,... | collective-permute-start | bytes 786440 | tf_op jit(solution)/shard_map/ppermute | solution.py:308
  76.1 0.1 add.58
  76.2 3.9 %collective-permute-start.17 = (bf16[64,2048]{1,0:T(8,128)(2,1)S(1)}, bf16[64,2048]{1,0:T(8,128)(2,1)S(1)}, u32[]{:S(2)}, u32[]{:S(2)}) collective-permute-start(bf16[64,2048]{1,0:T(8,128)(2,1)S(1)} %add.58), channel_id=1, source_target_pairs={{0,6},{1,7},{2,0},{3,1},{4,2},{5,3},{6,4},{7,5},{8,14},{9,15},{10,... | collective-permute-start | bytes 786440 | tf_op jit(solution)/shard_map/ppermute | solution.py:313
  80.1 0.1 add.57
  80.2 1.9 %collective-permute-start.15 = (bf16[64,2048]{1,0:T(8,128)(2,1)S(1)}, bf16[64,2048]{1,0:T(8,128)(2,1)S(1)}, u32[]{:S(2)}, u32[]{:S(2)}) collective-permute-start(bf16[64,2048]{1,0:T(8,128)(2,1)S(1)} %add.57), channel_id=1, source_target_pairs={{0,2},{1,3},{2,4},{3,5},{4,6},{5,7},{6,0},{7,1},{8,10},{9,11},{10,... | collective-permute-start | bytes 786440 | tf_op jit(solution)/shard_map/ppermute | solution.py:312
  82.1 1.8 %collective-permute-done.18.right_b = bf16[64,2048]{1,0:T(8,128)(2,1)S(1)} collective-permute-done((bf16[64,2048]{1,0:T(8,128)(2,1)S(1)}, bf16[64,2048]{1,0:T(8,128)(2,1)S(1)}, u32[]{:S(2)}, u32[]{:S(2)}) %collective-permute-start.18) | collective-permute-done | bytes 262176 | tf_op jit(solution)/shard_map/ppermute | solution.py:311
  83.9 3.1 %collective-permute-done.17.left_b = bf16[64,2048]{1,0:T(8,128)(2,1)S(1)} collective-permute-done((bf16[64,2048]{1,0:T(8,128)(2,1)S(1)}, bf16[64,2048]{1,0:T(8,128)(2,1)S(1)}, u32[]{:S(2)}, u32[]{:S(2)}) %collective-permute-start.17) | collective-permute-done | bytes 262176 | tf_op jit(solution)/shard_map/ppermute | solution.py:313
  87.0 3.2 %collective-permute-done.15.right_a = bf16[64,2048]{1,0:T(8,128)(2,1)S(1)} collective-permute-done((bf16[64,2048]{1,0:T(8,128)(2,1)S(1)}, bf16[64,2048]{1,0:T(8,128)(2,1)S(1)}, u32[]{:S(2)}, u32[]{:S(2)}) %collective-permute-start.15) | collective-permute-done | bytes 262176 | tf_op jit(solution)/shard_map/ppermute | solution.py:312
  90.3 1.0 %shard_map.64 = bf16[64,4096]{1,0:T(8,128)(2,1)} custom-call(bf16[64,2048]{1,0:T(8,128)(2,1)S(1)} %get-tuple-element.43.own_a, bf16[64,2048]{1,0:T(8,128)(2,1)S(1)} %collective-permute-done.13.left_a, bf16[64,2048]{1,0:T(8,128)(2,1)S(1)} %collective-permute-done.15.right_a, bf16[64,2048]{1,0:T(8,128)(2,1)S(1)} %get-tuple-element.47.own_b, ...), custom_call_target="tpu_custom_call" | custom-call | flops 786432 | bytes 2000000 | tf_op jit(solution)/shard_map/pallas_call | solution.py:244
  (13 shorter events, 0.1 us)
Async XLA Ops:
  0.0 28.9 %collective-permute-start.7 = (bf16[512,4096]{1,0:T(8,128)(2,1)}, bf16[512,4096]{1,0:T(8,128)(2,1)}, u32[]{:S(2)}, u32[]{:S(2)}) collective-permute-start(bf16[512,4096]{1,0:T(8,128)(2,1)} %w_own_ref.3), channel_id=1, source_target_pairs={{0,1},{1,0},{2,3},{3,2},{4,5},{5,4},{6,7},{7,6},{8,9},{9,8},{10,11... | collective-permute-start | bytes 12582920 | tf_op jit(solution)/shard_map/ppermute | solution.py:284
  3.2 14.8 %collective-permute-start.3 = (bf16[144,128]{1,0:T(8,128)(2,1)S(1)}, bf16[144,128]{1,0:T(8,128)(2,1)S(1)}, u32[]{:S(2)}, u32[]{:S(2)}) collective-permute-start(bf16[144,128]{1,0:T(8,128)(2,1)S(1)} %get-tuple-element.29), channel_id=1, source_target_pairs={{0,8},{8,0},{16,24},{24,16},{32,40},{40,32},{48,56},{56,48},{64,72... | collective-permute-start | bytes 110600 | tf_op jit(solution)/shard_map/ppermute | solution.py:281
  10.2 10.6 %collective-permute-start.4 = (bf16[144,128]{1,0:T(8,128)(2,1)S(1)}, bf16[144,128]{1,0:T(8,128)(2,1)S(1)}, u32[]{:S(2)}, u32[]{:S(2)}) collective-permute-start(bf16[144,128]{1,0:T(8,128)(2,1)S(1)} %get-tuple-element.29), channel_id=1, source_target_pairs={{0,16},{8,24},{16,0},{24,8},{32,48},{40,56},{48,32},{56,40},{64,80... | collective-permute-start | bytes 110600 | tf_op jit(solution)/shard_map/ppermute | solution.py:281
  12.1 9.4 %collective-permute-start.5 = (bf16[144,128]{1,0:T(8,128)(2,1)S(1)}, bf16[144,128]{1,0:T(8,128)(2,1)S(1)}, u32[]{:S(2)}, u32[]{:S(2)}) collective-permute-start(bf16[144,128]{1,0:T(8,128)(2,1)S(1)} %get-tuple-element.29), channel_id=1, source_target_pairs={{0,24},{8,16},{16,8},{24,0},{32,56},{40,48},{48,40},{56,32},{64,88... | collective-permute-start | bytes 110600 | tf_op jit(solution)/shard_map/ppermute | solution.py:281
  15.5 32.3 %collective-permute-start.2 = (bf16[512,256]{1,0:T(8,128)(2,1)S(1)}, bf16[512,256]{1,0:T(8,128)(2,1)S(1)}, u32[]{:S(2)}, u32[]{:S(2)}) collective-permute-start(bf16[512,256]{1,0:T(8,128)(2,1)S(1)} %pad_add_fusion.kv_ref), channel_id=1, source_target_pairs={{0,8},{8,16},{16,24},{32,40},{40,48},{48,56},{64,72},{72,80},{80,8... | collective-permute-start | bytes 786440 | tf_op jit(solution)/shard_map/ppermute | solution.py:281
  18.0 35.5 %collective-permute-start.1 = (bf16[512,256]{1,0:T(8,128)(2,1)S(1)}, bf16[512,256]{1,0:T(8,128)(2,1)S(1)}, u32[]{:S(2)}, u32[]{:S(2)}) collective-permute-start(bf16[512,256]{1,0:T(8,128)(2,1)S(1)} %pad_add_fusion.kv_ref), channel_id=1, source_target_pairs={{0,16},{8,24},{32,48},{40,56},{64,80},{72,88},{96,112},{104,120},{... | collective-permute-start | bytes 786440 | tf_op jit(solution)/shard_map/ppermute | solution.py:281
  20.8 33.4 %collective-permute-start = (bf16[512,256]{1,0:T(8,128)(2,1)S(1)}, bf16[512,256]{1,0:T(8,128)(2,1)S(1)}, u32[]{:S(2)}, u32[]{:S(2)}) collective-permute-start(bf16[512,256]{1,0:T(8,128)(2,1)S(1)} %pad_add_fusion.kv_ref), channel_id=1, source_target_pairs={{0,24},{32,56},{64,88},{96,120},{128,152},{160,184},{192,216},{224... | collective-permute-start | bytes 786440 | tf_op jit(solution)/shard_map/ppermute | solution.py:281
  21.5 12.0 %collective-permute-start.6 = (bf16[144,128]{1,0:T(8,128)(2,1)S(1)}, bf16[144,128]{1,0:T(8,128)(2,1)S(1)}, u32[]{:S(2)}, u32[]{:S(2)}) collective-permute-start(bf16[144,128]{1,0:T(8,128)(2,1)S(1)} %get-tuple-element.51), channel_id=1, source_target_pairs={{0,40},{8,48},{16,56},{24,32},{32,8},{40,16},{48,24},{56,0},{64,10... | collective-permute-start | bytes 110600 | tf_op jit(solution)/shard_map/ppermute | solution.py:281
  28.9 8.1 %copy-start.1 = (bf16[512,512]{1,0:T(8,128)(2,1)S(1)}, bf16[512,512]{1,0:T(8,128)(2,1)}, u32[]{:S(2)}) copy-start(bf16[512,512]{1,0:T(8,128)(2,1)} %q_ref.9) | copy-start | bytes 1572868
  33.5 5.9 %collective-permute-start.8 = (bf16[144,128]{1,0:T(8,128)(2,1)S(1)}, bf16[144,128]{1,0:T(8,128)(2,1)S(1)}, u32[]{:S(2)}, u32[]{:S(2)}) collective-permute-start(bf16[144,128]{1,0:T(8,128)(2,1)S(1)} %fusion.2.order), channel_id=1, source_target_pairs={{0,64},{8,72},{16,80},{24,88},{32,96},{40,104},{48,112},{56,120},{... | collective-permute-start | bytes 110600 | tf_op jit(solution)/shard_map/ppermute | solution.py:281
  39.4 15.6 %collective-permute-start.11 = (bf16[144,128]{1,0:T(8,128)(2,1)S(1)}, bf16[144,128]{1,0:T(8,128)(2,1)S(1)}, u32[]{:S(2)}, u32[]{:S(2)}) collective-permute-start(bf16[144,128]{1,0:T(8,128)(2,1)S(1)} %get-tuple-element.54.order), channel_id=1, source_target_pairs={{0,384},{8,392},{16,400},{24,408},{32,416},{40,424},{48,432},{56,4... | collective-permute-start | bytes 110600 | tf_op jit(solution)/shard_map/ppermute | solution.py:281
  45.6 9.4 %collective-permute-start.10 = (bf16[144,128]{1,0:T(8,128)(2,1)S(1)}, bf16[144,128]{1,0:T(8,128)(2,1)S(1)}, u32[]{:S(2)}, u32[]{:S(2)}) collective-permute-start(bf16[144,128]{1,0:T(8,128)(2,1)S(1)} %get-tuple-element.54.order), channel_id=1, source_target_pairs={{0,256},{8,264},{16,272},{24,280},{32,288},{40,296},{48,304},{56,3... | collective-permute-start | bytes 110600 | tf_op jit(solution)/shard_map/ppermute | solution.py:281
  47.8 7.2 %collective-permute-start.9 = (bf16[144,128]{1,0:T(8,128)(2,1)S(1)}, bf16[144,128]{1,0:T(8,128)(2,1)S(1)}, u32[]{:S(2)}, u32[]{:S(2)}) collective-permute-start(bf16[144,128]{1,0:T(8,128)(2,1)S(1)} %get-tuple-element.54.order), channel_id=1, source_target_pairs={{0,128},{8,136},{16,144},{24,152},{32,160},{40,168},{48,176},{56,1... | collective-permute-start | bytes 110600 | tf_op jit(solution)/shard_map/ppermute | solution.py:281
  54.3 0.8 copy-start.2
  54.3 5.7 %copy-start = (bf16[512,4096]{1,0:T(8,128)(2,1)S(1)}, bf16[512,4096]{1,0:T(8,128)(2,1)}, u32[]{:S(2)}) copy-start(bf16[512,4096]{1,0:T(8,128)(2,1)} %w_own_ref.3) | copy-start | bytes 12582916
  56.5 3.4 %collective-permute-start.12 = (bf16[256,512]{1,0:T(8,128)(2,1)S(1)}, bf16[256,512]{1,0:T(8,128)(2,1)S(1)}, u32[]{:S(2)}, u32[]{:S(2)}) collective-permute-start(bf16[256,512]{1,0:T(8,128)(2,1)S(1)} %get-tuple-element.42), channel_id=1, source_target_pairs={{0,1},{1,0},{2,3},{3,2},{4,5},{5,4},{6,7},{7,6},{8,9},{9,8},{10,11... | collective-permute-start | bytes 786440 | tf_op jit(solution)/shard_map/ppermute | solution.py:305
  61.2 14.9 %collective-permute-start.16 = (bf16[64,2048]{1,0:T(8,128)(2,1)S(1)}, bf16[64,2048]{1,0:T(8,128)(2,1)S(1)}, u32[]{:S(2)}, u32[]{:S(2)}) collective-permute-start(bf16[64,2048]{1,0:T(8,128)(2,1)S(1)} %get-tuple-element.49), channel_id=1, source_target_pairs={{0,6},{1,7},{2,0},{3,1},{4,2},{5,3},{6,4},{7,5},{8,14},{9,15},{10,... | collective-permute-start | bytes 786440 | tf_op jit(solution)/shard_map/ppermute | solution.py:310
  67.1 13.0 %collective-permute-start.14 = (bf16[64,2048]{1,0:T(8,128)(2,1)S(1)}, bf16[64,2048]{1,0:T(8,128)(2,1)S(1)}, u32[]{:S(2)}, u32[]{:S(2)}) collective-permute-start(bf16[64,2048]{1,0:T(8,128)(2,1)S(1)} %get-tuple-element.46), channel_id=1, source_target_pairs={{0,2},{1,3},{2,4},{3,5},{4,6},{5,7},{6,0},{7,1},{8,10},{9,11},{10,... | collective-permute-start | bytes 786440 | tf_op jit(solution)/shard_map/ppermute | solution.py:307
  69.0 14.9 %collective-permute-start.18 = (bf16[64,2048]{1,0:T(8,128)(2,1)S(1)}, bf16[64,2048]{1,0:T(8,128)(2,1)S(1)}, u32[]{:S(2)}, u32[]{:S(2)}) collective-permute-start(bf16[64,2048]{1,0:T(8,128)(2,1)S(1)} %get-tuple-element.50), channel_id=1, source_target_pairs={{0,2},{1,3},{2,4},{3,5},{4,6},{5,7},{6,0},{7,1},{8,10},{9,11},{10,... | collective-permute-start | bytes 786440 | tf_op jit(solution)/shard_map/ppermute | solution.py:311
  71.7 12.2 %collective-permute-start.13 = (bf16[64,2048]{1,0:T(8,128)(2,1)S(1)}, bf16[64,2048]{1,0:T(8,128)(2,1)S(1)}, u32[]{:S(2)}, u32[]{:S(2)}) collective-permute-start(bf16[64,2048]{1,0:T(8,128)(2,1)S(1)} %get-tuple-element.44), channel_id=1, source_target_pairs={{0,6},{1,7},{2,0},{3,1},{4,2},{5,3},{6,4},{7,5},{8,14},{9,15},{10,... | collective-permute-start | bytes 786440 | tf_op jit(solution)/shard_map/ppermute | solution.py:308
  76.2 10.8 %collective-permute-start.17 = (bf16[64,2048]{1,0:T(8,128)(2,1)S(1)}, bf16[64,2048]{1,0:T(8,128)(2,1)S(1)}, u32[]{:S(2)}, u32[]{:S(2)}) collective-permute-start(bf16[64,2048]{1,0:T(8,128)(2,1)S(1)} %add.58), channel_id=1, source_target_pairs={{0,6},{1,7},{2,0},{3,1},{4,2},{5,3},{6,4},{7,5},{8,14},{9,15},{10,... | collective-permute-start | bytes 786440 | tf_op jit(solution)/shard_map/ppermute | solution.py:313
  80.2 10.1 %collective-permute-start.15 = (bf16[64,2048]{1,0:T(8,128)(2,1)S(1)}, bf16[64,2048]{1,0:T(8,128)(2,1)S(1)}, u32[]{:S(2)}, u32[]{:S(2)}) collective-permute-start(bf16[64,2048]{1,0:T(8,128)(2,1)S(1)} %add.57), channel_id=1, source_target_pairs={{0,2},{1,3},{2,4},{3,5},{4,6},{5,7},{6,0},{7,1},{8,10},{9,11},{10,... | collective-permute-start | bytes 786440 | tf_op jit(solution)/shard_map/ppermute | solution.py:312

commit v9 on v8

--- a/solution.py
+++ b/solution.py
@@ -293,11 +293,11 @@
     sent = line.astype(BF16)
     got = send(sent, swap(8, N_CTX))
     acc, top = own_call(queries, kv, sent)
+    acc, top = step_call(1, place, queries, kv1, acc, top, sent)
     got = after(got, acc).astype(F32)
     start = start + jnp.where(ctx // 8 % 2 == 1, got, 0.0)
     sent = (line + got).astype(BF16)
-    pairs = [send(sent, along_y(2 * k)) for k in (1, 2, 3)]
-    acc, top = step_call(1, place, queries, kv1, acc, top, sent)
+    pairs = [send(sent, along_y(2 * k)) for k in (3, 2, 1)]
     acc, top = step_call(2, place, queries, kv2, acc, top, sent)
     (acc,) = step_call(3, place, queries, kv3, acc, top, sent)
     pairs = [after(part, acc) for part in pairs]

time: 91.8 us -> 90.9 us (level)
  the two profiles are of different devices: /device:TPU:64 before, /device:TPU:120 now
where the time goes in v9:
time: 90.9 us; the launch traced here: 90.3 us
  starting transfers between devices  55.9 us (61%)
  waiting for transfers between devices  20.1 us (22%)
  Pallas kernels  12.6 us (14%)
  other arithmetic  1.28 us (1%)
    ppermute x11, starting transfers between devices, on_device(): send = lambda x, route: lax.ppermute(x.astype(BF16), 'ctx', route)  32.6 us
    ppermute x11, waiting for transfers between devices, on_device(): send = lambda x, route: lax.ppermute(x.astype(BF16), 'ctx', route)  10.4 us
    ppermute x1, starting transfers between devices, on_device(): far_b = lax.ppermute(far_b, 'tp', turned(-1))  4.67 us
    ppermute x1, starting transfers between devices, on_device(): left_a = lax.ppermute(left_a, 'tp', turned(-1))  4.4 us
    ppermute x1, starting transfers between devices, on_device(): left_b = lax.ppermute(left_b + far_b, 'tp', turned(-1))  3.92 us
    pallas_call x3, Pallas kernels, step_call(): call(functools.partial(step_kernel, distance), kept, (GROUP * ROWS * ROWS...  3.75 us
    ppermute x1, waiting for transfers between devices, on_device(): right_a = lax.ppermute(right_a + far_a, 'tp', turned(1))  3.25 us
    ppermute x1, waiting for transfers between devices, on_device(): left_b = lax.ppermute(left_b + far_b, 'tp', turned(-1))  3.11 us
  transfers between devices with their start and end apart: 19, of which 8 were waited for; matrix products, arithmetic and copies ran while one was open for 1% of the time, Pallas kernels for 10%

profile of v9, /device:TPU:120, one launch (start us, length us, event | category | flops | bytes accessed | tf_op | source)
XLA Modules:
  0.0 90.3 jit_solution(15549088680025917313)
XLA Ops:
  0.0 1.9 %collective-permute-start.7 = (bf16[512,4096]{1,0:T(8,128)(2,1)}, bf16[512,4096]{1,0:T(8,128)(2,1)}, u32[]{:S(2)}, u32[]{:S(2)}) collective-permute-start(bf16[512,4096]{1,0:T(8,128)(2,1)} %w_own_ref.3), channel_id=1, source_target_pairs={{0,1},{1,0},{2,3},{3,2},{4,5},{5,4},{6,7},{7,6},{8,9},{9,8},{10,11... | collective-permute-start | bytes 12582920 | tf_op jit(solution)/shard_map/ppermute | solution.py:284
  1.9 1.0 %pad_add_fusion.kv_ref = bf16[512,256]{1,0:T(8,128)(2,1)S(1)} fusion(bf16[512,128]{1,0:T(8,128)(2,1)} %param.7, bf16[512,128]{1,0:T(8,128)(2,1)} %param.6), kind=kLoop, calls=%fused_computation | loop fusion | flops 524288 | bytes 524288 | tf_op jit(solution)/shard_map/add | solution.py:282
  2.9 0.3 shard_map.55
  3.2 1.9 %collective-permute-start.3 = (bf16[144,128]{1,0:T(8,128)(2,1)S(1)}, bf16[144,128]{1,0:T(8,128)(2,1)S(1)}, u32[]{:S(2)}, u32[]{:S(2)}) collective-permute-start(bf16[144,128]{1,0:T(8,128)(2,1)S(1)} %get-tuple-element.29), channel_id=1, source_target_pairs={{0,8},{8,0},{16,24},{24,16},{32,40},{40,32},{48,56},{56,48},{64,72... | collective-permute-start | bytes 110600 | tf_op jit(solution)/shard_map/ppermute | solution.py:281
  5.2 6.1 %collective-permute-start.4 = (bf16[144,128]{1,0:T(8,128)(2,1)S(1)}, bf16[144,128]{1,0:T(8,128)(2,1)S(1)}, u32[]{:S(2)}, u32[]{:S(2)}) collective-permute-start(bf16[144,128]{1,0:T(8,128)(2,1)S(1)} %get-tuple-element.29), channel_id=1, source_target_pairs={{0,16},{8,24},{16,0},{24,8},{32,48},{40,56},{48,32},{56,40},{64,80... | collective-permute-start | bytes 110600 | tf_op jit(solution)/shard_map/ppermute | solution.py:281
  11.2 2.5 %collective-permute-start.5 = (bf16[144,128]{1,0:T(8,128)(2,1)S(1)}, bf16[144,128]{1,0:T(8,128)(2,1)S(1)}, u32[]{:S(2)}, u32[]{:S(2)}) collective-permute-start(bf16[144,128]{1,0:T(8,128)(2,1)S(1)} %get-tuple-element.29), channel_id=1, source_target_pairs={{0,24},{8,16},{16,8},{24,0},{32,56},{40,48},{48,40},{56,32},{64,88... | collective-permute-start | bytes 110600 | tf_op jit(solution)/shard_map/ppermute | solution.py:281
  13.7 3.4 %collective-permute-start.2 = (bf16[512,256]{1,0:T(8,128)(2,1)S(1)}, bf16[512,256]{1,0:T(8,128)(2,1)S(1)}, u32[]{:S(2)}, u32[]{:S(2)}) collective-permute-start(bf16[512,256]{1,0:T(8,128)(2,1)S(1)} %pad_add_fusion.kv_ref), channel_id=1, source_target_pairs={{0,8},{8,16},{16,24},{32,40},{40,48},{48,56},{64,72},{72,80},{80,8... | collective-permute-start | bytes 786440 | tf_op jit(solution)/shard_map/ppermute | solution.py:281
  17.1 3.7 %collective-permute-start.1 = (bf16[512,256]{1,0:T(8,128)(2,1)S(1)}, bf16[512,256]{1,0:T(8,128)(2,1)S(1)}, u32[]{:S(2)}, u32[]{:S(2)}) collective-permute-start(bf16[512,256]{1,0:T(8,128)(2,1)S(1)} %pad_add_fusion.kv_ref), channel_id=1, source_target_pairs={{0,16},{8,24},{32,48},{40,56},{64,80},{72,88},{96,112},{104,120},{... | collective-permute-start | bytes 786440 | tf_op jit(solution)/shard_map/ppermute | solution.py:281
  20.8 0.7 collective-permute-start
  21.5 0.0 collective-permute-done.5
  21.5 7.3 %collective-permute-start.6 = (bf16[144,128]{1,0:T(8,128)(2,1)S(1)}, bf16[144,128]{1,0:T(8,128)(2,1)S(1)}, u32[]{:S(2)}, u32[]{:S(2)}) collective-permute-start(bf16[144,128]{1,0:T(8,128)(2,1)S(1)} %get-tuple-element.51), channel_id=1, source_target_pairs={{0,40},{8,48},{16,56},{24,32},{32,8},{40,16},{48,24},{56,0},{64,10... | collective-permute-start | bytes 110600 | tf_op jit(solution)/shard_map/ppermute | solution.py:281
  28.9 0.1 pad_add_fusion.1.place_ref
  28.9 0.0 collective-permute-done.7.w_hbm
  28.9 2.3 %shard_map.56.w_other_ref = bf16[512,4096]{1,0:T(8,128)(2,1)S(1)} custom-call(bf16[512,4096]{1,0:T(8,128)(2,1)} %collective-permute-done.7.w_hbm), custom_call_target="tpu_custom_call" | custom-call | bytes 8000000 | tf_op jit(solution)/shard_map/pallas_call | solution.py:163
  31.2 2.3 %collective-permute-done.6 = bf16[144,128]{1,0:T(8,128)(2,1)S(1)} collective-permute-done((bf16[144,128]{1,0:T(8,128)(2,1)S(1)}, bf16[144,128]{1,0:T(8,128)(2,1)S(1)}, u32[]{:S(2)}, u32[]{:S(2)}) %collective-permute-start.6) | collective-permute-done | bytes 36896 | tf_op jit(solution)/shard_map/ppermute | solution.py:281
  33.5 3.3 %collective-permute-start.8 = (bf16[144,128]{1,0:T(8,128)(2,1)S(1)}, bf16[144,128]{1,0:T(8,128)(2,1)S(1)}, u32[]{:S(2)}, u32[]{:S(2)}) collective-permute-start(bf16[144,128]{1,0:T(8,128)(2,1)S(1)} %fusion.2.order), channel_id=1, source_target_pairs={{0,64},{8,72},{16,80},{24,88},{32,96},{40,104},{48,112},{56,120},{... | collective-permute-start | bytes 110600 | tf_op jit(solution)/shard_map/ppermute | solution.py:281
  36.8 1.4 %shard_map.57 = (f32[4,512,256]{2,1,0:T(8,128)S(1)}, f32[4,512,128]{2,1,0:T(8,128)S(1)}) custom-call(bf16[512,512]{1,0:T(8,128)(2,1)S(1)} %copy-done.1, bf16[512,256]{1,0:T(8,128)(2,1)S(1)} %pad_add_fusion.kv_ref, bf16[144,128]{1,0:T(8,128)(2,1)S(1)} %fusion.2.order), custom_call_target="tpu_custom_call" | custom-call | flops 536870912 | bytes 4000000 | tf_op jit(solution)/shard_map/pallas_call | solution.py:101
  38.2 0.0 collective-permute-done.2.kv_ref
  38.2 2.3 %shard_map.58 = (f32[4,512,256]{2,1,0:T(8,128)S(1)}, f32[4,512,128]{2,1,0:T(8,128)S(1)}) custom-call(s32[3]{0:T(128)S(1)} %pad_add_fusion.1.place_ref, bf16[512,512]{1,0:T(8,128)(2,1)S(1)} %copy-done.1, bf16[512,256]{1,0:T(8,128)(2,1)S(1)} %collective-permute-done.2.kv_ref, f32[4,512,256]{2,1,0:T(8,128)S(1)} %get-tuple-element.31.acc_in, ...), custom_call_target="tpu_custom_call" | custom-call | flops 536870912 | bytes 4000000 | tf_op jit(solution)/shard_map/pallas_call | solution.py:147
  40.5 0.0 collective-permute-done.8
  40.6 1.3 %collective-permute-start.11 = (bf16[144,128]{1,0:T(8,128)(2,1)S(1)}, bf16[144,128]{1,0:T(8,128)(2,1)S(1)}, u32[]{:S(2)}, u32[]{:S(2)}) collective-permute-start(bf16[144,128]{1,0:T(8,128)(2,1)S(1)} %get-tuple-element.54.order), channel_id=1, source_target_pairs={{0,128},{8,136},{16,144},{24,152},{32,160},{40,168},{48,176},{56,1... | collective-permute-start | bytes 110600 | tf_op jit(solution)/shard_map/ppermute | solution.py:281
  41.9 1.3 %collective-permute-start.10 = (bf16[144,128]{1,0:T(8,128)(2,1)S(1)}, bf16[144,128]{1,0:T(8,128)(2,1)S(1)}, u32[]{:S(2)}, u32[]{:S(2)}) collective-permute-start(bf16[144,128]{1,0:T(8,128)(2,1)S(1)} %get-tuple-element.54.order), channel_id=1, source_target_pairs={{0,256},{8,264},{16,272},{24,280},{32,288},{40,296},{48,304},{56,3... | collective-permute-start | bytes 110600 | tf_op jit(solution)/shard_map/ppermute | solution.py:281
  43.2 1.3 %collective-permute-start.9 = (bf16[144,128]{1,0:T(8,128)(2,1)S(1)}, bf16[144,128]{1,0:T(8,128)(2,1)S(1)}, u32[]{:S(2)}, u32[]{:S(2)}) collective-permute-start(bf16[144,128]{1,0:T(8,128)(2,1)S(1)} %get-tuple-element.54.order), channel_id=1, source_target_pairs={{0,384},{8,392},{16,400},{24,408},{32,416},{40,424},{48,432},{56,4... | collective-permute-start | bytes 110600 | tf_op jit(solution)/shard_map/ppermute | solution.py:281
  44.5 0.0 collective-permute-done.1.kv_ref
  44.5 0.8 shard_map.59
  45.3 0.0 copy-start.2
  45.3 0.0 copy-start
  45.3 0.7 shard_map.60.acc_ref
  46.0 1.7 %collective-permute-done.11.mem3 = bf16[144,128]{1,0:T(8,128)(2,1)S(1)} collective-permute-done((bf16[144,128]{1,0:T(8,128)(2,1)S(1)}, bf16[144,128]{1,0:T(8,128)(2,1)S(1)}, u32[]{:S(2)}, u32[]{:S(2)}) %collective-permute-start.11) | collective-permute-done | bytes 36896 | tf_op jit(solution)/shard_map/ppermute | solution.py:281
  47.7 4.0 %collective-permute-done.10.mem2 = bf16[144,128]{1,0:T(8,128)(2,1)S(1)} collective-permute-done((bf16[144,128]{1,0:T(8,128)(2,1)S(1)}, bf16[144,128]{1,0:T(8,128)(2,1)S(1)}, u32[]{:S(2)}, u32[]{:S(2)}) %collective-permute-start.10) | collective-permute-done | bytes 36896 | tf_op jit(solution)/shard_map/ppermute | solution.py:281
  51.7 2.4 %collective-permute-done.9.mem1 = bf16[144,128]{1,0:T(8,128)(2,1)S(1)} collective-permute-done((bf16[144,128]{1,0:T(8,128)(2,1)S(1)}, bf16[144,128]{1,0:T(8,128)(2,1)S(1)}, u32[]{:S(2)}, u32[]{:S(2)}) %collective-permute-start.9) | collective-permute-done | bytes 36896 | tf_op jit(solution)/shard_map/ppermute | solution.py:281
  54.1 1.5 %shard_map.61 = (bf16[256,512]{1,0:T(8,128)(2,1)S(1)}, bf16[256,512]{1,0:T(8,128)(2,1)S(1)}) custom-call(s32[3]{0:T(128)S(1)} %pad_add_fusion.1.place_ref, f32[4]{0:T(128)S(1)} %copy-done.2, bf16[512,512]{1,0:T(8,128)(2,1)S(1)} %copy-done.1, f32[4,512,256]{2,1,0:T(8,128)S(1)} %shard_map.60.acc_ref, f32[144,128]{1,0:T(8,128)S(1)} %get-tuple-element.53.mem0, ...), custom_call_target="tpu_custom_call" | custom-call | flops 402653184 | bytes 4000000 | tf_op jit(solution)/shard_map/pallas_call | solution.py:200
  55.6 1.9 %collective-permute-start.12 = (bf16[256,512]{1,0:T(8,128)(2,1)S(1)}, bf16[256,512]{1,0:T(8,128)(2,1)S(1)}, u32[]{:S(2)}, u32[]{:S(2)}) collective-permute-start(bf16[256,512]{1,0:T(8,128)(2,1)S(1)} %get-tuple-element.42), channel_id=1, source_target_pairs={{0,1},{1,0},{2,3},{3,2},{4,5},{5,4},{6,7},{7,6},{8,9},{9,8},{10,11... | collective-permute-start | bytes 786440 | tf_op jit(solution)/shard_map/ppermute | solution.py:305
  57.5 1.5 %collective-permute-done.12.got_ref = bf16[256,512]{1,0:T(8,128)(2,1)S(1)} collective-permute-done((bf16[256,512]{1,0:T(8,128)(2,1)S(1)}, bf16[256,512]{1,0:T(8,128)(2,1)S(1)}, u32[]{:S(2)}, u32[]{:S(2)}) %collective-permute-start.12) | collective-permute-done | bytes 262176 | tf_op jit(solution)/shard_map/ppermute | solution.py:305
  59.0 1.2 %shard_map.63 = (bf16[64,2048]{1,0:T(8,128)(2,1)S(1)}, bf16[64,2048]{1,0:T(8,128)(2,1)S(1)}, bf16[64,2048]{1,0:T(8,128)(2,1)S(1)}, bf16[64,2048]{1,0:T(8,128)(2,1)S(1)}) custom-call(bf16[256,512]{1,0:T(8,128)(2,1)S(1)} %get-tuple-element.41.keep_ref, bf16[256,512]{1,0:T(8,128)(2,1)S(1)} %collective-permute-done.12.got_ref, bf16[512,4096]{1,0:T(8,128)(2,1)S(1)} %copy-done, ...), custom_call_target="tpu_custom_call" | custom-call | flops 1073741824 | bytes 6000000 | tf_op jit(solution)/shard_map/pallas_call | solution.py:226
  60.3 4.7 %collective-permute-start.16 = (bf16[64,2048]{1,0:T(8,128)(2,1)S(1)}, bf16[64,2048]{1,0:T(8,128)(2,1)S(1)}, u32[]{:S(2)}, u32[]{:S(2)}) collective-permute-start(bf16[64,2048]{1,0:T(8,128)(2,1)S(1)} %get-tuple-element.49), channel_id=1, source_target_pairs={{0,6},{1,7},{2,0},{3,1},{4,2},{5,3},{6,4},{7,5},{8,14},{9,15},{10,... | collective-permute-start | bytes 786440 | tf_op jit(solution)/shard_map/ppermute | solution.py:310
  65.0 1.2 %shard_map.62 = (bf16[64,2048]{1,0:T(8,128)(2,1)S(1)}, bf16[64,2048]{1,0:T(8,128)(2,1)S(1)}, bf16[64,2048]{1,0:T(8,128)(2,1)S(1)}, bf16[64,2048]{1,0:T(8,128)(2,1)S(1)}) custom-call(bf16[256,512]{1,0:T(8,128)(2,1)S(1)} %get-tuple-element.41.keep_ref, bf16[256,512]{1,0:T(8,128)(2,1)S(1)} %collective-permute-done.12.got_ref, bf16[512,4096]{1,0:T(8,128)(2,1)S(1)} %copy-done, ...), custom_call_target="tpu_custom_call" | custom-call | flops 1073741824 | bytes 6000000 | tf_op jit(solution)/shard_map/pallas_call | solution.py:226
  66.2 1.9 %collective-permute-start.14 = (bf16[64,2048]{1,0:T(8,128)(2,1)S(1)}, bf16[64,2048]{1,0:T(8,128)(2,1)S(1)}, u32[]{:S(2)}, u32[]{:S(2)}) collective-permute-start(bf16[64,2048]{1,0:T(8,128)(2,1)S(1)} %get-tuple-element.46), channel_id=1, source_target_pairs={{0,2},{1,3},{2,4},{3,5},{4,6},{5,7},{6,0},{7,1},{8,10},{9,11},{10,... | collective-permute-start | bytes 786440 | tf_op jit(solution)/shard_map/ppermute | solution.py:307
  68.1 2.7 %collective-permute-start.18 = (bf16[64,2048]{1,0:T(8,128)(2,1)S(1)}, bf16[64,2048]{1,0:T(8,128)(2,1)S(1)}, u32[]{:S(2)}, u32[]{:S(2)}) collective-permute-start(bf16[64,2048]{1,0:T(8,128)(2,1)S(1)} %get-tuple-element.50), channel_id=1, source_target_pairs={{0,2},{1,3},{2,4},{3,5},{4,6},{5,7},{6,0},{7,1},{8,10},{9,11},{10,... | collective-permute-start | bytes 786440 | tf_op jit(solution)/shard_map/ppermute | solution.py:311
  70.8 4.4 %collective-permute-start.13 = (bf16[64,2048]{1,0:T(8,128)(2,1)S(1)}, bf16[64,2048]{1,0:T(8,128)(2,1)S(1)}, u32[]{:S(2)}, u32[]{:S(2)}) collective-permute-start(bf16[64,2048]{1,0:T(8,128)(2,1)S(1)} %get-tuple-element.44), channel_id=1, source_target_pairs={{0,6},{1,7},{2,0},{3,1},{4,2},{5,3},{6,4},{7,5},{8,14},{9,15},{10,... | collective-permute-start | bytes 786440 | tf_op jit(solution)/shard_map/ppermute | solution.py:308
  75.2 0.1 add.58
  75.3 3.9 %collective-permute-start.17 = (bf16[64,2048]{1,0:T(8,128)(2,1)S(1)}, bf16[64,2048]{1,0:T(8,128)(2,1)S(1)}, u32[]{:S(2)}, u32[]{:S(2)}) collective-permute-start(bf16[64,2048]{1,0:T(8,128)(2,1)S(1)} %add.58), channel_id=1, source_target_pairs={{0,6},{1,7},{2,0},{3,1},{4,2},{5,3},{6,4},{7,5},{8,14},{9,15},{10,... | collective-permute-start | bytes 786440 | tf_op jit(solution)/shard_map/ppermute | solution.py:313
  79.2 0.1 add.57
  79.3 1.9 %collective-permute-start.15 = (bf16[64,2048]{1,0:T(8,128)(2,1)S(1)}, bf16[64,2048]{1,0:T(8,128)(2,1)S(1)}, u32[]{:S(2)}, u32[]{:S(2)}) collective-permute-start(bf16[64,2048]{1,0:T(8,128)(2,1)S(1)} %add.57), channel_id=1, source_target_pairs={{0,2},{1,3},{2,4},{3,5},{4,6},{5,7},{6,0},{7,1},{8,10},{9,11},{10,... | collective-permute-start | bytes 786440 | tf_op jit(solution)/shard_map/ppermute | solution.py:312
  81.2 1.8 %collective-permute-done.18.right_b = bf16[64,2048]{1,0:T(8,128)(2,1)S(1)} collective-permute-done((bf16[64,2048]{1,0:T(8,128)(2,1)S(1)}, bf16[64,2048]{1,0:T(8,128)(2,1)S(1)}, u32[]{:S(2)}, u32[]{:S(2)}) %collective-permute-start.18) | collective-permute-done | bytes 262176 | tf_op jit(solution)/shard_map/ppermute | solution.py:311
  83.0 3.1 %collective-permute-done.17.left_b = bf16[64,2048]{1,0:T(8,128)(2,1)S(1)} collective-permute-done((bf16[64,2048]{1,0:T(8,128)(2,1)S(1)}, bf16[64,2048]{1,0:T(8,128)(2,1)S(1)}, u32[]{:S(2)}, u32[]{:S(2)}) %collective-permute-start.17) | collective-permute-done | bytes 262176 | tf_op jit(solution)/shard_map/ppermute | solution.py:313
  86.1 3.2 %collective-permute-done.15.right_a = bf16[64,2048]{1,0:T(8,128)(2,1)S(1)} collective-permute-done((bf16[64,2048]{1,0:T(8,128)(2,1)S(1)}, bf16[64,2048]{1,0:T(8,128)(2,1)S(1)}, u32[]{:S(2)}, u32[]{:S(2)}) %collective-permute-start.15) | collective-permute-done | bytes 262176 | tf_op jit(solution)/shard_map/ppermute | solution.py:312
  89.4 1.0 %shard_map.64 = bf16[64,4096]{1,0:T(8,128)(2,1)} custom-call(bf16[64,2048]{1,0:T(8,128)(2,1)S(1)} %get-tuple-element.43.own_a, bf16[64,2048]{1,0:T(8,128)(2,1)S(1)} %collective-permute-done.13.left_a, bf16[64,2048]{1,0:T(8,128)(2,1)S(1)} %collective-permute-done.15.right_a, bf16[64,2048]{1,0:T(8,128)(2,1)S(1)} %get-tuple-element.47.own_b, ...), custom_call_target="tpu_custom_call" | custom-call | flops 786432 | bytes 2000000 | tf_op jit(solution)/shard_map/pallas_call | solution.py:244
  (13 shorter events, 0.1 us)
Async XLA Ops:
  0.0 28.9 %collective-permute-start.7 = (bf16[512,4096]{1,0:T(8,128)(2,1)}, bf16[512,4096]{1,0:T(8,128)(2,1)}, u32[]{:S(2)}, u32[]{:S(2)}) collective-permute-start(bf16[512,4096]{1,0:T(8,128)(2,1)} %w_own_ref.3), channel_id=1, source_target_pairs={{0,1},{1,0},{2,3},{3,2},{4,5},{5,4},{6,7},{7,6},{8,9},{9,8},{10,11... | collective-permute-start | bytes 12582920 | tf_op jit(solution)/shard_map/ppermute | solution.py:284
  3.2 13.9 %collective-permute-start.3 = (bf16[144,128]{1,0:T(8,128)(2,1)S(1)}, bf16[144,128]{1,0:T(8,128)(2,1)S(1)}, u32[]{:S(2)}, u32[]{:S(2)}) collective-permute-start(bf16[144,128]{1,0:T(8,128)(2,1)S(1)} %get-tuple-element.29), channel_id=1, source_target_pairs={{0,8},{8,0},{16,24},{24,16},{32,40},{40,32},{48,56},{56,48},{64,72... | collective-permute-start | bytes 110600 | tf_op jit(solution)/shard_map/ppermute | solution.py:281
  5.2 15.7 %collective-permute-start.4 = (bf16[144,128]{1,0:T(8,128)(2,1)S(1)}, bf16[144,128]{1,0:T(8,128)(2,1)S(1)}, u32[]{:S(2)}, u32[]{:S(2)}) collective-permute-start(bf16[144,128]{1,0:T(8,128)(2,1)S(1)} %get-tuple-element.29), channel_id=1, source_target_pairs={{0,16},{8,24},{16,0},{24,8},{32,48},{40,56},{48,32},{56,40},{64,80... | collective-permute-start | bytes 110600 | tf_op jit(solution)/shard_map/ppermute | solution.py:281
  11.2 10.3 %collective-permute-start.5 = (bf16[144,128]{1,0:T(8,128)(2,1)S(1)}, bf16[144,128]{1,0:T(8,128)(2,1)S(1)}, u32[]{:S(2)}, u32[]{:S(2)}) collective-permute-start(bf16[144,128]{1,0:T(8,128)(2,1)S(1)} %get-tuple-element.29), channel_id=1, source_target_pairs={{0,24},{8,16},{16,8},{24,0},{32,56},{40,48},{48,40},{56,32},{64,88... | collective-permute-start | bytes 110600 | tf_op jit(solution)/shard_map/ppermute | solution.py:281
  13.7 24.5 %collective-permute-start.2 = (bf16[512,256]{1,0:T(8,128)(2,1)S(1)}, bf16[512,256]{1,0:T(8,128)(2,1)S(1)}, u32[]{:S(2)}, u32[]{:S(2)}) collective-permute-start(bf16[512,256]{1,0:T(8,128)(2,1)S(1)} %pad_add_fusion.kv_ref), channel_id=1, source_target_pairs={{0,8},{8,16},{16,24},{32,40},{40,48},{48,56},{64,72},{72,80},{80,8... | collective-permute-start | bytes 786440 | tf_op jit(solution)/shard_map/ppermute | solution.py:281
  17.1 27.3 %collective-permute-start.1 = (bf16[512,256]{1,0:T(8,128)(2,1)S(1)}, bf16[512,256]{1,0:T(8,128)(2,1)S(1)}, u32[]{:S(2)}, u32[]{:S(2)}) collective-permute-start(bf16[512,256]{1,0:T(8,128)(2,1)S(1)} %pad_add_fusion.kv_ref), channel_id=1, source_target_pairs={{0,16},{8,24},{32,48},{40,56},{64,80},{72,88},{96,112},{104,120},{... | collective-permute-start | bytes 786440 | tf_op jit(solution)/shard_map/ppermute | solution.py:281
  20.8 24.4 %collective-permute-start = (bf16[512,256]{1,0:T(8,128)(2,1)S(1)}, bf16[512,256]{1,0:T(8,128)(2,1)S(1)}, u32[]{:S(2)}, u32[]{:S(2)}) collective-permute-start(bf16[512,256]{1,0:T(8,128)(2,1)S(1)} %pad_add_fusion.kv_ref), channel_id=1, source_target_pairs={{0,24},{32,56},{64,88},{96,120},{128,152},{160,184},{192,216},{224... | collective-permute-start | bytes 786440 | tf_op jit(solution)/shard_map/ppermute | solution.py:281
  21.5 12.0 %collective-permute-start.6 = (bf16[144,128]{1,0:T(8,128)(2,1)S(1)}, bf16[144,128]{1,0:T(8,128)(2,1)S(1)}, u32[]{:S(2)}, u32[]{:S(2)}) collective-permute-start(bf16[144,128]{1,0:T(8,128)(2,1)S(1)} %get-tuple-element.51), channel_id=1, source_target_pairs={{0,40},{8,48},{16,56},{24,32},{32,8},{40,16},{48,24},{56,0},{64,10... | collective-permute-start | bytes 110600 | tf_op jit(solution)/shard_map/ppermute | solution.py:281
  28.9 7.8 %copy-start.1 = (bf16[512,512]{1,0:T(8,128)(2,1)S(1)}, bf16[512,512]{1,0:T(8,128)(2,1)}, u32[]{:S(2)}) copy-start(bf16[512,512]{1,0:T(8,128)(2,1)} %q_ref.9) | copy-start | bytes 1572868
  33.5 7.0 %collective-permute-start.8 = (bf16[144,128]{1,0:T(8,128)(2,1)S(1)}, bf16[144,128]{1,0:T(8,128)(2,1)S(1)}, u32[]{:S(2)}, u32[]{:S(2)}) collective-permute-start(bf16[144,128]{1,0:T(8,128)(2,1)S(1)} %fusion.2.order), channel_id=1, source_target_pairs={{0,64},{8,72},{16,80},{24,88},{32,96},{40,104},{48,112},{56,120},{... | collective-permute-start | bytes 110600 | tf_op jit(solution)/shard_map/ppermute | solution.py:281
  40.6 7.1 %collective-permute-start.11 = (bf16[144,128]{1,0:T(8,128)(2,1)S(1)}, bf16[144,128]{1,0:T(8,128)(2,1)S(1)}, u32[]{:S(2)}, u32[]{:S(2)}) collective-permute-start(bf16[144,128]{1,0:T(8,128)(2,1)S(1)} %get-tuple-element.54.order), channel_id=1, source_target_pairs={{0,128},{8,136},{16,144},{24,152},{32,160},{40,168},{48,176},{56,1... | collective-permute-start | bytes 110600 | tf_op jit(solution)/shard_map/ppermute | solution.py:281
  41.9 9.9 %collective-permute-start.10 = (bf16[144,128]{1,0:T(8,128)(2,1)S(1)}, bf16[144,128]{1,0:T(8,128)(2,1)S(1)}, u32[]{:S(2)}, u32[]{:S(2)}) collective-permute-start(bf16[144,128]{1,0:T(8,128)(2,1)S(1)} %get-tuple-element.54.order), channel_id=1, source_target_pairs={{0,256},{8,264},{16,272},{24,280},{32,288},{40,296},{48,304},{56,3... | collective-permute-start | bytes 110600 | tf_op jit(solution)/shard_map/ppermute | solution.py:281
  43.2 10.9 %collective-permute-start.9 = (bf16[144,128]{1,0:T(8,128)(2,1)S(1)}, bf16[144,128]{1,0:T(8,128)(2,1)S(1)}, u32[]{:S(2)}, u32[]{:S(2)}) collective-permute-start(bf16[144,128]{1,0:T(8,128)(2,1)S(1)} %get-tuple-element.54.order), channel_id=1, source_target_pairs={{0,384},{8,392},{16,400},{24,408},{32,416},{40,424},{48,432},{56,4... | collective-permute-start | bytes 110600 | tf_op jit(solution)/shard_map/ppermute | solution.py:281
  45.3 8.9 %copy-start.2 = (f32[4]{0:T(128)S(1)}, f32[4]{0:T(128)}, u32[]{:S(2)}) copy-start(f32[4]{0:T(128)} %gate_ref.1) | copy-start | bytes 52
  45.3 13.8 %copy-start = (bf16[512,4096]{1,0:T(8,128)(2,1)S(1)}, bf16[512,4096]{1,0:T(8,128)(2,1)}, u32[]{:S(2)}) copy-start(bf16[512,4096]{1,0:T(8,128)(2,1)} %w_own_ref.3) | copy-start | bytes 12582916
  55.6 3.4 %collective-permute-start.12 = (bf16[256,512]{1,0:T(8,128)(2,1)S(1)}, bf16[256,512]{1,0:T(8,128)(2,1)S(1)}, u32[]{:S(2)}, u32[]{:S(2)}) collective-permute-start(bf16[256,512]{1,0:T(8,128)(2,1)S(1)} %get-tuple-element.42), channel_id=1, source_target_pairs={{0,1},{1,0},{2,3},{3,2},{4,5},{5,4},{6,7},{7,6},{8,9},{9,8},{10,11... | collective-permute-start | bytes 786440 | tf_op jit(solution)/shard_map/ppermute | solution.py:305
  60.3 14.9 %collective-permute-start.16 = (bf16[64,2048]{1,0:T(8,128)(2,1)S(1)}, bf16[64,2048]{1,0:T(8,128)(2,1)S(1)}, u32[]{:S(2)}, u32[]{:S(2)}) collective-permute-start(bf16[64,2048]{1,0:T(8,128)(2,1)S(1)} %get-tuple-element.49), channel_id=1, source_target_pairs={{0,6},{1,7},{2,0},{3,1},{4,2},{5,3},{6,4},{7,5},{8,14},{9,15},{10,... | collective-permute-start | bytes 786440 | tf_op jit(solution)/shard_map/ppermute | solution.py:310
  66.2 13.0 %collective-permute-start.14 = (bf16[64,2048]{1,0:T(8,128)(2,1)S(1)}, bf16[64,2048]{1,0:T(8,128)(2,1)S(1)}, u32[]{:S(2)}, u32[]{:S(2)}) collective-permute-start(bf16[64,2048]{1,0:T(8,128)(2,1)S(1)} %get-tuple-element.46), channel_id=1, source_target_pairs={{0,2},{1,3},{2,4},{3,5},{4,6},{5,7},{6,0},{7,1},{8,10},{9,11},{10,... | collective-permute-start | bytes 786440 | tf_op jit(solution)/shard_map/ppermute | solution.py:307
  68.1 14.9 %collective-permute-start.18 = (bf16[64,2048]{1,0:T(8,128)(2,1)S(1)}, bf16[64,2048]{1,0:T(8,128)(2,1)S(1)}, u32[]{:S(2)}, u32[]{:S(2)}) collective-permute-start(bf16[64,2048]{1,0:T(8,128)(2,1)S(1)} %get-tuple-element.50), channel_id=1, source_target_pairs={{0,2},{1,3},{2,4},{3,5},{4,6},{5,7},{6,0},{7,1},{8,10},{9,11},{10,... | collective-permute-start | bytes 786440 | tf_op jit(solution)/shard_map/ppermute | solution.py:311
  70.8 12.2 %collective-permute-start.13 = (bf16[64,2048]{1,0:T(8,128)(2,1)S(1)}, bf16[64,2048]{1,0:T(8,128)(2,1)S(1)}, u32[]{:S(2)}, u32[]{:S(2)}) collective-permute-start(bf16[64,2048]{1,0:T(8,128)(2,1)S(1)} %get-tuple-element.44), channel_id=1, source_target_pairs={{0,6},{1,7},{2,0},{3,1},{4,2},{5,3},{6,4},{7,5},{8,14},{9,15},{10,... | collective-permute-start | bytes 786440 | tf_op jit(solution)/shard_map/ppermute | solution.py:308
  75.3 10.8 %collective-permute-start.17 = (bf16[64,2048]{1,0:T(8,128)(2,1)S(1)}, bf16[64,2048]{1,0:T(8,128)(2,1)S(1)}, u32[]{:S(2)}, u32[]{:S(2)}) collective-permute-start(bf16[64,2048]{1,0:T(8,128)(2,1)S(1)} %add.58), channel_id=1, source_target_pairs={{0,6},{1,7},{2,0},{3,1},{4,2},{5,3},{6,4},{7,5},{8,14},{9,15},{10,... | collective-permute-start | bytes 786440 | tf_op jit(solution)/shard_map/ppermute | solution.py:313
  79.3 10.1 %collective-permute-start.15 = (bf16[64,2048]{1,0:T(8,128)(2,1)S(1)}, bf16[64,2048]{1,0:T(8,128)(2,1)S(1)}, u32[]{:S(2)}, u32[]{:S(2)}) collective-permute-start(bf16[64,2048]{1,0:T(8,128)(2,1)S(1)} %add.57), channel_id=1, source_target_pairs={{0,2},{1,3},{2,4},{3,5},{4,6},{5,7},{6,0},{7,1},{8,10},{9,11},{10,... | collective-permute-start | bytes 786440 | tf_op jit(solution)/shard_map/ppermute | solution.py:312

commit v10 on v9

--- a/solution.py
+++ b/solution.py
@@ -110,8 +110,9 @@
     )(queries, kv, order)
 
 
-def step_kernel(distance, place_ref, q_ref, kv_ref, acc_in, top_in, order, acc_ref, top_ref=None):
+def step_kernel(distance, place_ref, gate_ref, q_ref, kv_ref, acc_in, top_in, order, acc_ref, top_ref):
     del order
+    last = distance == SPAN - 1
 
     @pl.when(place_ref[0] >= distance)
     def _():
@@ -127,30 +128,45 @@
                 shrink = jnp.exp2((before - top) * SCALE)
                 p = jnp.exp2((s - jnp.concatenate([top] * SPAN, axis=1)) * SCALE).astype(BF16)
                 pv = jnp.dot(p, wide, preferred_element_type=F32)
-                acc_ref[h, rows, :] = acc_in[h, rows, :] * jnp.concatenate([shrink, shrink], axis=1) + pv
-                if top_ref is not None:
+                acc = acc_in[h, rows, :] * jnp.concatenate([shrink, shrink], axis=1) + pv
+                if last:
+                    share = 1.0 - jax.nn.sigmoid(jnp.full((1, HD), gate_ref[h], F32))
+                    acc_ref[rows, h * HD : (h + 1) * HD] = share * (acc[:, :HD] / acc[:, HD:])
+                else:
+                    acc_ref[h, rows, :] = acc
                     top_ref[h, rows, :] = top
 
     @pl.when(place_ref[0] < distance)
     def _():
-        acc_ref[...] = acc_in[...]
-        if top_ref is not None:
+        if last:
+            for h in range(GROUP):
+                share = 1.0 - jax.nn.sigmoid(jnp.full((1, HD), gate_ref[h], F32))
+                acc_ref[:, h * HD : (h + 1) * HD] = share * (acc_in[h, :, :HD] / acc_in[h, :, HD:])
+        else:
+            acc_ref[...] = acc_in[...]
             top_ref[...] = top_in[...]
 
-
-def step_call(distance, place, queries, kv, acc, top, order):
-    state = (
-        jax.ShapeDtypeStruct((GROUP, ROWS, 2 * HD), F32),
-        jax.ShapeDtypeStruct((GROUP, ROWS, HD), F32),
+    if last:
+        for h in range(GROUP):
+            feat = feature_map(q_ref[:, h * HD : (h + 1) * HD].astype(F32))
+            high, low = split_two(feat)
+            top_ref[:, 2 * h * HD : (2 * h + 1) * HD] = high
+            top_ref[:, (2 * h + 1) * HD : (2 * h + 2) * HD] = low
+
+
+def step_call(distance, place, gates, queries, kv, acc, top, order):
+    last = distance == SPAN - 1
+    out = (
+        jax.ShapeDtypeStruct((ROWS, GROUP * HD), F32) if last else jax.ShapeDtypeStruct(acc.shape, F32),
+        jax.ShapeDtypeStruct((ROWS, 2 * GROUP * HD), BF16) if last else jax.ShapeDtypeStruct(top.shape, F32),
     )
-    kept = state[: 1 if distance == SPAN - 1 else 2]
     return call(
         functools.partial(step_kernel, distance),
-        kept,
+        out,
         (GROUP * ROWS * ROWS * HD * 4, 4000000, GROUP * ROWS * ROWS),
-        in_specs=[SM] + [VM] * 4 + [pl.BlockSpec(memory_space=pl.ANY)],
-        out_specs=(VM,) * len(kept),
-    )(place, queries, kv, acc, top, order)
+        in_specs=[SM, SM] + [VM] * 4 + [pl.BlockSpec(memory_space=pl.ANY)],
+        out_specs=(VM, VM),
+    )(place, gates, queries, kv, acc, top, order)
 
 
 def stage_kernel(w_hbm, w_ref, sem):
@@ -170,7 +186,9 @@
     )(w)
 
 
-def merge_kernel(place_ref, gate_ref, q_ref, acc_ref, mem0, mem1, mem2, mem3, keep_ref, send_ref, out_ref):
+def merge_kernel(
+    place_ref, gate_ref, feat_ref, local_ref, mem0, mem1, mem2, mem3, keep_ref, send_ref, out_ref
+):
     x = place_ref[1]
     core = place_ref[2]
     mem = mem0[...] + mem1[...].astype(F32) + (mem2[...].astype(F32) + mem3[...].astype(F32))
@@ -179,14 +197,12 @@
     mem_twice = jnp.concatenate([mem_high, mem_high], axis=1)
     for h in range(GROUP):
         gate = jax.nn.sigmoid(jnp.full((1, HD), gate_ref[h], F32))
-        feat = feature_map(q_ref[:, h * HD : (h + 1) * HD].astype(F32))
-        high, low = split_two(feat)
-        both = jnp.concatenate([high, low], axis=1)
+        both = feat_ref[:, 2 * h * HD : (2 * h + 2) * HD]
         read = lax.dot_general(both, mem_twice, NT, preferred_element_type=F32)
-        read = read + lax.dot_general(high, mem_low, NT, preferred_element_type=F32)
+        read = read + lax.dot_general(both[:, :HD], mem_low, NT, preferred_element_type=F32)
         retrieved = read[:, :HD] / jnp.maximum(read[:, HD:], 1.0)
-        local = acc_ref[h, :, :HD] / acc_ref[h, :, HD:]
-        out_ref[:, h * HD : (h + 1) * HD] = (gate * retrieved + (1.0 - gate) * local).astype(BF16)
+        cols = slice(h * HD, (h + 1) * HD)
+        out_ref[:, cols] = (gate * retrieved + local_ref[:, cols]).astype(BF16)
     for b in range(N_TP // 2):
         chip = (x + b) % (N_TP // 2)
         mine = pl.multiple_of((2 * chip + core) * BLOCK, BLOCK)
@@ -195,7 +211,7 @@
         send_ref[b * BLOCK : (b + 1) * BLOCK, :] = out_ref[pl.ds(other, BLOCK), :]
 
 
-def merge_call(place, gates, queries, acc, mems):
+def merge_call(place, gates, feats, local, mems):
     half = jax.ShapeDtypeStruct((ROWS // 2, GROUP * HD), BF16)
     return call(
         merge_kernel,
@@ -204,32 +220,48 @@
         in_specs=[SM, SM] + [VM] * 6,
         out_specs=(VM, VM),
         scratch_shapes=[pltpu.VMEM((ROWS, GROUP * HD), BF16)],
-    )(place, gates, queries, acc, *mems)
-
-
-def project_kernel(first, keep_ref, got_ref, w_own_ref, w_other_ref, own_ref, right_ref, far_ref, left_ref):
-    width = own_ref.shape[1]
+    )(place, gates, feats, local, *mems)
+
+
+def own_heads_kernel(keep_ref, w_ref, out_ref):
     tile = 512
-    for j in range(width // tile):
+    for j in range(w_ref.shape[1] // tile):
+        cols = slice(j * tile, (j + 1) * tile)
+        out_ref[:, cols] = jnp.dot(keep_ref[...], w_ref[:, cols], preferred_element_type=F32)
+
+
+def own_heads_call(keep, w):
+    rows, depth = keep.shape
+    return call(
+        own_heads_kernel,
+        jax.ShapeDtypeStruct((rows, w.shape[1]), F32),
+        (2 * rows * depth * w.shape[1], 8000000, 0),
+        in_specs=[VM] * 2,
+        out_specs=VM,
+    )(keep, w)
+
+
+def project_kernel(first, part_ref, got_ref, w_ref, own_ref, right_ref, far_ref, left_ref):
+    tile = 512
+    for j in range(own_ref.shape[1] // tile):
         cols = slice(j * tile, (j + 1) * tile)
         from_w = slice(first + j * tile, first + (j + 1) * tile)
-        out = jnp.dot(keep_ref[...], w_own_ref[:, from_w], preferred_element_type=F32)
-        out = out + jnp.dot(got_ref[...], w_other_ref[:, from_w], preferred_element_type=F32)
+        out = part_ref[:, from_w] + jnp.dot(got_ref[...], w_ref[:, from_w], preferred_element_type=F32)
         out = out.astype(BF16)
         for b, ref in enumerate((own_ref, right_ref, far_ref, left_ref)):
             ref[:, cols] = out[b * BLOCK : (b + 1) * BLOCK]
 
 
-def project_call(first, keep, got, w_own, w_other):
-    rows, depth = keep.shape
-    half = w_own.shape[1] // 2
+def project_call(first, part, got, w):
+    rows, depth = got.shape
+    half = w.shape[1] // 2
     return call(
         functools.partial(project_kernel, first),
         (jax.ShapeDtypeStruct((BLOCK, half), BF16),) * 4,
-        (4 * rows * depth * half, 6000000, 0),
-        in_specs=[VM] * 4,
+        (2 * rows * depth * half, 4000000, 0),
+        in_specs=[VM] * 3,
         out_specs=(VM,) * 4,
-    )(keep, got, w_own, w_other)
+    )(part, got, w)
 
 
 def total_kernel(own_a, left_a, right_a, own_b, left_b, right_b, out_ref):
@@ -293,20 +325,22 @@
     sent = line.astype(BF16)
     got = send(sent, swap(8, N_CTX))
     acc, top = own_call(queries, kv, sent)
-    acc, top = step_call(1, place, queries, kv1, acc, top, sent)
+    acc, top = step_call(1, place, gates, queries, kv1, acc, top, sent)
     got = after(got, acc).astype(F32)
     start = start + jnp.where(ctx // 8 % 2 == 1, got, 0.0)
     sent = (line + got).astype(BF16)
     pairs = [send(sent, along_y(2 * k)) for k in (3, 2, 1)]
-    acc, top = step_call(2, place, queries, kv2, acc, top, sent)
-    (acc,) = step_call(3, place, queries, kv3, acc, top, sent)
-    pairs = [after(part, acc) for part in pairs]
-    keep, give = merge_call(place, gates, queries, acc, [start] + pairs)
+    acc, top = step_call(2, place, gates, queries, kv2, acc, top, sent)
+    local, feats = step_call(3, place, gates, queries, kv3, acc, top, sent)
+    pairs = [after(part, local) for part in pairs]
+    keep, give = merge_call(place, gates, feats, local, [start] + pairs)
     got = lax.ppermute(give, "tp", swap(1, N_TP))
-    own_a, right_a, far_a, left_a = project_call(0, keep, got, out_weight, w_other)
+    part = own_heads_call(keep, out_weight)
+    got = after(got, part)
+    own_a, right_a, far_a, left_a = project_call(0, part, got, w_other)
     far_a = lax.ppermute(far_a, "tp", turned(1))
     left_a = lax.ppermute(left_a, "tp", turned(-1))
-    own_b, right_b, far_b, left_b = project_call(own_a.shape[1], keep, got, out_weight, w_other)
+    own_b, right_b, far_b, left_b = project_call(own_a.shape[1], part, got, w_other)
     far_b = lax.ppermute(far_b, "tp", turned(-1))
     right_b = lax.ppermute(right_b, "tp", turned(1))
     right_a = lax.ppermute(right_a + far_a, "tp", turned(1))

time: 90.9 us -> 89.9 us (0.989)
  waiting for transfers between devices: 20.1 us -> 18.5 us
    pallas_call x3 -> x4, Pallas kernels: 3.75 us -> 5.51 us  [the longest x3 4.22 us: step_call(): call(functools.partial(step_kernel, distance), out, (GROUP * ROWS * ROWS...]
    ppermute x1, waiting for transfers between devices: 1.5 us -> 0.2 us  [on_device(): got = lax.ppermute(give, 'tp', swap(1, N_TP))]
    pallas_call x2, Pallas kernels: 2.49 us -> 1.42 us  [project_call(): call(functools.partial(project_kernel, first), (jax.ShapeDtypeStruct((BLO...]
  transfers between devices with their start and end apart: 19 -> 19, of which waited for: 8 -> 8; matrix products, arithmetic and copies ran while one was open for 1% -> 1% of each run, Pallas kernels for 10% -> 11%
where the time goes in v10:
time: 89.9 us; the launch traced here: 89.3 us
  starting transfers between devices  55.9 us (62%)
  waiting for transfers between devices  18.5 us (21%)
  Pallas kernels  13.2 us (15%)
  other arithmetic  1.28 us (1%)
    ppermute x11, starting transfers between devices, on_device(): send = lambda x, route: lax.ppermute(x.astype(BF16), 'ctx', route)  32.6 us
    ppermute x11, waiting for transfers between devices, on_device(): send = lambda x, route: lax.ppermute(x.astype(BF16), 'ctx', route)  9.99 us
    ppermute x1, starting transfers between devices, on_device(): far_b = lax.ppermute(far_b, 'tp', turned(-1))  4.66 us
    ppermute x1, starting transfers between devices, on_device(): left_a = lax.ppermute(left_a, 'tp', turned(-1))  4.39 us
    pallas_call x3, Pallas kernels, step_call(): call(functools.partial(step_kernel, distance), out, (GROUP * ROWS * ROWS...  4.22 us
    ppermute x1, starting transfers between devices, on_device(): left_b = lax.ppermute(left_b + far_b, 'tp', turned(-1))  3.92 us
    ppermute x1, waiting for transfers between devices, on_device(): right_a = lax.ppermute(right_a + far_a, 'tp', turned(1))  3.25 us
    ppermute x1, waiting for transfers between devices, on_device(): left_b = lax.ppermute(left_b + far_b, 'tp', turned(-1))  3.11 us
  transfers between devices with their start and end apart: 19, of which 8 were waited for; matrix products, arithmetic and copies ran while one was open for 1% of the time, Pallas kernels for 11%

profile of v10, /device:TPU:120, one launch (start us, length us, event | category | flops | bytes accessed | tf_op | source)
XLA Modules:
  0.0 89.3 jit_solution(15191535500190541933)
XLA Ops:
  0.0 1.9 %collective-permute-start.7 = (bf16[512,4096]{1,0:T(8,128)(2,1)}, bf16[512,4096]{1,0:T(8,128)(2,1)}, u32[]{:S(2)}, u32[]{:S(2)}) collective-permute-start(bf16[512,4096]{1,0:T(8,128)(2,1)} %w_ref.1), channel_id=1, source_target_pairs={{0,1},{1,0},{2,3},{3,2},{4,5},{5,4},{6,7},{7,6},{8,9},{9,8},{10,11... | collective-permute-start | bytes 12582920 | tf_op jit(solution)/shard_map/ppermute | solution.py:316
  1.9 1.0 %pad_add_fusion.kv_ref = bf16[512,256]{1,0:T(8,128)(2,1)S(1)} fusion(bf16[512,128]{1,0:T(8,128)(2,1)} %param.7, bf16[512,128]{1,0:T(8,128)(2,1)} %param.6), kind=kLoop, calls=%fused_computation | loop fusion | flops 524288 | bytes 524288 | tf_op jit(solution)/shard_map/add | solution.py:314
  2.9 0.3 shard_map.55
  3.2 1.9 %collective-permute-start.3 = (bf16[144,128]{1,0:T(8,128)(2,1)S(1)}, bf16[144,128]{1,0:T(8,128)(2,1)S(1)}, u32[]{:S(2)}, u32[]{:S(2)}) collective-permute-start(bf16[144,128]{1,0:T(8,128)(2,1)S(1)} %get-tuple-element.32), channel_id=1, source_target_pairs={{0,8},{8,0},{16,24},{24,16},{32,40},{40,32},{48,56},{56,48},{64,72... | collective-permute-start | bytes 110600 | tf_op jit(solution)/shard_map/ppermute | solution.py:313
  5.2 6.1 %collective-permute-start.4 = (bf16[144,128]{1,0:T(8,128)(2,1)S(1)}, bf16[144,128]{1,0:T(8,128)(2,1)S(1)}, u32[]{:S(2)}, u32[]{:S(2)}) collective-permute-start(bf16[144,128]{1,0:T(8,128)(2,1)S(1)} %get-tuple-element.32), channel_id=1, source_target_pairs={{0,16},{8,24},{16,0},{24,8},{32,48},{40,56},{48,32},{56,40},{64,80... | collective-permute-start | bytes 110600 | tf_op jit(solution)/shard_map/ppermute | solution.py:313
  11.2 2.5 %collective-permute-start.5 = (bf16[144,128]{1,0:T(8,128)(2,1)S(1)}, bf16[144,128]{1,0:T(8,128)(2,1)S(1)}, u32[]{:S(2)}, u32[]{:S(2)}) collective-permute-start(bf16[144,128]{1,0:T(8,128)(2,1)S(1)} %get-tuple-element.32), channel_id=1, source_target_pairs={{0,24},{8,16},{16,8},{24,0},{32,56},{40,48},{48,40},{56,32},{64,88... | collective-permute-start | bytes 110600 | tf_op jit(solution)/shard_map/ppermute | solution.py:313
  13.7 3.4 %collective-permute-start.2 = (bf16[512,256]{1,0:T(8,128)(2,1)S(1)}, bf16[512,256]{1,0:T(8,128)(2,1)S(1)}, u32[]{:S(2)}, u32[]{:S(2)}) collective-permute-start(bf16[512,256]{1,0:T(8,128)(2,1)S(1)} %pad_add_fusion.kv_ref), channel_id=1, source_target_pairs={{0,8},{8,16},{16,24},{32,40},{40,48},{48,56},{64,72},{72,80},{80,8... | collective-permute-start | bytes 786440 | tf_op jit(solution)/shard_map/ppermute | solution.py:313
  17.1 3.7 %collective-permute-start.1 = (bf16[512,256]{1,0:T(8,128)(2,1)S(1)}, bf16[512,256]{1,0:T(8,128)(2,1)S(1)}, u32[]{:S(2)}, u32[]{:S(2)}) collective-permute-start(bf16[512,256]{1,0:T(8,128)(2,1)S(1)} %pad_add_fusion.kv_ref), channel_id=1, source_target_pairs={{0,16},{8,24},{32,48},{40,56},{64,80},{72,88},{96,112},{104,120},{... | collective-permute-start | bytes 786440 | tf_op jit(solution)/shard_map/ppermute | solution.py:313
  20.8 0.7 collective-permute-start
  21.5 0.0 collective-permute-done.5
  21.5 7.3 %collective-permute-start.6 = (bf16[144,128]{1,0:T(8,128)(2,1)S(1)}, bf16[144,128]{1,0:T(8,128)(2,1)S(1)}, u32[]{:S(2)}, u32[]{:S(2)}) collective-permute-start(bf16[144,128]{1,0:T(8,128)(2,1)S(1)} %get-tuple-element.57), channel_id=1, source_target_pairs={{0,40},{8,48},{16,56},{24,32},{32,8},{40,16},{48,24},{56,0},{64,10... | collective-permute-start | bytes 110600 | tf_op jit(solution)/shard_map/ppermute | solution.py:313
  28.9 0.1 pad_add_fusion.1.place_ref
  28.9 0.0 collective-permute-done.7.w_hbm
  29.0 2.3 %shard_map.56.w_ref = bf16[512,4096]{1,0:T(8,128)(2,1)S(1)} custom-call(bf16[512,4096]{1,0:T(8,128)(2,1)} %collective-permute-done.7.w_hbm), custom_call_target="tpu_custom_call" | custom-call | bytes 8000000 | tf_op jit(solution)/shard_map/pallas_call | solution.py:179
  31.2 2.3 %collective-permute-done.6 = bf16[144,128]{1,0:T(8,128)(2,1)S(1)} collective-permute-done((bf16[144,128]{1,0:T(8,128)(2,1)S(1)}, bf16[144,128]{1,0:T(8,128)(2,1)S(1)}, u32[]{:S(2)}, u32[]{:S(2)}) %collective-permute-start.6) | collective-permute-done | bytes 36896 | tf_op jit(solution)/shard_map/ppermute | solution.py:313
  33.5 3.3 %collective-permute-start.8 = (bf16[144,128]{1,0:T(8,128)(2,1)S(1)}, bf16[144,128]{1,0:T(8,128)(2,1)S(1)}, u32[]{:S(2)}, u32[]{:S(2)}) collective-permute-start(bf16[144,128]{1,0:T(8,128)(2,1)S(1)} %fusion.2.order), channel_id=1, source_target_pairs={{0,64},{8,72},{16,80},{24,88},{32,96},{40,104},{48,112},{56,120},{... | collective-permute-start | bytes 110600 | tf_op jit(solution)/shard_map/ppermute | solution.py:313
  36.8 1.4 %shard_map.57 = (f32[4,512,256]{2,1,0:T(8,128)S(1)}, f32[4,512,128]{2,1,0:T(8,128)S(1)}) custom-call(bf16[512,512]{1,0:T(8,128)(2,1)S(1)} %copy-done, bf16[512,256]{1,0:T(8,128)(2,1)S(1)} %pad_add_fusion.kv_ref, bf16[144,128]{1,0:T(8,128)(2,1)S(1)} %fusion.2.order), custom_call_target="tpu_custom_call" | custom-call | flops 536870912 | bytes 4000000 | tf_op jit(solution)/shard_map/pallas_call | solution.py:101
  38.2 0.0 collective-permute-done.2.kv_ref
  38.2 2.3 %shard_map.58 = (f32[4,512,256]{2,1,0:T(8,128)S(1)}, f32[4,512,128]{2,1,0:T(8,128)S(1)}) custom-call(s32[3]{0:T(128)S(1)} %pad_add_fusion.1.place_ref, f32[4]{0:T(128)S(1)} %copy-done.2, bf16[512,512]{1,0:T(8,128)(2,1)S(1)} %copy-done, bf16[512,256]{1,0:T(8,128)(2,1)S(1)} %collective-permute-done.2.kv_ref, f32[4,512,256]{2,1,0:T(8,128)S(1)} %get-tuple-element.34.acc_in, ...), custom_call_target="tpu_custom_call" | custom-call | flops 536870912 | bytes 4000000 | tf_op jit(solution)/shard_map/pallas_call | solution.py:163
  40.6 0.0 collective-permute-done.8
  40.6 1.3 %collective-permute-start.11 = (bf16[144,128]{1,0:T(8,128)(2,1)S(1)}, bf16[144,128]{1,0:T(8,128)(2,1)S(1)}, u32[]{:S(2)}, u32[]{:S(2)}) collective-permute-start(bf16[144,128]{1,0:T(8,128)(2,1)S(1)} %get-tuple-element.60.order), channel_id=1, source_target_pairs={{0,128},{8,136},{16,144},{24,152},{32,160},{40,168},{48,176},{56,1... | collective-permute-start | bytes 110600 | tf_op jit(solution)/shard_map/ppermute | solution.py:313
  41.9 1.3 %collective-permute-start.10 = (bf16[144,128]{1,0:T(8,128)(2,1)S(1)}, bf16[144,128]{1,0:T(8,128)(2,1)S(1)}, u32[]{:S(2)}, u32[]{:S(2)}) collective-permute-start(bf16[144,128]{1,0:T(8,128)(2,1)S(1)} %get-tuple-element.60.order), channel_id=1, source_target_pairs={{0,256},{8,264},{16,272},{24,280},{32,288},{40,296},{48,304},{56,3... | collective-permute-start | bytes 110600 | tf_op jit(solution)/shard_map/ppermute | solution.py:313
  43.2 1.3 %collective-permute-start.9 = (bf16[144,128]{1,0:T(8,128)(2,1)S(1)}, bf16[144,128]{1,0:T(8,128)(2,1)S(1)}, u32[]{:S(2)}, u32[]{:S(2)}) collective-permute-start(bf16[144,128]{1,0:T(8,128)(2,1)S(1)} %get-tuple-element.60.order), channel_id=1, source_target_pairs={{0,384},{8,392},{16,400},{24,408},{32,416},{40,424},{48,432},{56,4... | collective-permute-start | bytes 110600 | tf_op jit(solution)/shard_map/ppermute | solution.py:313
  44.5 0.0 collective-permute-done.1.kv_ref
  44.5 0.0 copy-start.1
  44.5 0.8 shard_map.59
  45.3 1.1 %shard_map.60 = (f32[512,512]{1,0:T(8,128)S(1)}, bf16[512,1024]{1,0:T(8,128)(2,1)S(1)}) custom-call(s32[3]{0:T(128)S(1)} %pad_add_fusion.1.place_ref, f32[4]{0:T(128)S(1)} %copy-done.2, bf16[512,512]{1,0:T(8,128)(2,1)S(1)} %copy-done, bf16[512,256]{1,0:T(8,128)(2,1)S(1)} %collective-permute-done.kv_ref, f32[4,512,256]{2,1,0:T(8,128)S(1)} %get-tuple-element.39.acc_in, ...), custom_call_target="tpu_custom_call" | custom-call | flops 536870912 | bytes 4000000 | tf_op jit(solution)/shard_map/pallas_call | solution.py:163
  46.4 1.3 %collective-permute-done.11.mem3 = bf16[144,128]{1,0:T(8,128)(2,1)S(1)} collective-permute-done((bf16[144,128]{1,0:T(8,128)(2,1)S(1)}, bf16[144,128]{1,0:T(8,128)(2,1)S(1)}, u32[]{:S(2)}, u32[]{:S(2)}) %collective-permute-start.11) | collective-permute-done | bytes 36896 | tf_op jit(solution)/shard_map/ppermute | solution.py:313
  47.7 4.0 %collective-permute-done.10.mem2 = bf16[144,128]{1,0:T(8,128)(2,1)S(1)} collective-permute-done((bf16[144,128]{1,0:T(8,128)(2,1)S(1)}, bf16[144,128]{1,0:T(8,128)(2,1)S(1)}, u32[]{:S(2)}, u32[]{:S(2)}) %collective-permute-start.10) | collective-permute-done | bytes 36896 | tf_op jit(solution)/shard_map/ppermute | solution.py:313
  51.8 2.4 %collective-permute-done.9.mem1 = bf16[144,128]{1,0:T(8,128)(2,1)S(1)} collective-permute-done((bf16[144,128]{1,0:T(8,128)(2,1)S(1)}, bf16[144,128]{1,0:T(8,128)(2,1)S(1)}, u32[]{:S(2)}, u32[]{:S(2)}) %collective-permute-start.9) | collective-permute-done | bytes 36896 | tf_op jit(solution)/shard_map/ppermute | solution.py:313
  54.1 1.3 %shard_map.61 = (bf16[256,512]{1,0:T(8,128)(2,1)S(1)}, bf16[256,512]{1,0:T(8,128)(2,1)S(1)}) custom-call(s32[3]{0:T(128)S(1)} %pad_add_fusion.1.place_ref, f32[4]{0:T(128)S(1)} %copy-done.2, bf16[512,1024]{1,0:T(8,128)(2,1)S(1)} %get-tuple-element.41.feat_ref, f32[512,512]{1,0:T(8,128)S(1)} %get-tuple-element.42.local_ref, ...), custom_call_target="tpu_custom_call" | custom-call | flops 402653184 | bytes 4000000 | tf_op jit(solution)/shard_map/pallas_call | solution.py:216
  55.5 1.9 %collective-permute-start.12 = (bf16[256,512]{1,0:T(8,128)(2,1)S(1)}, bf16[256,512]{1,0:T(8,128)(2,1)S(1)}, u32[]{:S(2)}, u32[]{:S(2)}) collective-permute-start(bf16[256,512]{1,0:T(8,128)(2,1)S(1)} %get-tuple-element.47), channel_id=1, source_target_pairs={{0,1},{1,0},{2,3},{3,2},{4,5},{5,4},{6,7},{7,6},{8,9},{9,8},{10,11... | collective-permute-start | bytes 786440 | tf_op jit(solution)/shard_map/ppermute | solution.py:337
  57.4 1.3 %shard_map.62.part_ref = f32[256,4096]{1,0:T(8,128)S(1)} custom-call(bf16[256,512]{1,0:T(8,128)(2,1)S(1)} %get-tuple-element.46.keep_ref, bf16[512,4096]{1,0:T(8,128)(2,1)S(1)} %copy-done.1), custom_call_target="tpu_custom_call" | custom-call | flops 1073741824 | bytes 8000000 | tf_op jit(solution)/shard_map/pallas_call | solution.py:235
  58.7 0.2 collective-permute-done.12.got_ref
  58.9 0.7 shard_map.64
  59.6 4.7 %collective-permute-start.16 = (bf16[64,2048]{1,0:T(8,128)(2,1)S(1)}, bf16[64,2048]{1,0:T(8,128)(2,1)S(1)}, u32[]{:S(2)}, u32[]{:S(2)}) collective-permute-start(bf16[64,2048]{1,0:T(8,128)(2,1)S(1)} %get-tuple-element.55), channel_id=1, source_target_pairs={{0,6},{1,7},{2,0},{3,1},{4,2},{5,3},{6,4},{7,5},{8,14},{9,15},{10,... | collective-permute-start | bytes 786440 | tf_op jit(solution)/shard_map/ppermute | solution.py:344
  64.3 0.7 shard_map.63
  65.0 1.9 %collective-permute-start.14 = (bf16[64,2048]{1,0:T(8,128)(2,1)S(1)}, bf16[64,2048]{1,0:T(8,128)(2,1)S(1)}, u32[]{:S(2)}, u32[]{:S(2)}) collective-permute-start(bf16[64,2048]{1,0:T(8,128)(2,1)S(1)} %get-tuple-element.52), channel_id=1, source_target_pairs={{0,2},{1,3},{2,4},{3,5},{4,6},{5,7},{6,0},{7,1},{8,10},{9,11},{10,... | collective-permute-start | bytes 786440 | tf_op jit(solution)/shard_map/ppermute | solution.py:341
  66.9 2.7 %collective-permute-start.18 = (bf16[64,2048]{1,0:T(8,128)(2,1)S(1)}, bf16[64,2048]{1,0:T(8,128)(2,1)S(1)}, u32[]{:S(2)}, u32[]{:S(2)}) collective-permute-start(bf16[64,2048]{1,0:T(8,128)(2,1)S(1)} %get-tuple-element.56), channel_id=1, source_target_pairs={{0,2},{1,3},{2,4},{3,5},{4,6},{5,7},{6,0},{7,1},{8,10},{9,11},{10,... | collective-permute-start | bytes 786440 | tf_op jit(solution)/shard_map/ppermute | solution.py:345
  69.6 4.4 %collective-permute-start.13 = (bf16[64,2048]{1,0:T(8,128)(2,1)S(1)}, bf16[64,2048]{1,0:T(8,128)(2,1)S(1)}, u32[]{:S(2)}, u32[]{:S(2)}) collective-permute-start(bf16[64,2048]{1,0:T(8,128)(2,1)S(1)} %get-tuple-element.50), channel_id=1, source_target_pairs={{0,6},{1,7},{2,0},{3,1},{4,2},{5,3},{6,4},{7,5},{8,14},{9,15},{10,... | collective-permute-start | bytes 786440 | tf_op jit(solution)/shard_map/ppermute | solution.py:342
  74.0 0.1 add.58
  74.1 3.9 %collective-permute-start.17 = (bf16[64,2048]{1,0:T(8,128)(2,1)S(1)}, bf16[64,2048]{1,0:T(8,128)(2,1)S(1)}, u32[]{:S(2)}, u32[]{:S(2)}) collective-permute-start(bf16[64,2048]{1,0:T(8,128)(2,1)S(1)} %add.58), channel_id=1, source_target_pairs={{0,6},{1,7},{2,0},{3,1},{4,2},{5,3},{6,4},{7,5},{8,14},{9,15},{10,... | collective-permute-start | bytes 786440 | tf_op jit(solution)/shard_map/ppermute | solution.py:347
  78.0 0.1 add.57
  78.1 1.9 %collective-permute-start.15 = (bf16[64,2048]{1,0:T(8,128)(2,1)S(1)}, bf16[64,2048]{1,0:T(8,128)(2,1)S(1)}, u32[]{:S(2)}, u32[]{:S(2)}) collective-permute-start(bf16[64,2048]{1,0:T(8,128)(2,1)S(1)} %add.57), channel_id=1, source_target_pairs={{0,2},{1,3},{2,4},{3,5},{4,6},{5,7},{6,0},{7,1},{8,10},{9,11},{10,... | collective-permute-start | bytes 786440 | tf_op jit(solution)/shard_map/ppermute | solution.py:346
  80.0 1.9 %collective-permute-done.18.right_b = bf16[64,2048]{1,0:T(8,128)(2,1)S(1)} collective-permute-done((bf16[64,2048]{1,0:T(8,128)(2,1)S(1)}, bf16[64,2048]{1,0:T(8,128)(2,1)S(1)}, u32[]{:S(2)}, u32[]{:S(2)}) %collective-permute-start.18) | collective-permute-done | bytes 262176 | tf_op jit(solution)/shard_map/ppermute | solution.py:345
  82.0 3.1 %collective-permute-done.17.left_b = bf16[64,2048]{1,0:T(8,128)(2,1)S(1)} collective-permute-done((bf16[64,2048]{1,0:T(8,128)(2,1)S(1)}, bf16[64,2048]{1,0:T(8,128)(2,1)S(1)}, u32[]{:S(2)}, u32[]{:S(2)}) %collective-permute-start.17) | collective-permute-done | bytes 262176 | tf_op jit(solution)/shard_map/ppermute | solution.py:347
  85.1 3.2 %collective-permute-done.15.right_a = bf16[64,2048]{1,0:T(8,128)(2,1)S(1)} collective-permute-done((bf16[64,2048]{1,0:T(8,128)(2,1)S(1)}, bf16[64,2048]{1,0:T(8,128)(2,1)S(1)}, u32[]{:S(2)}, u32[]{:S(2)}) %collective-permute-start.15) | collective-permute-done | bytes 262176 | tf_op jit(solution)/shard_map/ppermute | solution.py:346
  88.3 1.0 %shard_map.65 = bf16[64,4096]{1,0:T(8,128)(2,1)} custom-call(bf16[64,2048]{1,0:T(8,128)(2,1)S(1)} %get-tuple-element.49.own_a, bf16[64,2048]{1,0:T(8,128)(2,1)S(1)} %collective-permute-done.13.left_a, bf16[64,2048]{1,0:T(8,128)(2,1)S(1)} %collective-permute-done.15.right_a, bf16[64,2048]{1,0:T(8,128)(2,1)S(1)} %get-tuple-element.53.own_b, ...), custom_call_target="tpu_custom_call" | custom-call | flops 786432 | bytes 2000000 | tf_op jit(solution)/shard_map/pallas_call | solution.py:276
  (14 shorter events, 0.1 us)
Async XLA Ops:
  0.0 28.9 %collective-permute-start.7 = (bf16[512,4096]{1,0:T(8,128)(2,1)}, bf16[512,4096]{1,0:T(8,128)(2,1)}, u32[]{:S(2)}, u32[]{:S(2)}) collective-permute-start(bf16[512,4096]{1,0:T(8,128)(2,1)} %w_ref.1), channel_id=1, source_target_pairs={{0,1},{1,0},{2,3},{3,2},{4,5},{5,4},{6,7},{7,6},{8,9},{9,8},{10,11... | collective-permute-start | bytes 12582920 | tf_op jit(solution)/shard_map/ppermute | solution.py:316
  3.2 13.9 %collective-permute-start.3 = (bf16[144,128]{1,0:T(8,128)(2,1)S(1)}, bf16[144,128]{1,0:T(8,128)(2,1)S(1)}, u32[]{:S(2)}, u32[]{:S(2)}) collective-permute-start(bf16[144,128]{1,0:T(8,128)(2,1)S(1)} %get-tuple-element.32), channel_id=1, source_target_pairs={{0,8},{8,0},{16,24},{24,16},{32,40},{40,32},{48,56},{56,48},{64,72... | collective-permute-start | bytes 110600 | tf_op jit(solution)/shard_map/ppermute | solution.py:313
  5.2 15.7 %collective-permute-start.4 = (bf16[144,128]{1,0:T(8,128)(2,1)S(1)}, bf16[144,128]{1,0:T(8,128)(2,1)S(1)}, u32[]{:S(2)}, u32[]{:S(2)}) collective-permute-start(bf16[144,128]{1,0:T(8,128)(2,1)S(1)} %get-tuple-element.32), channel_id=1, source_target_pairs={{0,16},{8,24},{16,0},{24,8},{32,48},{40,56},{48,32},{56,40},{64,80... | collective-permute-start | bytes 110600 | tf_op jit(solution)/shard_map/ppermute | solution.py:313
  11.2 10.3 %collective-permute-start.5 = (bf16[144,128]{1,0:T(8,128)(2,1)S(1)}, bf16[144,128]{1,0:T(8,128)(2,1)S(1)}, u32[]{:S(2)}, u32[]{:S(2)}) collective-permute-start(bf16[144,128]{1,0:T(8,128)(2,1)S(1)} %get-tuple-element.32), channel_id=1, source_target_pairs={{0,24},{8,16},{16,8},{24,0},{32,56},{40,48},{48,40},{56,32},{64,88... | collective-permute-start | bytes 110600 | tf_op jit(solution)/shard_map/ppermute | solution.py:313
  13.7 24.5 %collective-permute-start.2 = (bf16[512,256]{1,0:T(8,128)(2,1)S(1)}, bf16[512,256]{1,0:T(8,128)(2,1)S(1)}, u32[]{:S(2)}, u32[]{:S(2)}) collective-permute-start(bf16[512,256]{1,0:T(8,128)(2,1)S(1)} %pad_add_fusion.kv_ref), channel_id=1, source_target_pairs={{0,8},{8,16},{16,24},{32,40},{40,48},{48,56},{64,72},{72,80},{80,8... | collective-permute-start | bytes 786440 | tf_op jit(solution)/shard_map/ppermute | solution.py:313
  17.1 27.4 %collective-permute-start.1 = (bf16[512,256]{1,0:T(8,128)(2,1)S(1)}, bf16[512,256]{1,0:T(8,128)(2,1)S(1)}, u32[]{:S(2)}, u32[]{:S(2)}) collective-permute-start(bf16[512,256]{1,0:T(8,128)(2,1)S(1)} %pad_add_fusion.kv_ref), channel_id=1, source_target_pairs={{0,16},{8,24},{32,48},{40,56},{64,80},{72,88},{96,112},{104,120},{... | collective-permute-start | bytes 786440 | tf_op jit(solution)/shard_map/ppermute | solution.py:313
  20.8 24.5 %collective-permute-start = (bf16[512,256]{1,0:T(8,128)(2,1)S(1)}, bf16[512,256]{1,0:T(8,128)(2,1)S(1)}, u32[]{:S(2)}, u32[]{:S(2)}) collective-permute-start(bf16[512,256]{1,0:T(8,128)(2,1)S(1)} %pad_add_fusion.kv_ref), channel_id=1, source_target_pairs={{0,24},{32,56},{64,88},{96,120},{128,152},{160,184},{192,216},{224... | collective-permute-start | bytes 786440 | tf_op jit(solution)/shard_map/ppermute | solution.py:313
  21.5 12.0 %collective-permute-start.6 = (bf16[144,128]{1,0:T(8,128)(2,1)S(1)}, bf16[144,128]{1,0:T(8,128)(2,1)S(1)}, u32[]{:S(2)}, u32[]{:S(2)}) collective-permute-start(bf16[144,128]{1,0:T(8,128)(2,1)S(1)} %get-tuple-element.57), channel_id=1, source_target_pairs={{0,40},{8,48},{16,56},{24,32},{32,8},{40,16},{48,24},{56,0},{64,10... | collective-permute-start | bytes 110600 | tf_op jit(solution)/shard_map/ppermute | solution.py:313
  28.9 7.8 %copy-start = (bf16[512,512]{1,0:T(8,128)(2,1)S(1)}, bf16[512,512]{1,0:T(8,128)(2,1)}, u32[]{:S(2)}) copy-start(bf16[512,512]{1,0:T(8,128)(2,1)} %q_ref.7) | copy-start | bytes 1572868
  28.9 9.3 %copy-start.2 = (f32[4]{0:T(128)S(1)}, f32[4]{0:T(128)}, u32[]{:S(2)}) copy-start(f32[4]{0:T(128)} %gate_ref.7) | copy-start | bytes 52
  33.5 7.0 %collective-permute-start.8 = (bf16[144,128]{1,0:T(8,128)(2,1)S(1)}, bf16[144,128]{1,0:T(8,128)(2,1)S(1)}, u32[]{:S(2)}, u32[]{:S(2)}) collective-permute-start(bf16[144,128]{1,0:T(8,128)(2,1)S(1)} %fusion.2.order), channel_id=1, source_target_pairs={{0,64},{8,72},{16,80},{24,88},{32,96},{40,104},{48,112},{56,120},{... | collective-permute-start | bytes 110600 | tf_op jit(solution)/shard_map/ppermute | solution.py:313
  40.6 7.1 %collective-permute-start.11 = (bf16[144,128]{1,0:T(8,128)(2,1)S(1)}, bf16[144,128]{1,0:T(8,128)(2,1)S(1)}, u32[]{:S(2)}, u32[]{:S(2)}) collective-permute-start(bf16[144,128]{1,0:T(8,128)(2,1)S(1)} %get-tuple-element.60.order), channel_id=1, source_target_pairs={{0,128},{8,136},{16,144},{24,152},{32,160},{40,168},{48,176},{56,1... | collective-permute-start | bytes 110600 | tf_op jit(solution)/shard_map/ppermute | solution.py:313
  41.9 9.9 %collective-permute-start.10 = (bf16[144,128]{1,0:T(8,128)(2,1)S(1)}, bf16[144,128]{1,0:T(8,128)(2,1)S(1)}, u32[]{:S(2)}, u32[]{:S(2)}) collective-permute-start(bf16[144,128]{1,0:T(8,128)(2,1)S(1)} %get-tuple-element.60.order), channel_id=1, source_target_pairs={{0,256},{8,264},{16,272},{24,280},{32,288},{40,296},{48,304},{56,3... | collective-permute-start | bytes 110600 | tf_op jit(solution)/shard_map/ppermute | solution.py:313
  43.2 10.9 %collective-permute-start.9 = (bf16[144,128]{1,0:T(8,128)(2,1)S(1)}, bf16[144,128]{1,0:T(8,128)(2,1)S(1)}, u32[]{:S(2)}, u32[]{:S(2)}) collective-permute-start(bf16[144,128]{1,0:T(8,128)(2,1)S(1)} %get-tuple-element.60.order), channel_id=1, source_target_pairs={{0,384},{8,392},{16,400},{24,408},{32,416},{40,424},{48,432},{56,4... | collective-permute-start | bytes 110600 | tf_op jit(solution)/shard_map/ppermute | solution.py:313
  44.5 12.9 %copy-start.1 = (bf16[512,4096]{1,0:T(8,128)(2,1)S(1)}, bf16[512,4096]{1,0:T(8,128)(2,1)}, u32[]{:S(2)}) copy-start(bf16[512,4096]{1,0:T(8,128)(2,1)} %w_ref.1) | copy-start | bytes 12582916
  55.5 3.4 %collective-permute-start.12 = (bf16[256,512]{1,0:T(8,128)(2,1)S(1)}, bf16[256,512]{1,0:T(8,128)(2,1)S(1)}, u32[]{:S(2)}, u32[]{:S(2)}) collective-permute-start(bf16[256,512]{1,0:T(8,128)(2,1)S(1)} %get-tuple-element.47), channel_id=1, source_target_pairs={{0,1},{1,0},{2,3},{3,2},{4,5},{5,4},{6,7},{7,6},{8,9},{9,8},{10,11... | collective-permute-start | bytes 786440 | tf_op jit(solution)/shard_map/ppermute | solution.py:337
  59.6 14.4 %collective-permute-start.16 = (bf16[64,2048]{1,0:T(8,128)(2,1)S(1)}, bf16[64,2048]{1,0:T(8,128)(2,1)S(1)}, u32[]{:S(2)}, u32[]{:S(2)}) collective-permute-start(bf16[64,2048]{1,0:T(8,128)(2,1)S(1)} %get-tuple-element.55), channel_id=1, source_target_pairs={{0,6},{1,7},{2,0},{3,1},{4,2},{5,3},{6,4},{7,5},{8,14},{9,15},{10,... | collective-permute-start | bytes 786440 | tf_op jit(solution)/shard_map/ppermute | solution.py:344
  65.0 13.0 %collective-permute-start.14 = (bf16[64,2048]{1,0:T(8,128)(2,1)S(1)}, bf16[64,2048]{1,0:T(8,128)(2,1)S(1)}, u32[]{:S(2)}, u32[]{:S(2)}) collective-permute-start(bf16[64,2048]{1,0:T(8,128)(2,1)S(1)} %get-tuple-element.52), channel_id=1, source_target_pairs={{0,2},{1,3},{2,4},{3,5},{4,6},{5,7},{6,0},{7,1},{8,10},{9,11},{10,... | collective-permute-start | bytes 786440 | tf_op jit(solution)/shard_map/ppermute | solution.py:341
  66.9 15.0 %collective-permute-start.18 = (bf16[64,2048]{1,0:T(8,128)(2,1)S(1)}, bf16[64,2048]{1,0:T(8,128)(2,1)S(1)}, u32[]{:S(2)}, u32[]{:S(2)}) collective-permute-start(bf16[64,2048]{1,0:T(8,128)(2,1)S(1)} %get-tuple-element.56), channel_id=1, source_target_pairs={{0,2},{1,3},{2,4},{3,5},{4,6},{5,7},{6,0},{7,1},{8,10},{9,11},{10,... | collective-permute-start | bytes 786440 | tf_op jit(solution)/shard_map/ppermute | solution.py:345
  69.6 12.4 %collective-permute-start.13 = (bf16[64,2048]{1,0:T(8,128)(2,1)S(1)}, bf16[64,2048]{1,0:T(8,128)(2,1)S(1)}, u32[]{:S(2)}, u32[]{:S(2)}) collective-permute-start(bf16[64,2048]{1,0:T(8,128)(2,1)S(1)} %get-tuple-element.50), channel_id=1, source_target_pairs={{0,6},{1,7},{2,0},{3,1},{4,2},{5,3},{6,4},{7,5},{8,14},{9,15},{10,... | collective-permute-start | bytes 786440 | tf_op jit(solution)/shard_map/ppermute | solution.py:342
  74.1 11.0 %collective-permute-start.17 = (bf16[64,2048]{1,0:T(8,128)(2,1)S(1)}, bf16[64,2048]{1,0:T(8,128)(2,1)S(1)}, u32[]{:S(2)}, u32[]{:S(2)}) collective-permute-start(bf16[64,2048]{1,0:T(8,128)(2,1)S(1)} %add.58), channel_id=1, source_target_pairs={{0,6},{1,7},{2,0},{3,1},{4,2},{5,3},{6,4},{7,5},{8,14},{9,15},{10,... | collective-permute-start | bytes 786440 | tf_op jit(solution)/shard_map/ppermute | solution.py:347
  78.1 10.2 %collective-permute-start.15 = (bf16[64,2048]{1,0:T(8,128)(2,1)S(1)}, bf16[64,2048]{1,0:T(8,128)(2,1)S(1)}, u32[]{:S(2)}, u32[]{:S(2)}) collective-permute-start(bf16[64,2048]{1,0:T(8,128)(2,1)S(1)} %add.57), channel_id=1, source_target_pairs={{0,2},{1,3},{2,4},{3,5},{4,6},{5,7},{6,0},{7,1},{8,10},{9,11},{10,... | collective-permute-start | bytes 786440 | tf_op jit(solution)/shard_map/ppermute | solution.py:346

commit v11 on v10

--- a/solution.py
+++ b/solution.py
@@ -298,6 +298,10 @@
     return [(i, i // 8 * 8 + (i % 8 + (1 if i % SPAN == SPAN - 1 else 5)) % 8) for i in range(N_CTX)]
 
 
+def two_pairs_on():
+    return [(i, (i // 8 + 4 ^ 1) * 8 + i % 8) for i in range(N_CTX // 2)]
+
+
 def after(x, *others):
     return lax.optimization_barrier((x, others))[0]
 
@@ -329,7 +333,7 @@
     got = after(got, acc).astype(F32)
     start = start + jnp.where(ctx // 8 % 2 == 1, got, 0.0)
     sent = (line + got).astype(BF16)
-    pairs = [send(sent, along_y(2 * k)) for k in (3, 2, 1)]
+    pairs = [send(sent, route) for route in (two_pairs_on(), along_y(6), along_y(2))]
     acc, top = step_call(2, place, gates, queries, kv2, acc, top, sent)
     local, feats = step_call(3, place, gates, queries, kv3, acc, top, sent)
     pairs = [after(part, local) for part in pairs]

time: 89.9 us -> 88.7 us (0.987)
  the two profiles are of different devices: /device:TPU:120 before, /device:TPU:64 now
where the time goes in v11:
time: 88.7 us; the launch traced here: 88.1 us
  starting transfers between devices  62.4 us (70%)
  Pallas kernels  13.2 us (15%)
  waiting for transfers between devices  10.8 us (12%)
  other arithmetic  1.28 us (1%)
    ppermute x11, starting transfers between devices, on_device(): send = lambda x, route: lax.ppermute(x.astype(BF16), 'ctx', route)  39.1 us
    ppermute x1, starting transfers between devices, on_device(): far_b = lax.ppermute(far_b, 'tp', turned(-1))  4.66 us
    ppermute x1, starting transfers between devices, on_device(): left_a = lax.ppermute(left_a, 'tp', turned(-1))  4.4 us
    pallas_call x3, Pallas kernels, step_call(): call(functools.partial(step_kernel, distance), out, (GROUP * ROWS * ROWS...  4.22 us
    ppermute x1, starting transfers between devices, on_device(): left_b = lax.ppermute(left_b + far_b, 'tp', turned(-1))  3.92 us
    ppermute x1, waiting for transfers between devices, on_device(): right_a = lax.ppermute(right_a + far_a, 'tp', turned(1))  3.25 us
    ppermute x1, waiting for transfers between devices, on_device(): left_b = lax.ppermute(left_b + far_b, 'tp', turned(-1))  3.11 us
    ppermute x1, starting transfers between devices, on_device(): right_b = lax.ppermute(right_b, 'tp', turned(1))  2.66 us
  transfers between devices with their start and end apart: 19, of which 5 were waited for; matrix products, arithmetic and copies ran while one was open for 1% of the time, Pallas kernels for 12%

profile of v11, /device:TPU:64, one launch (start us, length us, event | category | flops | bytes accessed | tf_op | source)
XLA Modules:
  0.0 88.1 jit_solution(6504448164525707848)
XLA Ops:
  0.0 1.9 %collective-permute-start.7 = (bf16[512,4096]{1,0:T(8,128)(2,1)}, bf16[512,4096]{1,0:T(8,128)(2,1)}, u32[]{:S(2)}, u32[]{:S(2)}) collective-permute-start(bf16[512,4096]{1,0:T(8,128)(2,1)} %w_ref.1), channel_id=1, source_target_pairs={{0,1},{1,0},{2,3},{3,2},{4,5},{5,4},{6,7},{7,6},{8,9},{9,8},{10,11... | collective-permute-start | bytes 12582920 | tf_op jit(solution)/shard_map/ppermute | solution.py:320
  1.9 1.0 %pad_add_fusion.kv_ref = bf16[512,256]{1,0:T(8,128)(2,1)S(1)} fusion(bf16[512,128]{1,0:T(8,128)(2,1)} %param.7, bf16[512,128]{1,0:T(8,128)(2,1)} %param.6), kind=kLoop, calls=%fused_computation | loop fusion | flops 524288 | bytes 524288 | tf_op jit(solution)/shard_map/add | solution.py:318
  2.9 0.3 shard_map.55
  3.2 6.9 %collective-permute-start.3 = (bf16[144,128]{1,0:T(8,128)(2,1)S(1)}, bf16[144,128]{1,0:T(8,128)(2,1)S(1)}, u32[]{:S(2)}, u32[]{:S(2)}) collective-permute-start(bf16[144,128]{1,0:T(8,128)(2,1)S(1)} %get-tuple-element.32), channel_id=1, source_target_pairs={{0,8},{8,0},{16,24},{24,16},{32,40},{40,32},{48,56},{56,48},{64,72... | collective-permute-start | bytes 110600 | tf_op jit(solution)/shard_map/ppermute | solution.py:317
  10.2 1.9 %collective-permute-start.4 = (bf16[144,128]{1,0:T(8,128)(2,1)S(1)}, bf16[144,128]{1,0:T(8,128)(2,1)S(1)}, u32[]{:S(2)}, u32[]{:S(2)}) collective-permute-start(bf16[144,128]{1,0:T(8,128)(2,1)S(1)} %get-tuple-element.32), channel_id=1, source_target_pairs={{0,16},{8,24},{16,0},{24,8},{32,48},{40,56},{48,32},{56,40},{64,80... | collective-permute-start | bytes 110600 | tf_op jit(solution)/shard_map/ppermute | solution.py:317
  12.1 3.4 %collective-permute-start.5 = (bf16[144,128]{1,0:T(8,128)(2,1)S(1)}, bf16[144,128]{1,0:T(8,128)(2,1)S(1)}, u32[]{:S(2)}, u32[]{:S(2)}) collective-permute-start(bf16[144,128]{1,0:T(8,128)(2,1)S(1)} %get-tuple-element.32), channel_id=1, source_target_pairs={{0,24},{8,16},{16,8},{24,0},{32,56},{40,48},{48,40},{56,32},{64,88... | collective-permute-start | bytes 110600 | tf_op jit(solution)/shard_map/ppermute | solution.py:317
  15.5 2.5 %collective-permute-start.2 = (bf16[512,256]{1,0:T(8,128)(2,1)S(1)}, bf16[512,256]{1,0:T(8,128)(2,1)S(1)}, u32[]{:S(2)}, u32[]{:S(2)}) collective-permute-start(bf16[512,256]{1,0:T(8,128)(2,1)S(1)} %pad_add_fusion.kv_ref), channel_id=1, source_target_pairs={{0,8},{8,16},{16,24},{32,40},{40,48},{48,56},{64,72},{72,80},{80,8... | collective-permute-start | bytes 786440 | tf_op jit(solution)/shard_map/ppermute | solution.py:317
  18.0 0.0 collective-permute-done.3
  18.0 2.8 %collective-permute-start.1 = (bf16[512,256]{1,0:T(8,128)(2,1)S(1)}, bf16[512,256]{1,0:T(8,128)(2,1)S(1)}, u32[]{:S(2)}, u32[]{:S(2)}) collective-permute-start(bf16[512,256]{1,0:T(8,128)(2,1)S(1)} %pad_add_fusion.kv_ref), channel_id=1, source_target_pairs={{0,16},{8,24},{32,48},{40,56},{64,80},{72,88},{96,112},{104,120},{... | collective-permute-start | bytes 786440 | tf_op jit(solution)/shard_map/ppermute | solution.py:317
  20.8 0.0 collective-permute-done.4
  20.8 0.7 collective-permute-start
  21.5 0.0 collective-permute-done.5
  21.5 7.3 %collective-permute-start.6 = (bf16[144,128]{1,0:T(8,128)(2,1)S(1)}, bf16[144,128]{1,0:T(8,128)(2,1)S(1)}, u32[]{:S(2)}, u32[]{:S(2)}) collective-permute-start(bf16[144,128]{1,0:T(8,128)(2,1)S(1)} %get-tuple-element.57), channel_id=1, source_target_pairs={{0,40},{8,48},{16,56},{24,32},{32,8},{40,16},{48,24},{56,0},{64,10... | collective-permute-start | bytes 110600 | tf_op jit(solution)/shard_map/ppermute | solution.py:317
  28.9 0.1 pad_add_fusion.1.place_ref
  28.9 0.0 collective-permute-done.7.w_hbm
  29.0 2.3 %shard_map.56.w_ref = bf16[512,4096]{1,0:T(8,128)(2,1)S(1)} custom-call(bf16[512,4096]{1,0:T(8,128)(2,1)} %collective-permute-done.7.w_hbm), custom_call_target="tpu_custom_call" | custom-call | bytes 8000000 | tf_op jit(solution)/shard_map/pallas_call | solution.py:179
  31.2 2.3 %collective-permute-done.6 = bf16[144,128]{1,0:T(8,128)(2,1)S(1)} collective-permute-done((bf16[144,128]{1,0:T(8,128)(2,1)S(1)}, bf16[144,128]{1,0:T(8,128)(2,1)S(1)}, u32[]{:S(2)}, u32[]{:S(2)}) %collective-permute-start.6) | collective-permute-done | bytes 36896 | tf_op jit(solution)/shard_map/ppermute | solution.py:317
  33.5 3.5 %collective-permute-start.8 = (bf16[144,128]{1,0:T(8,128)(2,1)S(1)}, bf16[144,128]{1,0:T(8,128)(2,1)S(1)}, u32[]{:S(2)}, u32[]{:S(2)}) collective-permute-start(bf16[144,128]{1,0:T(8,128)(2,1)S(1)} %fusion.2.order), channel_id=1, source_target_pairs={{0,64},{8,72},{16,80},{24,88},{32,96},{40,104},{48,112},{56,120},{... | collective-permute-start | bytes 110600 | tf_op jit(solution)/shard_map/ppermute | solution.py:317
  37.0 1.4 %shard_map.57 = (f32[4,512,256]{2,1,0:T(8,128)S(1)}, f32[4,512,128]{2,1,0:T(8,128)S(1)}) custom-call(bf16[512,512]{1,0:T(8,128)(2,1)S(1)} %copy-done, bf16[512,256]{1,0:T(8,128)(2,1)S(1)} %pad_add_fusion.kv_ref, bf16[144,128]{1,0:T(8,128)(2,1)S(1)} %fusion.2.order), custom_call_target="tpu_custom_call" | custom-call | flops 536870912 | bytes 4000000 | tf_op jit(solution)/shard_map/pallas_call | solution.py:101
  38.4 0.0 collective-permute-done.2.kv_ref
  38.5 2.3 %shard_map.58 = (f32[4,512,256]{2,1,0:T(8,128)S(1)}, f32[4,512,128]{2,1,0:T(8,128)S(1)}) custom-call(s32[3]{0:T(128)S(1)} %pad_add_fusion.1.place_ref, f32[4]{0:T(128)S(1)} %copy-done.2, bf16[512,512]{1,0:T(8,128)(2,1)S(1)} %copy-done, bf16[512,256]{1,0:T(8,128)(2,1)S(1)} %collective-permute-done.2.kv_ref, f32[4,512,256]{2,1,0:T(8,128)S(1)} %get-tuple-element.34.acc_in, ...), custom_call_target="tpu_custom_call" | custom-call | flops 536870912 | bytes 4000000 | tf_op jit(solution)/shard_map/pallas_call | solution.py:163
  40.8 0.0 collective-permute-done.8
  40.8 4.5 %collective-permute-start.11 = (bf16[144,128]{1,0:T(8,128)(2,1)S(1)}, bf16[144,128]{1,0:T(8,128)(2,1)S(1)}, u32[]{:S(2)}, u32[]{:S(2)}) collective-permute-start(bf16[144,128]{1,0:T(8,128)(2,1)S(1)} %get-tuple-element.60.order), channel_id=1, source_target_pairs={{0,128},{8,136},{16,144},{24,152},{32,160},{40,168},{48,176},{56,1... | collective-permute-start | bytes 110600 | tf_op jit(solution)/shard_map/ppermute | solution.py:317
  45.3 2.1 %collective-permute-start.10 = (bf16[144,128]{1,0:T(8,128)(2,1)S(1)}, bf16[144,128]{1,0:T(8,128)(2,1)S(1)}, u32[]{:S(2)}, u32[]{:S(2)}) collective-permute-start(bf16[144,128]{1,0:T(8,128)(2,1)S(1)} %get-tuple-element.60.order), channel_id=1, source_target_pairs={{0,384},{8,392},{16,400},{24,408},{32,416},{40,424},{48,432},{56,4... | collective-permute-start | bytes 110600 | tf_op jit(solution)/shard_map/ppermute | solution.py:317
  47.4 3.5 %collective-permute-start.9 = (bf16[144,128]{1,0:T(8,128)(2,1)S(1)}, bf16[144,128]{1,0:T(8,128)(2,1)S(1)}, u32[]{:S(2)}, u32[]{:S(2)}) collective-permute-start(bf16[144,128]{1,0:T(8,128)(2,1)S(1)} %get-tuple-element.60.order), channel_id=1, source_target_pairs={{0,320},{8,328},{16,336},{24,344},{32,352},{40,360},{48,368},{56,3... | collective-permute-start | bytes 110600 | tf_op jit(solution)/shard_map/ppermute | solution.py:317
  50.9 0.0 copy-start.1
  51.0 0.8 shard_map.59
  51.7 1.1 %shard_map.60 = (f32[512,512]{1,0:T(8,128)S(1)}, bf16[512,1024]{1,0:T(8,128)(2,1)S(1)}) custom-call(s32[3]{0:T(128)S(1)} %pad_add_fusion.1.place_ref, f32[4]{0:T(128)S(1)} %copy-done.2, bf16[512,512]{1,0:T(8,128)(2,1)S(1)} %copy-done, bf16[512,256]{1,0:T(8,128)(2,1)S(1)} %collective-permute-done.kv_ref, f32[4,512,256]{2,1,0:T(8,128)S(1)} %get-tuple-element.39.acc_in, ...), custom_call_target="tpu_custom_call" | custom-call | flops 536870912 | bytes 4000000 | tf_op jit(solution)/shard_map/pallas_call | solution.py:163
  52.9 0.0 collective-permute-done.11.mem3
  52.9 0.0 collective-permute-done.10.mem2
  52.9 1.3 %shard_map.61 = (bf16[256,512]{1,0:T(8,128)(2,1)S(1)}, bf16[256,512]{1,0:T(8,128)(2,1)S(1)}) custom-call(s32[3]{0:T(128)S(1)} %pad_add_fusion.1.place_ref, f32[4]{0:T(128)S(1)} %copy-done.2, bf16[512,1024]{1,0:T(8,128)(2,1)S(1)} %get-tuple-element.41.feat_ref, f32[512,512]{1,0:T(8,128)S(1)} %get-tuple-element.42.local_ref, ...), custom_call_target="tpu_custom_call" | custom-call | flops 402653184 | bytes 4000000 | tf_op jit(solution)/shard_map/pallas_call | solution.py:216
  54.2 1.9 %collective-permute-start.12 = (bf16[256,512]{1,0:T(8,128)(2,1)S(1)}, bf16[256,512]{1,0:T(8,128)(2,1)S(1)}, u32[]{:S(2)}, u32[]{:S(2)}) collective-permute-start(bf16[256,512]{1,0:T(8,128)(2,1)S(1)} %get-tuple-element.47), channel_id=1, source_target_pairs={{0,1},{1,0},{2,3},{3,2},{4,5},{5,4},{6,7},{7,6},{8,9},{9,8},{10,11... | collective-permute-start | bytes 786440 | tf_op jit(solution)/shard_map/ppermute | solution.py:341
  56.2 1.3 %shard_map.62.part_ref = f32[256,4096]{1,0:T(8,128)S(1)} custom-call(bf16[256,512]{1,0:T(8,128)(2,1)S(1)} %get-tuple-element.46.keep_ref, bf16[512,4096]{1,0:T(8,128)(2,1)S(1)} %copy-done.1), custom_call_target="tpu_custom_call" | custom-call | flops 1073741824 | bytes 8000000 | tf_op jit(solution)/shard_map/pallas_call | solution.py:235
  57.5 0.2 collective-permute-done.12.got_ref
  57.7 0.7 shard_map.64
  58.4 4.7 %collective-permute-start.16 = (bf16[64,2048]{1,0:T(8,128)(2,1)S(1)}, bf16[64,2048]{1,0:T(8,128)(2,1)S(1)}, u32[]{:S(2)}, u32[]{:S(2)}) collective-permute-start(bf16[64,2048]{1,0:T(8,128)(2,1)S(1)} %get-tuple-element.55), channel_id=1, source_target_pairs={{0,6},{1,7},{2,0},{3,1},{4,2},{5,3},{6,4},{7,5},{8,14},{9,15},{10,... | collective-permute-start | bytes 786440 | tf_op jit(solution)/shard_map/ppermute | solution.py:348
  63.1 0.7 shard_map.63
  63.8 1.9 %collective-permute-start.14 = (bf16[64,2048]{1,0:T(8,128)(2,1)S(1)}, bf16[64,2048]{1,0:T(8,128)(2,1)S(1)}, u32[]{:S(2)}, u32[]{:S(2)}) collective-permute-start(bf16[64,2048]{1,0:T(8,128)(2,1)S(1)} %get-tuple-element.52), channel_id=1, source_target_pairs={{0,2},{1,3},{2,4},{3,5},{4,6},{5,7},{6,0},{7,1},{8,10},{9,11},{10,... | collective-permute-start | bytes 786440 | tf_op jit(solution)/shard_map/ppermute | solution.py:345
  65.7 2.7 %collective-permute-start.18 = (bf16[64,2048]{1,0:T(8,128)(2,1)S(1)}, bf16[64,2048]{1,0:T(8,128)(2,1)S(1)}, u32[]{:S(2)}, u32[]{:S(2)}) collective-permute-start(bf16[64,2048]{1,0:T(8,128)(2,1)S(1)} %get-tuple-element.56), channel_id=1, source_target_pairs={{0,2},{1,3},{2,4},{3,5},{4,6},{5,7},{6,0},{7,1},{8,10},{9,11},{10,... | collective-permute-start | bytes 786440 | tf_op jit(solution)/shard_map/ppermute | solution.py:349
  68.4 4.4 %collective-permute-start.13 = (bf16[64,2048]{1,0:T(8,128)(2,1)S(1)}, bf16[64,2048]{1,0:T(8,128)(2,1)S(1)}, u32[]{:S(2)}, u32[]{:S(2)}) collective-permute-start(bf16[64,2048]{1,0:T(8,128)(2,1)S(1)} %get-tuple-element.50), channel_id=1, source_target_pairs={{0,6},{1,7},{2,0},{3,1},{4,2},{5,3},{6,4},{7,5},{8,14},{9,15},{10,... | collective-permute-start | bytes 786440 | tf_op jit(solution)/shard_map/ppermute | solution.py:346
  72.8 0.1 add.58
  72.9 3.9 %collective-permute-start.17 = (bf16[64,2048]{1,0:T(8,128)(2,1)S(1)}, bf16[64,2048]{1,0:T(8,128)(2,1)S(1)}, u32[]{:S(2)}, u32[]{:S(2)}) collective-permute-start(bf16[64,2048]{1,0:T(8,128)(2,1)S(1)} %add.58), channel_id=1, source_target_pairs={{0,6},{1,7},{2,0},{3,1},{4,2},{5,3},{6,4},{7,5},{8,14},{9,15},{10,... | collective-permute-start | bytes 786440 | tf_op jit(solution)/shard_map/ppermute | solution.py:351
  76.8 0.1 add.57
  76.9 1.9 %collective-permute-start.15 = (bf16[64,2048]{1,0:T(8,128)(2,1)S(1)}, bf16[64,2048]{1,0:T(8,128)(2,1)S(1)}, u32[]{:S(2)}, u32[]{:S(2)}) collective-permute-start(bf16[64,2048]{1,0:T(8,128)(2,1)S(1)} %add.57), channel_id=1, source_target_pairs={{0,2},{1,3},{2,4},{3,5},{4,6},{5,7},{6,0},{7,1},{8,10},{9,11},{10,... | collective-permute-start | bytes 786440 | tf_op jit(solution)/shard_map/ppermute | solution.py:350
  78.8 1.9 %collective-permute-done.18.right_b = bf16[64,2048]{1,0:T(8,128)(2,1)S(1)} collective-permute-done((bf16[64,2048]{1,0:T(8,128)(2,1)S(1)}, bf16[64,2048]{1,0:T(8,128)(2,1)S(1)}, u32[]{:S(2)}, u32[]{:S(2)}) %collective-permute-start.18) | collective-permute-done | bytes 262176 | tf_op jit(solution)/shard_map/ppermute | solution.py:349
  80.8 3.1 %collective-permute-done.17.left_b = bf16[64,2048]{1,0:T(8,128)(2,1)S(1)} collective-permute-done((bf16[64,2048]{1,0:T(8,128)(2,1)S(1)}, bf16[64,2048]{1,0:T(8,128)(2,1)S(1)}, u32[]{:S(2)}, u32[]{:S(2)}) %collective-permute-start.17) | collective-permute-done | bytes 262176 | tf_op jit(solution)/shard_map/ppermute | solution.py:351
  83.9 3.2 %collective-permute-done.15.right_a = bf16[64,2048]{1,0:T(8,128)(2,1)S(1)} collective-permute-done((bf16[64,2048]{1,0:T(8,128)(2,1)S(1)}, bf16[64,2048]{1,0:T(8,128)(2,1)S(1)}, u32[]{:S(2)}, u32[]{:S(2)}) %collective-permute-start.15) | collective-permute-done | bytes 262176 | tf_op jit(solution)/shard_map/ppermute | solution.py:350
  87.1 1.0 %shard_map.65 = bf16[64,4096]{1,0:T(8,128)(2,1)} custom-call(bf16[64,2048]{1,0:T(8,128)(2,1)S(1)} %get-tuple-element.49.own_a, bf16[64,2048]{1,0:T(8,128)(2,1)S(1)} %collective-permute-done.13.left_a, bf16[64,2048]{1,0:T(8,128)(2,1)S(1)} %collective-permute-done.15.right_a, bf16[64,2048]{1,0:T(8,128)(2,1)S(1)} %get-tuple-element.53.own_b, ...), custom_call_target="tpu_custom_call" | custom-call | flops 786432 | bytes 2000000 | tf_op jit(solution)/shard_map/pallas_call | solution.py:276
  (14 shorter events, 0.1 us)
Async XLA Ops:
  0.0 28.9 %collective-permute-start.7 = (bf16[512,4096]{1,0:T(8,128)(2,1)}, bf16[512,4096]{1,0:T(8,128)(2,1)}, u32[]{:S(2)}, u32[]{:S(2)}) collective-permute-start(bf16[512,4096]{1,0:T(8,128)(2,1)} %w_ref.1), channel_id=1, source_target_pairs={{0,1},{1,0},{2,3},{3,2},{4,5},{5,4},{6,7},{7,6},{8,9},{9,8},{10,11... | collective-permute-start | bytes 12582920 | tf_op jit(solution)/shard_map/ppermute | solution.py:320
  3.2 14.8 %collective-permute-start.3 = (bf16[144,128]{1,0:T(8,128)(2,1)S(1)}, bf16[144,128]{1,0:T(8,128)(2,1)S(1)}, u32[]{:S(2)}, u32[]{:S(2)}) collective-permute-start(bf16[144,128]{1,0:T(8,128)(2,1)S(1)} %get-tuple-element.32), channel_id=1, source_target_pairs={{0,8},{8,0},{16,24},{24,16},{32,40},{40,32},{48,56},{56,48},{64,72... | collective-permute-start | bytes 110600 | tf_op jit(solution)/shard_map/ppermute | solution.py:317
  10.2 10.6 %collective-permute-start.4 = (bf16[144,128]{1,0:T(8,128)(2,1)S(1)}, bf16[144,128]{1,0:T(8,128)(2,1)S(1)}, u32[]{:S(2)}, u32[]{:S(2)}) collective-permute-start(bf16[144,128]{1,0:T(8,128)(2,1)S(1)} %get-tuple-element.32), channel_id=1, source_target_pairs={{0,16},{8,24},{16,0},{24,8},{32,48},{40,56},{48,32},{56,40},{64,80... | collective-permute-start | bytes 110600 | tf_op jit(solution)/shard_map/ppermute | solution.py:317
  12.1 9.4 %collective-permute-start.5 = (bf16[144,128]{1,0:T(8,128)(2,1)S(1)}, bf16[144,128]{1,0:T(8,128)(2,1)S(1)}, u32[]{:S(2)}, u32[]{:S(2)}) collective-permute-start(bf16[144,128]{1,0:T(8,128)(2,1)S(1)} %get-tuple-element.32), channel_id=1, source_target_pairs={{0,24},{8,16},{16,8},{24,0},{32,56},{40,48},{48,40},{56,32},{64,88... | collective-permute-start | bytes 110600 | tf_op jit(solution)/shard_map/ppermute | solution.py:317
  15.5 23.0 %collective-permute-start.2 = (bf16[512,256]{1,0:T(8,128)(2,1)S(1)}, bf16[512,256]{1,0:T(8,128)(2,1)S(1)}, u32[]{:S(2)}, u32[]{:S(2)}) collective-permute-start(bf16[512,256]{1,0:T(8,128)(2,1)S(1)} %pad_add_fusion.kv_ref), channel_id=1, source_target_pairs={{0,8},{8,16},{16,24},{32,40},{40,48},{48,56},{64,72},{72,80},{80,8... | collective-permute-start | bytes 786440 | tf_op jit(solution)/shard_map/ppermute | solution.py:317
  18.0 32.9 %collective-permute-start.1 = (bf16[512,256]{1,0:T(8,128)(2,1)S(1)}, bf16[512,256]{1,0:T(8,128)(2,1)S(1)}, u32[]{:S(2)}, u32[]{:S(2)}) collective-permute-start(bf16[512,256]{1,0:T(8,128)(2,1)S(1)} %pad_add_fusion.kv_ref), channel_id=1, source_target_pairs={{0,16},{8,24},{32,48},{40,56},{64,80},{72,88},{96,112},{104,120},{... | collective-permute-start | bytes 786440 | tf_op jit(solution)/shard_map/ppermute | solution.py:317
  20.8 30.9 %collective-permute-start = (bf16[512,256]{1,0:T(8,128)(2,1)S(1)}, bf16[512,256]{1,0:T(8,128)(2,1)S(1)}, u32[]{:S(2)}, u32[]{:S(2)}) collective-permute-start(bf16[512,256]{1,0:T(8,128)(2,1)S(1)} %pad_add_fusion.kv_ref), channel_id=1, source_target_pairs={{0,24},{32,56},{64,88},{96,120},{128,152},{160,184},{192,216},{224... | collective-permute-start | bytes 786440 | tf_op jit(solution)/shard_map/ppermute | solution.py:317
  21.5 12.0 %collective-permute-start.6 = (bf16[144,128]{1,0:T(8,128)(2,1)S(1)}, bf16[144,128]{1,0:T(8,128)(2,1)S(1)}, u32[]{:S(2)}, u32[]{:S(2)}) collective-permute-start(bf16[144,128]{1,0:T(8,128)(2,1)S(1)} %get-tuple-element.57), channel_id=1, source_target_pairs={{0,40},{8,48},{16,56},{24,32},{32,8},{40,16},{48,24},{56,0},{64,10... | collective-permute-start | bytes 110600 | tf_op jit(solution)/shard_map/ppermute | solution.py:317
  28.9 8.1 %copy-start = (bf16[512,512]{1,0:T(8,128)(2,1)S(1)}, bf16[512,512]{1,0:T(8,128)(2,1)}, u32[]{:S(2)}) copy-start(bf16[512,512]{1,0:T(8,128)(2,1)} %q_ref.7) | copy-start | bytes 1572868
  28.9 9.5 %copy-start.2 = (f32[4]{0:T(128)S(1)}, f32[4]{0:T(128)}, u32[]{:S(2)}) copy-start(f32[4]{0:T(128)} %gate_ref.7) | copy-start | bytes 52
  33.5 7.3 %collective-permute-start.8 = (bf16[144,128]{1,0:T(8,128)(2,1)S(1)}, bf16[144,128]{1,0:T(8,128)(2,1)S(1)}, u32[]{:S(2)}, u32[]{:S(2)}) collective-permute-start(bf16[144,128]{1,0:T(8,128)(2,1)S(1)} %fusion.2.order), channel_id=1, source_target_pairs={{0,64},{8,72},{16,80},{24,88},{32,96},{40,104},{48,112},{56,120},{... | collective-permute-start | bytes 110600 | tf_op jit(solution)/shard_map/ppermute | solution.py:317
  40.8 12.1 %collective-permute-start.11 = (bf16[144,128]{1,0:T(8,128)(2,1)S(1)}, bf16[144,128]{1,0:T(8,128)(2,1)S(1)}, u32[]{:S(2)}, u32[]{:S(2)}) collective-permute-start(bf16[144,128]{1,0:T(8,128)(2,1)S(1)} %get-tuple-element.60.order), channel_id=1, source_target_pairs={{0,128},{8,136},{16,144},{24,152},{32,160},{40,168},{48,176},{56,1... | collective-permute-start | bytes 110600 | tf_op jit(solution)/shard_map/ppermute | solution.py:317
  45.3 7.6 %collective-permute-start.10 = (bf16[144,128]{1,0:T(8,128)(2,1)S(1)}, bf16[144,128]{1,0:T(8,128)(2,1)S(1)}, u32[]{:S(2)}, u32[]{:S(2)}) collective-permute-start(bf16[144,128]{1,0:T(8,128)(2,1)S(1)} %get-tuple-element.60.order), channel_id=1, source_target_pairs={{0,384},{8,392},{16,400},{24,408},{32,416},{40,424},{48,432},{56,4... | collective-permute-start | bytes 110600 | tf_op jit(solution)/shard_map/ppermute | solution.py:317
  47.4 5.5 %collective-permute-start.9 = (bf16[144,128]{1,0:T(8,128)(2,1)S(1)}, bf16[144,128]{1,0:T(8,128)(2,1)S(1)}, u32[]{:S(2)}, u32[]{:S(2)}) collective-permute-start(bf16[144,128]{1,0:T(8,128)(2,1)S(1)} %get-tuple-element.60.order), channel_id=1, source_target_pairs={{0,320},{8,328},{16,336},{24,344},{32,352},{40,360},{48,368},{56,3... | collective-permute-start | bytes 110600 | tf_op jit(solution)/shard_map/ppermute | solution.py:317
  50.9 5.2 %copy-start.1 = (bf16[512,4096]{1,0:T(8,128)(2,1)S(1)}, bf16[512,4096]{1,0:T(8,128)(2,1)}, u32[]{:S(2)}) copy-start(bf16[512,4096]{1,0:T(8,128)(2,1)} %w_ref.1) | copy-start | bytes 12582916
  54.2 3.4 %collective-permute-start.12 = (bf16[256,512]{1,0:T(8,128)(2,1)S(1)}, bf16[256,512]{1,0:T(8,128)(2,1)S(1)}, u32[]{:S(2)}, u32[]{:S(2)}) collective-permute-start(bf16[256,512]{1,0:T(8,128)(2,1)S(1)} %get-tuple-element.47), channel_id=1, source_target_pairs={{0,1},{1,0},{2,3},{3,2},{4,5},{5,4},{6,7},{7,6},{8,9},{9,8},{10,11... | collective-permute-start | bytes 786440 | tf_op jit(solution)/shard_map/ppermute | solution.py:341
  58.4 14.4 %collective-permute-start.16 = (bf16[64,2048]{1,0:T(8,128)(2,1)S(1)}, bf16[64,2048]{1,0:T(8,128)(2,1)S(1)}, u32[]{:S(2)}, u32[]{:S(2)}) collective-permute-start(bf16[64,2048]{1,0:T(8,128)(2,1)S(1)} %get-tuple-element.55), channel_id=1, source_target_pairs={{0,6},{1,7},{2,0},{3,1},{4,2},{5,3},{6,4},{7,5},{8,14},{9,15},{10,... | collective-permute-start | bytes 786440 | tf_op jit(solution)/shard_map/ppermute | solution.py:348
  63.8 13.0 %collective-permute-start.14 = (bf16[64,2048]{1,0:T(8,128)(2,1)S(1)}, bf16[64,2048]{1,0:T(8,128)(2,1)S(1)}, u32[]{:S(2)}, u32[]{:S(2)}) collective-permute-start(bf16[64,2048]{1,0:T(8,128)(2,1)S(1)} %get-tuple-element.52), channel_id=1, source_target_pairs={{0,2},{1,3},{2,4},{3,5},{4,6},{5,7},{6,0},{7,1},{8,10},{9,11},{10,... | collective-permute-start | bytes 786440 | tf_op jit(solution)/shard_map/ppermute | solution.py:345
  65.7 15.0 %collective-permute-start.18 = (bf16[64,2048]{1,0:T(8,128)(2,1)S(1)}, bf16[64,2048]{1,0:T(8,128)(2,1)S(1)}, u32[]{:S(2)}, u32[]{:S(2)}) collective-permute-start(bf16[64,2048]{1,0:T(8,128)(2,1)S(1)} %get-tuple-element.56), channel_id=1, source_target_pairs={{0,2},{1,3},{2,4},{3,5},{4,6},{5,7},{6,0},{7,1},{8,10},{9,11},{10,... | collective-permute-start | bytes 786440 | tf_op jit(solution)/shard_map/ppermute | solution.py:349
  68.4 12.4 %collective-permute-start.13 = (bf16[64,2048]{1,0:T(8,128)(2,1)S(1)}, bf16[64,2048]{1,0:T(8,128)(2,1)S(1)}, u32[]{:S(2)}, u32[]{:S(2)}) collective-permute-start(bf16[64,2048]{1,0:T(8,128)(2,1)S(1)} %get-tuple-element.50), channel_id=1, source_target_pairs={{0,6},{1,7},{2,0},{3,1},{4,2},{5,3},{6,4},{7,5},{8,14},{9,15},{10,... | collective-permute-start | bytes 786440 | tf_op jit(solution)/shard_map/ppermute | solution.py:346
  72.9 11.0 %collective-permute-start.17 = (bf16[64,2048]{1,0:T(8,128)(2,1)S(1)}, bf16[64,2048]{1,0:T(8,128)(2,1)S(1)}, u32[]{:S(2)}, u32[]{:S(2)}) collective-permute-start(bf16[64,2048]{1,0:T(8,128)(2,1)S(1)} %add.58), channel_id=1, source_target_pairs={{0,6},{1,7},{2,0},{3,1},{4,2},{5,3},{6,4},{7,5},{8,14},{9,15},{10,... | collective-permute-start | bytes 786440 | tf_op jit(solution)/shard_map/ppermute | solution.py:351
  76.9 10.2 %collective-permute-start.15 = (bf16[64,2048]{1,0:T(8,128)(2,1)S(1)}, bf16[64,2048]{1,0:T(8,128)(2,1)S(1)}, u32[]{:S(2)}, u32[]{:S(2)}) collective-permute-start(bf16[64,2048]{1,0:T(8,128)(2,1)S(1)} %add.57), channel_id=1, source_target_pairs={{0,2},{1,3},{2,4},{3,5},{4,6},{5,7},{6,0},{7,1},{8,10},{9,11},{10,... | collective-permute-start | bytes 786440 | tf_op jit(solution)/shard_map/ppermute | solution.py:350

commit v12 on v11

--- a/solution.py
+++ b/solution.py
@@ -264,11 +264,24 @@
     )(part, got, w)
 
 
-def total_kernel(own_a, left_a, right_a, own_b, left_b, right_b, out_ref):
+def total_kernel(own_a, left_a, right_a, own_b, left_b, right_b, out_hbm, out_ref, sems):
     half = own_a.shape[1]
-    for first, parts in ((0, (own_a, left_a, right_a)), (half, (own_b, left_b, right_b))):
-        total = parts[0][...].astype(F32) + parts[1][...].astype(F32) + parts[2][...].astype(F32)
-        out_ref[:, first : first + half] = total.astype(BF16)
+    tile = half // 2
+    copies = []
+    for i, (parts, at) in enumerate(
+        (parts, at) for parts in ((own_b, left_b, right_b), (own_a, left_a, right_a)) for at in (0, tile)
+    ):
+        cols = slice(at, at + tile)
+        first = at + (half if i < 2 else 0)
+        total = parts[0][:, cols].astype(F32) + parts[1][:, cols].astype(F32) + parts[2][:, cols].astype(F32)
+        out_ref[:, first : first + tile] = total.astype(BF16)
+        copy = pltpu.make_async_copy(
+            out_ref.at[:, first : first + tile], out_hbm.at[:, first : first + tile], sems.at[i]
+        )
+        copy.start()
+        copies.append(copy)
+    for copy in copies:
+        copy.wait()
 
 
 def total_call(*parts):
@@ -278,7 +291,8 @@
         jax.ShapeDtypeStruct((rows, 2 * half), BF16),
         (6 * rows * half, 2000000, 0),
         in_specs=[VM] * 6,
-        out_specs=VM,
+        out_specs=pl.BlockSpec(memory_space=pl.ANY),
+        scratch_shapes=[pltpu.VMEM((rows, 2 * half), BF16), pltpu.SemaphoreType.DMA((4,))],
     )(*parts)
 
 

time: 88.7 us -> 88.6 us (level)
  no operation moved by 1% of the time
where the time goes in v12:
time: 88.6 us; the launch traced here: 88 us
  starting transfers between devices  62.4 us (70%)
  Pallas kernels  13.1 us (15%)
  waiting for transfers between devices  10.8 us (12%)
  other arithmetic  1.28 us (1%)
    ppermute x11, starting transfers between devices, on_device(): send = lambda x, route: lax.ppermute(x.astype(BF16), 'ctx', route)  39.1 us
    ppermute x1, starting transfers between devices, on_device(): far_b = lax.ppermute(far_b, 'tp', turned(-1))  4.66 us
    ppermute x1, starting transfers between devices, on_device(): left_a = lax.ppermute(left_a, 'tp', turned(-1))  4.4 us
    pallas_call x3, Pallas kernels, step_call(): call(functools.partial(step_kernel, distance), out, (GROUP * ROWS * ROWS...  4.22 us
    ppermute x1, starting transfers between devices, on_device(): left_b = lax.ppermute(left_b + far_b, 'tp', turned(-1))  3.92 us
    ppermute x1, waiting for transfers between devices, on_device(): right_a = lax.ppermute(right_a + far_a, 'tp', turned(1))  3.25 us
    ppermute x1, waiting for transfers between devices, on_device(): left_b = lax.ppermute(left_b + far_b, 'tp', turned(-1))  3.11 us
    ppermute x1, starting transfers between devices, on_device(): right_b = lax.ppermute(right_b, 'tp', turned(1))  2.66 us
  transfers between devices with their start and end apart: 19, of which 5 were waited for; matrix products, arithmetic and copies ran while one was open for 1% of the time, Pallas kernels for 12%

profile of v12, /device:TPU:64, one launch (start us, length us, event | category | flops | bytes accessed | tf_op | source)
XLA Modules:
  0.0 88.0 jit_solution(1977133019191997800)
XLA Ops:
  0.0 1.9 %collective-permute-start.7 = (bf16[512,4096]{1,0:T(8,128)(2,1)}, bf16[512,4096]{1,0:T(8,128)(2,1)}, u32[]{:S(2)}, u32[]{:S(2)}) collective-permute-start(bf16[512,4096]{1,0:T(8,128)(2,1)} %w_ref.1), channel_id=1, source_target_pairs={{0,1},{1,0},{2,3},{3,2},{4,5},{5,4},{6,7},{7,6},{8,9},{9,8},{10,11... | collective-permute-start | bytes 12582920 | tf_op jit(solution)/shard_map/ppermute | solution.py:334
  1.9 1.0 %pad_add_fusion.kv_ref = bf16[512,256]{1,0:T(8,128)(2,1)S(1)} fusion(bf16[512,128]{1,0:T(8,128)(2,1)} %param.7, bf16[512,128]{1,0:T(8,128)(2,1)} %param.6), kind=kLoop, calls=%fused_computation | loop fusion | flops 524288 | bytes 524288 | tf_op jit(solution)/shard_map/add | solution.py:332
  2.9 0.3 shard_map.55
  3.2 6.9 %collective-permute-start.3 = (bf16[144,128]{1,0:T(8,128)(2,1)S(1)}, bf16[144,128]{1,0:T(8,128)(2,1)S(1)}, u32[]{:S(2)}, u32[]{:S(2)}) collective-permute-start(bf16[144,128]{1,0:T(8,128)(2,1)S(1)} %get-tuple-element.32), channel_id=1, source_target_pairs={{0,8},{8,0},{16,24},{24,16},{32,40},{40,32},{48,56},{56,48},{64,72... | collective-permute-start | bytes 110600 | tf_op jit(solution)/shard_map/ppermute | solution.py:331
  10.2 1.9 %collective-permute-start.4 = (bf16[144,128]{1,0:T(8,128)(2,1)S(1)}, bf16[144,128]{1,0:T(8,128)(2,1)S(1)}, u32[]{:S(2)}, u32[]{:S(2)}) collective-permute-start(bf16[144,128]{1,0:T(8,128)(2,1)S(1)} %get-tuple-element.32), channel_id=1, source_target_pairs={{0,16},{8,24},{16,0},{24,8},{32,48},{40,56},{48,32},{56,40},{64,80... | collective-permute-start | bytes 110600 | tf_op jit(solution)/shard_map/ppermute | solution.py:331
  12.1 3.4 %collective-permute-start.5 = (bf16[144,128]{1,0:T(8,128)(2,1)S(1)}, bf16[144,128]{1,0:T(8,128)(2,1)S(1)}, u32[]{:S(2)}, u32[]{:S(2)}) collective-permute-start(bf16[144,128]{1,0:T(8,128)(2,1)S(1)} %get-tuple-element.32), channel_id=1, source_target_pairs={{0,24},{8,16},{16,8},{24,0},{32,56},{40,48},{48,40},{56,32},{64,88... | collective-permute-start | bytes 110600 | tf_op jit(solution)/shard_map/ppermute | solution.py:331
  15.5 2.5 %collective-permute-start.2 = (bf16[512,256]{1,0:T(8,128)(2,1)S(1)}, bf16[512,256]{1,0:T(8,128)(2,1)S(1)}, u32[]{:S(2)}, u32[]{:S(2)}) collective-permute-start(bf16[512,256]{1,0:T(8,128)(2,1)S(1)} %pad_add_fusion.kv_ref), channel_id=1, source_target_pairs={{0,8},{8,16},{16,24},{32,40},{40,48},{48,56},{64,72},{72,80},{80,8... | collective-permute-start | bytes 786440 | tf_op jit(solution)/shard_map/ppermute | solution.py:331
  18.0 0.0 collective-permute-done.3
  18.0 2.8 %collective-permute-start.1 = (bf16[512,256]{1,0:T(8,128)(2,1)S(1)}, bf16[512,256]{1,0:T(8,128)(2,1)S(1)}, u32[]{:S(2)}, u32[]{:S(2)}) collective-permute-start(bf16[512,256]{1,0:T(8,128)(2,1)S(1)} %pad_add_fusion.kv_ref), channel_id=1, source_target_pairs={{0,16},{8,24},{32,48},{40,56},{64,80},{72,88},{96,112},{104,120},{... | collective-permute-start | bytes 786440 | tf_op jit(solution)/shard_map/ppermute | solution.py:331
  20.8 0.0 collective-permute-done.4
  20.8 0.7 collective-permute-start
  21.5 7.3 %collective-permute-start.6 = (bf16[144,128]{1,0:T(8,128)(2,1)S(1)}, bf16[144,128]{1,0:T(8,128)(2,1)S(1)}, u32[]{:S(2)}, u32[]{:S(2)}) collective-permute-start(bf16[144,128]{1,0:T(8,128)(2,1)S(1)} %get-tuple-element.57), channel_id=1, source_target_pairs={{0,40},{8,48},{16,56},{24,32},{32,8},{40,16},{48,24},{56,0},{64,10... | collective-permute-start | bytes 110600 | tf_op jit(solution)/shard_map/ppermute | solution.py:331
  28.9 0.1 pad_add_fusion.1.place_ref
  28.9 0.0 collective-permute-done.7.w_hbm
  29.0 2.3 %shard_map.56.w_ref = bf16[512,4096]{1,0:T(8,128)(2,1)S(1)} custom-call(bf16[512,4096]{1,0:T(8,128)(2,1)} %collective-permute-done.7.w_hbm), custom_call_target="tpu_custom_call" | custom-call | bytes 8000000 | tf_op jit(solution)/shard_map/pallas_call | solution.py:179
  31.2 2.3 %collective-permute-done.6 = bf16[144,128]{1,0:T(8,128)(2,1)S(1)} collective-permute-done((bf16[144,128]{1,0:T(8,128)(2,1)S(1)}, bf16[144,128]{1,0:T(8,128)(2,1)S(1)}, u32[]{:S(2)}, u32[]{:S(2)}) %collective-permute-start.6) | collective-permute-done | bytes 36896 | tf_op jit(solution)/shard_map/ppermute | solution.py:331
  33.5 3.5 %collective-permute-start.8 = (bf16[144,128]{1,0:T(8,128)(2,1)S(1)}, bf16[144,128]{1,0:T(8,128)(2,1)S(1)}, u32[]{:S(2)}, u32[]{:S(2)}) collective-permute-start(bf16[144,128]{1,0:T(8,128)(2,1)S(1)} %fusion.2.order), channel_id=1, source_target_pairs={{0,64},{8,72},{16,80},{24,88},{32,96},{40,104},{48,112},{56,120},{... | collective-permute-start | bytes 110600 | tf_op jit(solution)/shard_map/ppermute | solution.py:331
  37.0 1.4 %shard_map.57 = (f32[4,512,256]{2,1,0:T(8,128)S(1)}, f32[4,512,128]{2,1,0:T(8,128)S(1)}) custom-call(bf16[512,512]{1,0:T(8,128)(2,1)S(1)} %copy-done, bf16[512,256]{1,0:T(8,128)(2,1)S(1)} %pad_add_fusion.kv_ref, bf16[144,128]{1,0:T(8,128)(2,1)S(1)} %fusion.2.order), custom_call_target="tpu_custom_call" | custom-call | flops 536870912 | bytes 4000000 | tf_op jit(solution)/shard_map/pallas_call | solution.py:101
  38.5 2.3 %shard_map.58 = (f32[4,512,256]{2,1,0:T(8,128)S(1)}, f32[4,512,128]{2,1,0:T(8,128)S(1)}) custom-call(s32[3]{0:T(128)S(1)} %pad_add_fusion.1.place_ref, f32[4]{0:T(128)S(1)} %copy-done.2, bf16[512,512]{1,0:T(8,128)(2,1)S(1)} %copy-done, bf16[512,256]{1,0:T(8,128)(2,1)S(1)} %collective-permute-done.2.kv_ref, f32[4,512,256]{2,1,0:T(8,128)S(1)} %get-tuple-element.34.acc_in, ...), custom_call_target="tpu_custom_call" | custom-call | flops 536870912 | bytes 4000000 | tf_op jit(solution)/shard_map/pallas_call | solution.py:163
  40.8 0.0 collective-permute-done.8
  40.8 4.5 %collective-permute-start.11 = (bf16[144,128]{1,0:T(8,128)(2,1)S(1)}, bf16[144,128]{1,0:T(8,128)(2,1)S(1)}, u32[]{:S(2)}, u32[]{:S(2)}) collective-permute-start(bf16[144,128]{1,0:T(8,128)(2,1)S(1)} %get-tuple-element.60.order), channel_id=1, source_target_pairs={{0,128},{8,136},{16,144},{24,152},{32,160},{40,168},{48,176},{56,1... | collective-permute-start | bytes 110600 | tf_op jit(solution)/shard_map/ppermute | solution.py:331
  45.3 2.1 %collective-permute-start.10 = (bf16[144,128]{1,0:T(8,128)(2,1)S(1)}, bf16[144,128]{1,0:T(8,128)(2,1)S(1)}, u32[]{:S(2)}, u32[]{:S(2)}) collective-permute-start(bf16[144,128]{1,0:T(8,128)(2,1)S(1)} %get-tuple-element.60.order), channel_id=1, source_target_pairs={{0,384},{8,392},{16,400},{24,408},{32,416},{40,424},{48,432},{56,4... | collective-permute-start | bytes 110600 | tf_op jit(solution)/shard_map/ppermute | solution.py:331
  47.4 3.5 %collective-permute-start.9 = (bf16[144,128]{1,0:T(8,128)(2,1)S(1)}, bf16[144,128]{1,0:T(8,128)(2,1)S(1)}, u32[]{:S(2)}, u32[]{:S(2)}) collective-permute-start(bf16[144,128]{1,0:T(8,128)(2,1)S(1)} %get-tuple-element.60.order), channel_id=1, source_target_pairs={{0,320},{8,328},{16,336},{24,344},{32,352},{40,360},{48,368},{56,3... | collective-permute-start | bytes 110600 | tf_op jit(solution)/shard_map/ppermute | solution.py:331
  50.9 0.0 collective-permute-done.1.kv_ref
  50.9 0.0 copy-start.1
  51.0 0.8 shard_map.59
  51.7 0.0 collective-permute-done.kv_ref
  51.7 1.1 %shard_map.60 = (f32[512,512]{1,0:T(8,128)S(1)}, bf16[512,1024]{1,0:T(8,128)(2,1)S(1)}) custom-call(s32[3]{0:T(128)S(1)} %pad_add_fusion.1.place_ref, f32[4]{0:T(128)S(1)} %copy-done.2, bf16[512,512]{1,0:T(8,128)(2,1)S(1)} %copy-done, bf16[512,256]{1,0:T(8,128)(2,1)S(1)} %collective-permute-done.kv_ref, f32[4,512,256]{2,1,0:T(8,128)S(1)} %get-tuple-element.39.acc_in, ...), custom_call_target="tpu_custom_call" | custom-call | flops 536870912 | bytes 4000000 | tf_op jit(solution)/shard_map/pallas_call | solution.py:163
  52.9 0.0 collective-permute-done.10.mem2
  52.9 0.0 collective-permute-done.9.mem1
  52.9 1.3 %shard_map.61 = (bf16[256,512]{1,0:T(8,128)(2,1)S(1)}, bf16[256,512]{1,0:T(8,128)(2,1)S(1)}) custom-call(s32[3]{0:T(128)S(1)} %pad_add_fusion.1.place_ref, f32[4]{0:T(128)S(1)} %copy-done.2, bf16[512,1024]{1,0:T(8,128)(2,1)S(1)} %get-tuple-element.41.feat_ref, f32[512,512]{1,0:T(8,128)S(1)} %get-tuple-element.42.local_ref, ...), custom_call_target="tpu_custom_call" | custom-call | flops 402653184 | bytes 4000000 | tf_op jit(solution)/shard_map/pallas_call | solution.py:216
  54.2 1.9 %collective-permute-start.12 = (bf16[256,512]{1,0:T(8,128)(2,1)S(1)}, bf16[256,512]{1,0:T(8,128)(2,1)S(1)}, u32[]{:S(2)}, u32[]{:S(2)}) collective-permute-start(bf16[256,512]{1,0:T(8,128)(2,1)S(1)} %get-tuple-element.47), channel_id=1, source_target_pairs={{0,1},{1,0},{2,3},{3,2},{4,5},{5,4},{6,7},{7,6},{8,9},{9,8},{10,11... | collective-permute-start | bytes 786440 | tf_op jit(solution)/shard_map/ppermute | solution.py:355
  56.2 1.3 %shard_map.62.part_ref = f32[256,4096]{1,0:T(8,128)S(1)} custom-call(bf16[256,512]{1,0:T(8,128)(2,1)S(1)} %get-tuple-element.46.keep_ref, bf16[512,4096]{1,0:T(8,128)(2,1)S(1)} %copy-done.1), custom_call_target="tpu_custom_call" | custom-call | flops 1073741824 | bytes 8000000 | tf_op jit(solution)/shard_map/pallas_call | solution.py:235
  57.5 0.2 collective-permute-done.12.got_ref
  57.7 0.7 shard_map.64
  58.4 4.7 %collective-permute-start.16 = (bf16[64,2048]{1,0:T(8,128)(2,1)S(1)}, bf16[64,2048]{1,0:T(8,128)(2,1)S(1)}, u32[]{:S(2)}, u32[]{:S(2)}) collective-permute-start(bf16[64,2048]{1,0:T(8,128)(2,1)S(1)} %get-tuple-element.55), channel_id=1, source_target_pairs={{0,6},{1,7},{2,0},{3,1},{4,2},{5,3},{6,4},{7,5},{8,14},{9,15},{10,... | collective-permute-start | bytes 786440 | tf_op jit(solution)/shard_map/ppermute | solution.py:362
  63.1 0.7 shard_map.63
  63.8 1.9 %collective-permute-start.14 = (bf16[64,2048]{1,0:T(8,128)(2,1)S(1)}, bf16[64,2048]{1,0:T(8,128)(2,1)S(1)}, u32[]{:S(2)}, u32[]{:S(2)}) collective-permute-start(bf16[64,2048]{1,0:T(8,128)(2,1)S(1)} %get-tuple-element.52), channel_id=1, source_target_pairs={{0,2},{1,3},{2,4},{3,5},{4,6},{5,7},{6,0},{7,1},{8,10},{9,11},{10,... | collective-permute-start | bytes 786440 | tf_op jit(solution)/shard_map/ppermute | solution.py:359
  65.7 2.7 %collective-permute-start.18 = (bf16[64,2048]{1,0:T(8,128)(2,1)S(1)}, bf16[64,2048]{1,0:T(8,128)(2,1)S(1)}, u32[]{:S(2)}, u32[]{:S(2)}) collective-permute-start(bf16[64,2048]{1,0:T(8,128)(2,1)S(1)} %get-tuple-element.56), channel_id=1, source_target_pairs={{0,2},{1,3},{2,4},{3,5},{4,6},{5,7},{6,0},{7,1},{8,10},{9,11},{10,... | collective-permute-start | bytes 786440 | tf_op jit(solution)/shard_map/ppermute | solution.py:363
  68.4 4.4 %collective-permute-start.13 = (bf16[64,2048]{1,0:T(8,128)(2,1)S(1)}, bf16[64,2048]{1,0:T(8,128)(2,1)S(1)}, u32[]{:S(2)}, u32[]{:S(2)}) collective-permute-start(bf16[64,2048]{1,0:T(8,128)(2,1)S(1)} %get-tuple-element.50), channel_id=1, source_target_pairs={{0,6},{1,7},{2,0},{3,1},{4,2},{5,3},{6,4},{7,5},{8,14},{9,15},{10,... | collective-permute-start | bytes 786440 | tf_op jit(solution)/shard_map/ppermute | solution.py:360
  72.8 0.1 add.58
  72.9 3.9 %collective-permute-start.17 = (bf16[64,2048]{1,0:T(8,128)(2,1)S(1)}, bf16[64,2048]{1,0:T(8,128)(2,1)S(1)}, u32[]{:S(2)}, u32[]{:S(2)}) collective-permute-start(bf16[64,2048]{1,0:T(8,128)(2,1)S(1)} %add.58), channel_id=1, source_target_pairs={{0,6},{1,7},{2,0},{3,1},{4,2},{5,3},{6,4},{7,5},{8,14},{9,15},{10,... | collective-permute-start | bytes 786440 | tf_op jit(solution)/shard_map/ppermute | solution.py:365
  76.8 0.1 add.57
  76.9 1.9 %collective-permute-start.15 = (bf16[64,2048]{1,0:T(8,128)(2,1)S(1)}, bf16[64,2048]{1,0:T(8,128)(2,1)S(1)}, u32[]{:S(2)}, u32[]{:S(2)}) collective-permute-start(bf16[64,2048]{1,0:T(8,128)(2,1)S(1)} %add.57), channel_id=1, source_target_pairs={{0,2},{1,3},{2,4},{3,5},{4,6},{5,7},{6,0},{7,1},{8,10},{9,11},{10,... | collective-permute-start | bytes 786440 | tf_op jit(solution)/shard_map/ppermute | solution.py:364
  78.8 1.9 %collective-permute-done.18.right_b = bf16[64,2048]{1,0:T(8,128)(2,1)S(1)} collective-permute-done((bf16[64,2048]{1,0:T(8,128)(2,1)S(1)}, bf16[64,2048]{1,0:T(8,128)(2,1)S(1)}, u32[]{:S(2)}, u32[]{:S(2)}) %collective-permute-start.18) | collective-permute-done | bytes 262176 | tf_op jit(solution)/shard_map/ppermute | solution.py:363
  80.8 3.1 %collective-permute-done.17.left_b = bf16[64,2048]{1,0:T(8,128)(2,1)S(1)} collective-permute-done((bf16[64,2048]{1,0:T(8,128)(2,1)S(1)}, bf16[64,2048]{1,0:T(8,128)(2,1)S(1)}, u32[]{:S(2)}, u32[]{:S(2)}) %collective-permute-start.17) | collective-permute-done | bytes 262176 | tf_op jit(solution)/shard_map/ppermute | solution.py:365
  83.9 3.2 %collective-permute-done.15.right_a = bf16[64,2048]{1,0:T(8,128)(2,1)S(1)} collective-permute-done((bf16[64,2048]{1,0:T(8,128)(2,1)S(1)}, bf16[64,2048]{1,0:T(8,128)(2,1)S(1)}, u32[]{:S(2)}, u32[]{:S(2)}) %collective-permute-start.15) | collective-permute-done | bytes 262176 | tf_op jit(solution)/shard_map/ppermute | solution.py:364
  87.1 0.9 shard_map.65
  (14 shorter events, 0.1 us)
Async XLA Ops:
  0.0 28.9 %collective-permute-start.7 = (bf16[512,4096]{1,0:T(8,128)(2,1)}, bf16[512,4096]{1,0:T(8,128)(2,1)}, u32[]{:S(2)}, u32[]{:S(2)}) collective-permute-start(bf16[512,4096]{1,0:T(8,128)(2,1)} %w_ref.1), channel_id=1, source_target_pairs={{0,1},{1,0},{2,3},{3,2},{4,5},{5,4},{6,7},{7,6},{8,9},{9,8},{10,11... | collective-permute-start | bytes 12582920 | tf_op jit(solution)/shard_map/ppermute | solution.py:334
  3.2 14.8 %collective-permute-start.3 = (bf16[144,128]{1,0:T(8,128)(2,1)S(1)}, bf16[144,128]{1,0:T(8,128)(2,1)S(1)}, u32[]{:S(2)}, u32[]{:S(2)}) collective-permute-start(bf16[144,128]{1,0:T(8,128)(2,1)S(1)} %get-tuple-element.32), channel_id=1, source_target_pairs={{0,8},{8,0},{16,24},{24,16},{32,40},{40,32},{48,56},{56,48},{64,72... | collective-permute-start | bytes 110600 | tf_op jit(solution)/shard_map/ppermute | solution.py:331
  10.2 10.6 %collective-permute-start.4 = (bf16[144,128]{1,0:T(8,128)(2,1)S(1)}, bf16[144,128]{1,0:T(8,128)(2,1)S(1)}, u32[]{:S(2)}, u32[]{:S(2)}) collective-permute-start(bf16[144,128]{1,0:T(8,128)(2,1)S(1)} %get-tuple-element.32), channel_id=1, source_target_pairs={{0,16},{8,24},{16,0},{24,8},{32,48},{40,56},{48,32},{56,40},{64,80... | collective-permute-start | bytes 110600 | tf_op jit(solution)/shard_map/ppermute | solution.py:331
  12.1 9.4 %collective-permute-start.5 = (bf16[144,128]{1,0:T(8,128)(2,1)S(1)}, bf16[144,128]{1,0:T(8,128)(2,1)S(1)}, u32[]{:S(2)}, u32[]{:S(2)}) collective-permute-start(bf16[144,128]{1,0:T(8,128)(2,1)S(1)} %get-tuple-element.32), channel_id=1, source_target_pairs={{0,24},{8,16},{16,8},{24,0},{32,56},{40,48},{48,40},{56,32},{64,88... | collective-permute-start | bytes 110600 | tf_op jit(solution)/shard_map/ppermute | solution.py:331
  15.5 23.0 %collective-permute-start.2 = (bf16[512,256]{1,0:T(8,128)(2,1)S(1)}, bf16[512,256]{1,0:T(8,128)(2,1)S(1)}, u32[]{:S(2)}, u32[]{:S(2)}) collective-permute-start(bf16[512,256]{1,0:T(8,128)(2,1)S(1)} %pad_add_fusion.kv_ref), channel_id=1, source_target_pairs={{0,8},{8,16},{16,24},{32,40},{40,48},{48,56},{64,72},{72,80},{80,8... | collective-permute-start | bytes 786440 | tf_op jit(solution)/shard_map/ppermute | solution.py:331
  18.0 32.9 %collective-permute-start.1 = (bf16[512,256]{1,0:T(8,128)(2,1)S(1)}, bf16[512,256]{1,0:T(8,128)(2,1)S(1)}, u32[]{:S(2)}, u32[]{:S(2)}) collective-permute-start(bf16[512,256]{1,0:T(8,128)(2,1)S(1)} %pad_add_fusion.kv_ref), channel_id=1, source_target_pairs={{0,16},{8,24},{32,48},{40,56},{64,80},{72,88},{96,112},{104,120},{... | collective-permute-start | bytes 786440 | tf_op jit(solution)/shard_map/ppermute | solution.py:331
  20.8 30.9 %collective-permute-start = (bf16[512,256]{1,0:T(8,128)(2,1)S(1)}, bf16[512,256]{1,0:T(8,128)(2,1)S(1)}, u32[]{:S(2)}, u32[]{:S(2)}) collective-permute-start(bf16[512,256]{1,0:T(8,128)(2,1)S(1)} %pad_add_fusion.kv_ref), channel_id=1, source_target_pairs={{0,24},{32,56},{64,88},{96,120},{128,152},{160,184},{192,216},{224... | collective-permute-start | bytes 786440 | tf_op jit(solution)/shard_map/ppermute | solution.py:331
  21.5 12.0 %collective-permute-start.6 = (bf16[144,128]{1,0:T(8,128)(2,1)S(1)}, bf16[144,128]{1,0:T(8,128)(2,1)S(1)}, u32[]{:S(2)}, u32[]{:S(2)}) collective-permute-start(bf16[144,128]{1,0:T(8,128)(2,1)S(1)} %get-tuple-element.57), channel_id=1, source_target_pairs={{0,40},{8,48},{16,56},{24,32},{32,8},{40,16},{48,24},{56,0},{64,10... | collective-permute-start | bytes 110600 | tf_op jit(solution)/shard_map/ppermute | solution.py:331
  28.9 8.1 %copy-start = (bf16[512,512]{1,0:T(8,128)(2,1)S(1)}, bf16[512,512]{1,0:T(8,128)(2,1)}, u32[]{:S(2)}) copy-start(bf16[512,512]{1,0:T(8,128)(2,1)} %q_ref.7) | copy-start | bytes 1572868
  28.9 9.5 %copy-start.2 = (f32[4]{0:T(128)S(1)}, f32[4]{0:T(128)}, u32[]{:S(2)}) copy-start(f32[4]{0:T(128)} %gate_ref.7) | copy-start | bytes 52
  33.5 7.3 %collective-permute-start.8 = (bf16[144,128]{1,0:T(8,128)(2,1)S(1)}, bf16[144,128]{1,0:T(8,128)(2,1)S(1)}, u32[]{:S(2)}, u32[]{:S(2)}) collective-permute-start(bf16[144,128]{1,0:T(8,128)(2,1)S(1)} %fusion.2.order), channel_id=1, source_target_pairs={{0,64},{8,72},{16,80},{24,88},{32,96},{40,104},{48,112},{56,120},{... | collective-permute-start | bytes 110600 | tf_op jit(solution)/shard_map/ppermute | solution.py:331
  40.8 12.1 %collective-permute-start.11 = (bf16[144,128]{1,0:T(8,128)(2,1)S(1)}, bf16[144,128]{1,0:T(8,128)(2,1)S(1)}, u32[]{:S(2)}, u32[]{:S(2)}) collective-permute-start(bf16[144,128]{1,0:T(8,128)(2,1)S(1)} %get-tuple-element.60.order), channel_id=1, source_target_pairs={{0,128},{8,136},{16,144},{24,152},{32,160},{40,168},{48,176},{56,1... | collective-permute-start | bytes 110600 | tf_op jit(solution)/shard_map/ppermute | solution.py:331
  45.3 7.6 %collective-permute-start.10 = (bf16[144,128]{1,0:T(8,128)(2,1)S(1)}, bf16[144,128]{1,0:T(8,128)(2,1)S(1)}, u32[]{:S(2)}, u32[]{:S(2)}) collective-permute-start(bf16[144,128]{1,0:T(8,128)(2,1)S(1)} %get-tuple-element.60.order), channel_id=1, source_target_pairs={{0,384},{8,392},{16,400},{24,408},{32,416},{40,424},{48,432},{56,4... | collective-permute-start | bytes 110600 | tf_op jit(solution)/shard_map/ppermute | solution.py:331
  47.4 5.5 %collective-permute-start.9 = (bf16[144,128]{1,0:T(8,128)(2,1)S(1)}, bf16[144,128]{1,0:T(8,128)(2,1)S(1)}, u32[]{:S(2)}, u32[]{:S(2)}) collective-permute-start(bf16[144,128]{1,0:T(8,128)(2,1)S(1)} %get-tuple-element.60.order), channel_id=1, source_target_pairs={{0,320},{8,328},{16,336},{24,344},{32,352},{40,360},{48,368},{56,3... | collective-permute-start | bytes 110600 | tf_op jit(solution)/shard_map/ppermute | solution.py:331
  50.9 5.2 %copy-start.1 = (bf16[512,4096]{1,0:T(8,128)(2,1)S(1)}, bf16[512,4096]{1,0:T(8,128)(2,1)}, u32[]{:S(2)}) copy-start(bf16[512,4096]{1,0:T(8,128)(2,1)} %w_ref.1) | copy-start | bytes 12582916
  54.2 3.4 %collective-permute-start.12 = (bf16[256,512]{1,0:T(8,128)(2,1)S(1)}, bf16[256,512]{1,0:T(8,128)(2,1)S(1)}, u32[]{:S(2)}, u32[]{:S(2)}) collective-permute-start(bf16[256,512]{1,0:T(8,128)(2,1)S(1)} %get-tuple-element.47), channel_id=1, source_target_pairs={{0,1},{1,0},{2,3},{3,2},{4,5},{5,4},{6,7},{7,6},{8,9},{9,8},{10,11... | collective-permute-start | bytes 786440 | tf_op jit(solution)/shard_map/ppermute | solution.py:355
  58.4 14.4 %collective-permute-start.16 = (bf16[64,2048]{1,0:T(8,128)(2,1)S(1)}, bf16[64,2048]{1,0:T(8,128)(2,1)S(1)}, u32[]{:S(2)}, u32[]{:S(2)}) collective-permute-start(bf16[64,2048]{1,0:T(8,128)(2,1)S(1)} %get-tuple-element.55), channel_id=1, source_target_pairs={{0,6},{1,7},{2,0},{3,1},{4,2},{5,3},{6,4},{7,5},{8,14},{9,15},{10,... | collective-permute-start | bytes 786440 | tf_op jit(solution)/shard_map/ppermute | solution.py:362
  63.8 13.0 %collective-permute-start.14 = (bf16[64,2048]{1,0:T(8,128)(2,1)S(1)}, bf16[64,2048]{1,0:T(8,128)(2,1)S(1)}, u32[]{:S(2)}, u32[]{:S(2)}) collective-permute-start(bf16[64,2048]{1,0:T(8,128)(2,1)S(1)} %get-tuple-element.52), channel_id=1, source_target_pairs={{0,2},{1,3},{2,4},{3,5},{4,6},{5,7},{6,0},{7,1},{8,10},{9,11},{10,... | collective-permute-start | bytes 786440 | tf_op jit(solution)/shard_map/ppermute | solution.py:359
  65.7 15.0 %collective-permute-start.18 = (bf16[64,2048]{1,0:T(8,128)(2,1)S(1)}, bf16[64,2048]{1,0:T(8,128)(2,1)S(1)}, u32[]{:S(2)}, u32[]{:S(2)}) collective-permute-start(bf16[64,2048]{1,0:T(8,128)(2,1)S(1)} %get-tuple-element.56), channel_id=1, source_target_pairs={{0,2},{1,3},{2,4},{3,5},{4,6},{5,7},{6,0},{7,1},{8,10},{9,11},{10,... | collective-permute-start | bytes 786440 | tf_op jit(solution)/shard_map/ppermute | solution.py:363
  68.4 12.4 %collective-permute-start.13 = (bf16[64,2048]{1,0:T(8,128)(2,1)S(1)}, bf16[64,2048]{1,0:T(8,128)(2,1)S(1)}, u32[]{:S(2)}, u32[]{:S(2)}) collective-permute-start(bf16[64,2048]{1,0:T(8,128)(2,1)S(1)} %get-tuple-element.50), channel_id=1, source_target_pairs={{0,6},{1,7},{2,0},{3,1},{4,2},{5,3},{6,4},{7,5},{8,14},{9,15},{10,... | collective-permute-start | bytes 786440 | tf_op jit(solution)/shard_map/ppermute | solution.py:360
  72.9 11.0 %collective-permute-start.17 = (bf16[64,2048]{1,0:T(8,128)(2,1)S(1)}, bf16[64,2048]{1,0:T(8,128)(2,1)S(1)}, u32[]{:S(2)}, u32[]{:S(2)}) collective-permute-start(bf16[64,2048]{1,0:T(8,128)(2,1)S(1)} %add.58), channel_id=1, source_target_pairs={{0,6},{1,7},{2,0},{3,1},{4,2},{5,3},{6,4},{7,5},{8,14},{9,15},{10,... | collective-permute-start | bytes 786440 | tf_op jit(solution)/shard_map/ppermute | solution.py:365
  76.9 10.2 %collective-permute-start.15 = (bf16[64,2048]{1,0:T(8,128)(2,1)S(1)}, bf16[64,2048]{1,0:T(8,128)(2,1)S(1)}, u32[]{:S(2)}, u32[]{:S(2)}) collective-permute-start(bf16[64,2048]{1,0:T(8,128)(2,1)S(1)} %add.57), channel_id=1, source_target_pairs={{0,2},{1,3},{2,4},{3,5},{4,6},{5,7},{6,0},{7,1},{8,10},{9,11},{10,... | collective-permute-start | bytes 786440 | tf_op jit(solution)/shard_map/ppermute | solution.py:364
